TPU v7x, 32 devices: a whole 2x2x4 slice. The times are simulated.
32 devices in a mesh: dp: 16 (over z, y, core), query: 2 (over x).
Axes of the slice: x: 2, y: 2, z: 4, core: 2. Of those that a mesh axis runs over, the one named last changes fastest.
Arguments:
- tokens: bfloat16 [32, 512, 1280], P(('dp', 'query')), may hold values from -6 to 6
- cell_lengths: int32 [32, 4], P(('dp', 'query')), may hold values from 1 to 256, 512 in all within a row
- out_cotangent: bfloat16 [32, 512, 1280], P(('dp', 'query')), may hold values from -6 to 6
- ln_gains: float32 [2, 1280], replicated, may hold values from 0.5 to 1.5
- ln_biases: float32 [2, 1280], replicated, may hold values from -1.2 to 1.2
- proj_biases: float32 [4, 1280], replicated, may hold values from -1.2 to 1.2
- ff_biases: float32 [2, 5120], replicated, may hold values from -3 to 3
- w_qkv: bfloat16 [1280, 3840], P('query'), may hold values from -0.15625 to 0.15625
- w_out: bfloat16 [1280, 1280], P('query'), may hold values from -0.3125 to 0.3125
- w_up: bfloat16 [1280, 5120], P('query'), may hold values from -0.15625 to 0.15625
- w_down: bfloat16 [5120, 1280], P('query'), may hold values from -0.078125 to 0.078125
- dec_cell: bfloat16 [1280, 5120], P('query'), may hold values from -0.125 to 0.125
- dec_gene: bfloat16 [1280, 5120], P('query'), may hold values from -0.125 to 0.125
- dec_out: bfloat16 [5120], replicated, may hold values from -0.3125 to 0.3125
- gene_table: bfloat16 [1024, 1280], P('query'), may hold values from -6 to 6
- query_ids: int32 [128, 16], P('dp', 'query'), may hold values from 0 to 1023
- labels: int32 [128, 16], P('dp', 'query'), may hold values 0 or 1
Outputs:
- encoded: float32 [32, 512, 1280], P(('dp', 'query'))
- grad_tokens: float32 [32, 512, 1280], P(('dp', 'query'))
- grad_ln_gains: float32 [2, 1280], P(None, ('dp', 'query'))
- grad_ln_biases: float32 [2, 1280], P(None, ('dp', 'query'))
- grad_proj_biases: float32 [4, 1280], P(None, ('dp', 'query'))
- grad_ff_biases: float32 [2, 5120], P(None, ('dp', 'query'))
- grad_w_qkv: float32 [1280, 3840], P(('dp', 'query'))
- grad_w_out: float32 [1280, 1280], P(('dp', 'query'))
- grad_w_up: float32 [1280, 5120], P(('dp', 'query'))
- grad_w_down: float32 [5120, 1280], P(('dp', 'query'))
- grad_dec_cell: float32 [1280, 5120], P(('dp', 'query'))
- grad_dec_gene: float32 [1280, 5120], P(('dp', 'query'))
- grad_dec_out: float32 [5120], P(('dp', 'query'))
- grad_gene_table: float32 [1024, 1280], P(('dp', 'query'))
Inputs may be any that keep to these rules, and one draw needn't show every extreme that they name: `cell_lengths`: the 4 cells of a row fill its 512 positions.
All inputs are finite; a program needn't handle non-finite values. No bound on the sum of `labels` on one device may be relied on, other than what follows from the above.
Results may differ from a plain program's by a relative error of at most 0.02.
Values may be sent and summed in bfloat16 or wider, within the bound.
No kernel may reach another device: no remote copies, remote signals or barrier semaphores. Data moves between devices by JAX's collectives and lax.ppermute only.
A program may use at most 576 MiB of HBM per device.

v0:
```python
import math

import jax
import jax.numpy as jnp
from jax import lax
from jax.sharding import PartitionSpec as P

D = 1280
HEADS = 20
HEAD_DIM = 64
FF = 5120
ROW_LEN = 512
CELLS_ROW = 4
GENES = 1024


EPSILON = 1e-05
HIGHEST = lax.Precision.HIGHEST


def layer_norm(values_in, scale_row, offset_row):
    center = values_in - jnp.mean(values_in, axis=-1, keepdims=True)
    spread = jnp.mean(center * center, axis=-1, keepdims=True)
    return center * lax.rsqrt(spread + EPSILON) * scale_row + offset_row


def smooth_gate(values_in):
    return jax.nn.gelu(values_in, approximate=False)


def cell_layout(lengths):
    cell_ends = jnp.cumsum(lengths, axis=-1, dtype=jnp.int32)
    starts = cell_ends - lengths
    places = jnp.arange(ROW_LEN, dtype=jnp.int32)
    segment = jnp.sum(
        (places[None, :, None] >= cell_ends[:, None, :]).astype(jnp.int32), axis=-1, dtype=jnp.int32
    )
    return (starts, segment)


def split_heads(qkv_row):
    queries = qkv_row[:, :D].reshape(ROW_LEN, HEADS, HEAD_DIM)
    keys_in = qkv_row[:, D : 2 * D].reshape(ROW_LEN, HEADS, HEAD_DIM)
    values_in = qkv_row[:, 2 * D :].reshape(ROW_LEN, HEADS, HEAD_DIM)
    return (queries, keys_in, values_in)


def row_scores(queries, keys_in, segment_row):
    scores = jnp.einsum("qhd,khd->hqk", queries, keys_in, preferred_element_type=jnp.float32) * (
        1.0 / math.sqrt(HEAD_DIM)
    )
    same_cell = segment_row[:, None] == segment_row[None, :]
    return jnp.where(same_cell[None], scores, -1e30)


def attend(member):
    qkv_row, segment_row = member
    queries, keys_in, values_in = split_heads(qkv_row)
    scores = row_scores(queries, keys_in, segment_row)
    highest_score = jnp.max(scores, axis=-1, keepdims=True)
    weights = jnp.exp(scores - highest_score)
    weight_sum = jnp.sum(weights, axis=-1, keepdims=True)
    attention = (weights / weight_sum).astype(jnp.bfloat16)
    mixed = jnp.einsum(
        "hqk,khd->qhd", attention, values_in, preferred_element_type=jnp.float32
    ).astype(jnp.bfloat16)
    return (mixed.reshape(ROW_LEN, D), (highest_score + jnp.log(weight_sum))[:, :, 0])


def attend_back(member):
    qkv_row, segment_row, log_total, grad_mixed = member
    queries, keys_in, values_in = split_heads(qkv_row)
    scores = row_scores(queries, keys_in, segment_row)
    attention = jnp.exp(scores - log_total[:, :, None])
    grad_heads = grad_mixed.reshape(ROW_LEN, HEADS, HEAD_DIM)
    grad_probs = jnp.einsum(
        "qhd,khd->hqk", grad_heads, values_in, preferred_element_type=jnp.float32
    )
    grad_scores = (
        attention * (grad_probs - jnp.sum(attention * grad_probs, axis=-1, keepdims=True))
    ).astype(jnp.bfloat16)
    scale_factor = 1.0 / math.sqrt(HEAD_DIM)
    grad_query = (
        jnp.einsum("hqk,khd->qhd", grad_scores, keys_in, preferred_element_type=jnp.float32)
        * scale_factor
    )
    grad_keys = (
        jnp.einsum("hqk,qhd->khd", grad_scores, queries, preferred_element_type=jnp.float32)
        * scale_factor
    )
    grad_values = jnp.einsum(
        "hqk,qhd->khd",
        attention.astype(jnp.bfloat16),
        grad_heads,
        preferred_element_type=jnp.float32,
    )
    return jnp.concatenate(
        [
            grad_query.reshape(ROW_LEN, D),
            grad_keys.reshape(ROW_LEN, D),
            grad_values.reshape(ROW_LEN, D),
        ],
        axis=1,
    )


def owned_cols(values_in, dp_count, query_count, place):
    width = values_in.shape[1] // (dp_count * query_count)
    shaped = values_in.reshape(values_in.shape[0], dp_count, query_count, width)
    return lax.dynamic_index_in_dim(shaped, place, axis=2, keepdims=False)


def owned_term(left, right, dp_count, query_count, place):
    return jnp.einsum(
        "ndr,ne->dre",
        owned_cols(left, dp_count, query_count, place),
        right,
        preferred_element_type=jnp.float32,
    )


def owner_blocks(values_in, dp_count, query_count):
    width = values_in.shape[0] // (dp_count * query_count)
    return values_in.reshape(dp_count, query_count, width, values_in.shape[1])


def shards(
    tokens,
    cell_lengths,
    out_cotangent,
    ln_gains,
    ln_biases,
    proj_biases,
    ff_biases,
    w_qkv,
    w_out,
    w_up,
    w_down,
    dec_cell,
    dec_gene,
    dec_out,
    gene_table,
    query_ids,
    labels,
):
    row_count = tokens.shape[0]
    token_count = row_count * ROW_LEN
    dp_count = lax.axis_size("dp")
    query_count = lax.axis_size("query")
    place = lax.axis_index("query")
    starts, segment = cell_layout(cell_lengths)
    gathered = (
        lax.all_gather(w_qkv, "query", axis=0, tiled=True),
        lax.all_gather(w_out, "query", axis=0, tiled=True),
        lax.all_gather(w_up, "query", axis=0, tiled=True),
        lax.all_gather(w_down, "query", axis=0, tiled=True),
        lax.all_gather(dec_cell, "query", axis=0, tiled=True),
        lax.all_gather(dec_gene, "query", axis=0, tiled=True),
        lax.all_gather(gene_table, "query", axis=0, tiled=True),
    )
    full_qkv, full_out, full_up, full_down, full_cell, full_gene, full_table = gathered
    flat_tokens = tokens.astype(jnp.float32).reshape(token_count, D)
    normed, first_pull = jax.vjp(layer_norm, flat_tokens, ln_gains[0], ln_biases[0])
    normed_low = normed.astype(jnp.bfloat16)
    zeroes = jnp.zeros((D,), jnp.float32)
    qkv_bias = jnp.concatenate([proj_biases[0], zeroes, proj_biases[1]])
    qkv_low = (jnp.dot(normed_low, full_qkv, preferred_element_type=jnp.float32) + qkv_bias).astype(
        jnp.bfloat16
    )
    qkv_rows = qkv_low.reshape(row_count, ROW_LEN, 3 * D)
    mixed_rows, log_totals = lax.map(attend, (qkv_rows, segment))
    mixed_low = mixed_rows.reshape(token_count, D)
    middle = (
        flat_tokens
        + jnp.dot(mixed_low, full_out, preferred_element_type=jnp.float32)
        + proj_biases[2]
    )
    second, second_pull = jax.vjp(layer_norm, middle, ln_gains[1], ln_biases[1])
    second_low = second.astype(jnp.bfloat16)
    hidden = jnp.dot(second_low, full_up, preferred_element_type=jnp.float32) + ff_biases[0]
    active, active_pull = jax.vjp(smooth_gate, hidden)
    active_low = active.astype(jnp.bfloat16)
    encoded = (
        middle + jnp.dot(active_low, full_down, preferred_element_type=jnp.float32) + proj_biases[3]
    )
    places = jnp.arange(ROW_LEN, dtype=jnp.int32)
    picker = (places[None, None, :] == starts[:, :, None]).astype(jnp.float32)
    local_cells = row_count * CELLS_ROW
    heads_low = (
        jnp.einsum(
            "rcl,rld->rcd", picker, encoded.reshape(row_count, ROW_LEN, D), precision=HIGHEST
        )
        .reshape(local_cells, D)
        .astype(jnp.bfloat16)
    )
    cell_heads = lax.all_gather(heads_low, "query", axis=0, tiled=True)
    cell_part = jnp.dot(cell_heads, full_cell, preferred_element_type=jnp.float32)
    gene_rows = jnp.take(full_table, query_ids, axis=0)
    before = (
        cell_part[:, None, :]
        + jnp.einsum("cqd,df->cqf", gene_rows, full_gene, preferred_element_type=jnp.float32)
        + ff_biases[1]
    )
    gated_dec, gated_pull = jax.vjp(smooth_gate, before)
    logit_weight = dec_out.astype(jnp.float32)
    logits = jnp.einsum("cqf,f->cq", gated_dec, logit_weight, precision=HIGHEST)
    logit_slope = jax.nn.sigmoid(logits) - labels.astype(jnp.float32)
    (grad_before,) = gated_pull(logit_slope[:, :, None] * logit_weight)
    before_low = grad_before.astype(jnp.bfloat16)
    grad_dec_bias = jnp.sum(before_low, axis=(0, 1), dtype=jnp.float32)
    grad_logit = jnp.einsum("cqf,cq->f", gated_dec, logit_slope, precision=HIGHEST)
    gene_terms = jnp.einsum(
        "cqd,cqf->df", gene_rows, before_low, preferred_element_type=jnp.float32
    )
    genes_back = jnp.einsum(
        "cqf,df->cqd", before_low, full_gene, preferred_element_type=jnp.float32
    ).astype(jnp.bfloat16)
    choose = (query_ids.reshape(-1)[:, None] == jnp.arange(GENES, dtype=jnp.int32)[None, :]).astype(
        jnp.bfloat16
    )
    table_terms = jnp.einsum(
        "ng,nd->gd", choose, genes_back.reshape(-1, D), preferred_element_type=jnp.float32
    )
    gene_parts, table_parts = (
        lax.all_to_all(
            owner_blocks(gene_terms, dp_count, query_count).astype(jnp.bfloat16),
            "query",
            split_axis=1,
            concat_axis=1,
            tiled=True,
        ).astype(jnp.float32),
        lax.all_to_all(
            owner_blocks(table_terms, dp_count, query_count).astype(jnp.bfloat16),
            "query",
            split_axis=1,
            concat_axis=1,
            tiled=True,
        ).astype(jnp.float32),
    )
    grad_gene = jnp.sum(gene_parts, axis=1)
    grad_table = jnp.sum(table_parts, axis=1)
    cell_total = lax.psum(
        jnp.sum(before_low, axis=1, dtype=jnp.float32).astype(jnp.bfloat16), "query"
    )
    grad_cell = owned_term(cell_heads, cell_total, dp_count, query_count, place)
    heads_all = jnp.einsum("cf,df->cd", cell_total, full_cell, preferred_element_type=jnp.float32)
    heads_back = (
        lax.dynamic_slice_in_dim(heads_all, place * local_cells, local_cells, 0)
        .astype(jnp.bfloat16)
        .astype(jnp.float32)
    )
    grad_encoded = out_cotangent.astype(jnp.float32) + jnp.einsum(
        "rcl,rcd->rld", picker, heads_back.reshape(row_count, CELLS_ROW, D), precision=HIGHEST
    )
    grad_flat = grad_encoded.reshape(token_count, D)

    def empty_term(left_width, right_width):
        return jnp.zeros(
            (dp_count, left_width // (dp_count * query_count), right_width), jnp.float32
        )

    branch_low = grad_flat.astype(jnp.bfloat16)
    grad_out_bias = jnp.sum(branch_low, axis=0, dtype=jnp.float32)
    grad_active = jnp.einsum("nd,fd->nf", branch_low, full_down, preferred_element_type=jnp.float32)
    (grad_hidden,) = active_pull(grad_active)
    hidden_low = grad_hidden.astype(jnp.bfloat16)
    grad_up_bias = jnp.sum(hidden_low, axis=0, dtype=jnp.float32)
    grad_second = jnp.einsum("nf,df->nd", hidden_low, full_up, preferred_element_type=jnp.float32)
    middle_part, grad_gain_two, grad_shift_two = second_pull(grad_second)
    grad_middle = grad_flat + middle_part
    ff_terms = jnp.stack([grad_up_bias, grad_dec_bias], axis=1)
    attn_low = grad_middle.astype(jnp.bfloat16)
    grad_attn_bias = jnp.sum(attn_low, axis=0, dtype=jnp.float32)
    mixed_back = jnp.einsum(
        "ne,de->nd", attn_low, full_out, preferred_element_type=jnp.float32
    ).astype(jnp.bfloat16)
    qkv_back = lax.map(
        attend_back, (qkv_rows, segment, log_totals, mixed_back.reshape(row_count, ROW_LEN, D))
    )
    qkv_back_low = qkv_back.reshape(token_count, 3 * D).astype(jnp.bfloat16)
    bias_sums = jnp.sum(qkv_back_low, axis=0, dtype=jnp.float32)
    grad_normed = jnp.einsum(
        "ne,de->nd", qkv_back_low, full_qkv, preferred_element_type=jnp.float32
    )
    token_part, grad_gain_one, grad_shift_one = first_pull(grad_normed)
    grad_tokens = (grad_middle + token_part).reshape(row_count, ROW_LEN, D)
    gain_terms = jnp.stack([grad_gain_one, grad_gain_two], axis=1)
    shift_terms = jnp.stack([grad_shift_one, grad_shift_two], axis=1)
    proj_terms = jnp.stack(
        [bias_sums[:D], bias_sums[2 * D :], grad_attn_bias, grad_out_bias], axis=1
    )
    totals = (empty_term(D, 3 * D), empty_term(D, D), empty_term(D, FF), empty_term(FF, D))
    pieces = (
        lax.all_gather(normed_low, "query", axis=0, tiled=True),
        lax.all_gather(qkv_back_low, "query", axis=0, tiled=True),
        lax.all_gather(mixed_low, "query", axis=0, tiled=True),
        lax.all_gather(attn_low, "query", axis=0, tiled=True),
        lax.all_gather(second_low, "query", axis=0, tiled=True),
        lax.all_gather(hidden_low, "query", axis=0, tiled=True),
        lax.all_gather(active_low, "query", axis=0, tiled=True),
        lax.all_gather(branch_low, "query", axis=0, tiled=True),
    )
    every_fold = tuple(
        (
            owned_term(pieces[2 * i], pieces[2 * i + 1], dp_count, query_count, place)
            for i in range(len(totals))
        )
    )
    every_sum = (
        lax.psum_scatter(
            every_fold[2].astype(jnp.bfloat16), "dp", scatter_dimension=0, tiled=True
        ).astype(jnp.float32),
        lax.psum_scatter(
            every_fold[3].astype(jnp.bfloat16), "dp", scatter_dimension=0, tiled=True
        ).astype(jnp.float32),
        lax.psum_scatter(
            grad_cell.astype(jnp.bfloat16), "dp", scatter_dimension=0, tiled=True
        ).astype(jnp.float32),
        lax.psum_scatter(
            grad_gene.astype(jnp.bfloat16), "dp", scatter_dimension=0, tiled=True
        ).astype(jnp.float32),
        lax.psum_scatter(
            grad_table.astype(jnp.bfloat16), "dp", scatter_dimension=0, tiled=True
        ).astype(jnp.float32),
        lax.psum_scatter(
            every_fold[0].astype(jnp.bfloat16), "dp", scatter_dimension=0, tiled=True
        ).astype(jnp.float32),
        lax.psum_scatter(
            every_fold[1].astype(jnp.bfloat16), "dp", scatter_dimension=0, tiled=True
        ).astype(jnp.float32),
    )
    ffn_sums = every_sum[:5]
    attn_sums = every_sum[5:]
    small_sums = (
        lax.psum_scatter(gain_terms, ("dp", "query"), scatter_dimension=0, tiled=True),
        lax.psum_scatter(shift_terms, ("dp", "query"), scatter_dimension=0, tiled=True),
        lax.psum_scatter(proj_terms, ("dp", "query"), scatter_dimension=0, tiled=True),
        lax.psum_scatter(ff_terms, ("dp", "query"), scatter_dimension=0, tiled=True),
        lax.psum_scatter(grad_logit, ("dp", "query"), scatter_dimension=0, tiled=True),
    )

    def flat_rows(values_in):
        return values_in.reshape(-1, values_in.shape[-1])

    return (
        encoded.reshape(row_count, ROW_LEN, D),
        grad_tokens,
        small_sums[0].T,
        small_sums[1].T,
        small_sums[2].T,
        small_sums[3].T,
        flat_rows(attn_sums[0]),
        flat_rows(attn_sums[1]),
        flat_rows(ffn_sums[0]),
        flat_rows(ffn_sums[1]),
        flat_rows(ffn_sums[2]),
        flat_rows(ffn_sums[3]),
        small_sums[4],
        flat_rows(ffn_sums[4]),
    )


def solution(mesh):
    placed = (
        P(("dp", "query"), None, None),
        P(("dp", "query"), None),
        P(("dp", "query"), None, None),
        P(),
        P(),
        P(),
        P(),
        P("query", None),
        P("query", None),
        P("query", None),
        P("query", None),
        P("query", None),
        P("query", None),
        P(),
        P("query", None),
        P("dp", "query"),
        P("dp", "query"),
    )
    return jax.shard_map(
        shards,
        mesh=mesh,
        in_specs=placed,
        out_specs=(
            P(("dp", "query"), None, None),
            P(("dp", "query"), None, None),
            P(None, ("dp", "query")),
            P(None, ("dp", "query")),
            P(None, ("dp", "query")),
            P(None, ("dp", "query")),
            P(("dp", "query"), None),
            P(("dp", "query"), None),
            P(("dp", "query"), None),
            P(("dp", "query"), None),
            P(("dp", "query"), None),
            P(("dp", "query"), None),
            P(("dp", "query")),
            P(("dp", "query"), None),
        ),
        check_vma=False,
    )
```

profile of v0, /device:TPU:0, one launch (start us, length us, event | category | flops | bytes accessed | tf_op | source)
XLA Modules:
  0.0 2341.5 jit_solution(1583919703912908653)
XLA Ops:
  17.2 34.1 %all-gather.27.cloned.1.call-done = bf16[1024,1280]{1,0:T(8,128)(2,1)} async-done(((bf16[512,1280]{1,0:T(8,128)(2,1)}), bf16[1024,1280]{1,0:T(8,128)(2,1)}) %all-gather.27.cloned.1.call-update) | async-done | bytes 2621456 | tf_op jit(solution)/shard_map/all_gather | solution.py:159
  54.9 120.3 %all-gather.17.cloned.1.call-done = bf16[1280,3840]{1,0:T(8,128)(2,1)} async-done(((bf16[640,3840]{1,0:T(8,128)(2,1)}), bf16[1280,3840]{1,0:T(8,128)(2,1)}) %all-gather.17.cloned.1.call-update) | async-done | bytes 9830416 | tf_op jit(solution)/shard_map/all_gather | solution.py:153
  175.2 9.7 add_convert_fusion.1
  192.7 5.9 fusion.114
  206.1 5.2 fusion.59
  211.4 11.8 all-gather.19.cloned.1.call-done
  230.4 152.5 %all-gather.21.cloned.1.call-done = bf16[1280,5120]{1,0:T(8,128)(2,1)} async-done(((bf16[640,5120]{1,0:T(8,128)(2,1)}), bf16[1280,5120]{1,0:T(8,128)(2,1)}) %all-gather.21.cloned.1.call-update) | async-done | bytes 13107216 | tf_op jit(solution)/shard_map/all_gather | solution.py:155
  382.9 33.7 %multiply_convert_fusion.1 = (bf16[512,5120]{1,0:T(8,128)(2,1)}, f32[512,5120]{1,0:T(8,128)}, f32[512,5120]{1,0:T(8,128)}) fusion(f32[5120]{0:T(1024)S(1)} %bitcast.239, bf16[512,1280]{1,0:T(8,128)(2,1)} %add_convert_fusion.2, bf16[1280,5120]{1,0:T(8,128)(2,1)} %all-gather.21.cloned.1.call-done), kind=kOutput, calls=%fused_computation.22 | convolution fusion | flops 6883901440 | bytes 40652800 | tf_op jit(solution)/shard_map/dot_general | solution.py:180
  416.7 126.0 %all-gather.23.cloned.1.call-done = bf16[5120,1280]{1,0:T(8,128)(2,1)} async-done(((bf16[2560,1280]{1,0:T(8,128)(2,1)}), bf16[5120,1280]{1,0:T(8,128)(2,1)}) %all-gather.23.cloned.1.call-update) | async-done | bytes 13107216 | tf_op jit(solution)/shard_map/all_gather | solution.py:156
  542.7 12.1 fusion.34
  557.3 4.4 all-gather
  561.7 140.6 %all-gather.25.cloned.1.call-done = bf16[1280,5120]{1,0:T(8,128)(2,1)} async-done(((bf16[640,5120]{1,0:T(8,128)(2,1)}), bf16[1280,5120]{1,0:T(8,128)(2,1)}) %all-gather.25.cloned.1.call-update) | async-done | bytes 13107216 | tf_op jit(solution)/shard_map/all_gather | solution.py:157
  702.4 6.5 fusion.116
  708.9 153.4 %all-gather.29.cloned.1.call-done = bf16[1280,5120]{1,0:T(8,128)(2,1)} async-done(((bf16[640,5120]{1,0:T(8,128)(2,1)}), bf16[1280,5120]{1,0:T(8,128)(2,1)}) %all-gather.29.cloned.1.call-update) | async-done | bytes 13107216 | tf_op jit(solution)/shard_map/all_gather | solution.py:158
  862.4 7.3 fusion.86
  872.7 4.4 fusion.84
  882.5 20.3 all-reduce.7.cloned.1.call-done
  902.8 8.3 fusion.117
  914.4 19.8 convert_reduce_fusion
  934.2 14.9 multiply_reduce_fusion.1
  955.2 4.4 convolution_convert_fusion.4
  961.6 14.0 multiply_reduce_fusion
  975.5 18.8 multiply_convert_fusion
  994.3 9.1 fusion.60
  1005.0 7.3 multiply_convert_fusion.2
  1013.7 5.8 multiply_convert_fusion.3
  1028.1 8.8 fusion.55
  1046.1 54.5 %all-to-all-done.1 = bf16[16,2,32,1280]{3,2,0,1:T(8,128)(2,1)S(1)} async-done(((bf16[16,2,32,1280]{3,2,0,1:T(8,128)(2,1)}), bf16[16,2,32,1280]{3,2,0,1:T(8,128)(2,1)S(1)}, u32[]{:S(2)}, u32[]{:S(2)}) %all-to-all-start.1) | async-done | bytes 2621472 | tf_op jit(solution)/shard_map/all_to_all | solution.py:232
  1102.6 5.2 convolution_convert_fusion.3
  1115.2 43.5 %all-gather.33.cloned.1.call-done = bf16[1024,3840]{1,0:T(8,128)(2,1)} async-done(((bf16[512,3840]{1,0:T(8,128)(2,1)}), bf16[1024,3840]{1,0:T(8,128)(2,1)}) %all-gather.33.cloned.1.call-update) | async-done | bytes 7864336 | tf_op jit(solution)/shard_map/all_gather | solution.py:295
  1158.7 10.1 fusion.23
  1176.0 276.9 %all_to_all.10 = bf16[16,2,40,5120]{3,2,0,1:T(8,128)(2,1)} all-to-all(bf16[16,2,40,5120]{3,2,0,1:T(8,128)(2,1)S(1)} %copy.101), channel_id=1, replica_groups=mesh['dp'=16,'query'=2] {'query'}, dimensions={1} | all-to-all | bytes 26214400 | tf_op jit(solution)/shard_map/all_to_all | solution.py:225
  1452.8 16.7 reduce_sum.271
  1469.6 14.5 copy.99
  1484.1 11.5 convolution_convert_fusion.1
  1501.9 128.0 %all-gather.41.cloned.1.call-done = bf16[1024,5120]{1,0:T(8,128)(2,1)} async-done(((bf16[512,5120]{1,0:T(8,128)(2,1)}), bf16[1024,5120]{1,0:T(8,128)(2,1)}) %all-gather.41.cloned.1.call-update) | async-done | bytes 10485776 | tf_op jit(solution)/shard_map/all_gather | solution.py:299
  1629.9 12.8 fusion.18
  1646.3 10.4 fusion.106
  1659.6 40.9 %all-reduce.4 = (f32[1280,2]{0,1:T(2,128)S(1)}, f32[1280,2]{0,1:T(2,128)S(1)}, f32[1280,4]{0,1:T(4,128)S(1)}, f32[5120]{0:T(1024)S(1)}) all-reduce(f32[1280,2]{0,1:T(2,128)S(1)} %pad_maximum_fusion.4, f32[1280,2]{0,1:T(2,128)S(1)} %pad_maximum_fusion.5, ...), channel_id=2, replica_groups=mesh['dp'=16,'query'=2] {'dp','query'}, use_global_device_ids=true, to_apply=%region_17.18.clone | all-reduce | flops 15360 | bytes 122880
  1702.4 5.0 add_bitcast_fusion
  1707.4 63.9 %reduce-scatter.28.cloned.1.call-done = f32[160,2]{1,0:T(8,128)} async-done(((f32[5120,2]{1,0:T(8,128)}), f32[160,2]{1,0:T(8,128)}) %reduce-scatter.28.cloned.1.call-update) | async-done | bytes 1296
  1772.8 56.3 %reduce-scatter.26.cloned.1.call-done = bf16[1,32,1280]{2,1,0:T(8,128)(2,1)} async-done(((bf16[16,32,1280]{2,1,0:T(8,128)(2,1)}), bf16[1,32,1280]{2,1,0:T(8,128)(2,1)}) %reduce-scatter.26.cloned.1.call-update) | async-done | bytes 81936 | tf_op jit(solution)/shard_map/reduce_scatter | solution.py:322
  1830.7 61.1 %reduce-scatter.16.cloned.1.call-done = bf16[1,40,1280]{2,1,0:T(8,128)(2,1)} async-done(((bf16[16,40,1280]{2,1,0:T(8,128)(2,1)}), bf16[1,40,1280]{2,1,0:T(8,128)(2,1)}) %reduce-scatter.16.cloned.1.call-update) | async-done | bytes 102416 | tf_op jit(solution)/shard_map/reduce_scatter | solution.py:328
  1893.3 88.3 %reduce-scatter.22.cloned.1.call-done = bf16[1,40,5120]{2,1,0:T(8,128)(2,1)} async-done(((bf16[16,40,5120]{2,1,0:T(8,128)(2,1)}), bf16[1,40,5120]{2,1,0:T(8,128)(2,1)}) %reduce-scatter.22.cloned.1.call-update) | async-done | bytes 409616 | tf_op jit(solution)/shard_map/reduce_scatter | solution.py:316
  1983.6 79.0 %reduce-scatter.14.cloned.1.call-done = bf16[1,40,3840]{2,1,0:T(8,128)(2,1)} async-done(((bf16[16,40,3840]{2,1,0:T(8,128)(2,1)}), bf16[1,40,3840]{2,1,0:T(8,128)(2,1)}) %reduce-scatter.14.cloned.1.call-update) | async-done | bytes 307216 | tf_op jit(solution)/shard_map/reduce_scatter | solution.py:325
  2064.4 87.9 %reduce-scatter.24.cloned.1.call-done = bf16[1,40,5120]{2,1,0:T(8,128)(2,1)} async-done(((bf16[16,40,5120]{2,1,0:T(8,128)(2,1)}), bf16[1,40,5120]{2,1,0:T(8,128)(2,1)}) %reduce-scatter.24.cloned.1.call-update) | async-done | bytes 409616 | tf_op jit(solution)/shard_map/reduce_scatter | solution.py:319
  2154.2 88.5 %reduce-scatter.20.cloned.1.call-done = bf16[1,160,1280]{2,1,0:T(8,128)(2,1)} async-done(((bf16[16,160,1280]{2,1,0:T(8,128)(2,1)}), bf16[1,160,1280]{2,1,0:T(8,128)(2,1)}) %reduce-scatter.20.cloned.1.call-update) | async-done | bytes 409616 | tf_op jit(solution)/shard_map/reduce_scatter | solution.py:313
  2244.7 87.8 %reduce-scatter.18.cloned.1.call-done = bf16[1,40,5120]{2,1,0:T(8,128)(2,1)} async-done(((bf16[16,40,5120]{2,1,0:T(8,128)(2,1)}), bf16[1,40,5120]{2,1,0:T(8,128)(2,1)}) %reduce-scatter.18.cloned.1.call-update) | async-done | bytes 409616 | tf_op jit(solution)/shard_map/reduce_scatter | solution.py:310
  (287 shorter events, 123.4 us)
Async XLA Ops:
  7.2 44.1 %all-gather.27.cloned.1.call-start = ((), (), s32[]{:S(2)}) async-start(), calls=%async_computation.15 | async-start | bytes 3932160 | tf_op jit(solution)/shard_map/all_gather | solution.py:159
  7.9 167.3 %all-gather.17.cloned.1.call-start = ((), (), s32[]{:S(2)}) async-start(), calls=%async_computation.10 | async-start | bytes 14745600 | tf_op jit(solution)/shard_map/all_gather | solution.py:153
  8.7 214.6 %all-gather.19.cloned.1.call-start = ((), (), s32[]{:S(2)}) async-start(), calls=%async_computation.11 | async-start | bytes 4915200 | tf_op jit(solution)/shard_map/all_gather | solution.py:154
  9.4 373.5 %all-gather.21.cloned.1.call-start = ((), (), s32[]{:S(2)}) async-start(), calls=%async_computation.12 | async-start | bytes 19660800 | tf_op jit(solution)/shard_map/all_gather | solution.py:155
  10.0 532.7 %all-gather.23.cloned.1.call-start = ((), (), s32[]{:S(2)}) async-start(), calls=%async_computation.13 | async-start | bytes 19660800 | tf_op jit(solution)/shard_map/all_gather | solution.py:156
  10.6 691.8 %all-gather.25.cloned.1.call-start = ((), (), s32[]{:S(2)}) async-start(), calls=%async_computation.14 | async-start | bytes 19660800 | tf_op jit(solution)/shard_map/all_gather | solution.py:157
  11.2 851.1 %all-gather.29.cloned.1.call-start = ((), (), s32[]{:S(2)}) async-start(), calls=%async_computation.16 | async-start | bytes 19660800 | tf_op jit(solution)/shard_map/all_gather | solution.py:158
  12.0 890.8 %all-reduce.7.cloned.1.call-start = ((), (), s32[]{:S(2)}) async-start(), calls=%async_computation.17 | async-start | bytes 163840 | tf_op jit(solution)/shard_map/psum | solution.py:242
  14.0 213.8 %copy-start.36 = (f32[1280]{0:T(1024)}, f32[1280]{0:T(1024)S(1)}, u32[]{:S(2)}) copy-start(f32[1280]{0:T(1024)S(1)} %get-tuple-element.58) | copy-start | bytes 15364
  14.3 40.6 %copy-start.39 = (f32[512]{0:T(512)}, f32[512]{0:T(512)S(1)}, u32[]{:S(2)}) copy-start(f32[512]{0:T(512)S(1)} %broadcast_multiply_fusion.1) | copy-start | bytes 6148
  14.8 170.2 %copy-start.47 = (f32[512]{0:T(512)}, f32[512]{0:T(512)S(1)}, u32[]{:S(2)}) copy-start(f32[512]{0:T(512)S(1)} %fusion.94) | copy-start | bytes 6148
  17.1 167.8 %copy-start.19 = (bf16[512,1280]{1,0:T(8,128)(2,1)}, bf16[512,1280]{1,0:T(8,128)(2,1)S(1)}, u32[]{:S(2)}) copy-start(bf16[512,1280]{1,0:T(8,128)(2,1)S(1)} %fusion.46) | copy-start | bytes 3932164
  201.7 9.7 copy-start.29
  211.4 15.9 copy-start.15
  227.8 188.9 %copy-start.60 = (f32[512]{0:T(512)}, f32[512]{0:T(512)S(1)}, u32[]{:S(2)}) copy-start(f32[512]{0:T(512)S(1)} %multiply_reduce_fusion.3) | copy-start | bytes 6148
  227.8 188.9 %copy-start.62 = (f32[512]{0:T(512)}, f32[512]{0:T(512)S(1)}, u32[]{:S(2)}) copy-start(f32[512]{0:T(512)S(1)} %fusion.95) | copy-start | bytes 6148
  382.9 159.7 %copy-start.4 = (f32[512,1280]{1,0:T(8,128)S(1)}, f32[512,1280]{1,0:T(8,128)}, u32[]{:S(2)}) copy-start(f32[512,1280]{1,0:T(8,128)} %copy-done.3) | copy-start | bytes 7864324
  542.7 13.6 copy-start.69
  561.7 300.7 %copy-start.24 = (bf16[64,1280]{1,0:T(8,128)(2,1)S(1)}, bf16[64,1280]{1,0:T(8,128)(2,1)}, u32[]{:S(2)}) copy-start(bf16[64,1280]{1,0:T(8,128)(2,1)} %gather_fusion) | copy-start | bytes 491524
  561.7 300.6 %copy-start.33 = (f32[1,5120]{1,0:T(1,128)S(1)}, f32[1,5120]{1,0:T(1,128)}, u32[]{:S(2)}) copy-start(f32[1,5120]{1,0:T(1,128)} %get-tuple-element.83) | copy-start | bytes 61444
  561.7 300.6 %copy-start.53 = (pred[8,8]{1,0:T(8,128)(4,1)S(1)}, pred[8,8]{1,0:T(8,128)(4,1)}, u32[]{:S(2)}) copy-start(pred[8,8]{1,0:T(8,128)(4,1)} %compare_and_fusion) | copy-start | bytes 196
  877.2 33.9 %copy-start.43 = (f32[8,8]{1,0:T(8,128)}, f32[8,8]{1,0:T(8,128)S(1)}, u32[]{:S(2)}) copy-start(f32[8,8]{1,0:T(8,128)S(1)} %convert_subtract_fusion) | copy-start | bytes 772
  880.6 30.5 %copy-start.16 = (bf16[8,8,5120]{2,1,0:T(8,128)(2,1)}, bf16[8,8,5120]{2,1,0:T(8,128)(2,1)S(1)}, u32[]{:S(2)}) copy-start(bf16[8,8,5120]{2,1,0:T(8,128)(2,1)S(1)} %get-tuple-element.69) | copy-start | bytes 1966084
  881.7 220.9 %all-gather.35.cloned.1.call-start = ((), (), s32[]{:S(2)}) async-start(), calls=%async_computation.21 | async-start | bytes 3932160 | tf_op jit(solution)/shard_map/all_gather | solution.py:296
  882.5 220.2 %all-gather.37.cloned.1.call-start = ((), (), s32[]{:S(2)}) async-start(), calls=%async_computation.22 | async-start | bytes 3932160 | tf_op jit(solution)/shard_map/all_gather | solution.py:297
  902.8 8.4 copy-start.23
  914.4 19.8 copy-start.37
  914.4 19.8 copy-start.52
  914.4 19.8 copy-start.63
  934.2 14.9 copy-start.61
  953.9 158.3 %all-gather.31.cloned.1.call-start = ((), (), s32[]{:S(2)}) async-start(), calls=%async_computation.18 | async-start | bytes 3932160 | tf_op jit(solution)/shard_map/all_gather | solution.py:294
  954.7 204.1 %all-gather.33.cloned.1.call-start = ((), (), s32[]{:S(2)}) async-start(), calls=%async_computation.19 | async-start | bytes 11796480 | tf_op jit(solution)/shard_map/all_gather | solution.py:295
  1025.1 444.5 %all-gather.43.cloned.1.call-start = ((), (), s32[]{:S(2)}) async-start(), calls=%async_computation.27 | async-start | bytes 15728640 | tf_op jit(solution)/shard_map/all_gather | solution.py:300
  1025.9 458.2 %all-gather.45.cloned.1.call-start = ((), (), s32[]{:S(2)}) async-start(), calls=%async_computation.28 | async-start | bytes 3932160 | tf_op jit(solution)/shard_map/all_gather | solution.py:301
  1026.4 472.5 %all-gather.39.cloned.1.call-start = ((), (), s32[]{:S(2)}) async-start(), calls=%async_computation.24 | async-start | bytes 3932160 | tf_op jit(solution)/shard_map/all_gather | solution.py:298
  1027.1 602.8 %all-gather.41.cloned.1.call-start = ((), (), s32[]{:S(2)}) async-start(), calls=%async_computation.25 | async-start | bytes 15728640 | tf_op jit(solution)/shard_map/all_gather | solution.py:299
  1039.5 61.0 %all-to-all-start.1 = ((bf16[16,2,32,1280]{3,2,0,1:T(8,128)(2,1)}), bf16[16,2,32,1280]{3,2,0,1:T(8,128)(2,1)S(1)}, u32[]{:S(2)}, u32[]{:S(2)}) async-start(bf16[16,2,32,1280]{3,2,0,1:T(8,128)(2,1)} %copy.102), calls=%async_computation.7 | async-start | bytes 5242880 | tf_op jit(solution)/shard_map/all_to_all | solution.py:232
  1043.6 727.7 %reduce-scatter.28.cloned.1.call-start = ((), (), s32[]{:S(2)}) async-start(), calls=%async_computation.33 | async-start | bytes 2703360
  1046.0 783.1 %reduce-scatter.26.cloned.1.call-start = ((), (), s32[]{:S(2)}) async-start(), calls=%async_computation.32 | async-start | bytes 1392640 | tf_op jit(solution)/shard_map/reduce_scatter | solution.py:322
  1102.5 789.2 %reduce-scatter.16.cloned.1.call-start = ((), (), s32[]{:S(2)}) async-start(), calls=%async_computation.23 | async-start | bytes 1740800 | tf_op jit(solution)/shard_map/reduce_scatter | solution.py:328
  1107.9 873.7 %reduce-scatter.22.cloned.1.call-start = ((), (), s32[]{:S(2)}) async-start(), calls=%async_computation.30 | async-start | bytes 6963200 | tf_op jit(solution)/shard_map/reduce_scatter | solution.py:316
  1112.1 950.4 %reduce-scatter.14.cloned.1.call-start = ((), (), s32[]{:S(2)}) async-start(), calls=%async_computation.20 | async-start | bytes 5222400 | tf_op jit(solution)/shard_map/reduce_scatter | solution.py:325
  1168.9 983.4 %reduce-scatter.24.cloned.1.call-start = ((), (), s32[]{:S(2)}) async-start(), calls=%async_computation.31 | async-start | bytes 6963200 | tf_op jit(solution)/shard_map/reduce_scatter | solution.py:319
  1469.5 773.2 %reduce-scatter.20.cloned.1.call-start = ((), (), s32[]{:S(2)}) async-start(), calls=%async_computation.29 | async-start | bytes 6963200 | tf_op jit(solution)/shard_map/reduce_scatter | solution.py:313
  1495.6 836.9 %reduce-scatter.18.cloned.1.call-start = ((), (), s32[]{:S(2)}) async-start(), calls=%async_computation.26 | async-start | bytes 6963200 | tf_op jit(solution)/shard_map/reduce_scatter | solution.py:310
  1646.3 10.5 copy-start.59
  1646.3 11.9 copy-start.48
  1656.8 45.6 %copy-start.57 = (f32[512]{0:T(512)S(1)}, f32[512]{0:T(512)}, u32[]{:S(2)}) copy-start(f32[512]{0:T(512)} %copy-done.56) | copy-start | bytes 6148
  (48 other events, 141.8 us)
Sparse Core Ops, SparseCore 0:
  9.6 41.7 all-gather.26
  52.9 122.3 all-gather.16
  176.8 46.3 all-gather.18
  224.6 158.2 all-gather.20
  384.3 158.2 all-gather.22
  544.1 158.2 all-gather.24
  703.9 158.3 all-gather.28
  881.8 20.8 all-reduce.6
  904.3 39.0 all-gather.34
  954.0 39.2 all-gather.36
  994.9 39.0 all-gather.30
  1035.4 123.3 all-gather.32
  1160.3 235.0 all-gather.42
  1396.8 61.6 all-gather.44
  1459.9 39.0 all-gather.38
  1500.4 129.5 all-gather.40
  1632.0 139.1 reduce-scatter.27
  1774.7 54.3 reduce-scatter.25
  1833.3 58.4 reduce-scatter.15
  1895.6 86.0 reduce-scatter.21
  1986.1 76.3 reduce-scatter.13
  2066.5 85.7 reduce-scatter.23
  2156.8 85.8 reduce-scatter.19
  2246.5 85.9 reduce-scatter.17
where the time goes:
time: 2350 us; the launch traced here: 2340 us
  waiting for transfers between devices  1610 us (69%)
  blocking collectives  322 us (14%)
  matrix products  247 us (11%)
  other arithmetic  81.2 us (3%)
  local copies, waits for them, and re-layouts  61.3 us (3%)
    all_to_all x1, blocking collectives, shards(): lax.all_to_all(owner_blocks(gene_terms, dp_count, query_count).astype(jnp...  277 us
    all_gather x1, waiting for transfers between devices, shards(): lax.all_gather(dec_gene, 'query', axis=0, tiled=True)  153 us
    all_gather x1, waiting for transfers between devices, shards(): lax.all_gather(w_up, 'query', axis=0, tiled=True)  153 us
    all_gather x1, waiting for transfers between devices, shards(): lax.all_gather(dec_cell, 'query', axis=0, tiled=True)  141 us
    all_gather x1, waiting for transfers between devices, shards(): lax.all_gather(hidden_low, 'query', axis=0, tiled=True)  128 us
    all_gather x1, waiting for transfers between devices, shards(): lax.all_gather(w_down, 'query', axis=0, tiled=True)  126 us
    all_gather x1, waiting for transfers between devices, shards(): lax.all_gather(w_qkv, 'query', axis=0, tiled=True)  120 us
    reduce_scatter x1, waiting for transfers between devices, shards(): lax.psum_scatter(every_fold[3].astype(jnp.bfloat16), 'dp', scatter_dimens...  88.5 us
  transfers between devices with their start and end apart: 25, of which 20 were waited for; matrix products, arithmetic and copies ran while one was open for 15% of the time, Pallas kernels for 0%

commit v1 on v0

v1 whole, which is shorter than its diff:
```python
import math

import jax
import jax.numpy as jnp
from jax import lax
from jax.experimental import pallas as pl
from jax.experimental.pallas import tpu as pltpu
from jax.sharding import PartitionSpec as P

D = 1280
HEADS = 20
HEAD_DIM = 64
FF = 5120
ROW_LEN = 512
CELLS_ROW = 4
GENES = 1024
EPSILON = 1e-05
HIGHEST = lax.Precision.HIGHEST
F32 = jnp.float32
BF16 = jnp.bfloat16


def layer_norm(values_in, scale_row, offset_row):
    center = values_in - jnp.mean(values_in, axis=-1, keepdims=True)
    spread = jnp.mean(center * center, axis=-1, keepdims=True)
    return center * lax.rsqrt(spread + EPSILON) * scale_row + offset_row


def smooth_gate(values_in):
    return jax.nn.gelu(values_in, approximate=False)


def dot(left, right):
    return jnp.dot(left, right, preferred_element_type=F32)


def dot_rt(left, right):
    return lax.dot_general(left, right, (((1,), (1,)), ((), ())), preferred_element_type=F32)


def dot_lt(left, right):
    return lax.dot_general(left, right, (((0,), (0,)), ((), ())), preferred_element_type=F32)


def cell_layout(lengths):
    cell_ends = jnp.cumsum(lengths, axis=-1, dtype=jnp.int32)
    starts = cell_ends - lengths
    places = jnp.arange(ROW_LEN, dtype=jnp.int32)
    segment = jnp.sum(
        (places[None, :, None] >= cell_ends[:, None, :]).astype(jnp.int32), axis=-1, dtype=jnp.int32
    )
    return (starts, segment)


def split_heads(qkv_row):
    queries = qkv_row[:, :D].reshape(ROW_LEN, HEADS, HEAD_DIM)
    keys_in = qkv_row[:, D : 2 * D].reshape(ROW_LEN, HEADS, HEAD_DIM)
    values_in = qkv_row[:, 2 * D :].reshape(ROW_LEN, HEADS, HEAD_DIM)
    return (queries, keys_in, values_in)


def row_scores(queries, keys_in, segment_row):
    scores = jnp.einsum("qhd,khd->hqk", queries, keys_in, preferred_element_type=F32) * (
        1.0 / math.sqrt(HEAD_DIM)
    )
    same_cell = segment_row[:, None] == segment_row[None, :]
    return jnp.where(same_cell[None], scores, -1e30)


def attend(member):
    qkv_row, segment_row = member
    queries, keys_in, values_in = split_heads(qkv_row)
    scores = row_scores(queries, keys_in, segment_row)
    highest_score = jnp.max(scores, axis=-1, keepdims=True)
    weights = jnp.exp(scores - highest_score)
    weight_sum = jnp.sum(weights, axis=-1, keepdims=True)
    attention = (weights / weight_sum).astype(BF16)
    mixed = jnp.einsum("hqk,khd->qhd", attention, values_in, preferred_element_type=F32).astype(BF16)
    return (mixed.reshape(ROW_LEN, D), (highest_score + jnp.log(weight_sum))[:, :, 0])


def attend_back(member):
    qkv_row, segment_row, log_total, grad_mixed = member
    queries, keys_in, values_in = split_heads(qkv_row)
    scores = row_scores(queries, keys_in, segment_row)
    attention = jnp.exp(scores - log_total[:, :, None])
    grad_heads = grad_mixed.reshape(ROW_LEN, HEADS, HEAD_DIM)
    grad_probs = jnp.einsum("qhd,khd->hqk", grad_heads, values_in, preferred_element_type=F32)
    grad_scores = (
        attention * (grad_probs - jnp.sum(attention * grad_probs, axis=-1, keepdims=True))
    ).astype(BF16)
    scale_factor = 1.0 / math.sqrt(HEAD_DIM)
    grad_query = (
        jnp.einsum("hqk,khd->qhd", grad_scores, keys_in, preferred_element_type=F32) * scale_factor
    )
    grad_keys = (
        jnp.einsum("hqk,qhd->khd", grad_scores, queries, preferred_element_type=F32) * scale_factor
    )
    grad_values = jnp.einsum(
        "hqk,qhd->khd", attention.astype(BF16), grad_heads, preferred_element_type=F32
    )
    return jnp.concatenate(
        [
            grad_query.reshape(ROW_LEN, D),
            grad_keys.reshape(ROW_LEN, D),
            grad_values.reshape(ROW_LEN, D),
        ],
        axis=1,
    )


def assemble_kernel(pieces, width, count, place_ref, *refs):
    sources, full, sems = refs[:count], refs[count], refs[count + 1]
    step = pl.program_id(0)
    copies = []
    for i, (source, row, rows, column) in enumerate(pieces):
        start = pl.multiple_of(place_ref[i], 16)
        columns = pl.ds(pl.multiple_of(column + step * width, 128), width)
        copies.append(
            pltpu.make_async_copy(
                sources[source].at[pl.ds(row, rows), columns],
                full.at[pl.ds(start, rows), :],
                sems.at[i],
            )
        )
    for copy in copies:
        copy.start()
    for copy in copies:
        copy.wait()


def assemble(sources, pieces, places, shape, width):
    count = len(sources)
    rows, columns = shape
    return pl.pallas_call(
        lambda *refs: assemble_kernel(pieces, width, count, *refs),
        grid=(columns // width,),
        out_shape=jax.ShapeDtypeStruct(shape, BF16),
        in_specs=[pl.BlockSpec(memory_space=pltpu.SMEM)]
        + [pl.BlockSpec(memory_space=pl.ANY)] * count,
        out_specs=pl.BlockSpec((rows, width), lambda j: (0, j)),
        scratch_shapes=[pltpu.SemaphoreType.DMA((len(pieces),))],
        compiler_params=pltpu.CompilerParams(vmem_limit_bytes=32 << 20),
        cost_estimate=pl.CostEstimate(flops=0, bytes_accessed=4 * rows * columns, transcendentals=0),
    )(jnp.stack(places).astype(jnp.int32), *sources)


def tie(value, *others):
    return lax.optimization_barrier((value, *others))[0]


class Grid:
    def __init__(self, mesh):
        dp, query = mesh.shape["dp"], mesh.shape["query"]
        core = 2 if dp % 2 == 0 else 1
        rest = dp // core
        outer = 4 if rest % 4 == 0 else rest
        inner = rest // outer
        self.dp, self.query = dp, query
        self.size = {"z": outer, "y": inner, "c": core, "x": query}
        self.stride = {"z": inner * core, "y": core, "c": 1}
        self.order = ["z", "y", "c", "x"]

    def place(self, axis):
        if axis == "x":
            return lax.axis_index("query")
        return (lax.axis_index("dp") // self.stride[axis]) % self.size[axis]

    def partner(self, axis, at, step):
        size = self.size[axis]
        return at ^ step if size & (size - 1) == 0 else (at + step) % size

    def sender(self, axis, at, step):
        size = self.size[axis]
        return at ^ step if size & (size - 1) == 0 else (at + size - step) % size

    def hop(self, value, axis, step=1):
        if axis == "x":
            pairs = [(i, self.partner("x", i, step)) for i in range(self.query)]
            return lax.ppermute(value, "query", pairs)
        stride, size = self.stride[axis], self.size[axis]
        pairs = []
        for i in range(self.dp):
            at = (i // stride) % size
            pairs.append((i, i + (self.partner(axis, at, step) - at) * stride))
        return lax.ppermute(value, "dp", pairs)

    def share(self, value, axis=0):
        if self.query == 1:
            return value
        if self.query != 2:
            return lax.all_gather(value, "query", axis=axis, tiled=True)
        other = self.hop(value, "x")
        first = lax.axis_index("query") == 0
        return jnp.concatenate(
            [jnp.where(first, value, other), jnp.where(first, other, value)], axis=axis
        )

    def total(self, value):
        if self.query == 1:
            return value
        if self.query != 2:
            return lax.psum(value, "query")
        return value + self.hop(value, "x")

    def scatter_step(self, value, axis, dim, kind):
        size = self.size[axis]
        me = self.place(axis)

        def part(index):
            return lax.dynamic_index_in_dim(value, index, axis=dim, keepdims=False)

        if size == 1:
            return part(0)
        sent = [
            self.hop(part(self.partner(axis, me, step)), axis, step) for step in range(1, size)
        ]
        total = part(me).astype(F32)
        for received in sent:
            total = total + received.astype(F32)
        return total.astype(kind)

    def scatter(self, value, order, kind=BF16):
        dims = [axis for axis in self.order if axis in order]
        for axis in order:
            dim = dims.index(axis)
            value = self.scatter_step(value, axis, dim, kind)
            dims.pop(dim)
        return value

    def scatter_z(self, value):
        stride, size = self.stride["z"], self.size["z"]
        groups = [[k * stride + i for k in range(size)] for i in range(stride)]
        return lax.psum_scatter(
            value, "dp", scatter_dimension=0, axis_index_groups=groups, tiled=True
        )

    def blocks(self, value):
        shape = [self.size[axis] for axis in self.order]
        rows = value.shape[0] // math.prod(shape)
        return value.reshape(*shape, rows, *value.shape[1:])

    def own_columns(self, value):
        width = value.shape[1] // (self.dp * self.query)
        shaped = value.reshape(value.shape[0], self.dp, self.query, width)
        mine = lax.dynamic_index_in_dim(shaped, self.place("x"), axis=2, keepdims=False)
        return mine.reshape(value.shape[0], self.dp * width)

    def gather_rows(self, shards):
        size = self.size
        if self.query != 2 or size["y"] != 2 or size["c"] != 2 or size["z"] % 2:
            return [lax.all_gather(shard, "query", axis=0, tiled=True) for shard in shards]
        zb, y, c, x = self.place("z") % 2, self.place("y"), self.place("c"), self.place("x")
        unit = min(shard.shape[0] for shard in shards) // 8

        def at(zb_, y_, c_):
            return (zb_ * 2 + y_) * 2 + c_

        mine = at(zb, y, c)
        columns = []
        for shard in shards:
            fold = shard.shape[0] // (8 * unit)
            for k in range(fold):
                columns.append(
                    lax.dynamic_slice_in_dim(shard, (mine * fold + k) * unit, unit, 0)
                )
        sent = jnp.concatenate(columns, axis=1) if len(columns) > 1 else columns[0]
        first = self.hop(sent, "x")
        by_y = self.hop(first, "y")
        by_z = self.hop(first, "z")
        cut = unit // 2 // 16 * 16
        corner_y = self.hop(by_z[:cut], "y")
        corner_z = self.hop(by_y[cut:], "z")
        near = jnp.concatenate([first, by_y, by_z, corner_y, corner_z], axis=0)
        far = self.hop(near, "c")
        wholes = []
        column = 0
        for shard in shards:
            rows, width = shard.shape
            fold = rows // (8 * unit)
            pieces, places = [(0, 0, rows, 0)], [x * rows]
            for source, c_ in ((1, c), (2, 1 - c)):
                for part, (zb_, y_) in enumerate(((zb, y), (zb, 1 - y), (1 - zb, y), (1 - zb, 1 - y))):
                    for k in range(fold):
                        pieces.append((source, part * unit, unit, column + k * width))
                        places.append((1 - x) * rows + (at(zb_, y_, c_) * fold + k) * unit)
            block = 640 if rows <= 640 else 256
            wholes.append(assemble([shard, near, far], pieces, places, (2 * rows, width), block))
            column += fold * width
        return wholes


def make_shards(grid):
    def weight_term(left, right):
        half = right.shape[1] // 2
        sums = []
        for part, order in ((right[:, :half], "cxy"), (right[:, half:], "cyx")):
            terms = grid.blocks(dot_lt(left, part).astype(BF16))
            dims = ["z", "y", "c", "x"]
            for axis in order:
                dim = dims.index(axis)
                terms = grid.scatter_step(terms, axis, dim, BF16)
                dims.pop(dim)
            sums.append(terms)
        whole = jnp.concatenate(sums, axis=-1)
        return grid.scatter_z(whole).reshape(whole.shape[1:]).astype(F32)

    def shards(
        tokens,
        cell_lengths,
        out_cotangent,
        ln_gains,
        ln_biases,
        proj_biases,
        ff_biases,
        w_qkv,
        w_out,
        w_up,
        w_down,
        dec_cell,
        dec_gene,
        dec_out,
        gene_table,
        query_ids,
        labels,
    ):
        row_count = tokens.shape[0]
        token_count = row_count * ROW_LEN
        dp_count, query_count = grid.dp, grid.query
        place = lax.axis_index("query")
        starts, segment = cell_layout(cell_lengths)
        local_cells = row_count * CELLS_ROW
        pair_cells, local_queries = query_ids.shape
        pairs = pair_cells * local_queries
        half_width = D // query_count

        full_qkv, full_out = grid.gather_rows([w_qkv, w_out])
        full_up, full_down = grid.gather_rows([w_up, w_down])

        ids = grid.share(query_ids.reshape(1, pairs)).reshape(query_count * pairs)
        table_rows = gene_table.shape[0]
        local_ids = ids - place * table_rows
        held = (local_ids[:, None] == jnp.arange(table_rows, dtype=jnp.int32)[None, :]).astype(BF16)
        gene_rows = grid.total(dot(held, gene_table).astype(BF16))
        gene_half = lax.dynamic_slice_in_dim(gene_rows, place * half_width, half_width, 1)
        gene_partial = dot(gene_half, dec_gene).reshape(query_count, pairs, FF)
        gene_part = grid.scatter_step(gene_partial.astype(BF16), "x", 0, F32) + ff_biases[1]

        flat_tokens = tokens.astype(F32).reshape(token_count, D)
        normed, first_pull = jax.vjp(layer_norm, flat_tokens, ln_gains[0], ln_biases[0])
        normed_low = normed.astype(BF16)
        zeroes = jnp.zeros((D,), F32)
        qkv_bias = jnp.concatenate([proj_biases[0], zeroes, proj_biases[1]])
        qkv_low = (dot(normed_low, full_qkv) + qkv_bias).astype(BF16)
        qkv_rows = qkv_low.reshape(row_count, ROW_LEN, 3 * D)
        mixed_rows, log_totals = lax.map(attend, (qkv_rows, segment))
        mixed_low = mixed_rows.reshape(token_count, D)
        middle = flat_tokens + dot(mixed_low, full_out) + proj_biases[2]
        second, second_pull = jax.vjp(layer_norm, middle, ln_gains[1], ln_biases[1])
        second_low = second.astype(BF16)
        hidden = dot(second_low, full_up) + ff_biases[0]
        active, active_pull = jax.vjp(smooth_gate, hidden)
        active_low = active.astype(BF16)
        encoded = middle + dot(active_low, full_down) + proj_biases[3]
        encoded_rows = encoded.reshape(row_count, ROW_LEN, D)
        heads_low = (
            jnp.take_along_axis(encoded_rows, starts[:, :, None], axis=1)
            .reshape(local_cells, D)
            .astype(BF16)
        )
        cell_heads = grid.share(heads_low)
        heads_half = lax.dynamic_slice_in_dim(cell_heads, place * half_width, half_width, 1)
        cell_part = grid.total(dot(heads_half, dec_cell))
        before = cell_part[:, None, :] + gene_part.reshape(pair_cells, local_queries, FF)
        gated_dec, gated_pull = jax.vjp(smooth_gate, before)
        logit_weight = dec_out.astype(F32)
        logits = jnp.sum(gated_dec * logit_weight, axis=-1)
        logit_slope = jax.nn.sigmoid(logits) - labels.astype(F32)
        (grad_before,) = gated_pull(logit_slope[:, :, None] * logit_weight)
        before_low = grad_before.astype(BF16)
        before_sums = jnp.sum(before_low, axis=1, dtype=F32)
        grad_dec_bias = jnp.sum(before_sums, axis=0)
        grad_logit = jnp.sum(gated_dec * logit_slope[:, :, None], axis=(0, 1))
        cell_total = grid.total(before_sums).astype(BF16)
        heads_part = dot_rt(cell_total, dec_cell).astype(BF16)
        heads_all = grid.share(heads_part, axis=1)
        heads_back = lax.dynamic_slice_in_dim(
            heads_all, place * local_cells, local_cells, 0
        ).astype(F32)

        places = jnp.arange(ROW_LEN, dtype=jnp.int32)
        picker = (places[None, :, None] == starts[:, None, :]).astype(F32)
        grad_encoded = out_cotangent.astype(F32) + jnp.sum(
            picker[:, :, :, None] * heads_back.reshape(row_count, 1, CELLS_ROW, D), axis=2
        )
        grad_flat = grad_encoded.reshape(token_count, D)

        branch_low = grad_flat.astype(BF16)
        grad_down = weight_term(active_low, branch_low)
        grad_out_bias = jnp.sum(branch_low, axis=0, dtype=F32)
        grad_active = dot_rt(branch_low, full_down)
        (grad_hidden,) = active_pull(grad_active)
        hidden_low = grad_hidden.astype(BF16)
        grad_up = weight_term(second_low, hidden_low)
        grad_up_bias = jnp.sum(hidden_low, axis=0, dtype=F32)
        grad_second = dot_rt(hidden_low, full_up)
        middle_part, grad_gain_two, grad_shift_two = second_pull(grad_second)
        grad_middle = grad_flat + middle_part

        before_all = grid.share(before_low.reshape(1, pairs, FF)).reshape(query_count * pairs, FF)
        gene_terms = dot_lt(grid.own_columns(gene_rows), before_all).astype(BF16)
        shape = [grid.size[axis] for axis in "zyc"]
        grad_gene = grid.scatter(gene_terms.reshape(*shape, -1, FF), "cyz").astype(F32)
        genes_part = dot_rt(before_all, dec_gene).astype(BF16)
        genes_back = grid.share(genes_part, axis=1)
        choose = (ids[:, None] == jnp.arange(GENES, dtype=jnp.int32)[None, :]).astype(BF16)
        table_terms = dot_lt(grid.own_columns(choose), genes_back).astype(BF16)
        grad_table = grid.scatter(table_terms.reshape(*shape, -1, D), "cyz").astype(F32)
        all_heads = lax.all_gather(cell_heads, "dp", axis=0, tiled=True)
        all_cells = lax.all_gather(cell_total, "dp", axis=0, tiled=True)
        owned = D // (dp_count * query_count)
        mine = lax.axis_index("dp") * query_count + place
        grad_cell = dot_lt(
            lax.dynamic_slice_in_dim(all_heads, mine * owned, owned, 1), all_cells
        )

        attn_low = grad_middle.astype(BF16)
        grad_attn_bias = jnp.sum(attn_low, axis=0, dtype=F32)
        grad_out = weight_term(mixed_low, attn_low)
        mixed_back = dot_rt(attn_low, full_out).astype(BF16)
        qkv_back = lax.map(
            attend_back, (qkv_rows, segment, log_totals, mixed_back.reshape(row_count, ROW_LEN, D))
        )
        qkv_back_low = qkv_back.reshape(token_count, 3 * D).astype(BF16)
        grad_qkv = weight_term(normed_low, qkv_back_low)
        bias_sums = jnp.sum(qkv_back_low, axis=0, dtype=F32)
        grad_normed = dot_rt(qkv_back_low, full_qkv)
        token_part, grad_gain_one, grad_shift_one = first_pull(grad_normed)
        grad_tokens = (grad_middle + token_part).reshape(row_count, ROW_LEN, D)

        owners = dp_count * query_count

        def owned_cols(values):
            return values.reshape(-1, owners, values.shape[-1] // owners).transpose(1, 0, 2).reshape(owners, -1)

        small = [
            jnp.stack([grad_gain_one, grad_gain_two]),
            jnp.stack([grad_shift_one, grad_shift_two]),
            jnp.stack([bias_sums[:D], bias_sums[2 * D :], grad_attn_bias, grad_out_bias]),
            jnp.stack([grad_up_bias, grad_dec_bias]),
            grad_logit[None, :],
        ]
        flat = [owned_cols(v) for v in small]
        joined = jnp.concatenate(flat, axis=1)
        summed = grid.scatter(grid.blocks(joined), "cxyz", F32).reshape(-1)
        outs = []
        start = 0
        for value, piece in zip(small, flat):
            size = piece.shape[1]
            outs.append(summed[start : start + size].reshape(value.shape[0], -1))
            start += size

        return (
            encoded_rows,
            grad_tokens,
            outs[0],
            outs[1],
            outs[2],
            outs[3],
            grad_qkv,
            grad_out,
            grad_up,
            grad_down,
            grad_cell,
            grad_gene,
            outs[4][0],
            grad_table,
        )

    return shards


def solution(mesh):
    placed = (
        P(("dp", "query"), None, None),
        P(("dp", "query"), None),
        P(("dp", "query"), None, None),
        P(),
        P(),
        P(),
        P(),
        P("query", None),
        P("query", None),
        P("query", None),
        P("query", None),
        P("query", None),
        P("query", None),
        P(),
        P("query", None),
        P("dp", "query"),
        P("dp", "query"),
    )
    rows = P(("dp", "query"), None)
    return jax.shard_map(
        make_shards(Grid(mesh)),
        mesh=mesh,
        in_specs=placed,
        out_specs=(
            P(("dp", "query"), None, None),
            P(("dp", "query"), None, None),
            P(None, ("dp", "query")),
            P(None, ("dp", "query")),
            P(None, ("dp", "query")),
            P(None, ("dp", "query")),
            rows,
            rows,
            rows,
            rows,
            rows,
            rows,
            P(("dp", "query")),
            rows,
        ),
        check_vma=False,
    )
```

time: 2350 us -> 918 us (0.39)
  waiting for transfers between devices: 1610 us -> 329 us
  blocking collectives: 322 us -> 24 us
  starting transfers between devices: 5.41 us -> 57.9 us
  local copies, waits for them, and re-layouts: 61.3 us -> 103 us
  other arithmetic: 81.2 us -> 121 us
  Pallas kernels: 0 us -> 34.7 us
  matrix products: 247 us -> 223 us
    all_gather x15 -> x1, waiting for transfers between devices: 914 us -> 0.03 us  [shards(): all_cells = lax.all_gather(cell_total, 'dp', axis=0, tiled=True)]
    reduce_scatter x7 -> x4, waiting for transfers between devices: 549 us -> 0.01 us  [scatter_z(): lax.psum_scatter(value, 'dp', scatter_dimension=0, axis_index_groups=grou...]
    ppermute x0 -> x61, waiting for transfers between devices: none -> 329 us  [the longest x41 215 us: hop(): return lax.ppermute(value, 'dp', pairs)]
    all_to_all x1 -> x0, blocking collectives: 277 us -> none  [shards(): lax.all_to_all(owner_blocks(gene_terms, dp_count, query_count).astype(jnp...]
    unnamed x25 -> x5, waiting for transfers between devices: 71.6 us -> 0.08 us
    ppermute x0 -> x61, starting transfers between devices: none -> 57.7 us  [the longest x41 35.2 us: hop(): return lax.ppermute(value, 'dp', pairs)]
    all_to_all x1 -> x0, waiting for transfers between devices: 54.5 us -> none  [shards(): lax.all_to_all(owner_blocks(table_terms, dp_count, query_count).astype(jn...]
    convert_element_type x3 -> x39, other arithmetic: 2.71 us -> 47.1 us  [the longest x28 36.5 us: scatter_step(): return total.astype(kind)]
  transfers between devices with their start and end apart: 25 -> 66, of which waited for: 20 -> 30; matrix products, arithmetic and copies ran while one was open for 15% -> 35% of each run, Pallas kernels for 0% -> 1%
where the time goes in v1:
time: 918 us; the launch traced here: 911 us
  waiting for transfers between devices  329 us (36%)
  matrix products  223 us (24%)
  other arithmetic  121 us (13%)
  local copies, waits for them, and re-layouts  103 us (11%)
  starting transfers between devices  57.9 us (6%)
  Pallas kernels  34.7 us (4%)
  blocking collectives  24 us (3%)
  between operations  17.7 us (2%)
    ppermute x41, waiting for transfers between devices, hop(): return lax.ppermute(value, 'dp', pairs)  215 us
    ppermute x20, waiting for transfers between devices, hop(): return lax.ppermute(value, 'query', pairs)  114 us
    dot_general x7, matrix products, dot(): return jnp.dot(left, right, preferred_element_type=F32)  63.5 us
    dot_general x6, matrix products, dot_rt(): lax.dot_general(left, right, (((1,), (1,)), ((), ())), preferred_element_...  55.2 us
    dot_general x11, matrix products, dot_lt(): lax.dot_general(left, right, (((0,), (0,)), ((), ())), preferred_element_...  48.6 us
    dynamic_slice x16, local copies, waits for them, and re-layouts, part(): return lax.dynamic_index_in_dim(value, index, axis=dim, keepdims=False)  39.9 us
    convert_element_type x28, other arithmetic, scatter_step(): return total.astype(kind)  36.5 us
    ppermute x41, starting transfers between devices, hop(): return lax.ppermute(value, 'dp', pairs)  35.2 us
  transfers between devices with their start and end apart: 66, of which 30 were waited for; matrix products, arithmetic and copies ran while one was open for 35% of the time, Pallas kernels for 1%

profile of v1, /device:TPU:0, one launch (start us, length us, event | category | flops | bytes accessed | tf_op | source)
XLA Modules:
  0.0 910.7 jit_solution(13957514348526704995)
XLA Ops:
  32.7 44.3 %collective-permute-done.15 = bf16[128,1280]{1,0:T(8,128)(2,1)S(1)} collective-permute-done((bf16[128,1280]{1,0:T(8,128)(2,1)S(1)}, bf16[128,1280]{1,0:T(8,128)(2,1)S(1)}, u32[]{:S(2)}, u32[]{:S(2)}) %collective-permute-start.15) | collective-permute-done | bytes 327712 | tf_op jit(solution)/shard_map/ppermute | solution.py:180
  80.2 5.2 convolution_convert_fusion.7
  86.6 9.6 %collective-permute-done.2 = bf16[80,5120]{1,0:T(8,128)(2,1)S(1)} collective-permute-done((bf16[80,5120]{1,0:T(8,128)(2,1)}, bf16[80,5120]{1,0:T(8,128)(2,1)S(1)}, u32[]{:S(2)}, u32[]{:S(2)}) %collective-permute-start.2) | collective-permute-done | bytes 819232 | tf_op jit(solution)/shard_map/ppermute | solution.py:186
  106.9 5.6 collective-permute-done.4
  112.6 31.4 %collective-permute-done.8 = bf16[80,10240]{1,0:T(8,128)(2,1)S(1)} collective-permute-done((bf16[80,10240]{1,0:T(8,128)(2,1)}, bf16[80,10240]{1,0:T(8,128)(2,1)S(1)}, u32[]{:S(2)}, u32[]{:S(2)}) %collective-permute-start.8) | collective-permute-done | bytes 1638432 | tf_op jit(solution)/shard_map/ppermute | solution.py:186
  148.5 7.8 collective-permute-done.9
  157.2 7.4 collective-permute-done.10
  169.1 5.9 add_convert_fusion.1
  189.5 9.0 fusion.154
  198.4 8.8 fusion
  207.3 9.2 %fusion.51 = bf16[20,64,512]{2,1,0:T(8,128)(2,1)S(1)} fusion(bf16[512,20,64]{0,2,1:T(8,128)(2,1)S(1)} %bitcast.496, f32[20,512,512]{1,2,0:T(8,128)} %get-tuple-element.130, f32[20,512]{1,0:T(8,128)S(1)} %fusion, f32[20,512]{1,0:T(8,128)S(1)} %get-tuple-element.129), kind=kOutput, calls=%fused_computation.153 | convolution fusion | flops 687472640 | bytes 23674880 | tf_op jit(solution)/shard_map/while/body/eval_jaxpr/hqk,khd->qhd/dot_general | solution.py:78
  220.3 16.1 %shard_map.274 = bf16[1280,5120]{1,0:T(8,128)(2,1)} custom-call(s32[9]{0:T(128)S(1)} %stack.203.refs_0_, bf16[640,5120]{1,0:T(8,128)(2,1)S(1)} %bitcast.467, bf16[320,10240]{1,0:T(8,128)(2,1)} %constant_dynamic-update-slice_fusion.5.refs_2_, bf16[320,10240]{1,0:T(8,128)(2,1)} %collective-permute-done.11.refs_3_), custom_call_target="tpu_custom_call" | custom-call | bytes 26214400 | tf_op jit(solution)/shard_map/pallas_call | solution.py:135
  236.4 34.0 %multiply_convert_fusion.1 = (bf16[512,5120]{1,0:T(8,128)(2,1)S(1)}, f32[512,5120]{1,0:T(8,128)}, f32[512,5120]{1,0:T(8,128)}) fusion(f32[5120]{0:T(1024)S(1)} %bitcast.522, bf16[1280,5120]{1,0:T(8,128)(2,1)} %shard_map.274, f32[512,1280]{1,0:T(8,128)S(1)} %get-tuple-element.132, f32[1280]{0:T(1024)S(1)} %copy-done.95, f32[1280]{0:T(1024)S(1)} %copy-done.68, ...), kind=kOutput, calls=%fused_computation.18 | convolution fusion | flops 6887178240 | bytes 41977856 | tf_op jit(solution)/shard_map/dot_general | solution.py:34
  270.4 14.0 %shard_map.275 = bf16[5120,1280]{1,0:T(8,128)(2,1)} custom-call(s32[33]{0:T(128)S(1)} %stack.237.refs_0_, bf16[2560,1280]{1,0:T(8,128)(2,1)S(1)} %bitcast.469, bf16[320,10240]{1,0:T(8,128)(2,1)} %constant_dynamic-update-slice_fusion.5.refs_2_, bf16[320,10240]{1,0:T(8,128)(2,1)} %collective-permute-done.11.refs_3_), custom_call_target="tpu_custom_call" | custom-call | bytes 26214400 | tf_op jit(solution)/shard_map/pallas_call | solution.py:135
  284.5 12.0 %fusion.19 = f32[512,1280]{1,0:T(8,128)} fusion(f32[512,1280]{1,0:T(8,128)S(1)} %get-tuple-element.132, bf16[512,5120]{1,0:T(8,128)(2,1)S(1)} %get-tuple-element.78, bf16[5120,1280]{1,0:T(8,128)(2,1)} %shard_map.275, f32[1280]{0:T(1024)S(1)} %copy-done.97), kind=kOutput, calls=%fused_computation.59 | convolution fusion | flops 6712197120 | bytes 23598080 | tf_op jit(solution)/shard_map/dot_general | solution.py:34
  307.2 12.9 %collective-permute-done.13 = f32[8,5120]{1,0:T(8,128)S(1)} collective-permute-done((f32[8,5120]{1,0:T(8,128)S(1)}, f32[8,5120]{1,0:T(8,128)S(1)}, u32[]{:S(2)}, u32[]{:S(2)}) %collective-permute-start.13) | collective-permute-done | bytes 163872 | tf_op jit(solution)/shard_map/ppermute | solution.py:180
  334.1 4.7 convolution_convert_fusion.14
  343.2 4.3 convert_reduce_fusion.3
  347.5 20.1 %convert_reduce_fusion = (f32[5120]{0:T(1024)}, bf16[512,5120]{1,0:T(8,128)(2,1)}) fusion(f32[512,5120]{1,0:T(8,128)} %get-tuple-element.79, f32[512,5120]{1,0:T(8,128)} %get-tuple-element.133, f32[5120]{0:T(1024)S(1)} %bitcast.523, bf16[512,1280]{1,0:T(8,128)(2,1)} %get-tuple-element.71, bf16[5120,1280]{1,0:T(8,128)(2,1)} %shard_map.275), kind=kOutput, calls=%fused_computation.14 | convolution fusion | flops 6755445760 | bytes 40673280 | tf_op jit(solution)/shard_map/dot_general | solution.py:38
  367.6 15.6 %multiply_reduce_fusion.2 = (f32[1280]{0:T(1024)}, f32[512]{0:T(512)S(1)}, f32[1280]{0:T(1024)}, f32[512,1280]{1,0:T(8,128)}) fusion(f32[512,1280]{1,0:T(8,128)} %copy-done.16, f32[512]{0:T(512)S(1)} %fusion.132, f32[512]{0:T(512)S(1)} %broadcast_multiply_fusion, f32[1280]{0:T(1024)S(1)} %copy-done.68, bf16[512,5120]{1,0:T(8,128)(2,1)} %get-tuple-element.65, ...), kind=kOutput, calls=%fused_computation.107 | convolution fusion | flops 6716126208 | bytes 23614464 | tf_op jit(solution)/shard_map/dot_general | solution.py:38
  400.2 8.0 collective-permute-done.32
  418.7 24.0 %all_gather.6 = bf16[128,1280]{1,0:T(8,128)(2,1)} all-gather(bf16[8,1280]{1,0:T(8,128)(2,1)S(1)} %pad_maximum_fusion.12), channel_id=1, replica_groups=mesh['dp'=16,'query'=2] {'dp'}, dimensions={0}, use_global_device_ids=true | all-gather | bytes 348160 | tf_op jit(solution)/shard_map/all_gather | solution.py:419
  447.6 4.5 convolution_convert_fusion.10
  452.1 8.3 convolution_convert_fusion.1
  460.4 6.1 convolution_convert_fusion
  466.5 6.3 convolution_convert_fusion.4
  472.8 6.3 convolution_convert_fusion.3
  479.7 10.1 %fusion.52 = bf16[20,64,512]{2,1,0:T(8,128)(2,1)} fusion(bf16[512,20,64]{0,2,1:T(8,128)(2,1)S(1)} %bitcast.477, f32[20,512,512]{1,2,0:T(8,128)} %get-tuple-element.130, f32[20,512]{1,0:T(8,128)S(1)} %log_add_fusion), kind=kOutput, calls=%fused_computation.154 | convolution fusion | flops 682229760 | bytes 23633920 | tf_op jit(solution)/shard_map/while/body/eval_jaxpr/hqk,qhd->khd/dot_general | solution.py:99
  489.8 13.4 %multiply_reduce_fusion = (f32[20,512]{1,0:T(8,128)S(1)}, f32[20,512,512]{1,2,0:T(8,128)}) fusion(f32[20,512,512]{1,2,0:T(8,128)} %get-tuple-element.130, f32[20,512]{1,0:T(8,128)S(1)} %log_add_fusion, bf16[512,20,64]{0,2,1:T(8,128)(2,1)S(1)} %bitcast.478, bf16[512,20,64]{0,2,1:T(8,128)(2,1)S(1)} %bitcast.497), kind=kOutput, calls=%fused_computation.2 | convolution fusion | flops 686807040 | bytes 44646400 | tf_op jit(solution)/shard_map/while/body/eval_jaxpr/qhd,khd->hqk/dot_general | solution.py:88
  503.3 18.9 %multiply_convert_fusion = bf16[20,512,512]{1,2,0:T(8,128)(2,1)} fusion(f32[20,512,512]{1,2,0:T(8,128)} %get-tuple-element.136, f32[20,512,512]{1,2,0:T(8,128)} %get-tuple-element.130, f32[20,512]{1,0:T(8,128)S(1)} %get-tuple-element.135, f32[20,512]{1,0:T(8,128)S(1)} %log_add_fusion), kind=kLoop, calls=%fused_computation.1 | loop fusion | flops 20971520 | bytes 52510720 | tf_op jit(solution)/shard_map/while/body/eval_jaxpr/convert_element_type | solution.py:91
  522.2 8.5 multiply_convert_fusion.2
  530.8 5.9 multiply_convert_fusion.3
  536.8 8.2 fusion.144
  547.9 5.5 convolution_convert_fusion.6
  554.1 7.7 constant_dynamic-slice_fusion.13
  569.5 5.0 add_bitcast_fusion
  576.0 7.4 convolution_convert_fusion.5
  584.7 7.5 constant_dynamic-slice_fusion.21
  604.5 5.2 constant_dynamic-slice_fusion.9
  626.3 6.7 collective-permute-done.57
  681.3 6.9 collective-permute-done.26
  698.7 40.4 %collective-permute-done.27 = bf16[4,40,1920]{2,1,0:T(8,128)(2,1)S(1)} collective-permute-done((bf16[4,40,1920]{2,1,0:T(8,128)(2,1)S(1)}, bf16[4,40,1920]{2,1,0:T(8,128)(2,1)S(1)}, u32[]{:S(2)}, u32[]{:S(2)}) %collective-permute-start.27) | collective-permute-done | bytes 614432 | tf_op jit(solution)/shard_map/ppermute | solution.py:186
  741.0 29.6 %collective-permute-done.30 = bf16[4,40,1920]{2,1,0:T(8,128)(2,1)S(1)} collective-permute-done((bf16[4,40,1920]{2,1,0:T(8,128)(2,1)S(1)}, bf16[4,40,1920]{2,1,0:T(8,128)(2,1)S(1)}, u32[]{:S(2)}, u32[]{:S(2)}) %collective-permute-start.30) | collective-permute-done | bytes 614432 | tf_op jit(solution)/shard_map/ppermute | solution.py:180
  780.8 14.9 %collective-permute-done.39 = bf16[4,40,2560]{2,1,0:T(8,128)(2,1)S(1)} collective-permute-done((bf16[4,40,2560]{2,1,0:T(8,128)(2,1)S(1)}, bf16[4,40,2560]{2,1,0:T(8,128)(2,1)S(1)}, u32[]{:S(2)}, u32[]{:S(2)}) %collective-permute-start.39) | collective-permute-done | bytes 819232 | tf_op jit(solution)/shard_map/ppermute | solution.py:186
  805.9 25.1 %collective-permute-done.51 = bf16[4,40,5120]{2,1,0:T(8,128)(2,1)} collective-permute-done((bf16[4,40,5120]{2,1,0:T(8,128)(2,1)}, bf16[4,40,5120]{2,1,0:T(8,128)(2,1)}, u32[]{:S(2)}, u32[]{:S(2)}) %collective-permute-start.51) | collective-permute-done | bytes 1638432 | tf_op jit(solution)/shard_map/ppermute | solution.py:186
  837.4 9.3 %collective-permute-done.45 = bf16[4,160,640]{2,1,0:T(8,128)(2,1)S(1)} collective-permute-done((bf16[4,160,640]{2,1,0:T(8,128)(2,1)S(1)}, bf16[4,160,640]{2,1,0:T(8,128)(2,1)S(1)}, u32[]{:S(2)}, u32[]{:S(2)}) %collective-permute-start.45) | collective-permute-done | bytes 819232 | tf_op jit(solution)/shard_map/ppermute | solution.py:186
  851.2 5.5 collective-permute-done.54
  856.7 38.5 %collective-permute-done.53 = bf16[40,5120]{1,0:T(8,128)(2,1)} collective-permute-done((bf16[40,5120]{1,0:T(8,128)(2,1)S(1)}, bf16[40,5120]{1,0:T(8,128)(2,1)}, u32[]{:S(2)}, u32[]{:S(2)}) %collective-permute-start.53) | collective-permute-done | bytes 409632 | tf_op jit(solution)/shard_map/ppermute | solution.py:186
  (584 shorter events, 271.6 us)
Async XLA Ops:
  8.0 640.6 %reduce-scatter.7.cloned.1.call-start = ((), (), s32[]{:S(2)}) async-start(), calls=%async_computation.5 | async-start | bytes 512000 | tf_op jit(solution)/shard_map/reduce_scatter | solution.py:234
  8.9 22.3 %collective-permute-start.14 = (s32[1,64]{1,0:T(1,128)S(1)}, s32[1,64]{1,0:T(1,128)S(1)}, u32[]{:S(2)}, u32[]{:S(2)}) collective-permute-start(s32[1,64]{1,0:T(1,128)S(1)} %reshape.690), channel_id=1, source_target_pairs={{0,1},{1,0},{2,3},{3,2},{4,5},{5,4},{6,7},{7,6},{8,9},{9,8},{10,11... | collective-permute-start | bytes 776 | tf_op jit(solution)/shard_map/ppermute | solution.py:180
  14.9 62.1 %collective-permute-start = (bf16[80,5120]{1,0:T(8,128)(2,1)}, bf16[80,5120]{1,0:T(8,128)(2,1)}, u32[]{:S(2)}, u32[]{:S(2)}) collective-permute-start(bf16[80,5120]{1,0:T(8,128)(2,1)} %pad_maximum_fusion.10), channel_id=1, source_target_pairs={{0,1},{1,0},{2,3},{3,2},{4,5},{5,4},{6,7},{7,6},{8,9},{9,8},{10,11... | collective-permute-start | bytes 2457608 | tf_op jit(solution)/shard_map/ppermute | solution.py:180
  23.7 75.8 %collective-permute-start.6 = (bf16[80,10240]{1,0:T(8,128)(2,1)}, bf16[80,10240]{1,0:T(8,128)(2,1)}, u32[]{:S(2)}, u32[]{:S(2)}) collective-permute-start(bf16[80,10240]{1,0:T(8,128)(2,1)} %dynamic-slice_dynamic-update-slice_fusion.1), channel_id=1, source_target_pairs={{0,1},{1,0},{2,3},{3,2},{4,5},{5,4},{6,7},{7,6},{8,9},{9,8},{10,11... | collective-permute-start | bytes 4915208 | tf_op jit(solution)/shard_map/ppermute | solution.py:180
  31.7 45.3 %collective-permute-start.15 = (bf16[128,1280]{1,0:T(8,128)(2,1)S(1)}, bf16[128,1280]{1,0:T(8,128)(2,1)S(1)}, u32[]{:S(2)}, u32[]{:S(2)}) collective-permute-start(bf16[128,1280]{1,0:T(8,128)(2,1)S(1)} %convolution_convert_fusion.12), channel_id=1, source_target_pairs={{0,1},{1,0},{2,3},{3,2},{4,5},{5,4},{6,7},{7,6},{8,9},{9,8},{10,11... | collective-permute-start | bytes 983048 | tf_op jit(solution)/shard_map/ppermute | solution.py:180
  77.1 19.1 %collective-permute-start.2 = (bf16[80,5120]{1,0:T(8,128)(2,1)}, bf16[80,5120]{1,0:T(8,128)(2,1)S(1)}, u32[]{:S(2)}, u32[]{:S(2)}) collective-permute-start(bf16[80,5120]{1,0:T(8,128)(2,1)} %collective-permute-done), channel_id=1, source_target_pairs={{0,8},{2,10},{4,12},{6,14},{8,0},{10,2},{12,4},{14,6},{16,24},{18,... | collective-permute-start | bytes 2457608 | tf_op jit(solution)/shard_map/ppermute | solution.py:186
  78.7 19.5 %collective-permute-start.1 = (bf16[80,5120]{1,0:T(8,128)(2,1)}, bf16[80,5120]{1,0:T(8,128)(2,1)S(1)}, u32[]{:S(2)}, u32[]{:S(2)}) collective-permute-start(bf16[80,5120]{1,0:T(8,128)(2,1)} %collective-permute-done), channel_id=1, source_target_pairs={{0,4},{2,6},{4,0},{6,2},{8,12},{10,14},{12,8},{14,10},{16,20},{18,... | collective-permute-start | bytes 2457608 | tf_op jit(solution)/shard_map/ppermute | solution.py:186
  98.3 14.2 %collective-permute-start.4 = (bf16[48,5120]{1,0:T(8,128)(2,1)S(1)}, bf16[48,5120]{1,0:T(8,128)(2,1)S(1)}, u32[]{:S(2)}, u32[]{:S(2)}) collective-permute-start(bf16[48,5120]{1,0:T(8,128)(2,1)S(1)} %slice.162), channel_id=1, source_target_pairs={{0,8},{2,10},{4,12},{6,14},{8,0},{10,2},{12,4},{14,6},{16,24},{18,... | collective-permute-start | bytes 1474568 | tf_op jit(solution)/shard_map/ppermute | solution.py:186
  99.4 44.5 %collective-permute-start.8 = (bf16[80,10240]{1,0:T(8,128)(2,1)}, bf16[80,10240]{1,0:T(8,128)(2,1)S(1)}, u32[]{:S(2)}, u32[]{:S(2)}) collective-permute-start(bf16[80,10240]{1,0:T(8,128)(2,1)} %collective-permute-done.6), channel_id=1, source_target_pairs={{0,8},{2,10},{4,12},{6,14},{8,0},{10,2},{12,4},{14,6},{16,24},{18,... | collective-permute-start | bytes 4915208 | tf_op jit(solution)/shard_map/ppermute | solution.py:186
  100.4 44.6 %collective-permute-start.7 = (bf16[80,10240]{1,0:T(8,128)(2,1)}, bf16[80,10240]{1,0:T(8,128)(2,1)S(1)}, u32[]{:S(2)}, u32[]{:S(2)}) collective-permute-start(bf16[80,10240]{1,0:T(8,128)(2,1)} %collective-permute-done.6), channel_id=1, source_target_pairs={{0,4},{2,6},{4,0},{6,2},{8,12},{10,14},{12,8},{14,10},{16,20},{18,... | collective-permute-start | bytes 4915208 | tf_op jit(solution)/shard_map/ppermute | solution.py:186
  112.6 53.2 %collective-permute-start.5 = (bf16[320,5120]{1,0:T(8,128)(2,1)S(1)}, bf16[320,5120]{1,0:T(8,128)(2,1)S(1)}, u32[]{:S(2)}, u32[]{:S(2)}) collective-permute-start(bf16[320,5120]{1,0:T(8,128)(2,1)S(1)} %constant_dynamic-update-slice_fusion.refs_2_), channel_id=1, source_target_pairs={{0,2},{2,0},{4,6},{6,4},{8,10},{10,8},{12,14},{14,12},{16,18},{18,... | collective-permute-start | bytes 9830408 | tf_op jit(solution)/shard_map/ppermute | solution.py:186
  144.0 12.3 %collective-permute-start.9 = (bf16[32,10240]{1,0:T(8,128)(2,1)S(1)}, bf16[32,10240]{1,0:T(8,128)(2,1)S(1)}, u32[]{:S(2)}, u32[]{:S(2)}) collective-permute-start(bf16[32,10240]{1,0:T(8,128)(2,1)S(1)} %slice.166), channel_id=1, source_target_pairs={{0,4},{2,6},{4,0},{6,2},{8,12},{10,14},{12,8},{14,10},{16,20},{18,... | collective-permute-start | bytes 1966088 | tf_op jit(solution)/shard_map/ppermute | solution.py:186
  145.1 19.5 %collective-permute-start.10 = (bf16[48,10240]{1,0:T(8,128)(2,1)S(1)}, bf16[48,10240]{1,0:T(8,128)(2,1)S(1)}, u32[]{:S(2)}, u32[]{:S(2)}) collective-permute-start(bf16[48,10240]{1,0:T(8,128)(2,1)S(1)} %slice.167), channel_id=1, source_target_pairs={{0,8},{2,10},{4,12},{6,14},{8,0},{10,2},{12,4},{14,6},{16,24},{18,... | collective-permute-start | bytes 2949128 | tf_op jit(solution)/shard_map/ppermute | solution.py:186
  165.7 53.6 %collective-permute-start.11 = (bf16[320,10240]{1,0:T(8,128)(2,1)}, bf16[320,10240]{1,0:T(8,128)(2,1)}, u32[]{:S(2)}, u32[]{:S(2)}) collective-permute-start(bf16[320,10240]{1,0:T(8,128)(2,1)} %constant_dynamic-update-slice_fusion.5.refs_2_), channel_id=1, source_target_pairs={{0,2},{2,0},{4,6},{6,4},{8,10},{10,8},{12,14},{14,12},{16,18},{18,... | collective-permute-start | bytes 19660808 | tf_op jit(solution)/shard_map/ppermute | solution.py:186
  299.6 20.5 %collective-permute-start.16 = (bf16[64,5120]{1,0:T(8,128)(2,1)S(1)}, bf16[64,5120]{1,0:T(8,128)(2,1)S(1)}, u32[]{:S(2)}, u32[]{:S(2)}) collective-permute-start(bf16[64,5120]{1,0:T(8,128)(2,1)S(1)} %dynamic-slice_bitcast_fusion.11), channel_id=1, source_target_pairs={{0,1},{1,0},{2,3},{3,2},{4,5},{5,4},{6,7},{7,6},{8,9},{9,8},{10,11... | collective-permute-start | bytes 1966088 | tf_op jit(solution)/shard_map/ppermute | solution.py:180
  306.8 13.3 %collective-permute-start.13 = (f32[8,5120]{1,0:T(8,128)S(1)}, f32[8,5120]{1,0:T(8,128)S(1)}, u32[]{:S(2)}, u32[]{:S(2)}) collective-permute-start(f32[8,5120]{1,0:T(8,128)S(1)} %fusion.119), channel_id=1, source_target_pairs={{0,1},{1,0},{2,3},{3,2},{4,5},{5,4},{6,7},{7,6},{8,9},{9,8},{10,11... | collective-permute-start | bytes 491528 | tf_op jit(solution)/shard_map/ppermute | solution.py:180
  416.8 431.6 %all-gather.2.cloned.1.call-start = ((), (), s32[]{:S(2)}) async-start(), calls=%async_computation.8 | async-start | bytes 1392640 | tf_op jit(solution)/shard_map/all_gather | solution.py:420
  446.5 145.9 %collective-permute-start.49 = (bf16[1,64,5120]{2,1,0:T(8,128)(2,1)}, bf16[1,64,5120]{2,1,0:T(8,128)(2,1)}, u32[]{:S(2)}, u32[]{:S(2)}) collective-permute-start(bf16[1,64,5120]{2,1,0:T(8,128)(2,1)} %bitcast.513), channel_id=1, source_target_pairs={{0,1},{1,0},{2,3},{3,2},{4,5},{5,4},{6,7},{7,6},{8,9},{9,8},{10,11... | collective-permute-start | bytes 1966088 | tf_op jit(solution)/shard_map/ppermute | solution.py:180
  447.5 450.1 %reduce-scatter.5.cloned.1.call-start = ((), (), s32[]{:S(2)}) async-start(), calls=%async_computation.4 | async-start | bytes 1536000 | tf_op jit(solution)/shard_map/reduce_scatter | solution.py:234
  565.9 92.3 %collective-permute-start.37 = (bf16[4,2,2,40,2560]{4,3,0,1,2:T(8,128)(2,1)}, bf16[4,2,2,40,2560]{4,3,0,1,2:T(8,128)(2,1)}, u32[]{:S(2)}, u32[]{:S(2)}) collective-permute-start(bf16[4,2,2,40,2560]{4,3,0,1,2:T(8,128)(2,1)} %bitcast.458), channel_id=1, source_target_pairs={{0,2},{2,0},{4,6},{6,4},{8,10},{10,8},{12,14},{14,12},{16,18},{18,... | collective-permute-start | bytes 9830408 | tf_op jit(solution)/shard_map/ppermute | solution.py:186
  597.1 20.4 %collective-permute-start.22 = (f32[1,800]{1,0:T(1,128)S(1)}, f32[1,800]{1,0:T(1,128)S(1)}, u32[]{:S(2)}, u32[]{:S(2)}) collective-permute-start(f32[1,800]{1,0:T(1,128)S(1)} %get-tuple-element.122), channel_id=1, source_target_pairs={{0,8},{2,10},{4,12},{6,14},{8,0},{10,2},{12,4},{14,6},{16,24},{18,... | collective-permute-start | bytes 9608 | tf_op jit(solution)/shard_map/ppermute | solution.py:186
  597.2 20.9 %collective-permute-start.24 = (f32[1,800]{1,0:T(1,128)S(1)}, f32[1,800]{1,0:T(1,128)S(1)}, u32[]{:S(2)}, u32[]{:S(2)}) collective-permute-start(f32[1,800]{1,0:T(1,128)S(1)} %get-tuple-element.123), channel_id=1, source_target_pairs={{0,24},{2,26},{4,28},{6,30},{8,16},{10,18},{12,20},{14,22},{16,8},... | collective-permute-start | bytes 9608 | tf_op jit(solution)/shard_map/ppermute | solution.py:186
  597.3 20.9 %collective-permute-start.23 = (f32[1,800]{1,0:T(1,128)S(1)}, f32[1,800]{1,0:T(1,128)S(1)}, u32[]{:S(2)}, u32[]{:S(2)}) collective-permute-start(f32[1,800]{1,0:T(1,128)S(1)} %get-tuple-element.124), channel_id=1, source_target_pairs={{0,16},{2,18},{4,20},{6,22},{8,24},{10,26},{12,28},{14,30},{16,0},... | collective-permute-start | bytes 9608 | tf_op jit(solution)/shard_map/ppermute | solution.py:186
  604.4 15.1 %collective-permute-start.56 = (bf16[4,2,32,1280]{3,2,0,1:T(8,128)(2,1)}, bf16[4,2,32,1280]{3,2,0,1:T(8,128)(2,1)}, u32[]{:S(2)}, u32[]{:S(2)}) collective-permute-start(bf16[4,2,32,1280]{3,2,0,1:T(8,128)(2,1)} %bitcast.463), channel_id=1, source_target_pairs={{0,2},{2,0},{4,6},{6,4},{8,10},{10,8},{12,14},{14,12},{16,18},{18,... | collective-permute-start | bytes 1966088 | tf_op jit(solution)/shard_map/ppermute | solution.py:186
  617.5 32.7 %collective-permute-start.25 = (bf16[4,2,2,40,1920]{4,3,0,1,2:T(8,128)(2,1)}, bf16[4,2,2,40,1920]{4,3,0,1,2:T(8,128)(2,1)}, u32[]{:S(2)}, u32[]{:S(2)}) collective-permute-start(bf16[4,2,2,40,1920]{4,3,0,1,2:T(8,128)(2,1)} %bitcast.460), channel_id=1, source_target_pairs={{0,2},{2,0},{4,6},{6,4},{8,10},{10,8},{12,14},{14,12},{16,18},{18,... | collective-permute-start | bytes 7372808 | tf_op jit(solution)/shard_map/ppermute | solution.py:186
  618.1 35.9 %collective-permute-start.28 = (bf16[4,2,2,40,1920]{4,3,0,2,1:T(8,128)(2,1)}, bf16[4,2,2,40,1920]{4,3,0,2,1:T(8,128)(2,1)}, u32[]{:S(2)}, u32[]{:S(2)}) collective-permute-start(bf16[4,2,2,40,1920]{4,3,0,2,1:T(8,128)(2,1)} %bitcast.459), channel_id=1, source_target_pairs={{0,2},{2,0},{4,6},{6,4},{8,10},{10,8},{12,14},{14,12},{16,18},{18,... | collective-permute-start | bytes 7372808 | tf_op jit(solution)/shard_map/ppermute | solution.py:186
  645.1 17.0 %collective-permute-start.40 = (bf16[4,2,2,40,2560]{4,3,0,2,1:T(8,128)(2,1)}, bf16[4,2,2,40,2560]{4,3,0,2,1:T(8,128)(2,1)}, u32[]{:S(2)}, u32[]{:S(2)}) collective-permute-start(bf16[4,2,2,40,2560]{4,3,0,2,1:T(8,128)(2,1)} %bitcast.457), channel_id=1, source_target_pairs={{0,2},{2,0},{4,6},{6,4},{8,10},{10,8},{12,14},{14,12},{16,18},{18,... | collective-permute-start | bytes 9830408 | tf_op jit(solution)/shard_map/ppermute | solution.py:186
  647.9 20.1 %collective-permute-start.43 = (bf16[4,2,2,160,640]{4,3,0,1,2:T(8,128)(2,1)}, bf16[4,2,2,160,640]{4,3,0,1,2:T(8,128)(2,1)}, u32[]{:S(2)}, u32[]{:S(2)}) collective-permute-start(bf16[4,2,2,160,640]{4,3,0,1,2:T(8,128)(2,1)} %bitcast.456), channel_id=1, source_target_pairs={{0,2},{2,0},{4,6},{6,4},{8,10},{10,8},{12,14},{14,12},{16,18},{18,... | collective-permute-start | bytes 9830408 | tf_op jit(solution)/shard_map/ppermute | solution.py:186
  650.2 25.8 %collective-permute-start.46 = (bf16[4,2,2,160,640]{4,3,0,2,1:T(8,128)(2,1)}, bf16[4,2,2,160,640]{4,3,0,2,1:T(8,128)(2,1)}, u32[]{:S(2)}, u32[]{:S(2)}) collective-permute-start(bf16[4,2,2,160,640]{4,3,0,2,1:T(8,128)(2,1)} %bitcast.511), channel_id=1, source_target_pairs={{0,2},{2,0},{4,6},{6,4},{8,10},{10,8},{12,14},{14,12},{16,18},{18,... | collective-permute-start | bytes 9830408 | tf_op jit(solution)/shard_map/ppermute | solution.py:186
  654.1 40.1 %collective-permute-start.50 = (bf16[4,2,40,5120]{3,2,0,1:T(8,128)(2,1)S(1)}, bf16[4,2,40,5120]{3,2,0,1:T(8,128)(2,1)}, u32[]{:S(2)}, u32[]{:S(2)}) collective-permute-start(bf16[4,2,40,5120]{3,2,0,1:T(8,128)(2,1)S(1)} %bitcast.512), channel_id=1, source_target_pairs={{0,2},{2,0},{4,6},{6,4},{8,10},{10,8},{12,14},{14,12},{16,18},{18,... | collective-permute-start | bytes 9830408 | tf_op jit(solution)/shard_map/ppermute | solution.py:186
  658.2 30.0 %collective-permute-start.26 = (bf16[4,2,40,1920]{3,2,0,1:T(8,128)(2,1)S(1)}, bf16[4,2,40,1920]{3,2,0,1:T(8,128)(2,1)S(1)}, u32[]{:S(2)}, u32[]{:S(2)}) collective-permute-start(bf16[4,2,40,1920]{3,2,0,1:T(8,128)(2,1)S(1)} %dynamic-slice_bitcast_fusion.6), channel_id=1, source_target_pairs={{0,1},{1,0},{2,3},{3,2},{4,5},{5,4},{6,7},{7,6},{8,9},{9,8},{10,11... | collective-permute-start | bytes 3686408 | tf_op jit(solution)/shard_map/ppermute | solution.py:180
  662.1 30.0 %collective-permute-start.29 = (bf16[4,2,40,1920]{3,2,0,1:T(8,128)(2,1)S(1)}, bf16[4,2,40,1920]{3,2,0,1:T(8,128)(2,1)S(1)}, u32[]{:S(2)}, u32[]{:S(2)}) collective-permute-start(bf16[4,2,40,1920]{3,2,0,1:T(8,128)(2,1)S(1)} %dynamic-slice_bitcast_fusion.5), channel_id=1, source_target_pairs={{0,4},{2,6},{4,0},{6,2},{8,12},{10,14},{12,8},{14,10},{16,20},{18,... | collective-permute-start | bytes 3686408 | tf_op jit(solution)/shard_map/ppermute | solution.py:186
  668.0 104.0 %collective-permute-start.38 = (bf16[4,2,40,2560]{3,2,0,1:T(8,128)(2,1)}, bf16[4,2,40,2560]{3,2,0,1:T(8,128)(2,1)}, u32[]{:S(2)}, u32[]{:S(2)}) collective-permute-start(bf16[4,2,40,2560]{3,2,0,1:T(8,128)(2,1)} %dynamic-slice_bitcast_fusion.4), channel_id=1, source_target_pairs={{0,1},{1,0},{2,3},{3,2},{4,5},{5,4},{6,7},{7,6},{8,9},{9,8},{10,11... | collective-permute-start | bytes 4915208 | tf_op jit(solution)/shard_map/ppermute | solution.py:180
  676.0 100.3 %collective-permute-start.41 = (bf16[4,2,40,2560]{3,2,0,1:T(8,128)(2,1)}, bf16[4,2,40,2560]{3,2,0,1:T(8,128)(2,1)}, u32[]{:S(2)}, u32[]{:S(2)}) collective-permute-start(bf16[4,2,40,2560]{3,2,0,1:T(8,128)(2,1)} %dynamic-slice_bitcast_fusion.3), channel_id=1, source_target_pairs={{0,4},{2,6},{4,0},{6,2},{8,12},{10,14},{12,8},{14,10},{16,20},{18,... | collective-permute-start | bytes 4915208 | tf_op jit(solution)/shard_map/ppermute | solution.py:186
  688.2 111.0 %collective-permute-start.44 = (bf16[4,2,160,640]{3,2,0,1:T(8,128)(2,1)}, bf16[4,2,160,640]{3,2,0,1:T(8,128)(2,1)}, u32[]{:S(2)}, u32[]{:S(2)}) collective-permute-start(bf16[4,2,160,640]{3,2,0,1:T(8,128)(2,1)} %dynamic-slice_bitcast_fusion.2), channel_id=1, source_target_pairs={{0,1},{1,0},{2,3},{3,2},{4,5},{5,4},{6,7},{7,6},{8,9},{9,8},{10,11... | collective-permute-start | bytes 4915208 | tf_op jit(solution)/shard_map/ppermute | solution.py:180
  692.1 47.0 %collective-permute-start.27 = (bf16[4,40,1920]{2,1,0:T(8,128)(2,1)S(1)}, bf16[4,40,1920]{2,1,0:T(8,128)(2,1)S(1)}, u32[]{:S(2)}, u32[]{:S(2)}) collective-permute-start(bf16[4,40,1920]{2,1,0:T(8,128)(2,1)S(1)} %dynamic-slice_bitcast_fusion.13), channel_id=1, source_target_pairs={{0,4},{2,6},{4,0},{6,2},{8,12},{10,14},{12,8},{14,10},{16,20},{18,... | collective-permute-start | bytes 1843208 | tf_op jit(solution)/shard_map/ppermute | solution.py:186
  694.2 76.4 %collective-permute-start.30 = (bf16[4,40,1920]{2,1,0:T(8,128)(2,1)S(1)}, bf16[4,40,1920]{2,1,0:T(8,128)(2,1)S(1)}, u32[]{:S(2)}, u32[]{:S(2)}) collective-permute-start(bf16[4,40,1920]{2,1,0:T(8,128)(2,1)S(1)} %dynamic-slice_bitcast_fusion.12), channel_id=1, source_target_pairs={{0,1},{1,0},{2,3},{3,2},{4,5},{5,4},{6,7},{7,6},{8,9},{9,8},{10,11... | collective-permute-start | bytes 1843208 | tf_op jit(solution)/shard_map/ppermute | solution.py:180
  739.1 63.6 %collective-permute-start.47 = (bf16[4,2,160,640]{3,2,0,1:T(8,128)(2,1)}, bf16[4,2,160,640]{3,2,0,1:T(8,128)(2,1)}, u32[]{:S(2)}, u32[]{:S(2)}) collective-permute-start(bf16[4,2,160,640]{3,2,0,1:T(8,128)(2,1)} %dynamic-slice_bitcast_fusion.1), channel_id=1, source_target_pairs={{0,4},{2,6},{4,0},{6,2},{8,12},{10,14},{12,8},{14,10},{16,20},{18,... | collective-permute-start | bytes 4915208 | tf_op jit(solution)/shard_map/ppermute | solution.py:186
  771.9 127.6 %reduce-scatter.9.cloned.1.call-start = ((), (), s32[]{:S(2)}) async-start(), calls=%async_computation.6 | async-start | bytes 2048000 | tf_op jit(solution)/shard_map/reduce_scatter | solution.py:234
  774.5 21.2 %collective-permute-start.39 = (bf16[4,40,2560]{2,1,0:T(8,128)(2,1)S(1)}, bf16[4,40,2560]{2,1,0:T(8,128)(2,1)S(1)}, u32[]{:S(2)}, u32[]{:S(2)}) collective-permute-start(bf16[4,40,2560]{2,1,0:T(8,128)(2,1)S(1)} %dynamic-slice_bitcast_fusion.10), channel_id=1, source_target_pairs={{0,4},{2,6},{4,0},{6,2},{8,12},{10,14},{12,8},{14,10},{16,20},{18,... | collective-permute-start | bytes 2457608 | tf_op jit(solution)/shard_map/ppermute | solution.py:186
  778.2 19.3 %collective-permute-start.42 = (bf16[4,40,2560]{2,1,0:T(8,128)(2,1)S(1)}, bf16[4,40,2560]{2,1,0:T(8,128)(2,1)S(1)}, u32[]{:S(2)}, u32[]{:S(2)}) collective-permute-start(bf16[4,40,2560]{2,1,0:T(8,128)(2,1)S(1)} %dynamic-slice_bitcast_fusion.9), channel_id=1, source_target_pairs={{0,1},{1,0},{2,3},{3,2},{4,5},{5,4},{6,7},{7,6},{8,9},{9,8},{10,11... | collective-permute-start | bytes 2457608 | tf_op jit(solution)/shard_map/ppermute | solution.py:180
  780.7 50.3 %collective-permute-start.51 = (bf16[4,40,5120]{2,1,0:T(8,128)(2,1)}, bf16[4,40,5120]{2,1,0:T(8,128)(2,1)}, u32[]{:S(2)}, u32[]{:S(2)}) collective-permute-start(bf16[4,40,5120]{2,1,0:T(8,128)(2,1)} %dynamic-slice_bitcast_fusion), channel_id=1, source_target_pairs={{0,4},{2,6},{4,0},{6,2},{8,12},{10,14},{12,8},{14,10},{16,20},{18,... | collective-permute-start | bytes 4915208 | tf_op jit(solution)/shard_map/ppermute | solution.py:186
  799.1 102.3 %reduce-scatter.11.cloned.1.call-start = ((), (), s32[]{:S(2)}) async-start(), calls=%async_computation.7 | async-start | bytes 2048000 | tf_op jit(solution)/shard_map/reduce_scatter | solution.py:234
  802.2 44.5 %collective-permute-start.45 = (bf16[4,160,640]{2,1,0:T(8,128)(2,1)S(1)}, bf16[4,160,640]{2,1,0:T(8,128)(2,1)S(1)}, u32[]{:S(2)}, u32[]{:S(2)}) collective-permute-start(bf16[4,160,640]{2,1,0:T(8,128)(2,1)S(1)} %dynamic-slice_bitcast_fusion.8), channel_id=1, source_target_pairs={{0,4},{2,6},{4,0},{6,2},{8,12},{10,14},{12,8},{14,10},{16,20},{18,... | collective-permute-start | bytes 2457608 | tf_op jit(solution)/shard_map/ppermute | solution.py:186
  804.9 41.9 %collective-permute-start.48 = (bf16[4,160,640]{2,1,0:T(8,128)(2,1)S(1)}, bf16[4,160,640]{2,1,0:T(8,128)(2,1)S(1)}, u32[]{:S(2)}, u32[]{:S(2)}) collective-permute-start(bf16[4,160,640]{2,1,0:T(8,128)(2,1)S(1)} %dynamic-slice_bitcast_fusion.7), channel_id=1, source_target_pairs={{0,1},{1,0},{2,3},{3,2},{4,5},{5,4},{6,7},{7,6},{8,9},{9,8},{10,11... | collective-permute-start | bytes 2457608 | tf_op jit(solution)/shard_map/ppermute | solution.py:180
  833.9 17.3 %collective-permute-start.52 = (bf16[40,5120]{1,0:T(8,128)(2,1)}, bf16[40,5120]{1,0:T(8,128)(2,1)}, u32[]{:S(2)}, u32[]{:S(2)}) collective-permute-start(bf16[40,5120]{1,0:T(8,128)(2,1)} %get-tuple-element.98), channel_id=1, source_target_pairs={{0,8},{2,10},{4,12},{6,14},{8,0},{10,2},{12,4},{14,6},{16,24},{18,... | collective-permute-start | bytes 1228808 | tf_op jit(solution)/shard_map/ppermute | solution.py:186
  834.0 22.7 %collective-permute-start.54 = (bf16[40,5120]{1,0:T(8,128)(2,1)}, bf16[40,5120]{1,0:T(8,128)(2,1)}, u32[]{:S(2)}, u32[]{:S(2)}) collective-permute-start(bf16[40,5120]{1,0:T(8,128)(2,1)} %get-tuple-element.99), channel_id=1, source_target_pairs={{0,24},{2,26},{4,28},{6,30},{8,16},{10,18},{12,20},{14,22},{16,8},... | collective-permute-start | bytes 1228808 | tf_op jit(solution)/shard_map/ppermute | solution.py:186
  834.9 60.4 %collective-permute-start.53 = (bf16[40,5120]{1,0:T(8,128)(2,1)S(1)}, bf16[40,5120]{1,0:T(8,128)(2,1)}, u32[]{:S(2)}, u32[]{:S(2)}) collective-permute-start(bf16[40,5120]{1,0:T(8,128)(2,1)S(1)} %get-tuple-element.100), channel_id=1, source_target_pairs={{0,16},{2,18},{4,20},{6,22},{8,24},{10,26},{12,28},{14,30},{16,0},... | collective-permute-start | bytes 1228808 | tf_op jit(solution)/shard_map/ppermute | solution.py:186
  (142 other events, 1907.2 us)
Sparse Core Ops, SparseCore 0:
  416.9 21.2 reduce-scatter.6
  772.0 28.2 reduce-scatter.4
  802.6 37.7 reduce-scatter.8
  848.5 48.4 reduce-scatter.10
Sparse Core Ops, SparseCore 1:
  447.6 35.6 all-gather.1

commit v2 on v0

--- a/solution.py
+++ b/solution.py
@@ -3,6 +3,8 @@
 import jax
 import jax.numpy as jnp
 from jax import lax
+from jax.experimental import pallas as pl
+from jax.experimental.pallas import tpu as pltpu
 from jax.sharding import PartitionSpec as P
 
 D = 1280
@@ -12,10 +14,11 @@
 ROW_LEN = 512
 CELLS_ROW = 4
 GENES = 1024
-
-
 EPSILON = 1e-05
 HIGHEST = lax.Precision.HIGHEST
+F32 = jnp.float32
+BF16 = jnp.bfloat16
+VMEM_ASKED = 56 << 20
 
 
 def layer_norm(values_in, scale_row, offset_row):
@@ -26,6 +29,18 @@
 
 def smooth_gate(values_in):
     return jax.nn.gelu(values_in, approximate=False)
+
+
+def dot(left, right):
+    return jnp.dot(left, right, preferred_element_type=F32)
+
+
+def dot_rt(left, right):
+    return lax.dot_general(left, right, (((1,), (1,)), ((), ())), preferred_element_type=F32)
+
+
+def dot_lt(left, right):
+    return lax.dot_general(left, right, (((0,), (0,)), ((), ())), preferred_element_type=F32)
 
 
 def cell_layout(lengths):
@@ -38,6 +53,1040 @@
     return (starts, segment)
 
 
+def cell_mask(segment_row, segment_column, mask):
+    same = segment_column[...] == segment_row[...]
+    mask[...] = jnp.where(same, 0.0, -1e30)
+
+
+def attend_kernel(segment_row, segment_column, query, key, value, mixed, totals, mask):
+    @pl.when(pl.program_id(1) == 0)
+    def _():
+        cell_mask(segment_row.at[0], segment_column.at[0], mask)
+
+    ones = jnp.ones((8, ROW_LEN), BF16)
+    value_t = value[0].T
+    parts = []
+    for head in range(2):
+        columns = slice(head * HEAD_DIM, (head + 1) * HEAD_DIM)
+        scaled = query[0, :, columns] * jnp.asarray(1.0 / math.sqrt(HEAD_DIM), BF16)
+        scores = dot_rt(key[0, :, columns], scaled) + mask[...]
+        top = jnp.max(scores, axis=0, keepdims=True)
+        weights = jnp.exp(scores - top).astype(BF16)
+        left = jnp.concatenate([value_t[columns], ones], axis=0)
+        product = dot(left, weights)
+        total = product[HEAD_DIM : HEAD_DIM + 1]
+        parts.append(product[:HEAD_DIM] / total)
+        totals[0, 0, head : head + 1] = top + jnp.log(total)
+    mixed[0] = jnp.concatenate(parts, axis=0).T.astype(BF16)
+
+
+def attend(qkv, segment, begin, pairs):
+    rows = qkv.shape[0]
+    every = HEADS // 2
+    wide = 2 * HEAD_DIM
+
+    def part(offset):
+        return pl.BlockSpec((1, ROW_LEN, wide), lambda r, i: (r, 0, offset + i))
+
+    return pl.pallas_call(
+        attend_kernel,
+        grid=(rows, pairs),
+        in_specs=[
+            pl.BlockSpec((1, 1, ROW_LEN), lambda r, i: (r, 0, 0)),
+            pl.BlockSpec((1, ROW_LEN, 1), lambda r, i: (r, 0, 0)),
+            part(begin),
+            part(every + begin),
+            part(2 * every + begin),
+        ],
+        out_specs=[
+            pl.BlockSpec((1, ROW_LEN, wide), lambda r, i: (r, 0, i)),
+            pl.BlockSpec((1, 1, 2, ROW_LEN), lambda r, i: (r, i, 0, 0)),
+        ],
+        out_shape=[
+            jax.ShapeDtypeStruct((rows, ROW_LEN, pairs * wide), BF16),
+            jax.ShapeDtypeStruct((rows, pairs, 2, ROW_LEN), F32),
+        ],
+        scratch_shapes=[pltpu.VMEM((ROW_LEN, ROW_LEN), F32)],
+        compiler_params=pltpu.CompilerParams(vmem_limit_bytes=VMEM_ASKED),
+        cost_estimate=pl.CostEstimate(flops=1, bytes_accessed=1, transcendentals=0),
+    )(segment[:, None, :], segment[:, :, None], qkv, qkv, qkv)
+
+
+def attend_back_kernel(
+    segment_row, segment_column, query, key, value, mixed, back, totals, d_query, d_key, d_value, mask
+):
+    @pl.when(pl.program_id(1) == 0)
+    def _():
+        cell_mask(segment_row.at[0], segment_column.at[0], mask)
+
+    scale = jnp.asarray(1.0 / math.sqrt(HEAD_DIM), BF16)
+    key_t = key[0].T
+    product_t = (back[0].astype(F32) * mixed[0].astype(F32)).T
+    queries, keys, values = [], [], []
+    for head in range(2):
+        columns = slice(head * HEAD_DIM, (head + 1) * HEAD_DIM)
+        scaled = query[0, :, columns] * scale
+        grad = back[0, :, columns]
+        scores = dot_rt(key[0, :, columns], scaled) + mask[...]
+        weights = jnp.exp(scores - totals[0, 0, head : head + 1])
+        d_weights = dot_rt(value[0, :, columns], grad)
+        shift = jnp.sum(product_t[columns], axis=0, keepdims=True)
+        d_scores = (weights * (d_weights - shift)).astype(BF16)
+        values.append(dot(weights.astype(BF16), grad))
+        keys.append(dot(d_scores, scaled))
+        queries.append(dot(key_t[columns], d_scores))
+    d_query[0] = (jnp.concatenate(queries, axis=0).T * (1.0 / math.sqrt(HEAD_DIM))).astype(BF16)
+    d_key[0] = jnp.concatenate(keys, axis=1).astype(BF16)
+    d_value[0] = jnp.concatenate(values, axis=1).astype(BF16)
+
+
+def attend_back(qkv, segment, mixed, back, totals):
+    rows = qkv.shape[0]
+    pairs = HEADS // 2
+    wide = 2 * HEAD_DIM
+
+    def part(offset):
+        return pl.BlockSpec((1, ROW_LEN, wide), lambda r, i: (r, 0, offset + i))
+
+    return pl.pallas_call(
+        attend_back_kernel,
+        grid=(rows, pairs),
+        in_specs=[
+            pl.BlockSpec((1, 1, ROW_LEN), lambda r, i: (r, 0, 0)),
+            pl.BlockSpec((1, ROW_LEN, 1), lambda r, i: (r, 0, 0)),
+            part(0),
+            part(pairs),
+            part(2 * pairs),
+            part(0),
+            part(0),
+            pl.BlockSpec((1, 1, 2, ROW_LEN), lambda r, i: (r, i, 0, 0)),
+        ],
+        out_specs=[part(0)] * 3,
+        out_shape=[jax.ShapeDtypeStruct((rows, ROW_LEN, D), BF16)] * 3,
+        scratch_shapes=[pltpu.VMEM((ROW_LEN, ROW_LEN), F32)],
+        compiler_params=pltpu.CompilerParams(vmem_limit_bytes=VMEM_ASKED),
+        cost_estimate=pl.CostEstimate(flops=1, bytes_accessed=1, transcendentals=0),
+    )(segment[:, None, :], segment[:, :, None], qkv, qkv, qkv, mixed, back, totals)
+
+
+CHUNK = 640
+
+
+def part_copies(sources, columns, place, buffer, sems, half_rows, act):
+    shard, *parts = sources
+    query, outer, inner, core = (place[i] for i in range(4))
+    unit = parts[1].shape[0]
+    act(
+        pltpu.make_async_copy(
+            shard.at[:, columns],
+            buffer.at[pl.ds(pl.multiple_of(query * half_rows, 16), half_rows), :],
+            sems.at[0],
+        )
+    )
+    for side in range(2):
+        c = core if side == 0 else 1 - core
+        for part in range(4):
+            zb, y = outer ^ (part // 2), inner ^ (part % 2)
+            row = (1 - query) * half_rows + ((zb * 2 + y) * 2 + c) * unit
+            source = parts[2 * side + part // 3]
+            act(
+                pltpu.make_async_copy(
+                    source.at[pl.ds(part % 3 * unit, unit), columns],
+                    buffer.at[pl.ds(pl.multiple_of(row, 16), unit), :],
+                    sems.at[1 + side * 4 + part],
+                )
+            )
+
+
+def chunk_place(step, place, half):
+    steps = half // CHUNK
+    own = step < steps
+    return jnp.where(own, place[0] * steps + step, (1 - place[0]) * steps + step - steps)
+
+
+def up_copies(sources, place, step, buffer, sems, act):
+    half = FF // 2
+    start = pl.multiple_of(chunk_place(step, place, half) * CHUNK, 128)
+    columns = pl.ds(start, CHUNK)
+    part_copies(sources, columns, place, buffer, sems, sources[0].shape[0], act)
+
+
+def down_copies(sources, place, step, buffer, sems, act):
+    shard, *parts = sources
+    query, outer, inner, core = (place[i] for i in range(4))
+    unit = parts[1].shape[0]
+    fold = shard.shape[0] // (8 * unit)
+    steps = shard.shape[0] // CHUNK
+    own = step < steps
+    local = jnp.where(own, step, step - steps)
+    part = ((local // 2) ^ outer) * 2 + ((local % 2) ^ inner)
+
+    @pl.when(own)
+    def _():
+        act(
+            pltpu.make_async_copy(
+                shard.at[pl.ds(pl.multiple_of(local * CHUNK, 16), CHUNK), :], buffer, sems.at[0]
+            )
+        )
+
+    def remote(corner):
+        for side in range(2):
+            c = core if side == 0 else 1 - core
+            row = 0 if corner else pl.multiple_of(part * unit, 16)
+            for k in range(fold):
+                act(
+                    pltpu.make_async_copy(
+                        parts[2 * side + corner].at[pl.ds(row, unit), pl.ds(k * D, D)],
+                        buffer.at[pl.ds(pl.multiple_of((c * fold + k) * unit, 16), unit), :],
+                        sems.at[1 + side * fold + k],
+                    )
+                )
+
+    @pl.when(jnp.logical_and(jnp.logical_not(own), part < 3))
+    def _():
+        remote(0)
+
+    @pl.when(jnp.logical_and(jnp.logical_not(own), part == 3))
+    def _():
+        remote(1)
+
+
+def stream(copies, buffer, sems):
+    step, steps = pl.program_id(0), pl.num_programs(0)
+    slot = lax.rem(step, 2)
+
+    @pl.when(step == 0)
+    def _():
+        copies(step, buffer.at[slot], sems.at[slot], lambda copy: copy.start())
+
+    @pl.when(step + 1 < steps)
+    def _():
+        copies(step + 1, buffer.at[1 - slot], sems.at[1 - slot], lambda copy: copy.start())
+
+    copies(step, buffer.at[slot], sems.at[slot], lambda copy: copy.wait())
+    return buffer.at[slot]
+
+
+def gate(values):
+    inner = 0.5 * lax.erf(values * math.sqrt(0.5)) + 0.5
+    bell = jnp.exp(values * values * -0.5) * (1.0 / math.sqrt(2.0 * math.pi))
+    return values * inner, inner + values * bell
+
+
+def up_kernel(place, second, bias, *refs):
+    sources, (active, slope, buffer, sems) = refs[:5], refs[5:]
+    weights = stream(lambda *at: up_copies(sources, place, *at), buffer, sems)
+    value, rise = gate(dot(second[...], weights[...]) + bias[...])
+    active[...] = value.astype(BF16)
+    slope[...] = rise.astype(BF16)
+
+
+def down_kernel(place, active, middle, *refs):
+    sources, (out, buffer, sems) = refs[:5], refs[5:]
+    weights = stream(lambda *at: down_copies(sources, place, *at), buffer, sems)
+
+    @pl.when(pl.program_id(0) == 0)
+    def _():
+        out[...] = middle[...]
+
+    out[...] += dot(active[...], weights[...])
+
+
+def back_kernel(place, branch, slope, *refs):
+    up, down = refs[:5], refs[5:10]
+    d_hidden, sums, out, buffer, sems, buffer_two, sems_two = refs[10:]
+    up_part = stream(lambda *at: up_copies(up, place, *at), buffer, sems)
+    down_part = stream(lambda *at: down_copies(down, place, *at), buffer_two, sems_two)
+
+    @pl.when(pl.program_id(0) == 0)
+    def _():
+        out[...] = jnp.zeros_like(out)
+
+    d_active = dot_rt(branch[...], down_part[...])
+    low = (d_active * slope[...].astype(F32)).astype(BF16)
+    d_hidden[...] = low
+    sums[...] = jnp.sum(low.astype(F32), axis=0, keepdims=True)
+    out[...] += dot_rt(low, up_part[...])
+
+
+def feed_call(kernel, count, inputs, outputs, slots, matmuls, place, *values):
+    def at(j, place):
+        return chunk_place(j, place, FF // 2)
+
+    specs = {
+        "hidden": pl.BlockSpec((count, CHUNK), lambda j, place: (0, at(j, place))),
+        "row": pl.BlockSpec((1, CHUNK), lambda j, place: (0, at(j, place))),
+        "whole": pl.BlockSpec((count, D), lambda j, place: (0, 0)),
+        "any": pl.BlockSpec(memory_space=pl.ANY),
+    }
+    shapes = {
+        "hidden": jax.ShapeDtypeStruct((count, FF), BF16),
+        "row": jax.ShapeDtypeStruct((1, FF), F32),
+        "whole": jax.ShapeDtypeStruct((count, D), F32),
+    }
+    scratch = []
+    for slot in slots:
+        scratch += [pltpu.VMEM((2, *slot), BF16), pltpu.SemaphoreType.DMA((2, 9))]
+    return pl.pallas_call(
+        kernel,
+        grid_spec=pltpu.PrefetchScalarGridSpec(
+            num_scalar_prefetch=1,
+            grid=(FF // CHUNK,),
+            in_specs=[specs[name] for name in inputs],
+            out_specs=[specs[name] for name in outputs],
+            scratch_shapes=scratch,
+        ),
+        out_shape=[shapes[name] for name in outputs],
+        compiler_params=pltpu.CompilerParams(vmem_limit_bytes=VMEM_ASKED),
+        cost_estimate=pl.CostEstimate(flops=1, bytes_accessed=1, transcendentals=0),
+    )(place, *values)
+
+
+UP_SLOT, DOWN_SLOT = (D, CHUNK), (CHUNK, D)
+
+
+def feed_up(place, second, bias, up):
+    names = ["whole", "row"] + ["any"] * 5
+    return feed_call(
+        up_kernel, second.shape[0], names, ["hidden", "hidden"], [UP_SLOT], 1, place, second, bias, *up
+    )
+
+
+def feed_down(place, active, middle, down):
+    names = ["hidden", "whole"] + ["any"] * 5
+    return feed_call(
+        down_kernel, active.shape[0], names, ["whole"], [DOWN_SLOT], 1, place, active, middle, *down
+    )[0]
+
+
+def feed_back(place, branch, slope, up, down):
+    names = ["whole", "hidden"] + ["any"] * 10
+    return feed_call(
+        back_kernel, branch.shape[0], names, ["hidden", "row", "whole"], [UP_SLOT, DOWN_SLOT], 2,
+        place, branch, slope, *up, *down,
+    )
+
+
+def term_kernel(steps, place, *refs):
+    count = len(steps)
+    query, _, inner, core = (place[i] for i in range(4))
+    lefts, rights, (own, sent, blocks), turned = (
+        refs[:count],
+        refs[count : 2 * count],
+        refs[2 * count : 2 * count + 3],
+        refs[2 * count + 3 :],
+    )
+    every = sum(steps)
+    step = pl.program_id(0)
+    half = jnp.where(step < every, 1 - core, core)
+
+    @pl.when(step % every == 0)
+    def _():
+        outer = blocks.shape[0] // 8
+        size = 2 * outer * blocks.shape[1]
+        for left, into in zip(lefts, turned):
+            blocks[...] = left[...].astype(F32).T.reshape(blocks.shape)
+            for to in range(4):
+                first, second = to // 2, to % 2
+                x = query ^ jnp.where(half == 0, first, second)
+                y = inner ^ jnp.where(half == 0, second, first)
+                rows = [
+                    blocks[((z * 2 + y) * 2 + c) * 2 + x] for z in range(outer) for c in range(2)
+                ]
+                into[pl.ds(to * size, size), :] = jnp.concatenate(rows, axis=0).astype(BF16)
+
+    column = step % every
+    begin = 0
+    for left, right, size in zip(turned, rights, steps):
+        for out, mine in ((own, True), (sent, False)):
+
+            @pl.when(
+                jnp.logical_and(
+                    jnp.logical_and(column >= begin, column < begin + size), (step >= every) == mine
+                )
+            )
+            def _():
+                out[...] = dot(left[...], right[...]).astype(BF16).reshape(out.shape)
+
+        begin += size
+
+
+def weight_terms(place, *pairs):
+    count, rows = pairs[0][0].shape
+    steps = [right.shape[1] // 2 // CHUNK for _, right in pairs]
+    every = sum(steps)
+    shape = (2, 2, rows // 4, every * CHUNK)
+
+    def right_spec(begin, size):
+        def at(j, place):
+            half = jnp.where(j < every, 1 - place[3], place[3])
+            return (0, half * size + jnp.clip(j % every - begin, 0, size - 1))
+
+        return pl.BlockSpec((count, CHUNK), at)
+
+    block = (2, 2, rows // 4, CHUNK)
+    left_spec = pl.BlockSpec((count, rows), lambda j, place: (0, 0))
+    return pl.pallas_call(
+        lambda *refs: term_kernel(steps, *refs),
+        grid_spec=pltpu.PrefetchScalarGridSpec(
+            num_scalar_prefetch=1,
+            grid=(2 * every,),
+            in_specs=[left_spec] * len(pairs)
+            + [right_spec(sum(steps[:i]), size) for i, size in enumerate(steps)],
+            out_specs=[
+                pl.BlockSpec(block, lambda j, place: (0, 0, 0, jnp.maximum(j - every, 0))),
+                pl.BlockSpec(block, lambda j, place: (0, 0, 0, jnp.minimum(j, every - 1))),
+            ],
+            scratch_shapes=[pltpu.VMEM((32, rows // 32, count), F32)]
+            + [pltpu.VMEM((rows, count), BF16)] * len(pairs),
+        ),
+        out_shape=[jax.ShapeDtypeStruct(shape, BF16)] * 2,
+        compiler_params=pltpu.CompilerParams(vmem_limit_bytes=VMEM_ASKED),
+        cost_estimate=pl.CostEstimate(flops=1, bytes_accessed=1, transcendentals=0),
+    )(place, *[left for left, _ in pairs], *[right for _, right in pairs])
+
+
+def tall_kernel(place, left, right, own, sent, blocks, turned):
+    query, _, inner, core = (place[i] for i in range(4))
+    width = blocks.shape[1]
+    blocks[...] = left[...].astype(F32).T.reshape(blocks.shape)
+    for to in range(4):
+        source = (to % 2) * 2 + to // 2
+        turned[pl.ds(to * width, width), :] = blocks[source].astype(BF16)
+    terms = dot(turned[...], right[...]).astype(BF16)
+    size = terms.shape[1] // 2
+    y_place = (pl.program_id(0) % 2) ^ inner
+    for half in range(2):
+        for x in range(2):
+            x_place = x ^ query
+            at = (y_place, x_place)
+            value = terms[2 * x * width : 2 * (x + 1) * width, half * size : (half + 1) * size]
+
+            @pl.when(core == half)
+            def _():
+                own[at[0], at[1], 0] = value
+
+            @pl.when(core != half)
+            def _():
+                sent[at[0], at[1], 0] = value
+
+
+def tall_terms(place, left, right, outer):
+    count, rows = left.shape
+    columns = right.shape[1]
+    wide = rows // (2 * outer)
+    shape = (2, 2, outer, wide // 2, columns // 2)
+    out = pl.BlockSpec(
+        (2, 2, 1, wide // 2, columns // 2), lambda j, place: (0, 0, j // 2, 0, 0)
+    )
+    own, sent = pl.pallas_call(
+        tall_kernel,
+        grid_spec=pltpu.PrefetchScalarGridSpec(
+            num_scalar_prefetch=1,
+            grid=(2 * outer,),
+            in_specs=[
+                pl.BlockSpec((count, wide), lambda j, place: (0, j)),
+                pl.BlockSpec((count, columns), lambda j, place: (0, 0)),
+            ],
+            out_specs=[out, out],
+            scratch_shapes=[
+                pltpu.VMEM((4, wide // 4, count), F32),
+                pltpu.VMEM((wide, count), BF16),
+            ],
+        ),
+        out_shape=[jax.ShapeDtypeStruct(shape, BF16)] * 2,
+        compiler_params=pltpu.CompilerParams(vmem_limit_bytes=VMEM_ASKED),
+        cost_estimate=pl.CostEstimate(flops=1, bytes_accessed=1, transcendentals=0),
+    )(place, left, right)
+    flat = (2, 2, outer * wide // 2, columns // 2)
+    return own.reshape(flat), sent.reshape(flat)
+
+
+def assemble_kernel(pieces, width, count, place_ref, *refs):
+    sources, full, sems = refs[:count], refs[count], refs[count + 1]
+    step = pl.program_id(0)
+    copies = []
+    for i, (source, row, rows, column) in enumerate(pieces):
+        start = pl.multiple_of(place_ref[i], 16)
+        columns = pl.ds(pl.multiple_of(column + step * width, 128), width)
+        copies.append(
+            pltpu.make_async_copy(
+                sources[source].at[pl.ds(row, rows), columns],
+                full.at[pl.ds(start, rows), :],
+                sems.at[i],
+            )
+        )
+    for copy in copies:
+        copy.start()
+    for copy in copies:
+        copy.wait()
+
+
+def assemble(sources, pieces, places, shape, width):
+    count = len(sources)
+    rows, columns = shape
+    return pl.pallas_call(
+        lambda *refs: assemble_kernel(pieces, width, count, *refs),
+        grid=(columns // width,),
+        out_shape=jax.ShapeDtypeStruct(shape, BF16),
+        in_specs=[pl.BlockSpec(memory_space=pltpu.SMEM)]
+        + [pl.BlockSpec(memory_space=pl.ANY)] * count,
+        out_specs=pl.BlockSpec((rows, width), lambda j: (0, j)),
+        scratch_shapes=[pltpu.SemaphoreType.DMA((len(pieces),))],
+        compiler_params=pltpu.CompilerParams(vmem_limit_bytes=32 << 20),
+        cost_estimate=pl.CostEstimate(flops=1, bytes_accessed=1, transcendentals=0),
+    )(jnp.stack(places).astype(jnp.int32), *sources)
+
+
+def sync(*values):
+    return lax.optimization_barrier(values)
+
+
+def tie(value, *others):
+    return lax.optimization_barrier((value, others))[0] if others else value
+
+
+class Grid:
+    def __init__(self, mesh):
+        dp, query = mesh.shape["dp"], mesh.shape["query"]
+        core = 2 if dp % 2 == 0 else 1
+        rest = dp // core
+        outer = 4 if rest % 4 == 0 else rest
+        inner = rest // outer
+        self.dp, self.query = dp, query
+        self.size = {"z": outer, "y": inner, "c": core, "x": query}
+        self.stride = {"z": inner * core, "y": core, "c": 1}
+        self.order = ["z", "y", "c", "x"]
+
+    def paired(self):
+        size = self.size
+        pairs = size["x"] == 2 and size["y"] == 2 and size["c"] == 2
+        return pairs and size["z"] in (2, 4) and D % (self.dp * self.query * 8) == 0
+
+    def place(self, axis):
+        if axis == "x":
+            return lax.axis_index("query")
+        return (lax.axis_index("dp") // self.stride[axis]) % self.size[axis]
+
+    def partner(self, axis, at, step):
+        size = self.size[axis]
+        return at ^ step if size & (size - 1) == 0 else (at + step) % size
+
+    def sender(self, axis, at, step):
+        size = self.size[axis]
+        return at ^ step if size & (size - 1) == 0 else (at + size - step) % size
+
+    def hop(self, value, axis, step=1):
+        if axis == "x":
+            pairs = [(i, self.partner("x", i, step)) for i in range(self.query)]
+            return lax.ppermute(value, "query", pairs)
+        stride, size = self.stride[axis], self.size[axis]
+        pairs = []
+        for i in range(self.dp):
+            at = (i // stride) % size
+            pairs.append((i, i + (self.partner(axis, at, step) - at) * stride))
+        return lax.ppermute(value, "dp", pairs)
+
+    def turn_hop(self, value, turn):
+        pairs = []
+        for i in range(self.dp):
+            core = i % 2
+            y = (i // self.stride["y"]) % 2
+            for x in range(2):
+                if core == turn:
+                    to = i * 2 + 1 - x
+                else:
+                    to = (i + (1 - 2 * y) * self.stride["y"]) * 2 + x
+                pairs.append((i * 2 + x, to))
+        return lax.ppermute(value, ("dp", "query"), pairs)
+
+    def share(self, value, axis=0, after=()):
+        if self.query == 1:
+            return value
+        if self.query != 2:
+            return lax.all_gather(value, "query", axis=axis, tiled=True)
+        other = tie(self.hop(value, "x"), *after)
+        first = lax.axis_index("query") == 0
+        return jnp.concatenate(
+            [jnp.where(first, value, other), jnp.where(first, other, value)], axis=axis
+        )
+
+    def joined(self, mine, other, axis=0):
+        first = lax.axis_index("query") == 0
+        return jnp.concatenate(
+            [jnp.where(first, mine, other), jnp.where(first, other, mine)], axis=axis
+        )
+
+    def total(self, value):
+        if self.query == 1:
+            return value
+        if self.query != 2:
+            return lax.psum(value, "query")
+        return value + self.hop(value, "x")
+
+    def cut_step(self, value, axis, dim):
+        me = self.place(axis)
+        return (
+            lax.dynamic_index_in_dim(value, me, axis=dim, keepdims=False),
+            lax.dynamic_index_in_dim(value, 1 - me, axis=dim, keepdims=False),
+        )
+
+    def cut_columns(self, terms):
+        half = terms.shape[1] // 2
+        first = self.place("c") == 0
+        left, right = terms[:, :half], terms[:, half:]
+        return jnp.where(first, left, right), jnp.where(first, right, left)
+
+    def join_columns(self, value):
+        value = value.reshape(2, -1, value.shape[-1])
+        mine, other = self.cut_step(value, "c", 0)
+        got = self.hop(other, "c")
+        first = self.place("c") == 0
+        return jnp.concatenate(
+            [jnp.where(first, mine, got), jnp.where(first, got, mine)], axis=1
+        )
+
+    def scatter_step(self, value, axis, dim, kind):
+        size = self.size[axis]
+        me = self.place(axis)
+
+        def part(index):
+            return lax.dynamic_index_in_dim(value, index, axis=dim, keepdims=False)
+
+        if size == 1:
+            return part(0)
+        sent = [
+            self.hop(part(self.partner(axis, me, step)), axis, step) for step in range(1, size)
+        ]
+        total = part(me).astype(F32)
+        for received in sent:
+            total = total + received.astype(F32)
+        return total.astype(kind)
+
+    def scatter(self, value, order, kind=BF16):
+        dims = [axis for axis in self.order if axis in order]
+        for axis in order:
+            dim = dims.index(axis)
+            value = self.scatter_step(value, axis, dim, kind)
+            dims.pop(dim)
+        return value
+
+    def scatter_z(self, value):
+        stride, size = self.stride["z"], self.size["z"]
+        groups = [[k * stride + i for k in range(size)] for i in range(stride)]
+        return lax.psum_scatter(
+            value, "dp", scatter_dimension=0, axis_index_groups=groups, tiled=True
+        )
+
+    def blocks(self, value):
+        shape = [self.size[axis] for axis in self.order]
+        rows = value.shape[0] // math.prod(shape)
+        return value.reshape(*shape, rows, *value.shape[1:])
+
+    def own_columns(self, value):
+        width = value.shape[1] // (self.dp * self.query)
+        shaped = value.reshape(value.shape[0], self.dp, self.query, width)
+        mine = lax.dynamic_index_in_dim(shaped, self.place("x"), axis=2, keepdims=False)
+        return mine.reshape(value.shape[0], self.dp * width)
+
+    def part_of(self, shards):
+        zb, y, c = self.place("z") % 2, self.place("y"), self.place("c")
+        unit = min(shard.shape[0] for shard in shards) // 8
+        mine = (zb * 2 + y) * 2 + c
+        columns = []
+        for shard in shards:
+            fold = shard.shape[0] // (8 * unit)
+            for k in range(fold):
+                columns.append(
+                    lax.dynamic_slice_in_dim(shard, (mine * fold + k) * unit, unit, 0)
+                )
+        return jnp.concatenate(columns, axis=1) if len(columns) > 1 else columns[0]
+
+    def sides_of(self, first, after=()):
+        first = tie(first, *after)
+        return [self.hop(first, "y"), self.hop(first, "z")]
+
+    def corners_of(self, sides, after=()):
+        by_y, by_z = tie(sides, *after)
+        cut = by_y.shape[0] // 2 // 16 * 16
+        sent = (by_z[:cut], by_y[cut:])
+        return sent, [self.hop(sent[0], "y"), self.hop(sent[1], "z")]
+
+    def most_of(self, first, sides, *after):
+        near = jnp.concatenate([tie(first, *after), *sides], axis=0)
+        return near, self.hop(near, "c")
+
+    def corner_of(self, corners, after=()):
+        near = jnp.concatenate(tie(corners, *after), axis=0)
+        return near, self.hop(near, "c")
+
+    def join(self, shard, parts, column):
+        zb, y, c, x = self.place("z") % 2, self.place("y"), self.place("c"), self.place("x")
+        rows, width = shard.shape
+        unit = rows // 8
+        pieces, places = [(0, 0, rows, 0)], [x * rows]
+        for side in range(2):
+            c_ = c if side == 0 else 1 - c
+            for part in range(4):
+                place = ((zb ^ (part // 2)) * 2 + (y ^ (part % 2))) * 2 + c_
+                pieces.append((1 + 2 * side + part // 3, part % 3 * unit, unit, column))
+                places.append((1 - x) * rows + place * unit)
+        return assemble([shard, *parts], pieces, places, (2 * rows, width), 640)
+
+    def places(self):
+        return jnp.stack(
+            [self.place("x"), self.place("z") % 2, self.place("y"), self.place("c")]
+        ).astype(jnp.int32)
+
+
+def added(*values):
+    total = values[0].astype(F32)
+    for value in values[1:]:
+        total = total + value.astype(F32)
+    return total.astype(BF16)
+
+
+def added_wide(*values):
+    total = values[0].astype(F32)
+    for value in values[1:]:
+        total = total + value.astype(F32)
+    return total
+
+
+class Sums:
+    def __init__(self, grid, own, sent):
+        self.grid, self.own, self.sent = grid, own, sent
+
+    def core(self, *after):
+        self.got = self.grid.hop(tie(self.sent, *after), "c")
+
+    def add_first(self, *after):
+        own, got = tie((self.own, self.got), *after)
+        self.first_in = [added(own[1, k], got[1, k]) for k in (1, 0)]
+
+    def add_turned(self, *after):
+        own, got = tie((self.own, self.got), *after)
+        self.one_in = added(own[1], got[1])
+
+    def go_turned(self, *after):
+        one = self.grid.turn_hop(tie(self.one_in, *after), 0)
+        self.one = [one[1], one[0]]
+
+    def add_second(self, *after):
+        own, got, one = tie((self.own, self.got, self.one[0]), *after)
+        self.two_in = added(own[0, 1], got[0, 1], one)
+
+    def add_last(self, *after):
+        own, got, one = tie((self.own, self.got, self.one[1]), *after)
+        whole = added(own[0, 0], got[0, 0], one, self.two)
+        size = self.grid.size["z"]
+        self.last_in = whole.reshape(size, whole.shape[0] // size, whole.shape[1])
+
+    def last(self, *after):
+        self.sum = self.grid.scatter_z(tie(self.last_in, *after))
+
+    def result(self, *after):
+        value = tie(self.sum, *after)[0]
+        value = value.reshape(2, value.shape[0] // 2, value.shape[1])
+        mine, other = self.grid.cut_step(value, "c", 0)
+        got = self.grid.hop(other, "c")
+        first = self.grid.place("c") == 0
+        return [
+            jnp.where(first, mine, got).astype(F32),
+            jnp.where(first, got, mine).astype(F32),
+        ]
+
+
+def make_shards(grid):
+    def shards(
+        tokens,
+        cell_lengths,
+        out_cotangent,
+        ln_gains,
+        ln_biases,
+        proj_biases,
+        ff_biases,
+        w_qkv,
+        w_out,
+        w_up,
+        w_down,
+        dec_cell,
+        dec_gene,
+        dec_out,
+        gene_table,
+        query_ids,
+        labels,
+    ):
+        row_count = tokens.shape[0]
+        token_count = row_count * ROW_LEN
+        dp_count, query_count = grid.dp, grid.query
+        place = lax.axis_index("query")
+        starts, segment = cell_layout(cell_lengths)
+        local_cells = row_count * CELLS_ROW
+        pair_cells, local_queries = query_ids.shape
+        pairs = pair_cells * local_queries
+        half_width = D // query_count
+
+        flat_tokens = tokens.astype(F32).reshape(token_count, D)
+        where = grid.places()
+        ids = grid.share(query_ids.reshape(1, pairs)).reshape(query_count * pairs)
+        qkv_first = grid.hop(grid.part_of([w_qkv]), "x")
+        normed, first_pull = jax.vjp(layer_norm, flat_tokens, ln_gains[0], ln_biases[0])
+        normed_low = normed.astype(BF16)
+        table_rows = gene_table.shape[0]
+        local_ids = ids - place * table_rows
+        held = (local_ids[:, None] == jnp.arange(table_rows, dtype=jnp.int32)[None, :]).astype(BF16)
+        gene_found = dot(held, gene_table).astype(BF16)
+        up_part = grid.part_of([w_up, w_out])
+        down_part = grid.part_of([w_down])
+        qkv_first, normed_low, gene_found, up_part, down_part = sync(
+            qkv_first, normed_low, gene_found, up_part, down_part
+        )
+        up_first = grid.hop(up_part, "x")
+        qkv_sides = sync(*grid.sides_of(qkv_first))
+        _, qkv_corners = grid.corners_of(qkv_sides)
+        qkv_near, qkv_far = grid.most_of(qkv_first, qkv_sides)
+        qkv_corners = sync(*qkv_corners, qkv_near)[:2]
+        qkv_end, qkv_end_far = grid.corner_of(qkv_corners)
+        qkv_end_far, qkv_far, up_first = sync(qkv_end_far, qkv_far, up_first)
+        up_sides = grid.sides_of(up_first)
+        gene_hop = grid.hop(tie(gene_found, up_first), "x")
+        full_qkv = grid.join(w_qkv, (qkv_near, qkv_end, qkv_far, qkv_end_far), 0)
+        zeroes = jnp.zeros((D,), F32)
+        qkv_bias = jnp.concatenate([proj_biases[0], zeroes, proj_biases[1]])
+        qkv_low = (dot(normed_low, full_qkv) + qkv_bias).astype(BF16)
+        qkv_low, *up_sides, gene_hop = sync(qkv_low, *up_sides, gene_hop)
+        qkv_rows = qkv_low.reshape(row_count, ROW_LEN, 3 * D)
+        up_sent, up_corners = grid.corners_of(up_sides)
+        down_first = grid.hop(tie(down_part, gene_hop), "x")
+        cut = HEADS // 4
+        mixed_one, totals_one = attend(tie(qkv_rows, up_sent), segment, 0, cut)
+        gene_rows = added(gene_found, tie(gene_hop, mixed_one)) if query_count == 2 else gene_found
+        up_near, up_far = grid.most_of(up_first, tie(up_sides, mixed_one))
+        mixed_two, totals_two = attend(
+            tie(qkv_rows, mixed_one, up_near), segment, cut, HEADS // 2 - cut
+        )
+        mixed_two, *up_corners, down_first = sync(mixed_two, *up_corners, down_first)
+        down_sides = grid.sides_of(down_first)
+        up_end, up_end_far = grid.corner_of(up_corners)
+        mixed_rows = jnp.concatenate([mixed_one, mixed_two], axis=2)
+        log_totals = jnp.concatenate([totals_one, totals_two], axis=1)
+        mixed_low = mixed_rows.reshape(token_count, D)
+        up_parts = (up_near, up_end, up_far, up_end_far)
+        up_weights = (w_up, *up_parts)
+        full_out = grid.join(w_out, up_parts, FF)
+        middle = flat_tokens + dot(mixed_low, full_out) + proj_biases[2]
+        second, second_pull = jax.vjp(layer_norm, middle, ln_gains[1], ln_biases[1])
+        second_low = second.astype(BF16)
+        gene_half = lax.dynamic_slice_in_dim(gene_rows, place * half_width, half_width, 1)
+        gene_partial = dot(tie(gene_half, mixed_two), dec_gene).astype(BF16).reshape(query_count, pairs, FF)
+        gene_mine, gene_sent = grid.cut_step(gene_partial, "x", 0)
+        second_low, gene_sent = sync(second_low, gene_sent)
+        gene_got = grid.hop(gene_sent, "x")
+        active_low, slope = feed_up(where, second_low, ff_biases[0][None, :], up_weights)
+        active_low, slope, *down_sides, gene_got = sync(active_low, slope, *down_sides, gene_got)
+        places = jnp.arange(ROW_LEN, dtype=jnp.int32)
+        leading = jnp.any(places[None, :, None] == starts[:, None, :], axis=2)
+        early_low = jnp.where(
+            leading[:, :, None], 0, out_cotangent
+        ).reshape(token_count, D).astype(BF16)
+        down_sent, down_corners = grid.corners_of(down_sides)
+        down_near, down_far = grid.most_of(down_first, down_sides, down_sent)
+        early_low = tie(early_low, down_near, down_sent)
+        down_sums = Sums(grid, *tall_terms(where, active_low, early_low, grid.size["z"]))
+        down_sums.sent, *down_corners, down_far = sync(down_sums.sent, *down_corners, down_far)
+        down_end, down_end_far = grid.corner_of(down_corners)
+        down_weights = (w_down, down_near, down_end, down_far, down_end_far)
+        down_sums.core(down_end_far)
+        encoded = feed_down(
+            where, tie(active_low, down_sums.sent), middle + proj_biases[3], down_weights
+        )
+        encoded, down_sums.got = sync(encoded, down_sums.got)
+        encoded_rows = encoded.reshape(row_count, ROW_LEN, D)
+        heads_low = (
+            jnp.take_along_axis(encoded_rows, starts[:, :, None], axis=1)
+            .reshape(local_cells, D)
+            .astype(BF16)
+        )
+        down_sums.add_first(heads_low)
+        heads_hop = grid.hop(heads_low, "x") if query_count == 2 else heads_low
+        one_b = grid.hop(down_sums.first_in[0], "y")
+        cell_heads = grid.joined(heads_low, tie(heads_hop, down_sums.first_in))
+        heads_half = lax.dynamic_slice_in_dim(cell_heads, place * half_width, half_width, 1)
+        cell_part = grid.total(dot(heads_half, dec_cell))
+        gene_part = added_wide(gene_mine, gene_got) + ff_biases[1]
+        before = cell_part[:, None, :] + gene_part.reshape(pair_cells, local_queries, FF)
+        gated_dec, gated_pull = jax.vjp(smooth_gate, before)
+        logit_weight = dec_out.astype(F32)
+        logits = jnp.sum(gated_dec * logit_weight, axis=-1)
+        logit_slope = jax.nn.sigmoid(logits) - labels.astype(F32)
+        (grad_before,) = gated_pull(logit_slope[:, :, None] * logit_weight)
+        before_low = grad_before.astype(BF16)
+        before_sums = jnp.sum(before_low, axis=1, dtype=F32)
+        grad_dec_bias = jnp.sum(before_sums, axis=0)
+        grad_logit = jnp.sum(gated_dec * logit_slope[:, :, None], axis=(0, 1))
+        cell_total = grid.total(before_sums).astype(BF16)
+        heads_part = dot_rt(cell_total, dec_cell).astype(BF16)
+        heads_all = grid.share(heads_part, axis=1)
+        heads_back = lax.dynamic_slice_in_dim(
+            heads_all, place * local_cells, local_cells, 0
+        ).astype(F32)
+        picker = (places[None, :, None] == starts[:, None, :]).astype(F32)
+        grad_encoded = out_cotangent.astype(F32) + jnp.sum(
+            picker[:, :, :, None] * heads_back.reshape(row_count, 1, CELLS_ROW, D), axis=2
+        )
+        grad_flat = grad_encoded.reshape(token_count, D)
+        branch_low = grad_flat.astype(BF16)
+        branch_low, one_b, before_low = sync(branch_low, one_b, before_low)
+        before_hop = grid.hop(before_low, "x") if query_count == 2 else before_low
+        one_a = grid.hop(down_sums.first_in[1], "y")
+        down_sums.one = [one_b, one_a]
+        down_sums.add_second()
+        down_sums.two = grid.hop(tie(down_sums.two_in, before_hop), "x")
+        hidden_low, up_bias_sums, grad_second = feed_back(
+            where, tie(branch_low, before_low, down_sums.two_in, before_hop), slope, up_weights, down_weights
+        )
+        hidden_low, grad_second, one_a = sync(hidden_low, grad_second, one_a)
+        grad_up_bias = up_bias_sums[0]
+        up_sums = Sums(grid, *weight_terms(where, (second_low, hidden_low)))
+        up_sums.sent, down_sums.two, one_a = sync(up_sums.sent, down_sums.two, one_a)
+        down_sums.one = [one_b, one_a]
+        up_sums.core()
+
+        middle_part, grad_gain_two, grad_shift_two = second_pull(tie(grad_second, up_sums.sent))
+        grad_middle = grad_flat + middle_part
+        attn_low = grad_middle.astype(BF16)
+        mixed_back = dot_rt(attn_low, full_out).astype(BF16)
+        before_all = grid.joined(before_low, tie(before_hop, mixed_back)).reshape(query_count * pairs, FF)
+        gene_terms = dot_lt(grid.own_columns(gene_rows), before_all).astype(BF16)
+        shape = [grid.size[axis] for axis in "zyc"]
+        gene_mine, gene_sent = grid.cut_columns(gene_terms)
+        up_sums.add_turned(gene_sent)
+        up_sums.one_in, gene_sent, mixed_back = sync(up_sums.one_in, gene_sent, mixed_back)
+        up_sums.go_turned()
+        gene_got = grid.hop(gene_sent, "c")
+        d_query, d_key, d_value = attend_back(
+            qkv_rows, segment, mixed_rows, mixed_back.reshape(row_count, ROW_LEN, D), log_totals
+        )
+        d_query, d_key, d_value, gene_got = sync(d_query, d_key, d_value, gene_got)
+        down_sums.add_last(d_query)
+        down_sums.last()
+        gene_sum = added(gene_mine, gene_got)
+        gene_sum = grid.scatter_z(tie(gene_sum.reshape(grid.size["z"], -1, gene_sum.shape[1]), down_sums.last_in))
+        qkv_back_low = jnp.concatenate([d_query, d_key, d_value], axis=2).reshape(token_count, 3 * D)
+        attn_sums = Sums(
+            grid,
+            *weight_terms(
+                where, (normed_low, tie(qkv_back_low, down_sums.last_in)), (mixed_low, attn_low)
+            ),
+        )
+        attn_sums.sent, qkv_back_low, *up_sums.one = sync(attn_sums.sent, qkv_back_low, *up_sums.one)
+        attn_sums.core()
+        up_sums.add_second(attn_sums.sent)
+        up_sums.two = grid.turn_hop(up_sums.two_in, 1)
+        grad_normed = dot_rt(tie(qkv_back_low, up_sums.two_in), full_qkv)
+        grad_normed, attn_sums.got = sync(grad_normed, attn_sums.got)
+        attn_sums.add_turned()
+        attn_sums.go_turned(up_sums.two)
+        bias_sums = jnp.sum(qkv_back_low, axis=0, dtype=F32)
+        token_part, grad_gain_one, grad_shift_one = first_pull(tie(grad_normed, attn_sums.one_in))
+        grad_tokens = (grad_middle + token_part).reshape(row_count, ROW_LEN, D)
+        grad_tokens, up_sums.two = sync(grad_tokens, up_sums.two)
+        up_sums.add_last()
+        up_sums.last()
+        grad_attn_bias = jnp.sum(attn_low, axis=0, dtype=F32)
+        grad_out_bias = jnp.sum(branch_low, axis=0, dtype=F32)
+
+        leading_low = tie(picker.astype(BF16).transpose(0, 2, 1), up_sums.last_in)
+        active_heads = jnp.einsum(
+            "rcl,rlf->rcf", leading_low, active_low.reshape(row_count, ROW_LEN, FF), preferred_element_type=F32
+        ).astype(BF16).reshape(local_cells, FF)
+        branch_heads = jnp.einsum(
+            "rcl,rld->rcd", leading_low, branch_low.reshape(row_count, ROW_LEN, D), preferred_element_type=F32
+        ).astype(BF16).reshape(local_cells, D)
+        late_low = jnp.concatenate([active_heads, branch_heads], axis=1)
+        genes_part = dot_rt(tie(before_all, up_sums.last_in), dec_gene).astype(BF16)
+        late_low, genes_part, *attn_sums.one = sync(late_low, genes_part, *attn_sums.one)
+        attn_sums.add_second()
+        attn_sums.two = grid.turn_hop(attn_sums.two_in, 1)
+        late_low, genes_part = tie((late_low, genes_part), attn_sums.two_in)
+        late = grid.share(late_low)
+        gathered = lax.all_gather(
+            jnp.concatenate([cell_heads, cell_total, late], axis=1), "dp", axis=0, tiled=True
+        )
+        genes_back = grid.share(genes_part, axis=1)
+        choose = (ids[:, None] == jnp.arange(GENES, dtype=jnp.int32)[None, :]).astype(BF16)
+        table_terms = dot_lt(grid.own_columns(choose), genes_back).astype(BF16)
+        table_terms = table_terms.reshape(*shape, -1, D)
+        table_terms = grid.scatter_step(table_terms, "c", 2, BF16)
+        table_terms = grid.scatter_step(table_terms, "y", 1, BF16)
+        attn_sums.two, table_terms = sync(attn_sums.two, table_terms)
+        attn_sums.add_last()
+        attn_sums.last()
+        grad_table = grid.scatter_z(tie(table_terms, attn_sums.last_in))[0].astype(F32)
+
+        gene_sum = tie(gene_sum, attn_sums.last_in).reshape(grid.size["y"], -1, gene_sum.shape[2])
+        gene_sum = grid.scatter_step(gene_sum, "y", 0, BF16)
+        grad_gene = grid.join_columns(gene_sum).astype(F32)
+        gathered = tie(gathered, attn_sums.last_in)
+        all_heads, all_cells, all_active, all_branch = jnp.split(
+            gathered, [D, D + FF, D + 2 * FF], axis=1
+        )
+        owned = D // (dp_count * query_count)
+        mine = lax.axis_index("dp") * query_count + place
+        grad_cell = dot_lt(
+            lax.dynamic_slice_in_dim(all_heads, mine * owned, owned, 1), all_cells
+        )
+        tall = FF // (dp_count * query_count)
+        late_down = dot_lt(
+            lax.dynamic_slice_in_dim(all_active, mine * tall, tall, 1), all_branch
+        )
+
+        owners = dp_count * query_count
+
+        def owned_cols(values):
+            return values.reshape(-1, owners, values.shape[-1] // owners).transpose(1, 0, 2).reshape(owners, -1)
+
+        small = [
+            jnp.stack([grad_gain_one, grad_gain_two]),
+            jnp.stack([grad_shift_one, grad_shift_two]),
+            jnp.stack([bias_sums[:D], bias_sums[2 * D :], grad_attn_bias, grad_out_bias]),
+            jnp.stack([grad_up_bias, grad_dec_bias]),
+            grad_logit[None, :],
+        ]
+        flat = [owned_cols(v) for v in small]
+        joined = jnp.concatenate(flat, axis=1)
+        summed = grid.scatter(grid.blocks(joined), "cxyz", F32).reshape(-1)
+        outs = []
+        start = 0
+        for value, piece in zip(small, flat):
+            size = piece.shape[1]
+            outs.append(summed[start : start + size].reshape(value.shape[0], -1))
+            start += size
+
+        attn_sum = attn_sums.result()
+        qkv_cut = 3 * D // 2
+
+        return (
+            encoded_rows,
+            grad_tokens,
+            outs[0],
+            outs[1],
+            outs[2],
+            outs[3],
+            jnp.concatenate([half[:, :qkv_cut] for half in attn_sum], axis=1),
+            jnp.concatenate([half[:, qkv_cut:] for half in attn_sum], axis=1),
+            jnp.concatenate(up_sums.result(attn_sums.last_in), axis=1),
+            jnp.concatenate(down_sums.result(attn_sums.last_in), axis=1) + late_down,
+            grad_cell,
+            grad_gene,
+            outs[4][0],
+            grad_table,
+        )
+
+    return shards
+
+
 def split_heads(qkv_row):
     queries = qkv_row[:, :D].reshape(ROW_LEN, HEADS, HEAD_DIM)
     keys_in = qkv_row[:, D : 2 * D].reshape(ROW_LEN, HEADS, HEAD_DIM)
@@ -53,7 +1102,7 @@
     return jnp.where(same_cell[None], scores, -1e30)
 
 
-def attend(member):
+def attend_any(member):
     qkv_row, segment_row = member
     queries, keys_in, values_in = split_heads(qkv_row)
     scores = row_scores(queries, keys_in, segment_row)
@@ -67,7 +1116,7 @@
     return (mixed.reshape(ROW_LEN, D), (highest_score + jnp.log(weight_sum))[:, :, 0])
 
 
-def attend_back(member):
+def attend_back_any(member):
     qkv_row, segment_row, log_total, grad_mixed = member
     queries, keys_in, values_in = split_heads(qkv_row)
     scores = row_scores(queries, keys_in, segment_row)
@@ -124,7 +1173,7 @@
     return values_in.reshape(dp_count, query_count, width, values_in.shape[1])
 
 
-def shards(
+def shards_any(
     tokens,
     cell_lengths,
     out_cotangent,
@@ -168,7 +1217,7 @@
         jnp.bfloat16
     )
     qkv_rows = qkv_low.reshape(row_count, ROW_LEN, 3 * D)
-    mixed_rows, log_totals = lax.map(attend, (qkv_rows, segment))
+    mixed_rows, log_totals = lax.map(attend_any, (qkv_rows, segment))
     mixed_low = mixed_rows.reshape(token_count, D)
     middle = (
         flat_tokens
@@ -275,7 +1324,7 @@
         "ne,de->nd", attn_low, full_out, preferred_element_type=jnp.float32
     ).astype(jnp.bfloat16)
     qkv_back = lax.map(
-        attend_back, (qkv_rows, segment, log_totals, mixed_back.reshape(row_count, ROW_LEN, D))
+        attend_back_any, (qkv_rows, segment, log_totals, mixed_back.reshape(row_count, ROW_LEN, D))
     )
     qkv_back_low = qkv_back.reshape(token_count, 3 * D).astype(jnp.bfloat16)
     bias_sums = jnp.sum(qkv_back_low, axis=0, dtype=jnp.float32)
@@ -380,8 +1429,10 @@
         P("dp", "query"),
         P("dp", "query"),
     )
+    rows = P(("dp", "query"), None)
+    grid = Grid(mesh)
     return jax.shard_map(
-        shards,
+        make_shards(grid) if grid.paired() else shards_any,
         mesh=mesh,
         in_specs=placed,
         out_specs=(
@@ -391,14 +1442,14 @@
             P(None, ("dp", "query")),
             P(None, ("dp", "query")),
             P(None, ("dp", "query")),
-            P(("dp", "query"), None),
-            P(("dp", "query"), None),
-            P(("dp", "query"), None),
-            P(("dp", "query"), None),
-            P(("dp", "query"), None),
-            P(("dp", "query"), None),
+            rows,
+            rows,
+            rows,
+            rows,
+            rows,
+            rows,
             P(("dp", "query")),
-            P(("dp", "query"), None),
+            rows,
         ),
         check_vma=False,
     )

time: 2350 us -> 635 us (0.27)
  waiting for transfers between devices: 1610 us -> 195 us
  blocking collectives: 322 us -> 0 us
  matrix products: 247 us -> 50.1 us
  Pallas kernels: 0 us -> 159 us
  starting transfers between devices: 5.41 us -> 46.3 us
    all_gather x15 -> x1, waiting for transfers between devices: 914 us -> 2.71 us  [shards(): lax.all_gather(jnp.concatenate([cell_heads, cell_total, late], axis=1), '...]
    reduce_scatter x7 -> x5, waiting for transfers between devices: 549 us -> 20.1 us  [scatter_z(): lax.psum_scatter(value, 'dp', scatter_dimension=0, axis_index_groups=grou...]
    all_to_all x1 -> x0, blocking collectives: 277 us -> none  [shards(): lax.all_to_all(owner_blocks(gene_terms, dp_count, query_count).astype(jnp...]
    dot_general x29 -> x15, matrix products: 247 us -> 50.1 us  [the longest x4 20.7 us: dot_rt(): lax.dot_general(left, right, (((1,), (1,)), ((), ())), preferred_element_...]
    ppermute x0 -> x55, waiting for transfers between devices: none -> 172 us  [the longest x36 89.3 us: hop(): return lax.ppermute(value, 'dp', pairs)]
    pallas_call x0 -> x11, Pallas kernels: none -> 159 us  [the longest x3 62.3 us: feed_call(): pl.pallas_call(kernel, grid_spec=pltpu.PrefetchScalarGridSpec(num_scalar_...]
    unnamed x25 -> x6, waiting for transfers between devices: 71.6 us -> 0.1 us
    all_to_all x1 -> x0, waiting for transfers between devices: 54.5 us -> none  [shards(): lax.all_to_all(owner_blocks(table_terms, dp_count, query_count).astype(jn...]
  transfers between devices with their start and end apart: 25 -> 61, of which waited for: 20 -> 27; matrix products, arithmetic and copies ran while one was open for 15% -> 26% of each run, Pallas kernels for 0% -> 25%
where the time goes in v2:
time: 635 us; the launch traced here: 629 us
  waiting for transfers between devices  195 us (31%)
  Pallas kernels  159 us (25%)
  other arithmetic  103 us (16%)
  local copies, waits for them, and re-layouts  58 us (9%)
  matrix products  50.1 us (8%)
  starting transfers between devices  46.3 us (7%)
  between operations  17.7 us (3%)
    ppermute x36, waiting for transfers between devices, hop(): return lax.ppermute(value, 'dp', pairs)  89.3 us
    pallas_call x3, Pallas kernels, feed_call(): pl.pallas_call(kernel, grid_spec=pltpu.PrefetchScalarGridSpec(num_scalar_...  62.3 us
    ppermute x15, waiting for transfers between devices, hop(): return lax.ppermute(value, 'query', pairs)  54.6 us
    convert_element_type x11, other arithmetic, added(): return total.astype(BF16)  42 us
    pallas_call x2, Pallas kernels, weight_terms(): pl.pallas_call(lambda *refs: term_kernel(steps, *refs), grid_spec=pltpu.P...  35.2 us
    ppermute x4, waiting for transfers between devices, turn_hop(): return lax.ppermute(value, ('dp', 'query'), pairs)  28.1 us
    ppermute x36, starting transfers between devices, hop(): return lax.ppermute(value, 'dp', pairs)  26.7 us
    dot_general x4, matrix products, dot_rt(): lax.dot_general(left, right, (((1,), (1,)), ((), ())), preferred_element_...  20.7 us
  transfers between devices with their start and end apart: 61, of which 27 were waited for; matrix products, arithmetic and copies ran while one was open for 26% of the time, Pallas kernels for 25%

profile of v2, /device:TPU:0, one launch (start us, length us, event | category | flops | bytes accessed | tf_op | source)
XLA Modules:
  0.0 629.4 jit_solution(1276821143891365818)
XLA Ops:
  23.9 5.6 collective-permute-done
  33.8 10.4 %collective-permute-done.3 = bf16[80,3840]{1,0:T(8,128)(2,1)S(1)} collective-permute-done((bf16[80,3840]{1,0:T(8,128)(2,1)}, bf16[80,3840]{1,0:T(8,128)(2,1)S(1)}, u32[]{:S(2)}, u32[]{:S(2)}) %collective-permute-start.3) | collective-permute-done | bytes 614432 | tf_op jit(solution)/shard_map/ppermute | solution.py:588
  48.3 6.3 %collective-permute-done.4 = bf16[32,3840]{1,0:T(8,128)(2,1)S(1)} collective-permute-done((bf16[32,3840]{1,0:T(8,128)(2,1)S(1)}, bf16[32,3840]{1,0:T(8,128)(2,1)S(1)}, u32[]{:S(2)}, u32[]{:S(2)}) %collective-permute-start.4) | collective-permute-done | bytes 245792 | tf_op jit(solution)/shard_map/ppermute | solution.py:588
  56.8 16.1 %collective-permute-done.8 = bf16[80,6400]{1,0:T(8,128)(2,1)} collective-permute-done((bf16[80,6400]{1,0:T(8,128)(2,1)}, bf16[80,6400]{1,0:T(8,128)(2,1)}, u32[]{:S(2)}, u32[]{:S(2)}) %collective-permute-start.8) | collective-permute-done | bytes 1024032 | tf_op jit(solution)/shard_map/ppermute | solution.py:582
  77.9 8.6 %shard_map.272 = bf16[1280,3840]{1,0:T(8,128)(2,1)S(1)} custom-call(s32[9]{0:T(128)S(1)} %stack.110.refs_0_, bf16[640,3840]{1,0:T(8,128)(2,1)S(1)} %copy-done.7, bf16[240,3840]{1,0:T(8,128)(2,1)S(1)} %constant_dynamic-update-slice_fusion.refs_2_, bf16[80,3840]{1,0:T(8,128)(2,1)S(1)} %constant_dynamic-update-slice_fusion.3.refs_3_, ...), custom_call_target="tpu_custom_call" | custom-call | flops 1 | bytes 1 | tf_op jit(solution)/shard_map/pallas_call | solution.py:528
  86.5 6.8 %add_convert_fusion = bf16[512,3840]{1,0:T(8,128)(2,1)} fusion(bf16[512,1280]{1,0:T(8,128)(2,1)S(1)} %copy-done.36, bf16[1280,3840]{1,0:T(8,128)(2,1)S(1)} %shard_map.272, f32[3840]{0:T(1024)S(1)} %pad_maximum_fusion.5), kind=kOutput, calls=%fused_computation.4 | convolution fusion | flops 5037096960 | bytes 15088640 | tf_op jit(solution)/shard_map/dot_general | solution.py:35
  101.7 8.2 %shard_map.273 = (bf16[1,512,640]{2,1,0:T(8,128)(2,1)}, f32[1,5,2,512]{3,2,1,0:T(2,128)}) custom-call(s32[1,1,512]{2,1,0:T(1,128)} %bitcast.350, s32[1,512,1]{2,1,0:T(8,128)} %copy.40.segment_column, bf16[1,512,3840]{2,1,0:T(8,128)(2,1)} %bitcast.304, bf16[1,512,3840]{2,1,0:T(8,128)(2,1)} %bitcast.305, bf16[1,512,3840]{2,1,0:T(8,128)(2,1)} %bitcast.306), custom_call_target="tpu_custom_call" | custom-call | flops 1 | bytes 1 | tf_op jit(solution)/shard_map/pallas_call | solution.py:91
  111.4 9.3 %shard_map.274 = (bf16[1,512,640]{2,1,0:T(8,128)(2,1)}, f32[1,5,2,512]{3,2,1,0:T(2,128)}) custom-call(s32[1,1,512]{2,1,0:T(1,128)} %bitcast.351, s32[1,512,1]{2,1,0:T(8,128)} %copy.40.segment_column, bf16[1,512,3840]{2,1,0:T(8,128)(2,1)} %bitcast.307, bf16[1,512,3840]{2,1,0:T(8,128)(2,1)} %bitcast.308, bf16[1,512,3840]{2,1,0:T(8,128)(2,1)} %bitcast.309), custom_call_target="tpu_custom_call" | custom-call | flops 1 | bytes 1 | tf_op jit(solution)/shard_map/pallas_call | solution.py:91
  120.9 7.5 %collective-permute-done.14 = bf16[320,1280]{1,0:T(8,128)(2,1)} collective-permute-done((bf16[320,1280]{1,0:T(8,128)(2,1)}, bf16[320,1280]{1,0:T(8,128)(2,1)}, u32[]{:S(2)}, u32[]{:S(2)}) %collective-permute-start.14) | collective-permute-done | bytes 819232 | tf_op jit(solution)/shard_map/ppermute | solution.py:582
  131.8 4.8 convolution_convert_fusion.1
  146.2 18.2 %shard_map.276 = (bf16[512,5120]{1,0:T(8,128)(2,1)}, bf16[512,5120]{1,0:T(8,128)(2,1)}) custom-call(s32[4]{0:T(128)} %pad_add_fusion.1.place.refs_0_, bf16[512,1280]{1,0:T(8,128)(2,1)} %get-tuple-element.165.second.refs_1_, f32[1,5120]{1,0:T(1,128)} %get-tuple-element.312.bias, bf16[640,5120]{1,0:T(8,128)(2,1)} %refs_0_.5, bf16[240,6400]{1,0:T(8,128)(2,1)} %copy-done.2, ...), custom_call_target="tpu_custom_call" | custom-call | flops 1 | bytes 1 | tf_op jit(solution)/shard_map/pallas_call | solution.py:330
  174.7 15.6 %shard_map.277 = (bf16[2,2,4,320,640]{4,3,2,1,0:T(8,128)(2,1)}, bf16[2,2,4,320,640]{4,3,2,1,0:T(8,128)(2,1)}) custom-call(s32[4]{0:T(128)} %pad_add_fusion.1.place.refs_0_, bf16[512,5120]{1,0:T(8,128)(2,1)} %get-tuple-element.177.left.active, bf16[512,1280]{1,0:T(8,128)(2,1)} %select_bitcast_fusion.right), custom_call_target="tpu_custom_call" | custom-call | flops 1 | bytes 1 | tf_op jit(solution)/shard_map/pallas_call | solution.py:482
  196.1 17.0 %shard_map.278 = f32[512,1280]{1,0:T(8,128)} custom-call(s32[4]{0:T(128)} %pad_add_fusion.1.place.refs_0_, bf16[512,5120]{1,0:T(8,128)(2,1)} %get-tuple-element.177.left.active, f32[512,1280]{1,0:T(8,128)} %get-tuple-element.293.middle, bf16[2560,1280]{1,0:T(8,128)(2,1)} %refs_5_.1, bf16[960,1280]{1,0:T(8,128)(2,1)} %copy-done.25, ...), custom_call_target="tpu_custom_call" | custom-call | flops 1 | bytes 1 | tf_op jit(solution)/shard_map/pallas_call | solution.py:330
  217.0 5.4 fusion.25
  222.5 4.0 fusion.77
  227.1 5.5 collective-permute-done.26
  233.6 4.1 multiply_reduce_fusion.5
  237.9 4.8 convert_reduce_fusion.5
  244.8 3.2 collective-permute-done.27
  248.0 4.6 convolution_convert_fusion.8
  259.1 23.2 %collective-permute-done.29 = bf16[1280,640]{1,0:T(8,128)(2,1)} collective-permute-done((bf16[1280,640]{1,0:T(8,128)(2,1)}, bf16[1280,640]{1,0:T(8,128)(2,1)}, u32[]{:S(2)}, u32[]{:S(2)}) %collective-permute-start.29) | collective-permute-done | bytes 1638432 | tf_op jit(solution)/shard_map/ppermute | solution.py:588
  283.8 3.0 fusion.11
  286.8 10.4 %collective-permute-done.30 = bf16[8,8,5120]{2,1,0:T(8,128)(2,1)S(1)} collective-permute-done((bf16[8,8,5120]{2,1,0:T(8,128)(2,1)S(1)}, bf16[8,8,5120]{2,1,0:T(8,128)(2,1)S(1)}, u32[]{:S(2)}, u32[]{:S(2)}) %collective-permute-start.30) | collective-permute-done | bytes 655392 | tf_op jit(solution)/shard_map/ppermute | solution.py:582
  298.7 27.1 %shard_map.279 = (bf16[512,5120]{1,0:T(8,128)(2,1)}, f32[1,5120]{1,0:T(1,128)}, f32[512,1280]{1,0:T(8,128)}) custom-call(s32[4]{0:T(128)} %pad_add_fusion.1.place.refs_0_, bf16[512,1280]{1,0:T(8,128)(2,1)} %bitcast_convert_fusion.branch, bf16[512,5120]{1,0:T(8,128)(2,1)} %get-tuple-element.193.slope, bf16[640,5120]{1,0:T(8,128)(2,1)} %refs_0_.5, ...), custom_call_target="tpu_custom_call" | custom-call | flops 1 | bytes 1 | tf_op jit(solution)/shard_map/pallas_call | solution.py:330
  325.8 16.5 %shard_map.280 = (bf16[2,2,320,2560]{3,2,1,0:T(8,128)(2,1)}, bf16[2,2,320,2560]{3,2,1,0:T(8,128)(2,1)}) custom-call(s32[4]{0:T(128)} %pad_add_fusion.1.place.refs_0_, bf16[512,1280]{1,0:T(8,128)(2,1)} %get-tuple-element.165.second.refs_1_, bf16[512,5120]{1,0:T(8,128)(2,1)} %get-tuple-element.197.refs_2_), custom_call_target="tpu_custom_call" | custom-call | flops 1 | bytes 1 | tf_op jit(solution)/shard_map/pallas_call | solution.py:429
  342.8 4.1 multiply_reduce_fusion.1
  350.9 3.0 convolution_convert_fusion.3
  358.0 4.5 fusion.1
  364.1 18.7 %shard_map.281 = (bf16[1,512,1280]{2,1,0:T(8,128)(2,1)}, bf16[1,512,1280]{2,1,0:T(8,128)(2,1)}, bf16[1,512,1280]{2,1,0:T(8,128)(2,1)}) custom-call(s32[1,1,512]{2,1,0:T(1,128)} %bitcast.352, s32[1,512,1]{2,1,0:T(8,128)} %copy.40.segment_column, bf16[1,512,3840]{2,1,0:T(8,128)(2,1)} %bitcast.310, bf16[1,512,3840]{2,1,0:T(8,128)(2,1)} %bitcast.311, ...), custom_call_target="tpu_custom_call" | custom-call | flops 1 | bytes 1 | tf_op jit(solution)/shard_map/pallas_call | solution.py:151
  382.8 4.9 fusion.10
  387.8 4.9 add_convert_fusion.1
  394.3 3.3 maximum_bitcast_fusion.refs_3_
  397.6 18.7 %shard_map.282 = (bf16[2,2,320,2560]{3,2,1,0:T(8,128)(2,1)}, bf16[2,2,320,2560]{3,2,1,0:T(8,128)(2,1)}) custom-call(s32[4]{0:T(128)} %pad_add_fusion.1.place.refs_0_, bf16[512,1280]{1,0:T(8,128)(2,1)} %fusion.20.refs_1_, bf16[512,1280]{1,0:T(8,128)(2,1)} %bitcast.318, bf16[512,3840]{1,0:T(8,128)(2,1)} %maximum_bitcast_fusion.refs_3_, ...), custom_call_target="tpu_custom_call" | custom-call | flops 1 | bytes 1 | tf_op jit(solution)/shard_map/pallas_call | solution.py:429
  416.4 3.4 slice_bitcast_fusion.2
  431.7 8.0 %fusion.111 = f32[512,1280]{1,0:T(8,128)S(1)} fusion(bf16[512,3840]{1,0:T(8,128)(2,1)S(1)} %copy-done.19, bf16[1280,3840]{1,0:T(8,128)(2,1)} %copy-done.5), kind=kOutput, calls=%fused_computation.310 | convolution fusion | flops 5033164800 | bytes 16384000 | tf_op jit(solution)/shard_map/dot_general | solution.py:39
  439.7 4.6 fusion.2
  444.3 7.3 %collective-permute-done.37 = bf16[320,2560]{1,0:T(8,128)(2,1)S(1)} collective-permute-done((bf16[320,2560]{1,0:T(8,128)(2,1)S(1)}, bf16[320,2560]{1,0:T(8,128)(2,1)S(1)}, u32[]{:S(2)}, u32[]{:S(2)}) %collective-permute-start.37) | collective-permute-done | bytes 1638432 | tf_op jit(solution)/shard_map/ppermute | solution.py:601
  458.2 3.9 fusion.5
  462.1 3.7 convolution_convert_fusion.2
  467.1 5.0 convolution_convert_fusion.7
  472.7 20.8 %collective-permute-done.44 = bf16[2,320,2560]{2,1,0:T(8,128)(2,1)} collective-permute-done((bf16[2,320,2560]{2,1,0:T(8,128)(2,1)}, bf16[2,320,2560]{2,1,0:T(8,128)(2,1)}, u32[]{:S(2)}, u32[]{:S(2)}) %collective-permute-start.44) | collective-permute-done | bytes 3276832 | tf_op jit(solution)/shard_map/ppermute | solution.py:601
  495.7 3.7 fusion.3
  518.5 21.9 %collective-permute-done.48 = bf16[4,32,1280]{2,1,0:T(8,128)(2,1)S(1)} collective-permute-done((bf16[4,32,1280]{2,1,0:T(8,128)(2,1)S(1)}, bf16[4,32,1280]{2,1,0:T(8,128)(2,1)S(1)}, u32[]{:S(2)}, u32[]{:S(2)}) %collective-permute-start.48) | collective-permute-done | bytes 327712 | tf_op jit(solution)/shard_map/ppermute | solution.py:588
  541.2 4.4 fusion.7
  554.6 3.1 collective-permute-start.43
  574.1 11.6 %collective-permute-done.53 = bf16[80,2560]{1,0:T(8,128)(2,1)S(1)} collective-permute-done((bf16[80,2560]{1,0:T(8,128)(2,1)S(1)}, bf16[80,2560]{1,0:T(8,128)(2,1)S(1)}, u32[]{:S(2)}, u32[]{:S(2)}) %collective-permute-start.53) | collective-permute-done | bytes 409632 | tf_op jit(solution)/shard_map/ppermute | solution.py:588
  589.4 20.0 %reduce-scatter.14.cloned.1.call-done = bf16[1,32,1280]{2,1,0:T(8,128)(2,1)} async-done(((bf16[4,32,1280]{2,1,0:T(8,128)(2,1)}), bf16[1,32,1280]{2,1,0:T(8,128)(2,1)}) %reduce-scatter.14.cloned.1.call-update) | async-done | bytes 81936 | tf_op jit(solution)/shard_map/reduce_scatter | solution.py:677
  617.4 3.1 fusion.44
  (512 shorter events, 178.8 us)
Async XLA Ops:
  8.0 560.1 %reduce-scatter.12.cloned.1.call-start = ((), (), s32[]{:S(2)}) async-start(), calls=%async_computation.9 | async-start | bytes 4096000 | tf_op jit(solution)/shard_map/reduce_scatter | solution.py:677
  9.0 14.4 %collective-permute-start.1 = (s32[1,64]{1,0:T(1,128)S(1)}, s32[1,64]{1,0:T(1,128)S(1)}, u32[]{:S(2)}, u32[]{:S(2)}) collective-permute-start(s32[1,64]{1,0:T(1,128)S(1)} %reshape.579), channel_id=1, source_target_pairs={{0,1},{1,0},{2,3},{3,2},{4,5},{5,4},{6,7},{7,6},{8,9},{9,8},{10,11... | collective-permute-start | bytes 776 | tf_op jit(solution)/shard_map/ppermute | solution.py:582
  13.9 15.6 %collective-permute-start = (bf16[80,3840]{1,0:T(8,128)(2,1)}, bf16[80,3840]{1,0:T(8,128)(2,1)}, u32[]{:S(2)}, u32[]{:S(2)}) collective-permute-start(bf16[80,3840]{1,0:T(8,128)(2,1)} %constant_dynamic-slice_fusion.12), channel_id=1, source_target_pairs={{0,1},{1,0},{2,3},{3,2},{4,5},{5,4},{6,7},{7,6},{8,9},{9,8},{10,11... | collective-permute-start | bytes 1843208 | tf_op jit(solution)/shard_map/ppermute | solution.py:582
  29.5 14.6 %collective-permute-start.3 = (bf16[80,3840]{1,0:T(8,128)(2,1)}, bf16[80,3840]{1,0:T(8,128)(2,1)S(1)}, u32[]{:S(2)}, u32[]{:S(2)}) collective-permute-start(bf16[80,3840]{1,0:T(8,128)(2,1)} %collective-permute-done), channel_id=1, source_target_pairs={{0,8},{2,10},{4,12},{6,14},{8,0},{10,2},{12,4},{14,6},{16,24},{18,... | collective-permute-start | bytes 1843208 | tf_op jit(solution)/shard_map/ppermute | solution.py:588
  31.1 14.3 %collective-permute-start.2 = (bf16[80,3840]{1,0:T(8,128)(2,1)}, bf16[80,3840]{1,0:T(8,128)(2,1)S(1)}, u32[]{:S(2)}, u32[]{:S(2)}) collective-permute-start(bf16[80,3840]{1,0:T(8,128)(2,1)} %collective-permute-done), channel_id=1, source_target_pairs={{0,4},{2,6},{4,0},{6,2},{8,12},{10,14},{12,8},{14,10},{16,20},{18,... | collective-permute-start | bytes 1843208 | tf_op jit(solution)/shard_map/ppermute | solution.py:588
  45.5 9.2 %collective-permute-start.5 = (bf16[48,3840]{1,0:T(8,128)(2,1)S(1)}, bf16[48,3840]{1,0:T(8,128)(2,1)S(1)}, u32[]{:S(2)}, u32[]{:S(2)}) collective-permute-start(bf16[48,3840]{1,0:T(8,128)(2,1)S(1)} %slice.181), channel_id=1, source_target_pairs={{0,8},{2,10},{4,12},{6,14},{8,0},{10,2},{12,4},{14,6},{16,24},{18,... | collective-permute-start | bytes 1105928 | tf_op jit(solution)/shard_map/ppermute | solution.py:588
  46.1 26.8 %collective-permute-start.7 = (bf16[240,3840]{1,0:T(8,128)(2,1)S(1)}, bf16[240,3840]{1,0:T(8,128)(2,1)}, u32[]{:S(2)}, u32[]{:S(2)}) collective-permute-start(bf16[240,3840]{1,0:T(8,128)(2,1)S(1)} %constant_dynamic-update-slice_fusion.refs_2_), channel_id=1, source_target_pairs={{0,2},{2,0},{4,6},{6,4},{8,10},{10,8},{12,14},{14,12},{16,18},{18,... | collective-permute-start | bytes 5529608 | tf_op jit(solution)/shard_map/ppermute | solution.py:588
  46.2 8.4 %collective-permute-start.4 = (bf16[32,3840]{1,0:T(8,128)(2,1)S(1)}, bf16[32,3840]{1,0:T(8,128)(2,1)S(1)}, u32[]{:S(2)}, u32[]{:S(2)}) collective-permute-start(bf16[32,3840]{1,0:T(8,128)(2,1)S(1)} %slice.180), channel_id=1, source_target_pairs={{0,4},{2,6},{4,0},{6,2},{8,12},{10,14},{12,8},{14,10},{16,20},{18,... | collective-permute-start | bytes 737288 | tf_op jit(solution)/shard_map/ppermute | solution.py:588
  47.8 25.1 %collective-permute-start.8 = (bf16[80,6400]{1,0:T(8,128)(2,1)}, bf16[80,6400]{1,0:T(8,128)(2,1)}, u32[]{:S(2)}, u32[]{:S(2)}) collective-permute-start(bf16[80,6400]{1,0:T(8,128)(2,1)} %pad_maximum_fusion), channel_id=1, source_target_pairs={{0,1},{1,0},{2,3},{3,2},{4,5},{5,4},{6,7},{7,6},{8,9},{9,8},{10,11... | collective-permute-start | bytes 3072008 | tf_op jit(solution)/shard_map/ppermute | solution.py:582
  54.7 18.2 %collective-permute-start.6 = (bf16[80,3840]{1,0:T(8,128)(2,1)S(1)}, bf16[80,3840]{1,0:T(8,128)(2,1)S(1)}, u32[]{:S(2)}, u32[]{:S(2)}) collective-permute-start(bf16[80,3840]{1,0:T(8,128)(2,1)S(1)} %constant_dynamic-update-slice_fusion.3.refs_3_), channel_id=1, source_target_pairs={{0,2},{2,0},{4,6},{6,4},{8,10},{10,8},{12,14},{14,12},{16,18},{18,... | collective-permute-start | bytes 1843208 | tf_op jit(solution)/shard_map/ppermute | solution.py:588
  72.9 24.1 %collective-permute-start.10 = (bf16[80,6400]{1,0:T(8,128)(2,1)}, bf16[80,6400]{1,0:T(8,128)(2,1)S(1)}, u32[]{:S(2)}, u32[]{:S(2)}) collective-permute-start(bf16[80,6400]{1,0:T(8,128)(2,1)} %collective-permute-done.8), channel_id=1, source_target_pairs={{0,8},{2,10},{4,12},{6,14},{8,0},{10,2},{12,4},{14,6},{16,24},{18,... | collective-permute-start | bytes 3072008 | tf_op jit(solution)/shard_map/ppermute | solution.py:588
  74.4 23.9 %collective-permute-start.9 = (bf16[80,6400]{1,0:T(8,128)(2,1)}, bf16[80,6400]{1,0:T(8,128)(2,1)S(1)}, u32[]{:S(2)}, u32[]{:S(2)}) collective-permute-start(bf16[80,6400]{1,0:T(8,128)(2,1)} %collective-permute-done.8), channel_id=1, source_target_pairs={{0,4},{2,6},{4,0},{6,2},{8,12},{10,14},{12,8},{14,10},{16,20},{18,... | collective-permute-start | bytes 3072008 | tf_op jit(solution)/shard_map/ppermute | solution.py:588
  74.9 19.6 %collective-permute-start.11 = (bf16[128,1280]{1,0:T(8,128)(2,1)S(1)}, bf16[128,1280]{1,0:T(8,128)(2,1)S(1)}, u32[]{:S(2)}, u32[]{:S(2)}) collective-permute-start(bf16[128,1280]{1,0:T(8,128)(2,1)S(1)} %convolution_convert_fusion.5), channel_id=1, source_target_pairs={{0,1},{1,0},{2,3},{3,2},{4,5},{5,4},{6,7},{7,6},{8,9},{9,8},{10,11... | collective-permute-start | bytes 983048 | tf_op jit(solution)/shard_map/ppermute | solution.py:582
  99.1 21.8 %collective-permute-start.12 = (bf16[32,6400]{1,0:T(8,128)(2,1)}, bf16[32,6400]{1,0:T(8,128)(2,1)S(1)}, u32[]{:S(2)}, u32[]{:S(2)}) collective-permute-start(bf16[32,6400]{1,0:T(8,128)(2,1)} %slice.184), channel_id=1, source_target_pairs={{0,4},{2,6},{4,0},{6,2},{8,12},{10,14},{12,8},{14,10},{16,20},{18,... | collective-permute-start | bytes 1228808 | tf_op jit(solution)/shard_map/ppermute | solution.py:588
  100.4 20.5 %collective-permute-start.13 = (bf16[48,6400]{1,0:T(8,128)(2,1)}, bf16[48,6400]{1,0:T(8,128)(2,1)}, u32[]{:S(2)}, u32[]{:S(2)}) collective-permute-start(bf16[48,6400]{1,0:T(8,128)(2,1)} %slice.185), channel_id=1, source_target_pairs={{0,8},{2,10},{4,12},{6,14},{8,0},{10,2},{12,4},{14,6},{16,24},{18,... | collective-permute-start | bytes 1843208 | tf_op jit(solution)/shard_map/ppermute | solution.py:588
  110.0 18.4 %collective-permute-start.14 = (bf16[320,1280]{1,0:T(8,128)(2,1)}, bf16[320,1280]{1,0:T(8,128)(2,1)}, u32[]{:S(2)}, u32[]{:S(2)}) collective-permute-start(bf16[320,1280]{1,0:T(8,128)(2,1)} %constant_dynamic-slice_fusion.9), channel_id=1, source_target_pairs={{0,1},{1,0},{2,3},{3,2},{4,5},{5,4},{6,7},{7,6},{8,9},{9,8},{10,11... | collective-permute-start | bytes 2457608 | tf_op jit(solution)/shard_map/ppermute | solution.py:582
  111.2 26.6 %collective-permute-start.15 = (bf16[240,6400]{1,0:T(8,128)(2,1)S(1)}, bf16[240,6400]{1,0:T(8,128)(2,1)S(1)}, u32[]{:S(2)}, u32[]{:S(2)}) collective-permute-start(bf16[240,6400]{1,0:T(8,128)(2,1)S(1)} %constant_dynamic-update-slice_fusion.5.refs_2_.refs_1_), channel_id=1, source_target_pairs={{0,2},{2,0},{4,6},{6,4},{8,10},{10,8},{12,14},{14,12},{16,18},{18,... | collective-permute-start | bytes 9216008 | tf_op jit(solution)/shard_map/ppermute | solution.py:588
  128.4 36.0 %collective-permute-start.18 = (bf16[320,1280]{1,0:T(8,128)(2,1)}, bf16[320,1280]{1,0:T(8,128)(2,1)}, u32[]{:S(2)}, u32[]{:S(2)}) collective-permute-start(bf16[320,1280]{1,0:T(8,128)(2,1)} %collective-permute-done.14), channel_id=1, source_target_pairs={{0,8},{2,10},{4,12},{6,14},{8,0},{10,2},{12,4},{14,6},{16,24},{18,... | collective-permute-start | bytes 2457608 | tf_op jit(solution)/shard_map/ppermute | solution.py:588
  128.9 35.5 %collective-permute-start.17 = (bf16[320,1280]{1,0:T(8,128)(2,1)}, bf16[320,1280]{1,0:T(8,128)(2,1)}, u32[]{:S(2)}, u32[]{:S(2)}) collective-permute-start(bf16[320,1280]{1,0:T(8,128)(2,1)} %collective-permute-done.14), channel_id=1, source_target_pairs={{0,4},{2,6},{4,0},{6,2},{8,12},{10,14},{12,8},{14,10},{16,20},{18,... | collective-permute-start | bytes 2457608 | tf_op jit(solution)/shard_map/ppermute | solution.py:588
  131.6 6.0 collective-permute-start.16
  144.9 19.5 %collective-permute-start.19 = (bf16[64,5120]{1,0:T(8,128)(2,1)}, bf16[64,5120]{1,0:T(8,128)(2,1)S(1)}, u32[]{:S(2)}, u32[]{:S(2)}) collective-permute-start(bf16[64,5120]{1,0:T(8,128)(2,1)} %dynamic-slice_bitcast_fusion), channel_id=1, source_target_pairs={{0,1},{1,0},{2,3},{3,2},{4,5},{5,4},{6,7},{7,6},{8,9},{9,8},{10,11... | collective-permute-start | bytes 1966088 | tf_op jit(solution)/shard_map/ppermute | solution.py:582
  170.5 19.9 %collective-permute-start.22 = (bf16[960,1280]{1,0:T(8,128)(2,1)S(1)}, bf16[960,1280]{1,0:T(8,128)(2,1)S(1)}, u32[]{:S(2)}, u32[]{:S(2)}) collective-permute-start(bf16[960,1280]{1,0:T(8,128)(2,1)S(1)} %constant_dynamic-update-slice_fusion.12.refs_1_.refs_6_), channel_id=1, source_target_pairs={{0,2},{2,0},{4,6},{6,4},{8,10},{10,8},{12,14},{14,12},{16,18},{18,... | collective-permute-start | bytes 7372808 | tf_op jit(solution)/shard_map/ppermute | solution.py:588
  171.5 18.9 %collective-permute-start.21 = (bf16[160,1280]{1,0:T(8,128)(2,1)S(1)}, bf16[160,1280]{1,0:T(8,128)(2,1)}, u32[]{:S(2)}, u32[]{:S(2)}) collective-permute-start(bf16[160,1280]{1,0:T(8,128)(2,1)S(1)} %slice.191), channel_id=1, source_target_pairs={{0,8},{2,10},{4,12},{6,14},{8,0},{10,2},{12,4},{14,6},{16,24},{18,... | collective-permute-start | bytes 1228808 | tf_op jit(solution)/shard_map/ppermute | solution.py:588
  173.0 17.4 %collective-permute-start.20 = (bf16[160,1280]{1,0:T(8,128)(2,1)S(1)}, bf16[160,1280]{1,0:T(8,128)(2,1)}, u32[]{:S(2)}, u32[]{:S(2)}) collective-permute-start(bf16[160,1280]{1,0:T(8,128)(2,1)S(1)} %slice.190), channel_id=1, source_target_pairs={{0,4},{2,6},{4,0},{6,2},{8,12},{10,14},{12,8},{14,10},{16,20},{18,... | collective-permute-start | bytes 1228808 | tf_op jit(solution)/shard_map/ppermute | solution.py:588
  195.2 17.9 %collective-permute-start.24 = (bf16[2,2,1280,640]{3,2,1,0:T(8,128)(2,1)}, bf16[2,2,1280,640]{3,2,1,0:T(8,128)(2,1)}, u32[]{:S(2)}, u32[]{:S(2)}) collective-permute-start(bf16[2,2,1280,640]{3,2,1,0:T(8,128)(2,1)} %bitcast.355), channel_id=1, source_target_pairs={{0,2},{2,0},{4,6},{6,4},{8,10},{10,8},{12,14},{14,12},{16,18},{18,... | collective-permute-start | bytes 19660808 | tf_op jit(solution)/shard_map/ppermute | solution.py:588
  215.5 6.9 %collective-permute-start.25 = (bf16[4,1280]{1,0:T(4,128)(2,1)S(1)}, bf16[4,1280]{1,0:T(4,128)(2,1)S(1)}, u32[]{:S(2)}, u32[]{:S(2)}) collective-permute-start(bf16[4,1280]{1,0:T(4,128)(2,1)S(1)} %select_convert_fusion), channel_id=1, source_target_pairs={{0,1},{1,0},{2,3},{3,2},{4,5},{5,4},{6,7},{7,6},{8,9},{9,8},{10,11... | collective-permute-start | bytes 30728 | tf_op jit(solution)/shard_map/ppermute | solution.py:582
  226.5 6.1 collective-permute-start.26
  243.2 39.1 %collective-permute-start.29 = (bf16[1280,640]{1,0:T(8,128)(2,1)}, bf16[1280,640]{1,0:T(8,128)(2,1)}, u32[]{:S(2)}, u32[]{:S(2)}) collective-permute-start(bf16[1280,640]{1,0:T(8,128)(2,1)} %get-tuple-element.288), channel_id=1, source_target_pairs={{0,4},{2,6},{4,0},{6,2},{8,12},{10,14},{12,8},{14,10},{16,20},{18,... | collective-permute-start | bytes 4915208 | tf_op jit(solution)/shard_map/ppermute | solution.py:588
  253.3 72.4 %collective-permute-start.31 = (bf16[1280,640]{1,0:T(8,128)(2,1)}, bf16[1280,640]{1,0:T(8,128)(2,1)S(1)}, u32[]{:S(2)}, u32[]{:S(2)}) collective-permute-start(bf16[1280,640]{1,0:T(8,128)(2,1)} %get-tuple-element.287), channel_id=1, source_target_pairs={{0,4},{2,6},{4,0},{6,2},{8,12},{10,14},{12,8},{14,10},{16,20},{18,... | collective-permute-start | bytes 4915208 | tf_op jit(solution)/shard_map/ppermute | solution.py:588
  282.3 14.9 %collective-permute-start.30 = (bf16[8,8,5120]{2,1,0:T(8,128)(2,1)S(1)}, bf16[8,8,5120]{2,1,0:T(8,128)(2,1)S(1)}, u32[]{:S(2)}, u32[]{:S(2)}) collective-permute-start(bf16[8,8,5120]{2,1,0:T(8,128)(2,1)S(1)} %copy-done.42), channel_id=1, source_target_pairs={{0,1},{1,0},{2,3},{3,2},{4,5},{5,4},{6,7},{7,6},{8,9},{9,8},{10,11... | collective-permute-start | bytes 1966088 | tf_op jit(solution)/shard_map/ppermute | solution.py:582
  297.2 45.2 %collective-permute-start.32 = (bf16[1280,640]{1,0:T(8,128)(2,1)S(1)}, bf16[1280,640]{1,0:T(8,128)(2,1)}, u32[]{:S(2)}, u32[]{:S(2)}) collective-permute-start(bf16[1280,640]{1,0:T(8,128)(2,1)S(1)} %fusion.11), channel_id=1, source_target_pairs={{0,1},{1,0},{2,3},{3,2},{4,5},{5,4},{6,7},{7,6},{8,9},{9,8},{10,11... | collective-permute-start | bytes 4915208 | tf_op jit(solution)/shard_map/ppermute | solution.py:582
  342.4 15.5 %collective-permute-start.33 = (bf16[2,2,320,2560]{3,2,1,0:T(8,128)(2,1)}, bf16[2,2,320,2560]{3,2,1,0:T(8,128)(2,1)}, u32[]{:S(2)}, u32[]{:S(2)}) collective-permute-start(bf16[2,2,320,2560]{3,2,1,0:T(8,128)(2,1)} %get-tuple-element.201), channel_id=1, source_target_pairs={{0,2},{2,0},{4,6},{6,4},{8,10},{10,8},{12,14},{14,12},{16,18},{18,... | collective-permute-start | bytes 19660808 | tf_op jit(solution)/shard_map/ppermute | solution.py:588
  362.4 20.4 %collective-permute-start.34 = (bf16[640,2560]{1,0:T(8,128)(2,1)}, bf16[640,2560]{1,0:T(8,128)(2,1)}, u32[]{:S(2)}, u32[]{:S(2)}) collective-permute-start(bf16[640,2560]{1,0:T(8,128)(2,1)} %broadcast_select_fusion), channel_id=1, source_target_pairs={{0,2},{2,0},{4,6},{6,4},{8,10},{10,8},{12,14},{14,12},{16,18},{18,... | collective-permute-start | bytes 9830408 | tf_op jit(solution)/shard_map/ppermute | solution.py:588
  362.9 53.4 %collective-permute-start.35 = (bf16[2,320,2560]{2,1,0:T(8,128)(2,1)}, bf16[2,320,2560]{2,1,0:T(8,128)(2,1)}, u32[]{:S(2)}, u32[]{:S(2)}) collective-permute-start(bf16[2,320,2560]{2,1,0:T(8,128)(2,1)} %fusion.1), channel_id=1, source_target_pairs={{0,1},{1,0},{2,6},{3,7},{4,5},{5,4},{6,2},{7,3},{8,9},{9,8},{10,14... | collective-permute-start | bytes 9830408 | tf_op jit(solution)/shard_map/ppermute | solution.py:601
  392.7 175.6 %reduce-scatter.10.cloned.1.call-start = ((), (), s32[]{:S(2)}) async-start(), calls=%async_computation.7 | async-start | bytes 2048000 | tf_op jit(solution)/shard_map/reduce_scatter | solution.py:677
  419.8 19.9 %collective-permute-start.36 = (bf16[2,2,320,2560]{3,2,1,0:T(8,128)(2,1)}, bf16[2,2,320,2560]{3,2,1,0:T(8,128)(2,1)}, u32[]{:S(2)}, u32[]{:S(2)}) collective-permute-start(bf16[2,2,320,2560]{3,2,1,0:T(8,128)(2,1)} %get-tuple-element.227), channel_id=1, source_target_pairs={{0,2},{2,0},{4,6},{6,4},{8,10},{10,8},{12,14},{14,12},{16,18},{18,... | collective-permute-start | bytes 19660808 | tf_op jit(solution)/shard_map/ppermute | solution.py:588
  427.7 140.6 %reduce-scatter.8.cloned.1.call-start = ((), (), s32[]{:S(2)}) async-start(), calls=%async_computation.6 | async-start | bytes 2048000 | tf_op jit(solution)/shard_map/reduce_scatter | solution.py:677
  430.4 21.2 %collective-permute-start.37 = (bf16[320,2560]{1,0:T(8,128)(2,1)S(1)}, bf16[320,2560]{1,0:T(8,128)(2,1)S(1)}, u32[]{:S(2)}, u32[]{:S(2)}) collective-permute-start(bf16[320,2560]{1,0:T(8,128)(2,1)S(1)} %fusion.8), channel_id=1, source_target_pairs={{0,4},{1,5},{2,3},{3,2},{4,0},{5,1},{6,7},{7,6},{8,12},{9,13},{10,... | collective-permute-start | bytes 4915208 | tf_op jit(solution)/shard_map/ppermute | solution.py:601
  454.6 39.0 %collective-permute-start.44 = (bf16[2,320,2560]{2,1,0:T(8,128)(2,1)}, bf16[2,320,2560]{2,1,0:T(8,128)(2,1)}, u32[]{:S(2)}, u32[]{:S(2)}) collective-permute-start(bf16[2,320,2560]{2,1,0:T(8,128)(2,1)} %fusion.2), channel_id=1, source_target_pairs={{0,1},{1,0},{2,6},{3,7},{4,5},{5,4},{6,2},{7,3},{8,9},{9,8},{10,14... | collective-permute-start | bytes 9830408 | tf_op jit(solution)/shard_map/ppermute | solution.py:601
  502.9 85.4 %reduce-scatter.6.cloned.1.call-start = ((), (), s32[]{:S(2)}) async-start(), calls=%async_computation.5 | async-start | bytes 2048000 | tf_op jit(solution)/shard_map/reduce_scatter | solution.py:677
  512.0 29.2 %collective-permute-start.45 = (bf16[320,2560]{1,0:T(8,128)(2,1)}, bf16[320,2560]{1,0:T(8,128)(2,1)}, u32[]{:S(2)}, u32[]{:S(2)}) collective-permute-start(bf16[320,2560]{1,0:T(8,128)(2,1)} %fusion.3), channel_id=1, source_target_pairs={{0,4},{1,5},{2,3},{3,2},{4,0},{5,1},{6,7},{7,6},{8,12},{9,13},{10,... | collective-permute-start | bytes 4915208 | tf_op jit(solution)/shard_map/ppermute | solution.py:601
  514.9 25.5 %collective-permute-start.48 = (bf16[4,32,1280]{2,1,0:T(8,128)(2,1)S(1)}, bf16[4,32,1280]{2,1,0:T(8,128)(2,1)S(1)}, u32[]{:S(2)}, u32[]{:S(2)}) collective-permute-start(bf16[4,32,1280]{2,1,0:T(8,128)(2,1)S(1)} %dynamic-slice_bitcast_fusion.2), channel_id=1, source_target_pairs={{0,4},{2,6},{4,0},{6,2},{8,12},{10,14},{12,8},{14,10},{16,20},{18,... | collective-permute-start | bytes 983048 | tf_op jit(solution)/shard_map/ppermute | solution.py:588
  517.9 27.8 %collective-permute-start.38 = (f32[4,2,2,1,800]{4,2,1,0,3:T(2,128)S(1)}, f32[4,2,2,1,800]{4,2,1,0,3:T(2,128)S(1)}, u32[]{:S(2)}, u32[]{:S(2)}) collective-permute-start(f32[4,2,2,1,800]{4,2,1,0,3:T(2,128)S(1)} %dynamic-slice_bitcast_fusion.7), channel_id=1, source_target_pairs={{0,2},{2,0},{4,6},{6,4},{8,10},{10,8},{12,14},{14,12},{16,18},{18,... | collective-permute-start | bytes 153608 | tf_op jit(solution)/shard_map/ppermute | solution.py:588
  545.7 63.8 %reduce-scatter.14.cloned.1.call-start = ((), (), s32[]{:S(2)}) async-start(), calls=%async_computation.10 | async-start | bytes 409600 | tf_op jit(solution)/shard_map/reduce_scatter | solution.py:677
  567.3 49.1 %all-gather.2.cloned.1.call-start = ((), (), s32[]{:S(2)}) async-start(), calls=%async_computation.8 | async-start | bytes 3481600 | tf_op jit(solution)/shard_map/all_gather | solution.py:1014
  570.3 15.5 %collective-permute-start.51 = (bf16[160,640]{1,0:T(8,128)(2,1)S(1)}, bf16[160,640]{1,0:T(8,128)(2,1)S(1)}, u32[]{:S(2)}, u32[]{:S(2)}) collective-permute-start(bf16[160,640]{1,0:T(8,128)(2,1)S(1)} %dynamic-slice_bitcast_fusion.4), channel_id=1, source_target_pairs={{0,2},{2,0},{4,6},{6,4},{8,10},{10,8},{12,14},{14,12},{16,18},{18,... | collective-permute-start | bytes 614408 | tf_op jit(solution)/shard_map/ppermute | solution.py:588
  571.9 13.7 %collective-permute-start.53 = (bf16[80,2560]{1,0:T(8,128)(2,1)S(1)}, bf16[80,2560]{1,0:T(8,128)(2,1)S(1)}, u32[]{:S(2)}, u32[]{:S(2)}) collective-permute-start(bf16[80,2560]{1,0:T(8,128)(2,1)S(1)} %dynamic-slice_bitcast_fusion.1), channel_id=1, source_target_pairs={{0,4},{2,6},{4,0},{6,2},{8,12},{10,14},{12,8},{14,10},{16,20},{18,... | collective-permute-start | bytes 1228808 | tf_op jit(solution)/shard_map/ppermute | solution.py:588
  589.2 21.8 %collective-permute-start.49 = (bf16[40,2560]{1,0:T(8,128)(2,1)S(1)}, bf16[40,2560]{1,0:T(8,128)(2,1)S(1)}, u32[]{:S(2)}, u32[]{:S(2)}) collective-permute-start(bf16[40,2560]{1,0:T(8,128)(2,1)S(1)} %dynamic-slice_bitcast_fusion.6), channel_id=1, source_target_pairs={{0,2},{2,0},{4,6},{6,4},{8,10},{10,8},{12,14},{14,12},{16,18},{18,... | collective-permute-start | bytes 614408 | tf_op jit(solution)/shard_map/ppermute | solution.py:588
  (126 other events, 1033.4 us)
Sparse Core Ops, SparseCore 0:
  392.8 62.5 reduce-scatter.11
  457.6 36.4 reduce-scatter.9
  503.0 35.5 reduce-scatter.7
  545.8 36.3 reduce-scatter.5
  584.9 24.4 reduce-scatter.13
Sparse Core Ops, SparseCore 1:
  570.9 45.4 all-gather.1

commit v3 on v2

--- a/solution.py
+++ b/solution.py
@@ -58,6 +58,10 @@
     mask[...] = jnp.where(same, 0.0, -1e30)
 
 
+PAIRS = 2
+WIDE = PAIRS * 2 * HEAD_DIM
+
+
 def attend_kernel(segment_row, segment_column, query, key, value, mixed, totals, mask):
     @pl.when(pl.program_id(1) == 0)
     def _():
@@ -66,7 +70,7 @@
     ones = jnp.ones((8, ROW_LEN), BF16)
     value_t = value[0].T
     parts = []
-    for head in range(2):
+    for head in range(2 * PAIRS):
         columns = slice(head * HEAD_DIM, (head + 1) * HEAD_DIM)
         scaled = query[0, :, columns] * jnp.asarray(1.0 / math.sqrt(HEAD_DIM), BF16)
         scores = dot_rt(key[0, :, columns], scaled) + mask[...]
@@ -80,10 +84,10 @@
     mixed[0] = jnp.concatenate(parts, axis=0).T.astype(BF16)
 
 
-def attend(qkv, segment, begin, pairs):
+def attend(qkv, segment):
     rows = qkv.shape[0]
-    every = HEADS // 2
-    wide = 2 * HEAD_DIM
+    pairs = HEADS // 2 // PAIRS
+    wide = WIDE
 
     def part(offset):
         return pl.BlockSpec((1, ROW_LEN, wide), lambda r, i: (r, 0, offset + i))
@@ -94,17 +98,17 @@
         in_specs=[
             pl.BlockSpec((1, 1, ROW_LEN), lambda r, i: (r, 0, 0)),
             pl.BlockSpec((1, ROW_LEN, 1), lambda r, i: (r, 0, 0)),
-            part(begin),
-            part(every + begin),
-            part(2 * every + begin),
+            part(0),
+            part(pairs),
+            part(2 * pairs),
         ],
         out_specs=[
             pl.BlockSpec((1, ROW_LEN, wide), lambda r, i: (r, 0, i)),
-            pl.BlockSpec((1, 1, 2, ROW_LEN), lambda r, i: (r, i, 0, 0)),
+            pl.BlockSpec((1, 1, 2 * PAIRS, ROW_LEN), lambda r, i: (r, i, 0, 0)),
         ],
         out_shape=[
             jax.ShapeDtypeStruct((rows, ROW_LEN, pairs * wide), BF16),
-            jax.ShapeDtypeStruct((rows, pairs, 2, ROW_LEN), F32),
+            jax.ShapeDtypeStruct((rows, pairs, 2 * PAIRS, ROW_LEN), F32),
         ],
         scratch_shapes=[pltpu.VMEM((ROW_LEN, ROW_LEN), F32)],
         compiler_params=pltpu.CompilerParams(vmem_limit_bytes=VMEM_ASKED),
@@ -113,7 +117,7 @@
 
 
 def attend_back_kernel(
-    segment_row, segment_column, query, key, value, mixed, back, totals, d_query, d_key, d_value, mask
+    segment_row, segment_column, query, key, value, mixed, back, totals, d_qkv, mask
 ):
     @pl.when(pl.program_id(1) == 0)
     def _():
@@ -123,7 +127,7 @@
     key_t = key[0].T
     product_t = (back[0].astype(F32) * mixed[0].astype(F32)).T
     queries, keys, values = [], [], []
-    for head in range(2):
+    for head in range(2 * PAIRS):
         columns = slice(head * HEAD_DIM, (head + 1) * HEAD_DIM)
         scaled = query[0, :, columns] * scale
         grad = back[0, :, columns]
@@ -135,15 +139,21 @@
         values.append(dot(weights.astype(BF16), grad))
         keys.append(dot(d_scores, scaled))
         queries.append(dot(key_t[columns], d_scores))
-    d_query[0] = (jnp.concatenate(queries, axis=0).T * (1.0 / math.sqrt(HEAD_DIM))).astype(BF16)
-    d_key[0] = jnp.concatenate(keys, axis=1).astype(BF16)
-    d_value[0] = jnp.concatenate(values, axis=1).astype(BF16)
+    pair = pl.program_id(1)
+    parts = [
+        jnp.concatenate(queries, axis=0).T * (1.0 / math.sqrt(HEAD_DIM)),
+        jnp.concatenate(keys, axis=1),
+        jnp.concatenate(values, axis=1),
+    ]
+    for i, part in enumerate(parts):
+        columns = pl.ds(pl.multiple_of(i * D + pair * WIDE, 128), WIDE)
+        d_qkv[0, :, columns] = part.astype(BF16)
 
 
 def attend_back(qkv, segment, mixed, back, totals):
     rows = qkv.shape[0]
-    pairs = HEADS // 2
-    wide = 2 * HEAD_DIM
+    pairs = HEADS // 2 // PAIRS
+    wide = WIDE
 
     def part(offset):
         return pl.BlockSpec((1, ROW_LEN, wide), lambda r, i: (r, 0, offset + i))
@@ -159,17 +169,18 @@
             part(2 * pairs),
             part(0),
             part(0),
-            pl.BlockSpec((1, 1, 2, ROW_LEN), lambda r, i: (r, i, 0, 0)),
+            pl.BlockSpec((1, 1, 2 * PAIRS, ROW_LEN), lambda r, i: (r, i, 0, 0)),
         ],
-        out_specs=[part(0)] * 3,
-        out_shape=[jax.ShapeDtypeStruct((rows, ROW_LEN, D), BF16)] * 3,
+        out_specs=pl.BlockSpec((1, ROW_LEN, 3 * D), lambda r, i: (r, 0, 0)),
+        out_shape=jax.ShapeDtypeStruct((rows, ROW_LEN, 3 * D), BF16),
         scratch_shapes=[pltpu.VMEM((ROW_LEN, ROW_LEN), F32)],
         compiler_params=pltpu.CompilerParams(vmem_limit_bytes=VMEM_ASKED),
         cost_estimate=pl.CostEstimate(flops=1, bytes_accessed=1, transcendentals=0),
     )(segment[:, None, :], segment[:, :, None], qkv, qkv, qkv, mixed, back, totals)
 
 
-CHUNK = 640
+CHUNK = 1280
+HALF_CHUNK = 640
 
 
 def part_copies(sources, columns, place, buffer, sems, half_rows, act):
@@ -219,7 +230,7 @@
     steps = shard.shape[0] // CHUNK
     own = step < steps
     local = jnp.where(own, step, step - steps)
-    part = ((local // 2) ^ outer) * 2 + ((local % 2) ^ inner)
+    size = 2 * fold * unit
 
     @pl.when(own)
     def _():
@@ -229,26 +240,25 @@
             )
         )
 
-    def remote(corner):
-        for side in range(2):
-            c = core if side == 0 else 1 - core
-            row = 0 if corner else pl.multiple_of(part * unit, 16)
-            for k in range(fold):
-                act(
-                    pltpu.make_async_copy(
-                        parts[2 * side + corner].at[pl.ds(row, unit), pl.ds(k * D, D)],
-                        buffer.at[pl.ds(pl.multiple_of((c * fold + k) * unit, 16), unit), :],
-                        sems.at[1 + side * fold + k],
-                    )
-                )
-
-    @pl.when(jnp.logical_and(jnp.logical_not(own), part < 3))
-    def _():
-        remote(0)
-
-    @pl.when(jnp.logical_and(jnp.logical_not(own), part == 3))
-    def _():
-        remote(1)
+    for piece in range(CHUNK // size):
+        at = local * (CHUNK // size) + piece
+        part = ((at // 2) ^ outer) * 2 + ((at % 2) ^ inner)
+        for corner in range(2):
+
+            @pl.when(jnp.logical_and(jnp.logical_not(own), (part == 3) == (corner == 1)))
+            def _():
+                row = 0 if corner else pl.multiple_of(part * unit, 16)
+                for side in range(2):
+                    c = core if side == 0 else 1 - core
+                    for k in range(fold):
+                        start = pl.multiple_of(piece * size + (c * fold + k) * unit, 16)
+                        act(
+                            pltpu.make_async_copy(
+                                parts[2 * side + corner].at[pl.ds(row, unit), pl.ds(k * D, D)],
+                                buffer.at[pl.ds(start, unit), :],
+                                sems.at[1 + (piece * 2 + side) * fold + k],
+                            )
+                        )
 
 
 def stream(copies, buffer, sems):
@@ -281,15 +291,19 @@
     slope[...] = rise.astype(BF16)
 
 
-def down_kernel(place, active, middle, *refs):
-    sources, (out, buffer, sems) = refs[:5], refs[5:]
+def down_kernel(place, active, middle, bias, picker, *refs):
+    sources, (out, heads, buffer, sems) = refs[:5], refs[5:]
     weights = stream(lambda *at: down_copies(sources, place, *at), buffer, sems)
 
     @pl.when(pl.program_id(0) == 0)
     def _():
-        out[...] = middle[...]
+        out[...] = middle[...] + bias[...]
 
     out[...] += dot(active[...], weights[...])
+
+    @pl.when(pl.program_id(0) == pl.num_programs(0) - 1)
+    def _():
+        heads[...] = dot(picker[...], out[...].astype(BF16)).astype(BF16)
 
 
 def back_kernel(place, branch, slope, *refs):
@@ -309,7 +323,72 @@
     out[...] += dot_rt(low, up_part[...])
 
 
-def feed_call(kernel, count, inputs, outputs, slots, matmuls, place, *values):
+def qkv_kernel(place, normed, bias, *refs):
+    sources, (out, buffer, sems) = refs[:5], refs[5:]
+
+    def copies(step, *at):
+        columns = pl.ds(pl.multiple_of(step * CHUNK, 128), CHUNK)
+        part_copies(sources, columns, place, *at[:2], sources[0].shape[0], at[2])
+
+    weights = stream(copies, buffer, sems)
+    out[...] = (dot(normed[...], weights[...]) + bias[...]).astype(BF16)
+
+
+def qkv_back_kernel(place, back, *refs):
+    sources, (out, buffer, sems) = refs[:5], refs[5:]
+
+    def copies(step, *at):
+        columns = pl.ds(pl.multiple_of(step * CHUNK, 128), CHUNK)
+        part_copies(sources, columns, place, *at[:2], sources[0].shape[0], at[2])
+
+    weights = stream(copies, buffer, sems)
+    terms = dot_rt(back[...], weights[...])
+
+    @pl.when(pl.program_id(0) == 0)
+    def _():
+        out[...] = terms
+
+    @pl.when(pl.program_id(0) > 0)
+    def _():
+        out[...] += terms
+
+
+def qkv_call(kernel, place, inputs, specs, out_shape, out_spec, columns, weights):
+    return pl.pallas_call(
+        kernel,
+        grid_spec=pltpu.PrefetchScalarGridSpec(
+            num_scalar_prefetch=1,
+            grid=(columns // CHUNK,),
+            in_specs=specs + [pl.BlockSpec(memory_space=pl.ANY)] * 5,
+            out_specs=out_spec,
+            scratch_shapes=[pltpu.VMEM((2, D, CHUNK), BF16), pltpu.SemaphoreType.DMA((2, 9))],
+        ),
+        out_shape=out_shape,
+        compiler_params=pltpu.CompilerParams(vmem_limit_bytes=VMEM_ASKED),
+        cost_estimate=pl.CostEstimate(flops=1, bytes_accessed=1, transcendentals=0),
+    )(place, *inputs, *weights)
+
+
+def project(place, normed, bias, weights):
+    count, columns = normed.shape[0], weights[0].shape[1]
+    whole = pl.BlockSpec((count, D), lambda j, place: (0, 0))
+    row = pl.BlockSpec((1, CHUNK), lambda j, place: (0, j))
+    out = pl.BlockSpec((count, CHUNK), lambda j, place: (0, j))
+    shape = jax.ShapeDtypeStruct((count, columns), BF16)
+    return qkv_call(
+        qkv_kernel, place, [normed, bias], [whole, row], shape, out, columns, weights
+    )
+
+
+def project_back(place, back, weights):
+    count, columns = back.shape
+    whole = pl.BlockSpec((count, D), lambda j, place: (0, 0))
+    chunk = pl.BlockSpec((count, CHUNK), lambda j, place: (0, j))
+    shape = jax.ShapeDtypeStruct((count, D), F32)
+    return qkv_call(qkv_back_kernel, place, [back], [chunk], shape, whole, columns, weights)
+
+
+def feed_call(kernel, count, inputs, outputs, slots, place, *values, keep=()):
     def at(j, place):
         return chunk_place(j, place, FF // 2)
 
@@ -318,15 +397,20 @@
         "row": pl.BlockSpec((1, CHUNK), lambda j, place: (0, at(j, place))),
         "whole": pl.BlockSpec((count, D), lambda j, place: (0, 0)),
         "any": pl.BlockSpec(memory_space=pl.ANY),
+        "vector": pl.BlockSpec((1, D), lambda j, place: (0, 0)),
     }
     shapes = {
         "hidden": jax.ShapeDtypeStruct((count, FF), BF16),
         "row": jax.ShapeDtypeStruct((1, FF), F32),
         "whole": jax.ShapeDtypeStruct((count, D), F32),
     }
+    for name, array in keep:
+        block = array.shape
+        specs[name] = pl.BlockSpec(block, lambda j, place: (0, 0))
+        shapes[name] = jax.ShapeDtypeStruct(block, BF16)
     scratch = []
     for slot in slots:
-        scratch += [pltpu.VMEM((2, *slot), BF16), pltpu.SemaphoreType.DMA((2, 9))]
+        scratch += [pltpu.VMEM((2, *slot), BF16), pltpu.SemaphoreType.DMA((2, 17))]
     return pl.pallas_call(
         kernel,
         grid_spec=pltpu.PrefetchScalarGridSpec(
@@ -348,39 +432,69 @@
 def feed_up(place, second, bias, up):
     names = ["whole", "row"] + ["any"] * 5
     return feed_call(
-        up_kernel, second.shape[0], names, ["hidden", "hidden"], [UP_SLOT], 1, place, second, bias, *up
-    )
-
-
-def feed_down(place, active, middle, down):
-    names = ["hidden", "whole"] + ["any"] * 5
+        up_kernel, second.shape[0], names, ["hidden", "hidden"], [UP_SLOT], place, second, bias, *up
+    )
+
+
+def feed_down(place, active, middle, bias, picker, down):
+    names = ["hidden", "whole", "vector", "picker"] + ["any"] * 5
+    heads = jax.ShapeDtypeStruct((picker.shape[0], D), BF16)
     return feed_call(
-        down_kernel, active.shape[0], names, ["whole"], [DOWN_SLOT], 1, place, active, middle, *down
-    )[0]
+        down_kernel, active.shape[0], names, ["whole", "heads"], [DOWN_SLOT],
+        place, active, middle, bias, picker, *down, keep=(("picker", picker), ("heads", heads)),
+    )
 
 
 def feed_back(place, branch, slope, up, down):
     names = ["whole", "hidden"] + ["any"] * 10
     return feed_call(
-        back_kernel, branch.shape[0], names, ["hidden", "row", "whole"], [UP_SLOT, DOWN_SLOT], 2,
+        back_kernel, branch.shape[0], names, ["hidden", "row", "whole"], [UP_SLOT, DOWN_SLOT],
         place, branch, slope, *up, *down,
     )
 
 
-def term_kernel(steps, place, *refs):
-    count = len(steps)
+def decode_kernel(mine, other, gene, got, bias, weight, labels, low, sums, by_weight):
+    cells = mine.shape[0]
+    shape = (cells, gene.shape[0] // cells, gene.shape[1])
+    parts = (gene[...].astype(F32) + got[...].astype(F32) + bias[...]).reshape(shape)
+    before = (mine[...] + other[...])[:, None, :] + parts
+    value, rise = gate(before)
+    row = weight[...].astype(F32)[None]
+    logits = jnp.sum(value * row, axis=2, keepdims=True)
+    slope = jax.nn.sigmoid(logits) - labels[...].astype(F32)
+    grad = (rise * (slope * row)).astype(BF16)
+    low[...] = grad.reshape(low.shape)
+    sums[...] = jnp.sum(grad.astype(F32), axis=1)
+    by_weight[...] = jnp.sum(jnp.sum(value * slope, axis=0), axis=0, keepdims=True)
+
+
+def decode(mine, other, gene, got, bias, weight, labels):
+    cells, queries = labels.shape
+    return pl.pallas_call(
+        decode_kernel,
+        out_shape=[
+            jax.ShapeDtypeStruct((cells * queries, FF), BF16),
+            jax.ShapeDtypeStruct((cells, FF), F32),
+            jax.ShapeDtypeStruct((1, FF), F32),
+        ],
+        compiler_params=pltpu.CompilerParams(vmem_limit_bytes=VMEM_ASKED),
+        cost_estimate=pl.CostEstimate(flops=1, bytes_accessed=1, transcendentals=0),
+    )(mine, other, gene, got, bias, weight, labels[:, :, None])
+
+
+def term_kernel(count, mine, units, place, *refs):
     query, _, inner, core = (place[i] for i in range(4))
-    lefts, rights, (own, sent, blocks), turned = (
+    inputs = 1 + max(source for unit in units for _, source in unit)
+    lefts, rights, (out, blocks), turned = (
         refs[:count],
-        refs[count : 2 * count],
-        refs[2 * count : 2 * count + 3],
-        refs[2 * count + 3 :],
-    )
-    every = sum(steps)
+        refs[count : count + inputs],
+        refs[count + inputs : count + inputs + 2],
+        refs[count + inputs + 2 :],
+    )
     step = pl.program_id(0)
-    half = jnp.where(step < every, 1 - core, core)
-
-    @pl.when(step % every == 0)
+    half = core if mine else 1 - core
+
+    @pl.when(step == 0)
     def _():
         outer = blocks.shape[0] // 8
         size = 2 * outer * blocks.shape[1]
@@ -395,55 +509,56 @@
                 ]
                 into[pl.ds(to * size, size), :] = jnp.concatenate(rows, axis=0).astype(BF16)
 
-    column = step % every
-    begin = 0
-    for left, right, size in zip(turned, rights, steps):
-        for out, mine in ((own, True), (sent, False)):
-
-            @pl.when(
-                jnp.logical_and(
-                    jnp.logical_and(column >= begin, column < begin + size), (step >= every) == mine
-                )
-            )
-            def _():
-                out[...] = dot(left[...], right[...]).astype(BF16).reshape(out.shape)
-
-        begin += size
-
-
-def weight_terms(place, *pairs):
+    for at, unit in enumerate(units):
+
+        @pl.when(step == at)
+        def _():
+            for side, (pair, source) in enumerate(unit):
+                terms = dot(turned[pair][...], rights[source][...]).astype(BF16)
+                columns = slice(side * HALF_CHUNK, (side + 1) * HALF_CHUNK)
+                out[:, :, :, columns] = terms.reshape(*out.shape[:3], HALF_CHUNK)
+
+
+def weight_terms(place, mine, *pairs):
     count, rows = pairs[0][0].shape
-    steps = [right.shape[1] // 2 // CHUNK for _, right in pairs]
-    every = sum(steps)
-    shape = (2, 2, rows // 4, every * CHUNK)
-
-    def right_spec(begin, size):
+    sizes = [right.shape[1] // 2 // HALF_CHUNK for _, right in pairs]
+    blocks = [(i, block) for i, size in enumerate(sizes) for block in range(size)]
+    plan = [blocks[i : i + 2] for i in range(0, len(blocks), 2)]
+    steps = len(plan)
+    sources = sorted({(side, unit[side][0]) for unit in plan for side in range(2)})
+
+    def right_spec(side, pair):
+        wanted = [unit[side][1] if unit[side][0] == pair else None for unit in plan]
+        known = [block for block in wanted if block is not None]
+
         def at(j, place):
-            half = jnp.where(j < every, 1 - place[3], place[3])
-            return (0, half * size + jnp.clip(j % every - begin, 0, size - 1))
-
-        return pl.BlockSpec((count, CHUNK), at)
-
-    block = (2, 2, rows // 4, CHUNK)
+            half = place[3] if mine else 1 - place[3]
+            index = known[0]
+            for step, block in enumerate(wanted):
+                if block is not None:
+                    index = jnp.where(j >= step, block, index)
+            return (0, half * sizes[pair] + index)
+
+        return pl.BlockSpec((count, HALF_CHUNK), at)
+
+    units = [
+        [(pair, sources.index((side, pair))) for side, (pair, _) in enumerate(unit)] for unit in plan
+    ]
     left_spec = pl.BlockSpec((count, rows), lambda j, place: (0, 0))
     return pl.pallas_call(
-        lambda *refs: term_kernel(steps, *refs),
+        lambda *refs: term_kernel(len(pairs), mine, units, *refs),
         grid_spec=pltpu.PrefetchScalarGridSpec(
             num_scalar_prefetch=1,
-            grid=(2 * every,),
-            in_specs=[left_spec] * len(pairs)
-            + [right_spec(sum(steps[:i]), size) for i, size in enumerate(steps)],
-            out_specs=[
-                pl.BlockSpec(block, lambda j, place: (0, 0, 0, jnp.maximum(j - every, 0))),
-                pl.BlockSpec(block, lambda j, place: (0, 0, 0, jnp.minimum(j, every - 1))),
-            ],
+            grid=(steps,),
+            in_specs=[left_spec] * len(pairs) + [right_spec(*source) for source in sources],
+            out_specs=pl.BlockSpec((2, 2, rows // 4, CHUNK), lambda j, place: (0, 0, 0, j)),
             scratch_shapes=[pltpu.VMEM((32, rows // 32, count), F32)]
             + [pltpu.VMEM((rows, count), BF16)] * len(pairs),
         ),
-        out_shape=[jax.ShapeDtypeStruct(shape, BF16)] * 2,
+        out_shape=jax.ShapeDtypeStruct((2, 2, rows // 4, steps * CHUNK), BF16),
         compiler_params=pltpu.CompilerParams(vmem_limit_bytes=VMEM_ASKED),
         cost_estimate=pl.CostEstimate(flops=1, bytes_accessed=1, transcendentals=0),
-    )(place, *[left for left, _ in pairs], *[right for _, right in pairs])
+    )(place, *[left for left, _ in pairs], *[pairs[pair][1] for _, pair in sources])
 
 
 def tall_kernel(place, left, right, own, sent, blocks, turned):
@@ -459,7 +574,7 @@
     for half in range(2):
         for x in range(2):
             x_place = x ^ query
-            at = (y_place, x_place)
+            at = (x_place, y_place) if half == 0 else (y_place, x_place)
             value = terms[2 * x * width : 2 * (x + 1) * width, half * size : (half + 1) * size]
 
             @pl.when(core == half)
@@ -502,6 +617,210 @@
     return own.reshape(flat), sent.reshape(flat)
 
 
+def small_cost():
+    return pl.CostEstimate(flops=1, bytes_accessed=1, transcendentals=0)
+
+
+def add_kernel(count, *refs):
+    ins, outs = refs[: len(refs) - count], refs[len(refs) - count :]
+    each = len(ins) // count
+    for i, out in enumerate(outs):
+        total = ins[i * each][...].astype(F32)
+        for other in ins[i * each + 1 : (i + 1) * each]:
+            total = total + other[...].astype(F32)
+        out[...] = total.astype(BF16)
+
+
+def add_call(*groups):
+    first, _ = groups[0][0]
+    rows, columns = first.shape[-2:]
+    steps = 2
+    size = rows // steps
+    specs, arrays = [], []
+    for group in groups:
+        for array, at in group:
+            lead = (None,) * len(at)
+            specs.append(
+                pl.BlockSpec((*lead, size, columns), lambda r, at=at: (*at, r, 0))
+            )
+            arrays.append(array)
+    out = pl.BlockSpec((size, columns), lambda r: (r, 0))
+    shape = jax.ShapeDtypeStruct((rows, columns), BF16)
+    return pl.pallas_call(
+        lambda *refs: add_kernel(len(groups), *refs),
+        grid=(steps,),
+        in_specs=specs,
+        out_specs=[out] * len(groups),
+        out_shape=[shape] * len(groups),
+        compiler_params=pltpu.CompilerParams(vmem_limit_bytes=VMEM_ASKED),
+        cost_estimate=small_cost(),
+    )(*arrays)
+
+
+def out_kernel(mixed, weight, tokens, bias, gain, shift, middle, second):
+    values = tokens[...].astype(F32) + dot(mixed[...], weight[...]) + bias[...]
+    middle[...] = values
+    second[...] = layer_norm(values, gain[...], shift[...]).astype(BF16)
+
+
+def attend_out(mixed, weight, tokens, bias, gain, shift):
+    count = tokens.shape[0]
+    size = 256
+    row = pl.BlockSpec((size, D), lambda r: (r, 0))
+    vector = pl.BlockSpec((1, D), lambda r: (0, 0))
+    whole = pl.BlockSpec((D, D), lambda r: (0, 0))
+    return pl.pallas_call(
+        out_kernel,
+        grid=(count // size,),
+        in_specs=[row, whole, row, vector, vector, vector],
+        out_specs=[row, row],
+        out_shape=[
+            jax.ShapeDtypeStruct((count, D), F32),
+            jax.ShapeDtypeStruct((count, D), BF16),
+        ],
+        compiler_params=pltpu.CompilerParams(vmem_limit_bytes=VMEM_ASKED),
+        cost_estimate=small_cost(),
+    )(mixed, weight, tokens, bias[None, :], gain[None, :], shift[None, :])
+
+
+def spread_kernel(left, right, out):
+    out[...] = dot(left[...], right[...]).astype(BF16)
+
+
+def spread(left, right):
+    count, depth = left.shape
+    columns = right.shape[1]
+    return pl.pallas_call(
+        spread_kernel,
+        grid=(columns // CHUNK,),
+        in_specs=[
+            pl.BlockSpec((count, depth), lambda j: (0, 0)),
+            pl.BlockSpec((depth, CHUNK), lambda j: (0, j)),
+        ],
+        out_specs=pl.BlockSpec((count, CHUNK), lambda j: (0, j)),
+        out_shape=jax.ShapeDtypeStruct((count, columns), BF16),
+        compiler_params=pltpu.CompilerParams(vmem_limit_bytes=VMEM_ASKED),
+        cost_estimate=small_cost(),
+    )(left, right)
+
+
+def gather_kernel(left, right, out, total):
+    terms = dot_rt(left[...], right[...])
+    step = pl.program_id(0)
+
+    @pl.when(step == 0)
+    def _():
+        total[...] = terms
+
+    @pl.when(step > 0)
+    def _():
+        total[...] += terms
+
+    @pl.when(step == pl.num_programs(0) - 1)
+    def _():
+        out[...] = total[...].astype(BF16)
+
+
+def gather(left, right):
+    count, columns = left.shape
+    rows = right.shape[0]
+    return pl.pallas_call(
+        gather_kernel,
+        grid=(columns // CHUNK,),
+        in_specs=[
+            pl.BlockSpec((count, CHUNK), lambda j: (0, j)),
+            pl.BlockSpec((rows, CHUNK), lambda j: (0, j)),
+        ],
+        out_specs=pl.BlockSpec((count, rows), lambda j: (0, 0)),
+        out_shape=jax.ShapeDtypeStruct((count, rows), BF16),
+        scratch_shapes=[pltpu.VMEM((count, rows), F32)],
+        compiler_params=pltpu.CompilerParams(vmem_limit_bytes=VMEM_ASKED),
+        cost_estimate=small_cost(),
+    )(left, right)
+
+
+def norm_terms(values, grad, gain):
+    center = values - jnp.mean(values, axis=-1, keepdims=True)
+    spread = jnp.mean(center * center, axis=-1, keepdims=True)
+    rise = lax.rsqrt(spread + EPSILON)
+    unit = center * rise
+    scaled = grad * gain
+    first = jnp.mean(scaled, axis=-1, keepdims=True)
+    second = jnp.mean(scaled * unit, axis=-1, keepdims=True)
+    return (
+        (scaled - first - unit * second) * rise,
+        jnp.sum(grad * unit, axis=0, keepdims=True),
+        jnp.sum(grad, axis=0, keepdims=True),
+    )
+
+
+def out_back_kernel(
+    grad, middle, gain, flat, weight, grad_middle, low, back, gain_sum, shift_sum
+):
+    part, by_gain, by_shift = norm_terms(middle[...], grad[...], gain[...])
+    total = flat[...] + part
+    grad_middle[...] = total
+    low[...] = total.astype(BF16)
+    back[...] = dot_rt(total.astype(BF16), weight[...]).astype(BF16)
+
+    @pl.when(pl.program_id(0) == 0)
+    def _():
+        gain_sum[...] = jnp.zeros_like(gain_sum)
+        shift_sum[...] = jnp.zeros_like(shift_sum)
+
+    gain_sum[...] += by_gain
+    shift_sum[...] += by_shift
+
+
+def attend_out_back(grad, middle, gain, flat, weight):
+    count = grad.shape[0]
+    size = 256
+    row = pl.BlockSpec((size, D), lambda r: (r, 0))
+    vector = pl.BlockSpec((1, D), lambda r: (0, 0))
+    whole = pl.BlockSpec((D, D), lambda r: (0, 0))
+    wide = jax.ShapeDtypeStruct((count, D), F32)
+    low = jax.ShapeDtypeStruct((count, D), BF16)
+    return pl.pallas_call(
+        out_back_kernel,
+        grid=(count // size,),
+        in_specs=[row, row, vector, row, whole],
+        out_specs=[row, row, row, vector, vector],
+        out_shape=[wide, low, low] + [jax.ShapeDtypeStruct((1, D), F32)] * 2,
+        compiler_params=pltpu.CompilerParams(vmem_limit_bytes=VMEM_ASKED),
+        cost_estimate=small_cost(),
+    )(grad, middle, gain[None, :], flat, weight)
+
+
+def tokens_back_kernel(grad, tokens, gain, flat, out, gain_sum, shift_sum):
+    part, by_gain, by_shift = norm_terms(tokens[...].astype(F32), grad[...], gain[...])
+    out[...] = flat[...] + part
+
+    @pl.when(pl.program_id(0) == 0)
+    def _():
+        gain_sum[...] = jnp.zeros_like(gain_sum)
+        shift_sum[...] = jnp.zeros_like(shift_sum)
+
+    gain_sum[...] += by_gain
+    shift_sum[...] += by_shift
+
+
+def tokens_back(grad, tokens, gain, flat):
+    count = grad.shape[0]
+    size = 256
+    row = pl.BlockSpec((size, D), lambda r: (r, 0))
+    vector = pl.BlockSpec((1, D), lambda r: (0, 0))
+    return pl.pallas_call(
+        tokens_back_kernel,
+        grid=(count // size,),
+        in_specs=[row, row, vector, row],
+        out_specs=[row, vector, vector],
+        out_shape=[jax.ShapeDtypeStruct((count, D), F32)]
+        + [jax.ShapeDtypeStruct((1, D), F32)] * 2,
+        compiler_params=pltpu.CompilerParams(vmem_limit_bytes=VMEM_ASKED),
+        cost_estimate=small_cost(),
+    )(grad, tokens, gain[None, :], flat)
+
+
 def assemble_kernel(pieces, width, count, place_ref, *refs):
     sources, full, sems = refs[:count], refs[count], refs[count + 1]
     step = pl.program_id(0)
@@ -561,9 +880,13 @@
     def paired(self):
         size = self.size
         pairs = size["x"] == 2 and size["y"] == 2 and size["c"] == 2
-        return pairs and size["z"] in (2, 4) and D % (self.dp * self.query * 8) == 0
+        return pairs and size["z"] == 4 and D % (self.dp * self.query * 8) == 0
 
     def place(self, axis):
+        if axis == "zb":
+            return self.place("z") % 2
+        if axis == "zh":
+            return self.place("z") // 2
         if axis == "x":
             return lax.axis_index("query")
         return (lax.axis_index("dp") // self.stride[axis]) % self.size[axis]
@@ -611,6 +934,26 @@
             [jnp.where(first, value, other), jnp.where(first, other, value)], axis=axis
         )
 
+    def joined_along(self, mine, other, axis):
+        first = self.place(axis) == 0
+        return jnp.concatenate(
+            [jnp.where(first, mine, other), jnp.where(first, other, mine)], axis=0
+        )
+
+    def cut_half(self, value, axis):
+        half = value.shape[1] // 2
+        first = self.place(axis) == 0
+        left, right = value[:, :half], value[:, half:]
+        return jnp.where(first, left, right), jnp.where(first, right, left)
+
+    def cut_fold(self, value, step):
+        bits = value.reshape(value.shape[0] // 2, 2, *value.shape[1:])
+        me = self.place("z") // step % 2
+        return (
+            lax.dynamic_index_in_dim(bits, me, axis=1, keepdims=False),
+            lax.dynamic_index_in_dim(bits, 1 - me, axis=1, keepdims=False),
+        )
+
     def joined(self, mine, other, axis=0):
         first = lax.axis_index("query") == 0
         return jnp.concatenate(
@@ -636,6 +979,14 @@
         first = self.place("c") == 0
         left, right = terms[:, :half], terms[:, half:]
         return jnp.where(first, left, right), jnp.where(first, right, left)
+
+    def trade(self, value, axis, dim, column):
+        mine, other = self.cut_step(value, axis, dim)
+        got = self.hop(other, axis) if axis != "zb" else self.hop(other, "z")
+        first = self.place(axis) == 0
+        return jnp.concatenate(
+            [jnp.where(first, mine, got), jnp.where(first, got, mine)], axis=column
+        )
 
     def join_columns(self, value):
         value = value.reshape(2, -1, value.shape[-1])
@@ -674,6 +1025,17 @@
     def scatter_z(self, value):
         stride, size = self.stride["z"], self.size["z"]
         groups = [[k * stride + i for k in range(size)] for i in range(stride)]
+        return lax.psum_scatter(
+            value, "dp", scatter_dimension=0, axis_index_groups=groups, tiled=True
+        )
+
+    def scatter_high(self, value):
+        stride, size = self.stride["z"], self.size["z"]
+        groups = [
+            [(high * 2 + low) * stride + i for high in range(size // 2)]
+            for low in range(2)
+            for i in range(stride)
+        ]
         return lax.psum_scatter(
             value, "dp", scatter_dimension=0, axis_index_groups=groups, tiled=True
         )
@@ -712,6 +1074,11 @@
         sent = (by_z[:cut], by_y[cut:])
         return sent, [self.hop(sent[0], "y"), self.hop(sent[1], "z")]
 
+    def corner_cuts(self, sides):
+        by_y, by_z = sides
+        cut = by_y.shape[0] // 2 // 16 * 16
+        return [by_z[:cut], by_y[cut:]]
+
     def most_of(self, first, sides, *after):
         near = jnp.concatenate([tie(first, *after), *sides], axis=0)
         return near, self.hop(near, "c")
@@ -754,36 +1121,34 @@
 
 
 class Sums:
-    def __init__(self, grid, own, sent):
-        self.grid, self.own, self.sent = grid, own, sent
+    def __init__(self, grid):
+        self.grid = grid
 
     def core(self, *after):
         self.got = self.grid.hop(tie(self.sent, *after), "c")
 
     def add_first(self, *after):
         own, got = tie((self.own, self.got), *after)
-        self.first_in = [added(own[1, k], got[1, k]) for k in (1, 0)]
-
-    def add_turned(self, *after):
-        own, got = tie((self.own, self.got), *after)
-        self.one_in = added(own[1], got[1])
-
-    def go_turned(self, *after):
-        one = self.grid.turn_hop(tie(self.one_in, *after), 0)
-        self.one = [one[1], one[0]]
-
-    def add_second(self, *after):
-        own, got, one = tie((self.own, self.got, self.one[0]), *after)
-        self.two_in = added(own[0, 1], got[0, 1], one)
-
-    def add_last(self, *after):
-        own, got, one = tie((self.own, self.got, self.one[1]), *after)
-        whole = added(own[0, 0], got[0, 0], one, self.two)
+        self.parts = add_call(*[[(own, (1, k)), (got, (1, k))] for k in (1, 0)])
+
+    def go_first(self, part):
+        return self.grid.turn_hop(self.parts[part], 0)
+
+    def add_second(self, one, *after):
+        own, got, one = tie((self.own, self.got, one), *after)
+        (self.two_in,) = add_call([(own, (0, 1)), (got, (0, 1)), (one, ())])
+
+    def go_second(self):
+        return self.grid.turn_hop(self.two_in, 1)
+
+    def add_last(self, one, two, *after):
+        own, got, one = tie((self.own, self.got, one), *after)
+        (whole,) = add_call([(own, (0, 0)), (got, (0, 0)), (one, ()), (two, ())])
         size = self.grid.size["z"]
         self.last_in = whole.reshape(size, whole.shape[0] // size, whole.shape[1])
 
-    def last(self, *after):
-        self.sum = self.grid.scatter_z(tie(self.last_in, *after))
+    def last(self):
+        self.sum = self.grid.scatter_z(self.last_in)
 
     def result(self, *after):
         value = tie(self.sum, *after)[0]
@@ -827,12 +1192,11 @@
         pairs = pair_cells * local_queries
         half_width = D // query_count
 
-        flat_tokens = tokens.astype(F32).reshape(token_count, D)
+        row_tokens = tokens.reshape(token_count, D)
         where = grid.places()
         ids = grid.share(query_ids.reshape(1, pairs)).reshape(query_count * pairs)
         qkv_first = grid.hop(grid.part_of([w_qkv]), "x")
-        normed, first_pull = jax.vjp(layer_norm, flat_tokens, ln_gains[0], ln_biases[0])
-        normed_low = normed.astype(BF16)
+        normed_low = layer_norm(row_tokens.astype(F32), ln_gains[0], ln_biases[0]).astype(BF16)
         table_rows = gene_table.shape[0]
         local_ids = ids - place * table_rows
         held = (local_ids[:, None] == jnp.arange(table_rows, dtype=jnp.int32)[None, :]).astype(BF16)
@@ -844,219 +1208,248 @@
         )
         up_first = grid.hop(up_part, "x")
         qkv_sides = sync(*grid.sides_of(qkv_first))
-        _, qkv_corners = grid.corners_of(qkv_sides)
-        qkv_near, qkv_far = grid.most_of(qkv_first, qkv_sides)
-        qkv_corners = sync(*qkv_corners, qkv_near)[:2]
+        qkv_sent = sync(*grid.corner_cuts(qkv_sides))
+        qkv_corners = [grid.hop(qkv_sent[0], "y"), grid.hop(qkv_sent[1], "z")]
+        qkv_near, qkv_far = grid.most_of(qkv_first, qkv_sides, qkv_sent)
+        *qkv_corners, qkv_near, up_first = sync(*qkv_corners, qkv_near, up_first)
+        up_sides = grid.sides_of(up_first)
         qkv_end, qkv_end_far = grid.corner_of(qkv_corners)
         qkv_end_far, qkv_far, up_first = sync(qkv_end_far, qkv_far, up_first)
-        up_sides = grid.sides_of(up_first)
-        gene_hop = grid.hop(tie(gene_found, up_first), "x")
-        full_qkv = grid.join(w_qkv, (qkv_near, qkv_end, qkv_far, qkv_end_far), 0)
+        gene_hop = grid.hop(gene_found, "x")
+        down_first = grid.hop(tie(down_part, up_first), "x")
+        qkv_weights = (w_qkv, qkv_near, qkv_end, qkv_far, qkv_end_far)
         zeroes = jnp.zeros((D,), F32)
         qkv_bias = jnp.concatenate([proj_biases[0], zeroes, proj_biases[1]])
-        qkv_low = (dot(normed_low, full_qkv) + qkv_bias).astype(BF16)
-        qkv_low, *up_sides, gene_hop = sync(qkv_low, *up_sides, gene_hop)
+        qkv_low = project(where, normed_low, qkv_bias[None, :], qkv_weights)
         qkv_rows = qkv_low.reshape(row_count, ROW_LEN, 3 * D)
-        up_sent, up_corners = grid.corners_of(up_sides)
-        down_first = grid.hop(tie(down_part, gene_hop), "x")
-        cut = HEADS // 4
-        mixed_one, totals_one = attend(tie(qkv_rows, up_sent), segment, 0, cut)
-        gene_rows = added(gene_found, tie(gene_hop, mixed_one)) if query_count == 2 else gene_found
-        up_near, up_far = grid.most_of(up_first, tie(up_sides, mixed_one))
-        mixed_two, totals_two = attend(
-            tie(qkv_rows, mixed_one, up_near), segment, cut, HEADS // 2 - cut
-        )
-        mixed_two, *up_corners, down_first = sync(mixed_two, *up_corners, down_first)
-        down_sides = grid.sides_of(down_first)
+        mixed_rows, log_totals = attend(qkv_rows, segment)
+        mixed_rows, *up_sides, down_first, gene_hop = sync(mixed_rows, *up_sides, down_first, gene_hop)
+        up_sent = sync(*grid.corner_cuts(up_sides))
+        up_corners = [grid.hop(up_sent[0], "y"), grid.hop(up_sent[1], "z")]
+        up_near, up_far = grid.most_of(up_first, up_sides, up_sent)
+        down_sides = grid.sides_of(down_first, (up_near,))
+        mixed_low = mixed_rows.reshape(token_count, D)
+        gene_rows = added(gene_found, gene_hop) if query_count == 2 else gene_found
+        gene_half = lax.dynamic_slice_in_dim(gene_rows, place * half_width, half_width, 1)
+        gene_partial = spread(tie(gene_half, up_near), dec_gene).reshape(query_count, pairs, FF)
+        gene_mine, gene_sent = grid.cut_step(gene_partial, "x", 0)
+        *up_corners, up_far, gene_sent = sync(*up_corners, up_far, gene_sent)
         up_end, up_end_far = grid.corner_of(up_corners)
-        mixed_rows = jnp.concatenate([mixed_one, mixed_two], axis=2)
-        log_totals = jnp.concatenate([totals_one, totals_two], axis=1)
-        mixed_low = mixed_rows.reshape(token_count, D)
         up_parts = (up_near, up_end, up_far, up_end_far)
         up_weights = (w_up, *up_parts)
         full_out = grid.join(w_out, up_parts, FF)
-        middle = flat_tokens + dot(mixed_low, full_out) + proj_biases[2]
-        second, second_pull = jax.vjp(layer_norm, middle, ln_gains[1], ln_biases[1])
-        second_low = second.astype(BF16)
-        gene_half = lax.dynamic_slice_in_dim(gene_rows, place * half_width, half_width, 1)
-        gene_partial = dot(tie(gene_half, mixed_two), dec_gene).astype(BF16).reshape(query_count, pairs, FF)
-        gene_mine, gene_sent = grid.cut_step(gene_partial, "x", 0)
-        second_low, gene_sent = sync(second_low, gene_sent)
+        middle, second_low = attend_out(
+            mixed_low, full_out, row_tokens, proj_biases[2], ln_gains[1], ln_biases[1]
+        )
+        second_low, down_first, *down_sides = sync(second_low, down_first, *down_sides)
+        down_sent = sync(*grid.corner_cuts(down_sides))
+        down_corners = [grid.hop(down_sent[0], "y"), grid.hop(down_sent[1], "z")]
+        down_near, down_far = grid.most_of(down_first, down_sides, down_sent)
         gene_got = grid.hop(gene_sent, "x")
-        active_low, slope = feed_up(where, second_low, ff_biases[0][None, :], up_weights)
-        active_low, slope, *down_sides, gene_got = sync(active_low, slope, *down_sides, gene_got)
-        places = jnp.arange(ROW_LEN, dtype=jnp.int32)
-        leading = jnp.any(places[None, :, None] == starts[:, None, :], axis=2)
-        early_low = jnp.where(
-            leading[:, :, None], 0, out_cotangent
-        ).reshape(token_count, D).astype(BF16)
-        down_sent, down_corners = grid.corners_of(down_sides)
-        down_near, down_far = grid.most_of(down_first, down_sides, down_sent)
-        early_low = tie(early_low, down_near, down_sent)
-        down_sums = Sums(grid, *tall_terms(where, active_low, early_low, grid.size["z"]))
-        down_sums.sent, *down_corners, down_far = sync(down_sums.sent, *down_corners, down_far)
+        gene_pair = grid.hop(gene_rows, "z")
+        active_low, slope = feed_up(
+            where, tie(second_low, down_near), ff_biases[0][None, :], up_weights
+        )
+        active_low, slope, *down_corners, down_far, gene_got, gene_pair = sync(
+            active_low, slope, *down_corners, down_far, gene_got, gene_pair
+        )
         down_end, down_end_far = grid.corner_of(down_corners)
         down_weights = (w_down, down_near, down_end, down_far, down_end_far)
-        down_sums.core(down_end_far)
-        encoded = feed_down(
-            where, tie(active_low, down_sums.sent), middle + proj_biases[3], down_weights
-        )
-        encoded, down_sums.got = sync(encoded, down_sums.got)
+        places = jnp.arange(ROW_LEN, dtype=jnp.int32)
+        picker = (places[None, :, None] == starts[:, None, :]).astype(F32)
+        rows_apart = jnp.arange(row_count)
+        choice = jnp.where(
+            rows_apart[:, None, None, None] == rows_apart[None, None, :, None],
+            picker.transpose(0, 2, 1)[:, :, None, :],
+            0,
+        ).reshape(local_cells, token_count).astype(BF16)
+        encoded, heads_low = feed_down(
+            where, active_low, middle, proj_biases[3:], choice, down_weights
+        )
         encoded_rows = encoded.reshape(row_count, ROW_LEN, D)
-        heads_low = (
-            jnp.take_along_axis(encoded_rows, starts[:, :, None], axis=1)
-            .reshape(local_cells, D)
-            .astype(BF16)
-        )
-        down_sums.add_first(heads_low)
-        heads_hop = grid.hop(heads_low, "x") if query_count == 2 else heads_low
-        one_b = grid.hop(down_sums.first_in[0], "y")
-        cell_heads = grid.joined(heads_low, tie(heads_hop, down_sums.first_in))
+        cell_heads = grid.share(heads_low)
         heads_half = lax.dynamic_slice_in_dim(cell_heads, place * half_width, half_width, 1)
-        cell_part = grid.total(dot(heads_half, dec_cell))
-        gene_part = added_wide(gene_mine, gene_got) + ff_biases[1]
-        before = cell_part[:, None, :] + gene_part.reshape(pair_cells, local_queries, FF)
-        gated_dec, gated_pull = jax.vjp(smooth_gate, before)
-        logit_weight = dec_out.astype(F32)
-        logits = jnp.sum(gated_dec * logit_weight, axis=-1)
-        logit_slope = jax.nn.sigmoid(logits) - labels.astype(F32)
-        (grad_before,) = gated_pull(logit_slope[:, :, None] * logit_weight)
-        before_low = grad_before.astype(BF16)
-        before_sums = jnp.sum(before_low, axis=1, dtype=F32)
-        grad_dec_bias = jnp.sum(before_sums, axis=0)
-        grad_logit = jnp.sum(gated_dec * logit_slope[:, :, None], axis=(0, 1))
+        cell_half = dot(heads_half, dec_cell)
+        cell_hop = grid.hop(cell_half, "x") if query_count == 2 else cell_half
+        before_low, before_sums, grad_logit = decode(
+            cell_half, cell_hop, gene_mine, gene_got, ff_biases[1][None, :], dec_out[None, :], labels
+        )
+        before_low = before_low.reshape(pair_cells, local_queries, FF)
         cell_total = grid.total(before_sums).astype(BF16)
         heads_part = dot_rt(cell_total, dec_cell).astype(BF16)
         heads_all = grid.share(heads_part, axis=1)
         heads_back = lax.dynamic_slice_in_dim(
             heads_all, place * local_cells, local_cells, 0
         ).astype(F32)
-        picker = (places[None, :, None] == starts[:, None, :]).astype(F32)
         grad_encoded = out_cotangent.astype(F32) + jnp.sum(
             picker[:, :, :, None] * heads_back.reshape(row_count, 1, CELLS_ROW, D), axis=2
         )
         grad_flat = grad_encoded.reshape(token_count, D)
         branch_low = grad_flat.astype(BF16)
-        branch_low, one_b, before_low = sync(branch_low, one_b, before_low)
+        branch_low, before_low = sync(branch_low, before_low)
         before_hop = grid.hop(before_low, "x") if query_count == 2 else before_low
-        one_a = grid.hop(down_sums.first_in[1], "y")
-        down_sums.one = [one_b, one_a]
-        down_sums.add_second()
-        down_sums.two = grid.hop(tie(down_sums.two_in, before_hop), "x")
+        gathered = lax.all_gather(
+            jnp.concatenate([cell_heads, cell_total], axis=1), "dp", axis=0, tiled=True
+        )
+        down_sums = Sums(grid)
+        down_sums.own, down_sums.sent = tall_terms(where, active_low, branch_low, grid.size["z"])
+        down_sums.own, down_sums.sent, before_hop = sync(down_sums.own, down_sums.sent, before_hop)
+        down_sums.core()
+        before_all = grid.joined(before_low, before_hop).reshape(query_count * pairs, FF)
+        before_mine, before_sent = grid.cut_half(before_all, "zb")
+        before_got = grid.hop(before_sent, "z")
         hidden_low, up_bias_sums, grad_second = feed_back(
-            where, tie(branch_low, before_low, down_sums.two_in, before_hop), slope, up_weights, down_weights
-        )
-        hidden_low, grad_second, one_a = sync(hidden_low, grad_second, one_a)
+            where, tie(branch_low, down_sums.sent, before_sent), slope, up_weights, down_weights
+        )
+        hidden_low, grad_second, before_got, down_sums.got = sync(
+            hidden_low, grad_second, before_got, down_sums.got
+        )
+        down_sums.add_first()
+        gene_wide = grid.joined_along(gene_rows, gene_pair, "zb")
+        before_wide = grid.joined_along(before_mine, before_got, "zb")
+        gene_left = grid.own_columns(gene_wide)
+        gene_half = before_wide.shape[1] // 2
+        core = grid.place("c")
+        gene_mine, gene_sent = [
+            dot_lt(
+                gene_left,
+                lax.dynamic_slice_in_dim(before_wide, at * gene_half, gene_half, 1),
+            ).astype(BF16)
+            for at in (core, 1 - core)
+        ]
+        *down_sums.parts, gene_sent, gene_mine = sync(*down_sums.parts, gene_sent, gene_mine)
+        one = down_sums.go_first(0)
+        gene_got = grid.hop(gene_sent, "c")
+        grad_middle, attn_low, mixed_back, grad_gain_two, grad_shift_two = attend_out_back(
+            tie(grad_second, down_sums.parts), middle, ln_gains[1], grad_flat, full_out
+        )
+        up_sums = Sums(grid)
+        up_sums.sent = weight_terms(where, False, (second_low, tie(hidden_low, mixed_back)))
+        up_sums.sent, one, gene_got, gathered = sync(up_sums.sent, one, gene_got, gathered)
+        one_more = down_sums.go_first(1)
+        down_sums.add_second(one)
+        up_sums.core()
+        two = down_sums.go_second()
+        up_sums.own = weight_terms(
+            where, True, (second_low, tie(hidden_low, up_sums.sent, down_sums.two_in))
+        )
+        (gene_sum,) = add_call([(gene_mine, ()), (tie(gene_got, up_sums.own), ())])
+        mixed_back, up_sums.own, up_sums.got, gene_sum = sync(
+            mixed_back, up_sums.own, up_sums.got, gene_sum
+        )
+        gene_sum = grid.scatter_high(gene_sum)
+        up_sums.add_first()
+        *up_sums.parts, mixed_back = sync(*up_sums.parts, mixed_back)
+        up_one, up_more = up_sums.go_first(0), up_sums.go_first(1)
+        qkv_back = attend_back(
+            qkv_rows,
+            segment,
+            mixed_rows,
+            mixed_back.reshape(row_count, ROW_LEN, D),
+            log_totals,
+        )
+        qkv_back, one_more, two = sync(qkv_back, one_more, two)
+        down_sums.add_last(one_more, two)
+        down_sums.last()
+        qkv_back_low = qkv_back.reshape(token_count, 3 * D)
+        attn_sums = Sums(grid)
+        attn_sums.sent = weight_terms(
+            where,
+            False,
+            (normed_low, tie(qkv_back_low, down_sums.last_in)),
+            (mixed_low, attn_low),
+        )
+        attn_sums.sent, qkv_back_low, up_one, gene_sum = sync(
+            attn_sums.sent, qkv_back_low, up_one, gene_sum
+        )
+        gene_sum = gene_sum.reshape(2, grid.size["y"], -1, gene_sum.shape[-1])
+        gene_mine, gene_sent = grid.cut_step(gene_sum, "y", 1)
+        up_sums.add_second(up_one, gene_sent)
+        up_two = up_sums.go_second()
+        attn_sums.core()
+        gene_got = grid.hop(gene_sent, "y")
+        attn_sums.own = weight_terms(
+            where, True, (normed_low, tie(qkv_back_low, up_sums.two_in)), (mixed_low, attn_low)
+        )
+        attn_sums.own, attn_sums.got = sync(attn_sums.own, attn_sums.got)
+        attn_sums.add_first()
+        attn_sums.parts = sync(*attn_sums.parts)
+        one, one_more = attn_sums.go_first(0), attn_sums.go_first(1)
+        grad_normed = project_back(where, tie(qkv_back_low, attn_sums.parts), qkv_weights)
+        grad_normed, up_more, up_two, gene_got, down_sums.sum = sync(
+            grad_normed, up_more, up_two, gene_got, down_sums.sum
+        )
+        up_sums.add_last(up_more, up_two)
+        up_sums.last()
+        grad_tokens, grad_gain_one, grad_shift_one = tokens_back(
+            tie(grad_normed, up_sums.last_in), row_tokens, ln_gains[0], grad_middle
+        )
+        gene_sum = added(tie(gene_mine, grad_tokens), gene_got).reshape(2, 2, -1, gene_mine.shape[-1])
+        genes_part = gather(tie(before_all, grad_tokens), dec_gene)
+        genes_part, gene_sum, one = sync(genes_part, gene_sum, one)
+        attn_sums.add_second(one)
+        two = attn_sums.go_second()
+
+        gene_sum, genes_part = tie((gene_sum, genes_part), attn_sums.two_in)
+        gene_sum = grid.trade(gene_sum, "c", 1, 2)
+        grad_tokens = grad_tokens.reshape(row_count, ROW_LEN, D)
+        choose = (
+            tie(ids, genes_part)[:, None] == jnp.arange(GENES, dtype=jnp.int32)[None, :]
+        ).astype(BF16)
+        table_terms = dot_lt(choose, genes_part).astype(BF16)
+        shape = [grid.size[axis] for axis in "zycx"]
+        table_terms = table_terms.reshape(*shape, -1, half_width)
+        table_mine, table_sent = grid.cut_step(table_terms, "c", 2)
+        table_sum = added(table_mine, grid.hop(table_sent, "c"))
+        late_ties = (qkv_back_low, attn_low, branch_low, up_bias_sums, before_sums)
+        qkv_late, attn_late, branch_late, up_bias_sums, sums_late = tie(late_ties, table_sent)
         grad_up_bias = up_bias_sums[0]
-        up_sums = Sums(grid, *weight_terms(where, (second_low, hidden_low)))
-        up_sums.sent, down_sums.two, one_a = sync(up_sums.sent, down_sums.two, one_a)
-        down_sums.one = [one_b, one_a]
-        up_sums.core()
-
-        middle_part, grad_gain_two, grad_shift_two = second_pull(tie(grad_second, up_sums.sent))
-        grad_middle = grad_flat + middle_part
-        attn_low = grad_middle.astype(BF16)
-        mixed_back = dot_rt(attn_low, full_out).astype(BF16)
-        before_all = grid.joined(before_low, tie(before_hop, mixed_back)).reshape(query_count * pairs, FF)
-        gene_terms = dot_lt(grid.own_columns(gene_rows), before_all).astype(BF16)
-        shape = [grid.size[axis] for axis in "zyc"]
-        gene_mine, gene_sent = grid.cut_columns(gene_terms)
-        up_sums.add_turned(gene_sent)
-        up_sums.one_in, gene_sent, mixed_back = sync(up_sums.one_in, gene_sent, mixed_back)
-        up_sums.go_turned()
-        gene_got = grid.hop(gene_sent, "c")
-        d_query, d_key, d_value = attend_back(
-            qkv_rows, segment, mixed_rows, mixed_back.reshape(row_count, ROW_LEN, D), log_totals
-        )
-        d_query, d_key, d_value, gene_got = sync(d_query, d_key, d_value, gene_got)
-        down_sums.add_last(d_query)
-        down_sums.last()
-        gene_sum = added(gene_mine, gene_got)
-        gene_sum = grid.scatter_z(tie(gene_sum.reshape(grid.size["z"], -1, gene_sum.shape[1]), down_sums.last_in))
-        qkv_back_low = jnp.concatenate([d_query, d_key, d_value], axis=2).reshape(token_count, 3 * D)
-        attn_sums = Sums(
-            grid,
-            *weight_terms(
-                where, (normed_low, tie(qkv_back_low, down_sums.last_in)), (mixed_low, attn_low)
-            ),
-        )
-        attn_sums.sent, qkv_back_low, *up_sums.one = sync(attn_sums.sent, qkv_back_low, *up_sums.one)
-        attn_sums.core()
-        up_sums.add_second(attn_sums.sent)
-        up_sums.two = grid.turn_hop(up_sums.two_in, 1)
-        grad_normed = dot_rt(tie(qkv_back_low, up_sums.two_in), full_qkv)
-        grad_normed, attn_sums.got = sync(grad_normed, attn_sums.got)
-        attn_sums.add_turned()
-        attn_sums.go_turned(up_sums.two)
-        bias_sums = jnp.sum(qkv_back_low, axis=0, dtype=F32)
-        token_part, grad_gain_one, grad_shift_one = first_pull(tie(grad_normed, attn_sums.one_in))
-        grad_tokens = (grad_middle + token_part).reshape(row_count, ROW_LEN, D)
-        grad_tokens, up_sums.two = sync(grad_tokens, up_sums.two)
-        up_sums.add_last()
-        up_sums.last()
-        grad_attn_bias = jnp.sum(attn_low, axis=0, dtype=F32)
-        grad_out_bias = jnp.sum(branch_low, axis=0, dtype=F32)
-
-        leading_low = tie(picker.astype(BF16).transpose(0, 2, 1), up_sums.last_in)
-        active_heads = jnp.einsum(
-            "rcl,rlf->rcf", leading_low, active_low.reshape(row_count, ROW_LEN, FF), preferred_element_type=F32
-        ).astype(BF16).reshape(local_cells, FF)
-        branch_heads = jnp.einsum(
-            "rcl,rld->rcd", leading_low, branch_low.reshape(row_count, ROW_LEN, D), preferred_element_type=F32
-        ).astype(BF16).reshape(local_cells, D)
-        late_low = jnp.concatenate([active_heads, branch_heads], axis=1)
-        genes_part = dot_rt(tie(before_all, up_sums.last_in), dec_gene).astype(BF16)
-        late_low, genes_part, *attn_sums.one = sync(late_low, genes_part, *attn_sums.one)
-        attn_sums.add_second()
-        attn_sums.two = grid.turn_hop(attn_sums.two_in, 1)
-        late_low, genes_part = tie((late_low, genes_part), attn_sums.two_in)
-        late = grid.share(late_low)
-        gathered = lax.all_gather(
-            jnp.concatenate([cell_heads, cell_total, late], axis=1), "dp", axis=0, tiled=True
-        )
-        genes_back = grid.share(genes_part, axis=1)
-        choose = (ids[:, None] == jnp.arange(GENES, dtype=jnp.int32)[None, :]).astype(BF16)
-        table_terms = dot_lt(grid.own_columns(choose), genes_back).astype(BF16)
-        table_terms = table_terms.reshape(*shape, -1, D)
-        table_terms = grid.scatter_step(table_terms, "c", 2, BF16)
-        table_terms = grid.scatter_step(table_terms, "y", 1, BF16)
-        attn_sums.two, table_terms = sync(attn_sums.two, table_terms)
-        attn_sums.add_last()
+        bias_sums = jnp.sum(qkv_late, axis=0, dtype=F32)
+        grad_attn_bias = jnp.sum(attn_late, axis=0, dtype=F32)
+        grad_out_bias = jnp.sum(branch_late, axis=0, dtype=F32)
+        grad_dec_bias = jnp.sum(sums_late, axis=0)
+        owners = dp_count * query_count
+
+        def owned_cols(values):
+            return values.reshape(-1, owners, values.shape[-1] // owners).transpose(1, 0, 2).reshape(owners, -1)
+
+        small = [
+            jnp.concatenate([grad_gain_one, grad_gain_two]),
+            jnp.concatenate([grad_shift_one, grad_shift_two]),
+            jnp.stack([bias_sums[:D], bias_sums[2 * D :], grad_attn_bias, grad_out_bias]),
+            jnp.stack([grad_up_bias, grad_dec_bias]),
+            grad_logit,
+        ]
+        flat = [owned_cols(value) for value in small]
+        sums = grid.scatter_step(grid.blocks(jnp.concatenate(flat, axis=1)), "c", 2, F32)
+        sums, table_sum, gene_sum, one_more, two, up_sums.sum = sync(
+            sums, table_sum, gene_sum, one_more, two, up_sums.sum
+        )
+        attn_sums.add_last(one_more, two)
         attn_sums.last()
-        grad_table = grid.scatter_z(tie(table_terms, attn_sums.last_in))[0].astype(F32)
-
-        gene_sum = tie(gene_sum, attn_sums.last_in).reshape(grid.size["y"], -1, gene_sum.shape[2])
-        gene_sum = grid.scatter_step(gene_sum, "y", 0, BF16)
-        grad_gene = grid.join_columns(gene_sum).astype(F32)
-        gathered = tie(gathered, attn_sums.last_in)
-        all_heads, all_cells, all_active, all_branch = jnp.split(
-            gathered, [D, D + FF, D + 2 * FF], axis=1
-        )
+
+        sums, table_sum, gene_sum = tie((sums, table_sum, gene_sum), attn_sums.last_in)
+        sums = grid.scatter_step(sums, "x", 2, F32)
+        table_sum = grid.scatter_step(table_sum, "y", 1, BF16)
+        grad_gene = grid.trade(gene_sum, "zb", 0, 1).astype(F32)
+        up_result, down_result = up_sums.result(attn_sums.last_in), down_sums.result(attn_sums.last_in)
+        sums, table_sum, grad_gene, up_result, down_result = sync(
+            sums, table_sum, grad_gene, up_result, down_result
+        )
+        sums = grid.scatter_step(sums, "y", 1, F32)
+        table_mine, table_sent = grid.cut_fold(table_sum, 1)
+        table_sum = added(table_mine, grid.hop(table_sent, "z", 1))
+        sums, table_sum = sync(sums, table_sum)
+        summed = grid.scatter_step(sums, "z", 0, F32).reshape(-1)
+        table_mine, table_sent = grid.cut_fold(table_sum, 2)
+        table_sum = added(table_mine, grid.hop(table_sent, "z", 2))[0]
+        grad_table = grid.trade(table_sum, "x", 0, 1).astype(F32)
+        all_heads, all_cells = jnp.split(tie(gathered, attn_sums.last_in), [D], axis=1)
         owned = D // (dp_count * query_count)
         mine = lax.axis_index("dp") * query_count + place
         grad_cell = dot_lt(
             lax.dynamic_slice_in_dim(all_heads, mine * owned, owned, 1), all_cells
         )
-        tall = FF // (dp_count * query_count)
-        late_down = dot_lt(
-            lax.dynamic_slice_in_dim(all_active, mine * tall, tall, 1), all_branch
-        )
-
-        owners = dp_count * query_count
-
-        def owned_cols(values):
-            return values.reshape(-1, owners, values.shape[-1] // owners).transpose(1, 0, 2).reshape(owners, -1)
-
-        small = [
-            jnp.stack([grad_gain_one, grad_gain_two]),
-            jnp.stack([grad_shift_one, grad_shift_two]),
-            jnp.stack([bias_sums[:D], bias_sums[2 * D :], grad_attn_bias, grad_out_bias]),
-            jnp.stack([grad_up_bias, grad_dec_bias]),
-            grad_logit[None, :],
-        ]
-        flat = [owned_cols(v) for v in small]
-        joined = jnp.concatenate(flat, axis=1)
-        summed = grid.scatter(grid.blocks(joined), "cxyz", F32).reshape(-1)
         outs = []
         start = 0
         for value, piece in zip(small, flat):
@@ -1076,8 +1469,8 @@
             outs[3],
             jnp.concatenate([half[:, :qkv_cut] for half in attn_sum], axis=1),
             jnp.concatenate([half[:, qkv_cut:] for half in attn_sum], axis=1),
-            jnp.concatenate(up_sums.result(attn_sums.last_in), axis=1),
-            jnp.concatenate(down_sums.result(attn_sums.last_in), axis=1) + late_down,
+            jnp.concatenate(up_result, axis=1),
+            jnp.concatenate(down_result, axis=1),
             grad_cell,
             grad_gene,
             outs[4][0],

time: 635 us -> 540 us (0.85)
  Pallas kernels: 159 us -> 245 us
  other arithmetic: 103 us -> 28 us
  waiting for transfers between devices: 195 us -> 124 us
  matrix products: 50.1 us -> 11.1 us
  starting transfers between devices: 46.3 us -> 58.2 us
    pallas_call x2 -> x22, Pallas kernels: 35.2 us -> 137 us  [the longest x10 40.2 us: add_call(): pl.pallas_call(lambda *refs: add_kernel(len(groups), *refs), grid=(steps,...]
    convert_element_type x11 -> x5, other arithmetic: 42 us -> 3.57 us  [added(): return total.astype(BF16)]
    ppermute x15 -> x13, waiting for transfers between devices: 54.6 us -> 19.6 us  [hop(): return lax.ppermute(value, 'query', pairs)]
    reduce_sum x9 -> x4, other arithmetic: 22.7 us -> 3.44 us  [the longest x1 2.97 us: shards(): bias_sums = jnp.sum(qkv_late, axis=0, dtype=F32)]
    dot_general x4 -> x1, matrix products: 20.7 us -> 4.64 us  [dot_rt(): lax.dot_general(left, right, (((1,), (1,)), ((), ())), preferred_element_...]
    dot_general x5 -> x2, matrix products: 17.9 us -> 2.11 us  [dot(): return jnp.dot(left, right, preferred_element_type=F32)]
    reduce_scatter x5 -> x3, waiting for transfers between devices: 20.1 us -> 6.69 us  [scatter_z(): lax.psum_scatter(value, 'dp', scatter_dimension=0, axis_index_groups=grou...]
    ppermute x4 -> x9, waiting for transfers between devices: 28.1 us -> 17.6 us  [turn_hop(): return lax.ppermute(value, ('dp', 'query'), pairs)]
  transfers between devices with their start and end apart: 61 -> 66, of which waited for: 27 -> 32; matrix products, arithmetic and copies ran while one was open for 26% -> 10% of each run, Pallas kernels for 25% -> 41%
where the time goes in v3:
time: 540 us; the launch traced here: 535 us
  Pallas kernels  245 us (45%)
  waiting for transfers between devices  124 us (23%)
  starting transfers between devices  58.2 us (11%)
  local copies, waits for them, and re-layouts  53.3 us (10%)
  other arithmetic  28 us (5%)
  between operations  15.6 us (3%)
  matrix products  11.1 us (2%)
    ppermute x39, waiting for transfers between devices, hop(): return lax.ppermute(value, 'dp', pairs)  80 us
    pallas_call x3, Pallas kernels, feed_call(): pl.pallas_call(kernel, grid_spec=pltpu.PrefetchScalarGridSpec(num_scalar_...  56.6 us
    pallas_call x10, Pallas kernels, add_call(): pl.pallas_call(lambda *refs: add_kernel(len(groups), *refs), grid=(steps,...  40.2 us
    pallas_call x4, Pallas kernels, weight_terms(): pl.pallas_call(lambda *refs: term_kernel(len(pairs), mine, units, *refs),...  38.1 us
    ppermute x39, starting transfers between devices, hop(): return lax.ppermute(value, 'dp', pairs)  34.3 us
    pallas_call x2, Pallas kernels, qkv_call(): pl.pallas_call(kernel, grid_spec=pltpu.PrefetchScalarGridSpec(num_scalar_...  23.5 us
    ppermute x13, waiting for transfers between devices, hop(): return lax.ppermute(value, 'query', pairs)  19.6 us
    pallas_call x1, Pallas kernels, attend_back(): pl.pallas_call(attend_back_kernel, grid=(rows, pairs), in_specs=[pl.Block...  18.8 us
  transfers between devices with their start and end apart: 66, of which 32 were waited for; matrix products, arithmetic and copies ran while one was open for 10% of the time, Pallas kernels for 41%

profile of v3, /device:TPU:0, one launch (start us, length us, event | category | flops | bytes accessed | tf_op | source)
XLA Modules:
  0.0 535.5 jit_solution(8089551567271372592)
XLA Ops:
  23.1 3.5 collective-permute-done.1
  32.6 10.4 %collective-permute-done.2 = bf16[80,3840]{1,0:T(8,128)(2,1)S(1)} collective-permute-done((bf16[80,3840]{1,0:T(8,128)(2,1)}, bf16[80,3840]{1,0:T(8,128)(2,1)S(1)}, u32[]{:S(2)}, u32[]{:S(2)}) %collective-permute-start.2) | collective-permute-done | bytes 614432 | tf_op jit(solution)/shard_map/ppermute | solution.py:911
  47.8 7.8 %collective-permute-done.4 = bf16[32,3840]{1,0:T(8,128)(2,1)S(1)} collective-permute-done((bf16[32,3840]{1,0:T(8,128)(2,1)S(1)}, bf16[32,3840]{1,0:T(8,128)(2,1)S(1)}, u32[]{:S(2)}, u32[]{:S(2)}) %collective-permute-start.4) | collective-permute-done | bytes 245792 | tf_op jit(solution)/shard_map/ppermute | solution.py:911
  64.9 11.4 %shard_map.272 = bf16[512,3840]{1,0:T(8,128)(2,1)} custom-call(s32[4]{0:T(128)} %pad_add_fusion.1.place.refs_0_, bf16[512,1280]{1,0:T(8,128)(2,1)} %fusion.5.normed.refs_1_, f32[1,3840]{1,0:T(1,128)} %broadcast_in_dim.23.bias, bf16[640,3840]{1,0:T(8,128)(2,1)} %refs_0_.9, bf16[240,3840]{1,0:T(8,128)(2,1)} %copy-done.10, bf16[80,3840]{1,0:T(8,128)(2,1)} %copy-done.14, ...), custom_call_target="tpu_custom_call" | custom-call | flops 1 | bytes 1 | tf_op jit(solution)/shard_map/pallas_call | solution.py:357
  76.3 13.3 %shard_map.273 = (bf16[1,512,1280]{2,1,0:T(8,128)(2,1)}, f32[1,5,4,512]{3,2,1,0:T(4,128)}) custom-call(s32[1,1,512]{2,1,0:T(1,128)} %bitcast.219, s32[1,512,1]{2,1,0:T(8,128)} %copy.42.segment_column, bf16[1,512,3840]{2,1,0:T(8,128)(2,1)} %bitcast.170, bf16[1,512,3840]{2,1,0:T(8,128)(2,1)} %bitcast.171, bf16[1,512,3840]{2,1,0:T(8,128)(2,1)} %bitcast.172), custom_call_target="tpu_custom_call" | custom-call | flops 1 | bytes 1 | tf_op jit(solution)/shard_map/pallas_call | solution.py:95
  99.7 5.3 shard_map.274
  107.7 4.7 collective-permute-done.14
  118.5 3.4 shard_map.275.weight
  123.6 6.1 %shard_map.276 = (f32[512,1280]{1,0:T(8,128)}, bf16[512,1280]{1,0:T(8,128)(2,1)}) custom-call(bf16[512,1280]{1,0:T(8,128)(2,1)} %bitcast.190, bf16[1280,1280]{1,0:T(8,128)(2,1)} %copy-done.3, bf16[512,1280]{1,0:T(8,128)(2,1)} %bitcast.186, f32[1,1280]{1,0:T(1,128)} %get-tuple-element.371.bias, f32[1,1280]{1,0:T(1,128)} %get-tuple-element.379.gain, ...), custom_call_target="tpu_custom_call" | custom-call | flops 1 | bytes 1 | tf_op jit(solution)/shard_map/pallas_call | solution.py:672
  129.7 5.4 %collective-permute-done.17 = bf16[320,1280]{1,0:T(8,128)(2,1)} collective-permute-done((bf16[320,1280]{1,0:T(8,128)(2,1)}, bf16[320,1280]{1,0:T(8,128)(2,1)}, u32[]{:S(2)}, u32[]{:S(2)}) %collective-permute-start.17) | collective-permute-done | bytes 819232 | tf_op jit(solution)/shard_map/ppermute | solution.py:911
  146.8 16.5 %shard_map.277 = (bf16[512,5120]{1,0:T(8,128)(2,1)}, bf16[512,5120]{1,0:T(8,128)(2,1)}) custom-call(s32[4]{0:T(128)} %pad_add_fusion.1.place.refs_0_, bf16[512,1280]{1,0:T(8,128)(2,1)} %get-tuple-element.215.second.refs_1_, f32[1,5120]{1,0:T(1,128)} %get-tuple-element.365.bias, bf16[640,5120]{1,0:T(8,128)(2,1)} %refs_0_.8, bf16[240,6400]{1,0:T(8,128)(2,1)} %copy-done.2, ...), custom_call_target="tpu_custom_call" | custom-call | flops 1 | bytes 1 | tf_op jit(solution)/shard_map/pallas_call | solution.py:414
  169.5 15.5 %shard_map.278 = (f32[512,1280]{1,0:T(8,128)}, bf16[4,1280]{1,0:T(4,128)(2,1)}) custom-call(s32[4]{0:T(128)} %pad_add_fusion.1.place.refs_0_, bf16[512,5120]{1,0:T(8,128)(2,1)} %get-tuple-element.219.active.left, f32[512,1280]{1,0:T(8,128)} %get-tuple-element.220.middle, f32[1,1280]{1,0:T(1,128)} %get-tuple-element.370.bias, bf16[4,512]{1,0:T(4,128)(2,1)} %fusion.34.picker, ...), custom_call_target="tpu_custom_call" | custom-call | flops 1 | bytes 1 | tf_op jit(solution)/shard_map/pallas_call | solution.py:414
  185.6 3.3 collective-permute-done.25
  192.6 3.4 collective-permute-done.26.other
  196.7 4.3 shard_map.279
  201.6 5.0 collective-permute-done.27
  207.5 4.6 convolution_convert_fusion.4
  212.8 3.0 collective-permute-done.28
  219.5 15.8 %shard_map.280 = (bf16[2,2,4,320,640]{4,3,2,1,0:T(8,128)(2,1)}, bf16[2,2,4,320,640]{4,3,2,1,0:T(8,128)(2,1)}) custom-call(s32[4]{0:T(128)} %pad_add_fusion.1.place.refs_0_, bf16[512,5120]{1,0:T(8,128)(2,1)} %get-tuple-element.219.active.left, bf16[512,1280]{1,0:T(8,128)(2,1)} %get-tuple-element.308.right.branch), custom_call_target="tpu_custom_call" | custom-call | flops 1 | bytes 1 | tf_op jit(solution)/shard_map/pallas_call | solution.py:597
  238.3 24.6 %shard_map.281 = (bf16[512,5120]{1,0:T(8,128)(2,1)}, f32[1,5120]{1,0:T(1,128)}, f32[512,1280]{1,0:T(8,128)}) custom-call(s32[4]{0:T(128)} %pad_add_fusion.1.place.refs_0_, bf16[512,1280]{1,0:T(8,128)(2,1)} %get-tuple-element.308.right.branch, bf16[512,5120]{1,0:T(8,128)(2,1)} %get-tuple-element.236.slope, bf16[640,5120]{1,0:T(8,128)(2,1)} %refs_0_.8, ...), custom_call_target="tpu_custom_call" | custom-call | flops 1 | bytes 1 | tf_op jit(solution)/shard_map/pallas_call | solution.py:414
  262.9 4.4 shard_map.282
  272.7 8.8 %shard_map.283 = (f32[512,1280]{1,0:T(8,128)}, bf16[512,1280]{1,0:T(8,128)(2,1)}, bf16[512,1280]{1,0:T(8,128)(2,1)}, f32[1,1280]{1,0:T(1,128)}, f32[1,1280]{1,0:T(1,128)}) custom-call(f32[512,1280]{1,0:T(8,128)} %get-tuple-element.248.grad, f32[512,1280]{1,0:T(8,128)} %get-tuple-element.220.middle, f32[1,1280]{1,0:T(1,128)} %get-tuple-element.379.gain, ...), custom_call_target="tpu_custom_call" | custom-call | flops 1 | bytes 1 | tf_op jit(solution)/shard_map/pallas_call | solution.py:783
  281.5 9.2 %shard_map.284 = bf16[2,2,320,2560]{3,2,1,0:T(8,128)(2,1)} custom-call(s32[4]{0:T(128)} %pad_add_fusion.1.place.refs_0_, bf16[512,1280]{1,0:T(8,128)(2,1)} %get-tuple-element.215.second.refs_1_, bf16[512,5120]{1,0:T(8,128)(2,1)} %get-tuple-element.255.refs_2_.refs_3_, bf16[512,5120]{1,0:T(8,128)(2,1)} %get-tuple-element.255.refs_2_.refs_3_), custom_call_target="tpu_custom_call" | custom-call | flops 1 | bytes 1 | tf_op jit(solution)/shard_map/pallas_call | solution.py:548
  292.4 4.2 shard_map.285
  296.6 9.4 %shard_map.286.refs_0_.refs_2_ = bf16[2,2,320,2560]{3,2,1,0:T(8,128)(2,1)} custom-call(s32[4]{0:T(128)} %pad_add_fusion.1.place.refs_0_, bf16[512,1280]{1,0:T(8,128)(2,1)} %get-tuple-element.215.second.refs_1_, bf16[512,5120]{1,0:T(8,128)(2,1)} %get-tuple-element.255.refs_2_.refs_3_, bf16[512,5120]{1,0:T(8,128)(2,1)} %get-tuple-element.255.refs_2_.refs_3_), custom_call_target="tpu_custom_call" | custom-call | flops 1 | bytes 1 | tf_op jit(solution)/shard_map/pallas_call | solution.py:548
  305.9 3.1 shard_map.287
  311.5 4.4 shard_map.288
  316.3 18.8 %shard_map.289 = bf16[1,512,3840]{2,1,0:T(8,128)(2,1)} custom-call(s32[1,1,512]{2,1,0:T(1,128)} %bitcast.220, s32[1,512,1]{2,1,0:T(8,128)} %copy.42.segment_column, bf16[1,512,3840]{2,1,0:T(8,128)(2,1)} %bitcast.173, bf16[1,512,3840]{2,1,0:T(8,128)(2,1)} %bitcast.174, bf16[1,512,3840]{2,1,0:T(8,128)(2,1)} %bitcast.175, ...), custom_call_target="tpu_custom_call" | custom-call | flops 1 | bytes 1 | tf_op jit(solution)/shard_map/pallas_call | solution.py:161
  335.0 12.2 %collective-permute-done.35.refs_2_ = bf16[1280,640]{1,0:T(8,128)(2,1)S(1)} collective-permute-done((bf16[1280,640]{1,0:T(8,128)(2,1)}, bf16[1280,640]{1,0:T(8,128)(2,1)S(1)}, u32[]{:S(2)}, u32[]{:S(2)}) %collective-permute-start.35) | collective-permute-done | bytes 1638432 | tf_op jit(solution)/shard_map/ppermute | solution.py:924
  350.8 4.2 shard_map.290
  355.0 9.8 %shard_map.291 = bf16[2,2,320,2560]{3,2,1,0:T(8,128)(2,1)} custom-call(s32[4]{0:T(128)} %pad_add_fusion.1.place.refs_0_, bf16[512,1280]{1,0:T(8,128)(2,1)} %fusion.5.normed.refs_1_, bf16[512,1280]{1,0:T(8,128)(2,1)} %bitcast.191, bf16[512,3840]{1,0:T(8,128)(2,1)} %bitcast.176, bf16[512,3840]{1,0:T(8,128)(2,1)} %bitcast.177, ...), custom_call_target="tpu_custom_call" | custom-call | flops 1 | bytes 1 | tf_op jit(solution)/shard_map/pallas_call | solution.py:548
  368.8 3.6 shard_map.292
  373.8 9.8 %shard_map.293.refs_0_.refs_2_ = bf16[2,2,320,2560]{3,2,1,0:T(8,128)(2,1)} custom-call(s32[4]{0:T(128)} %pad_add_fusion.1.place.refs_0_, bf16[512,1280]{1,0:T(8,128)(2,1)} %fusion.5.normed.refs_1_, bf16[512,1280]{1,0:T(8,128)(2,1)} %bitcast.192, bf16[512,3840]{1,0:T(8,128)(2,1)} %bitcast.178, bf16[512,3840]{1,0:T(8,128)(2,1)} %bitcast.179, ...), custom_call_target="tpu_custom_call" | custom-call | flops 1 | bytes 1 | tf_op jit(solution)/shard_map/pallas_call | solution.py:548
  383.6 4.4 shard_map.294
  392.1 12.1 %shard_map.295.grad = f32[512,1280]{1,0:T(8,128)} custom-call(s32[4]{0:T(128)} %pad_add_fusion.1.place.refs_0_, bf16[512,3840]{1,0:T(8,128)(2,1)} %bitcast.180, bf16[640,3840]{1,0:T(8,128)(2,1)} %refs_0_.9, bf16[240,3840]{1,0:T(8,128)(2,1)} %copy-done.10, bf16[80,3840]{1,0:T(8,128)(2,1)} %copy-done.14, bf16[240,3840]{1,0:T(8,128)(2,1)} %copy-done.12, ...), custom_call_target="tpu_custom_call" | custom-call | flops 1 | bytes 1 | tf_op jit(solution)/shard_map/pallas_call | solution.py:357
  404.2 16.0 %collective-permute-done.41 = bf16[2,80,1280]{2,1,0:T(8,128)(2,1)} collective-permute-done((bf16[2,80,1280]{2,1,0:T(8,128)(2,1)}, bf16[2,80,1280]{2,1,0:T(8,128)(2,1)}, u32[]{:S(2)}, u32[]{:S(2)}) %collective-permute-start.41) | collective-permute-done | bytes 409632 | tf_op jit(solution)/shard_map/ppermute | solution.py:911
  421.5 4.2 shard_map.296
  426.0 5.0 shard_map.297
  431.0 6.0 %shard_map.298 = bf16[128,640]{1,0:T(8,128)(2,1)} custom-call(bf16[128,5120]{1,0:T(8,128)(2,1)} %copy-done.7, bf16[640,5120]{1,0:T(8,128)(2,1)} %right.3), custom_call_target="tpu_custom_call" | custom-call | flops 1 | bytes 1 | tf_op jit(solution)/shard_map/pallas_call | solution.py:727
  438.7 3.6 shard_map.299
  445.2 10.1 %collective-permute-start.44 = (bf16[4,2,2,32,640]{4,3,2,1,0:T(8,128)(2,1)}, bf16[4,2,2,32,640]{4,3,2,1,0:T(8,128)(2,1)}, u32[]{:S(2)}, u32[]{:S(2)}) collective-permute-start(bf16[4,2,2,32,640]{4,3,2,1,0:T(8,128)(2,1)} %dynamic-slice_bitcast_fusion), channel_id=1, source_target_pairs={{0,2},{2,0},{4,6},{6,4},{8,10},{10,8},{12,14},{14,12},{16,18},{18,... | collective-permute-start | bytes 1966088 | tf_op jit(solution)/shard_map/ppermute | solution.py:911
  456.0 3.0 convert_reduce_fusion
  465.2 6.6 %reduce-scatter.9.cloned.1.call-done = bf16[1,80,2560]{2,1,0:T(8,128)(2,1)} async-done(((bf16[4,80,2560]{2,1,0:T(8,128)(2,1)}), bf16[1,80,2560]{2,1,0:T(8,128)(2,1)}) %reduce-scatter.9.cloned.1.call-update) | async-done | bytes 409616 | tf_op jit(solution)/shard_map/reduce_scatter | solution.py:1028
  471.9 4.2 shard_map.300
  483.0 7.0 %collective-permute-done.50 = bf16[40,2560]{1,0:T(8,128)(2,1)S(1)} collective-permute-done((bf16[40,2560]{1,0:T(8,128)(2,1)S(1)}, bf16[40,2560]{1,0:T(8,128)(2,1)S(1)}, u32[]{:S(2)}, u32[]{:S(2)}) %collective-permute-start.50) | collective-permute-done | bytes 204832 | tf_op jit(solution)/shard_map/ppermute | solution.py:911
  495.0 9.7 %collective-permute-done.54 = bf16[2,2,32,640]{3,2,1,0:T(8,128)(2,1)S(1)} collective-permute-done((bf16[2,2,32,640]{3,2,1,0:T(8,128)(2,1)S(1)}, bf16[2,2,32,640]{3,2,1,0:T(8,128)(2,1)S(1)}, u32[]{:S(2)}, u32[]{:S(2)}) %collective-permute-start.54) | collective-permute-done | bytes 163872 | tf_op jit(solution)/shard_map/ppermute | solution.py:911
  506.0 3.2 collective-permute-start.55
  512.0 7.3 %collective-permute-done.59 = bf16[1,2,32,640]{3,2,1,0:T(8,128)(2,1)S(1)} collective-permute-done((bf16[1,2,32,640]{3,2,1,0:T(8,128)(2,1)S(1)}, bf16[1,2,32,640]{3,2,1,0:T(8,128)(2,1)S(1)}, u32[]{:S(2)}, u32[]{:S(2)}) %collective-permute-start.59) | collective-permute-done | bytes 81952 | tf_op jit(solution)/shard_map/ppermute | solution.py:911
  (390 shorter events, 148.4 us)
Async XLA Ops:
  7.2 283.5 %all-gather.2.cloned.1.call-start = ((), (), s32[]{:S(2)}) async-start(), calls=%async_computation.4 | async-start | bytes 1740800 | tf_op jit(solution)/shard_map/all_gather | solution.py:1291
  9.5 18.3 %collective-permute-start = (bf16[80,3840]{1,0:T(8,128)(2,1)}, bf16[80,3840]{1,0:T(8,128)(2,1)}, u32[]{:S(2)}, u32[]{:S(2)}) collective-permute-start(bf16[80,3840]{1,0:T(8,128)(2,1)} %constant_dynamic-slice_fusion.10), channel_id=1, source_target_pairs={{0,1},{1,0},{2,3},{3,2},{4,5},{5,4},{6,7},{7,6},{8,9},{9,8},{10,11... | collective-permute-start | bytes 1843208 | tf_op jit(solution)/shard_map/ppermute | solution.py:905
  13.2 13.4 %collective-permute-start.1 = (s32[1,64]{1,0:T(1,128)S(1)}, s32[1,64]{1,0:T(1,128)S(1)}, u32[]{:S(2)}, u32[]{:S(2)}) collective-permute-start(s32[1,64]{1,0:T(1,128)S(1)} %reshape.331), channel_id=1, source_target_pairs={{0,1},{1,0},{2,3},{3,2},{4,5},{5,4},{6,7},{7,6},{8,9},{9,8},{10,11... | collective-permute-start | bytes 776 | tf_op jit(solution)/shard_map/ppermute | solution.py:905
  27.8 15.3 %collective-permute-start.2 = (bf16[80,3840]{1,0:T(8,128)(2,1)}, bf16[80,3840]{1,0:T(8,128)(2,1)S(1)}, u32[]{:S(2)}, u32[]{:S(2)}) collective-permute-start(bf16[80,3840]{1,0:T(8,128)(2,1)} %collective-permute-done), channel_id=1, source_target_pairs={{0,4},{2,6},{4,0},{6,2},{8,12},{10,14},{12,8},{14,10},{16,20},{18,... | collective-permute-start | bytes 1843208 | tf_op jit(solution)/shard_map/ppermute | solution.py:911
  29.6 14.6 %collective-permute-start.3 = (bf16[80,3840]{1,0:T(8,128)(2,1)}, bf16[80,3840]{1,0:T(8,128)(2,1)S(1)}, u32[]{:S(2)}, u32[]{:S(2)}) collective-permute-start(bf16[80,3840]{1,0:T(8,128)(2,1)} %collective-permute-done), channel_id=1, source_target_pairs={{0,8},{2,10},{4,12},{6,14},{8,0},{10,2},{12,4},{14,6},{16,24},{18,... | collective-permute-start | bytes 1843208 | tf_op jit(solution)/shard_map/ppermute | solution.py:911
  31.1 24.5 %collective-permute-start.6 = (bf16[80,6400]{1,0:T(8,128)(2,1)}, bf16[80,6400]{1,0:T(8,128)(2,1)}, u32[]{:S(2)}, u32[]{:S(2)}) collective-permute-start(bf16[80,6400]{1,0:T(8,128)(2,1)} %pad_maximum_fusion), channel_id=1, source_target_pairs={{0,1},{1,0},{2,3},{3,2},{4,5},{5,4},{6,7},{7,6},{8,9},{9,8},{10,11... | collective-permute-start | bytes 3072008 | tf_op jit(solution)/shard_map/ppermute | solution.py:905
  44.3 11.3 %collective-permute-start.5 = (bf16[48,3840]{1,0:T(8,128)(2,1)S(1)}, bf16[48,3840]{1,0:T(8,128)(2,1)S(1)}, u32[]{:S(2)}, u32[]{:S(2)}) collective-permute-start(bf16[48,3840]{1,0:T(8,128)(2,1)S(1)} %slice.113), channel_id=1, source_target_pairs={{0,8},{2,10},{4,12},{6,14},{8,0},{10,2},{12,4},{14,6},{16,24},{18,... | collective-permute-start | bytes 1105928 | tf_op jit(solution)/shard_map/ppermute | solution.py:911
  47.2 10.6 %collective-permute-start.8 = (bf16[240,3840]{1,0:T(8,128)(2,1)S(1)}, bf16[240,3840]{1,0:T(8,128)(2,1)S(1)}, u32[]{:S(2)}, u32[]{:S(2)}) collective-permute-start(bf16[240,3840]{1,0:T(8,128)(2,1)S(1)} %constant_dynamic-update-slice_fusion.refs_1_), channel_id=1, source_target_pairs={{0,2},{2,0},{4,6},{6,4},{8,10},{10,8},{12,14},{14,12},{16,18},{18,... | collective-permute-start | bytes 5529608 | tf_op jit(solution)/shard_map/ppermute | solution.py:911
  55.8 33.9 %collective-permute-start.9 = (bf16[80,6400]{1,0:T(8,128)(2,1)}, bf16[80,6400]{1,0:T(8,128)(2,1)S(1)}, u32[]{:S(2)}, u32[]{:S(2)}) collective-permute-start(bf16[80,6400]{1,0:T(8,128)(2,1)} %collective-permute-done.6), channel_id=1, source_target_pairs={{0,4},{2,6},{4,0},{6,2},{8,12},{10,14},{12,8},{14,10},{16,20},{18,... | collective-permute-start | bytes 3072008 | tf_op jit(solution)/shard_map/ppermute | solution.py:911
  56.3 33.3 %collective-permute-start.10 = (bf16[80,6400]{1,0:T(8,128)(2,1)}, bf16[80,6400]{1,0:T(8,128)(2,1)}, u32[]{:S(2)}, u32[]{:S(2)}) collective-permute-start(bf16[80,6400]{1,0:T(8,128)(2,1)} %collective-permute-done.6), channel_id=1, source_target_pairs={{0,8},{2,10},{4,12},{6,14},{8,0},{10,2},{12,4},{14,6},{16,24},{18,... | collective-permute-start | bytes 3072008 | tf_op jit(solution)/shard_map/ppermute | solution.py:911
  59.9 29.8 %collective-permute-start.11 = (bf16[320,1280]{1,0:T(8,128)(2,1)}, bf16[320,1280]{1,0:T(8,128)(2,1)}, u32[]{:S(2)}, u32[]{:S(2)}) collective-permute-start(bf16[320,1280]{1,0:T(8,128)(2,1)} %constant_dynamic-slice_fusion.7), channel_id=1, source_target_pairs={{0,1},{1,0},{2,3},{3,2},{4,5},{5,4},{6,7},{7,6},{8,9},{9,8},{10,11... | collective-permute-start | bytes 2457608 | tf_op jit(solution)/shard_map/ppermute | solution.py:905
  62.2 27.5 %collective-permute-start.12 = (bf16[128,1280]{1,0:T(8,128)(2,1)}, bf16[128,1280]{1,0:T(8,128)(2,1)}, u32[]{:S(2)}, u32[]{:S(2)}) collective-permute-start(bf16[128,1280]{1,0:T(8,128)(2,1)} %convolution_convert_fusion.2), channel_id=1, source_target_pairs={{0,1},{1,0},{2,3},{3,2},{4,5},{5,4},{6,7},{7,6},{8,9},{9,8},{10,11... | collective-permute-start | bytes 983048 | tf_op jit(solution)/shard_map/ppermute | solution.py:905
  95.5 16.9 %collective-permute-start.15 = (bf16[240,6400]{1,0:T(8,128)(2,1)S(1)}, bf16[240,6400]{1,0:T(8,128)(2,1)}, u32[]{:S(2)}, u32[]{:S(2)}) collective-permute-start(bf16[240,6400]{1,0:T(8,128)(2,1)S(1)} %constant_dynamic-update-slice_fusion.5.refs_2_.refs_1_), channel_id=1, source_target_pairs={{0,2},{2,0},{4,6},{6,4},{8,10},{10,8},{12,14},{14,12},{16,18},{18,... | collective-permute-start | bytes 9216008 | tf_op jit(solution)/shard_map/ppermute | solution.py:911
  95.6 12.1 %collective-permute-start.13 = (bf16[32,6400]{1,0:T(8,128)(2,1)}, bf16[32,6400]{1,0:T(8,128)(2,1)S(1)}, u32[]{:S(2)}, u32[]{:S(2)}) collective-permute-start(bf16[32,6400]{1,0:T(8,128)(2,1)} %slice.114), channel_id=1, source_target_pairs={{0,4},{2,6},{4,0},{6,2},{8,12},{10,14},{12,8},{14,10},{16,20},{18,... | collective-permute-start | bytes 1228808 | tf_op jit(solution)/shard_map/ppermute | solution.py:911
  96.3 16.1 %collective-permute-start.14 = (bf16[48,6400]{1,0:T(8,128)(2,1)}, bf16[48,6400]{1,0:T(8,128)(2,1)S(1)}, u32[]{:S(2)}, u32[]{:S(2)}) collective-permute-start(bf16[48,6400]{1,0:T(8,128)(2,1)} %slice.115), channel_id=1, source_target_pairs={{0,8},{2,10},{4,12},{6,14},{8,0},{10,2},{12,4},{14,6},{16,24},{18,... | collective-permute-start | bytes 1843208 | tf_op jit(solution)/shard_map/ppermute | solution.py:911
  114.1 21.0 %collective-permute-start.17 = (bf16[320,1280]{1,0:T(8,128)(2,1)}, bf16[320,1280]{1,0:T(8,128)(2,1)}, u32[]{:S(2)}, u32[]{:S(2)}) collective-permute-start(bf16[320,1280]{1,0:T(8,128)(2,1)} %collective-permute-done.11), channel_id=1, source_target_pairs={{0,4},{2,6},{4,0},{6,2},{8,12},{10,14},{12,8},{14,10},{16,20},{18,... | collective-permute-start | bytes 2457608 | tf_op jit(solution)/shard_map/ppermute | solution.py:911
  115.5 20.7 %collective-permute-start.18 = (bf16[320,1280]{1,0:T(8,128)(2,1)}, bf16[320,1280]{1,0:T(8,128)(2,1)}, u32[]{:S(2)}, u32[]{:S(2)}) collective-permute-start(bf16[320,1280]{1,0:T(8,128)(2,1)} %collective-permute-done.11), channel_id=1, source_target_pairs={{0,8},{2,10},{4,12},{6,14},{8,0},{10,2},{12,4},{14,6},{16,24},{18,... | collective-permute-start | bytes 2457608 | tf_op jit(solution)/shard_map/ppermute | solution.py:911
  142.0 21.4 %collective-permute-start.21 = (bf16[960,1280]{1,0:T(8,128)(2,1)S(1)}, bf16[960,1280]{1,0:T(8,128)(2,1)S(1)}, u32[]{:S(2)}, u32[]{:S(2)}) collective-permute-start(bf16[960,1280]{1,0:T(8,128)(2,1)S(1)} %constant_dynamic-update-slice_fusion.10.refs_1_.refs_6_), channel_id=1, source_target_pairs={{0,2},{2,0},{4,6},{6,4},{8,10},{10,8},{12,14},{14,12},{16,18},{18,... | collective-permute-start | bytes 7372808 | tf_op jit(solution)/shard_map/ppermute | solution.py:911
  142.1 21.3 %collective-permute-start.23 = (bf16[128,1280]{1,0:T(8,128)(2,1)S(1)}, bf16[128,1280]{1,0:T(8,128)(2,1)S(1)}, u32[]{:S(2)}, u32[]{:S(2)}) collective-permute-start(bf16[128,1280]{1,0:T(8,128)(2,1)S(1)} %add_convert_fusion.1), channel_id=1, source_target_pairs={{0,8},{2,10},{4,12},{6,14},{8,0},{10,2},{12,4},{14,6},{16,24},{18,... | collective-permute-start | bytes 983048 | tf_op jit(solution)/shard_map/ppermute | solution.py:911
  142.7 20.7 %collective-permute-start.22 = (bf16[64,5120]{1,0:T(8,128)(2,1)S(1)}, bf16[64,5120]{1,0:T(8,128)(2,1)S(1)}, u32[]{:S(2)}, u32[]{:S(2)}) collective-permute-start(bf16[64,5120]{1,0:T(8,128)(2,1)S(1)} %copy-done.34), channel_id=1, source_target_pairs={{0,1},{1,0},{2,3},{3,2},{4,5},{5,4},{6,7},{7,6},{8,9},{9,8},{10,11... | collective-permute-start | bytes 1966088 | tf_op jit(solution)/shard_map/ppermute | solution.py:905
  144.3 19.1 %collective-permute-start.19 = (bf16[160,1280]{1,0:T(8,128)(2,1)S(1)}, bf16[160,1280]{1,0:T(8,128)(2,1)S(1)}, u32[]{:S(2)}, u32[]{:S(2)}) collective-permute-start(bf16[160,1280]{1,0:T(8,128)(2,1)S(1)} %slice.119), channel_id=1, source_target_pairs={{0,4},{2,6},{4,0},{6,2},{8,12},{10,14},{12,8},{14,10},{16,20},{18,... | collective-permute-start | bytes 1228808 | tf_op jit(solution)/shard_map/ppermute | solution.py:911
  145.7 17.7 %collective-permute-start.20 = (bf16[160,1280]{1,0:T(8,128)(2,1)S(1)}, bf16[160,1280]{1,0:T(8,128)(2,1)}, u32[]{:S(2)}, u32[]{:S(2)}) collective-permute-start(bf16[160,1280]{1,0:T(8,128)(2,1)S(1)} %slice.120), channel_id=1, source_target_pairs={{0,8},{2,10},{4,12},{6,14},{8,0},{10,2},{12,4},{14,6},{16,24},{18,... | collective-permute-start | bytes 1228808 | tf_op jit(solution)/shard_map/ppermute | solution.py:911
  218.9 16.4 %collective-permute-start.29 = (bf16[8,8,5120]{2,1,0:T(8,128)(2,1)S(1)}, bf16[8,8,5120]{2,1,0:T(8,128)(2,1)S(1)}, u32[]{:S(2)}, u32[]{:S(2)}) collective-permute-start(bf16[8,8,5120]{2,1,0:T(8,128)(2,1)S(1)} %bitcast.208), channel_id=1, source_target_pairs={{0,1},{1,0},{2,3},{3,2},{4,5},{5,4},{6,7},{7,6},{8,9},{9,8},{10,11... | collective-permute-start | bytes 1966088 | tf_op jit(solution)/shard_map/ppermute | solution.py:905
  235.3 27.6 %collective-permute-start.31 = (bf16[2,2,1280,640]{3,2,1,0:T(8,128)(2,1)}, bf16[2,2,1280,640]{3,2,1,0:T(8,128)(2,1)}, u32[]{:S(2)}, u32[]{:S(2)}) collective-permute-start(bf16[2,2,1280,640]{3,2,1,0:T(8,128)(2,1)} %bitcast.224), channel_id=1, source_target_pairs={{0,2},{2,0},{4,6},{6,4},{8,10},{10,8},{12,14},{14,12},{16,18},{18,... | collective-permute-start | bytes 19660808 | tf_op jit(solution)/shard_map/ppermute | solution.py:911
  235.7 27.2 %collective-permute-start.30 = (bf16[128,2560]{1,0:T(8,128)(2,1)S(1)}, bf16[128,2560]{1,0:T(8,128)(2,1)}, u32[]{:S(2)}, u32[]{:S(2)}) collective-permute-start(bf16[128,2560]{1,0:T(8,128)(2,1)S(1)} %broadcast_select_fusion.5), channel_id=1, source_target_pairs={{0,8},{2,10},{4,12},{6,14},{8,0},{10,2},{12,4},{14,6},{16,24},{18,... | collective-permute-start | bytes 1966088 | tf_op jit(solution)/shard_map/ppermute | solution.py:911
  238.0 126.9 %reduce-scatter.5.cloned.1.call-start = ((), (), s32[]{:S(2)}) async-start(), calls=%async_computation.5 | async-start | bytes 2457600 | tf_op jit(solution)/shard_map/reduce_scatter | solution.py:1039
  271.0 21.4 %collective-permute-start.32 = (bf16[1280,640]{1,0:T(8,128)(2,1)}, bf16[1280,640]{1,0:T(8,128)(2,1)}, u32[]{:S(2)}, u32[]{:S(2)}) collective-permute-start(bf16[1280,640]{1,0:T(8,128)(2,1)} %get-tuple-element.246), channel_id=1, source_target_pairs={{0,1},{1,0},{2,6},{3,7},{4,5},{5,4},{6,2},{7,3},{8,9},{9,8},{10,14... | collective-permute-start | bytes 4915208 | tf_op jit(solution)/shard_map/ppermute | solution.py:924
  272.7 19.7 %collective-permute-start.33 = (bf16[640,1280]{1,0:T(8,128)(2,1)S(1)}, bf16[640,1280]{1,0:T(8,128)(2,1)S(1)}, u32[]{:S(2)}, u32[]{:S(2)}) collective-permute-start(bf16[640,1280]{1,0:T(8,128)(2,1)S(1)} %convolution_convert_fusion.1), channel_id=1, source_target_pairs={{0,2},{2,0},{4,6},{6,4},{8,10},{10,8},{12,14},{14,12},{16,18},{18,... | collective-permute-start | bytes 4915208 | tf_op jit(solution)/shard_map/ppermute | solution.py:911
  292.4 16.6 %collective-permute-start.34 = (bf16[2,2,320,2560]{3,2,1,0:T(8,128)(2,1)}, bf16[2,2,320,2560]{3,2,1,0:T(8,128)(2,1)}, u32[]{:S(2)}, u32[]{:S(2)}) collective-permute-start(bf16[2,2,320,2560]{3,2,1,0:T(8,128)(2,1)} %shard_map.284), channel_id=1, source_target_pairs={{0,2},{2,0},{4,6},{6,4},{8,10},{10,8},{12,14},{14,12},{16,18},{18,... | collective-permute-start | bytes 19660808 | tf_op jit(solution)/shard_map/ppermute | solution.py:911
  309.1 95.1 %reduce-scatter.7.cloned.1.call-start = ((), (), s32[]{:S(2)}) async-start(), calls=%async_computation.6 | async-start | bytes 2048000 | tf_op jit(solution)/shard_map/reduce_scatter | solution.py:1028
  309.1 38.1 %collective-permute-start.35 = (bf16[1280,640]{1,0:T(8,128)(2,1)}, bf16[1280,640]{1,0:T(8,128)(2,1)S(1)}, u32[]{:S(2)}, u32[]{:S(2)}) collective-permute-start(bf16[1280,640]{1,0:T(8,128)(2,1)} %get-tuple-element.247), channel_id=1, source_target_pairs={{0,1},{1,0},{2,6},{3,7},{4,5},{5,4},{6,2},{7,3},{8,9},{9,8},{10,14... | collective-permute-start | bytes 4915208 | tf_op jit(solution)/shard_map/ppermute | solution.py:924
  310.9 38.7 %collective-permute-start.36 = (bf16[1280,640]{1,0:T(8,128)(2,1)S(1)}, bf16[1280,640]{1,0:T(8,128)(2,1)S(1)}, u32[]{:S(2)}, u32[]{:S(2)}) collective-permute-start(bf16[1280,640]{1,0:T(8,128)(2,1)S(1)} %copy-done.29), channel_id=1, source_target_pairs={{0,4},{1,5},{2,3},{3,2},{4,0},{5,1},{6,7},{7,6},{8,12},{9,13},{10,... | collective-permute-start | bytes 4915208 | tf_op jit(solution)/shard_map/ppermute | solution.py:924
  315.9 48.9 %collective-permute-start.37 = (bf16[320,2560]{1,0:T(8,128)(2,1)}, bf16[320,2560]{1,0:T(8,128)(2,1)S(1)}, u32[]{:S(2)}, u32[]{:S(2)}) collective-permute-start(bf16[320,2560]{1,0:T(8,128)(2,1)} %get-tuple-element.271), channel_id=1, source_target_pairs={{0,1},{1,0},{2,6},{3,7},{4,5},{5,4},{6,2},{7,3},{8,9},{9,8},{10,14... | collective-permute-start | bytes 4915208 | tf_op jit(solution)/shard_map/ppermute | solution.py:924
  364.8 18.8 %collective-permute-start.38 = (bf16[2,2,320,2560]{3,2,1,0:T(8,128)(2,1)}, bf16[2,2,320,2560]{3,2,1,0:T(8,128)(2,1)}, u32[]{:S(2)}, u32[]{:S(2)}) collective-permute-start(bf16[2,2,320,2560]{3,2,1,0:T(8,128)(2,1)} %shard_map.291), channel_id=1, source_target_pairs={{0,2},{2,0},{4,6},{6,4},{8,10},{10,8},{12,14},{14,12},{16,18},{18,... | collective-permute-start | bytes 19660808 | tf_op jit(solution)/shard_map/ppermute | solution.py:911
  364.9 106.9 %reduce-scatter.9.cloned.1.call-start = ((), (), s32[]{:S(2)}) async-start(), calls=%async_computation.7 | async-start | bytes 2048000 | tf_op jit(solution)/shard_map/reduce_scatter | solution.py:1028
  365.2 39.0 %collective-permute-start.39 = (bf16[320,2560]{1,0:T(8,128)(2,1)}, bf16[320,2560]{1,0:T(8,128)(2,1)S(1)}, u32[]{:S(2)}, u32[]{:S(2)}) collective-permute-start(bf16[320,2560]{1,0:T(8,128)(2,1)} %get-tuple-element.286), channel_id=1, source_target_pairs={{0,1},{1,0},{2,6},{3,7},{4,5},{5,4},{6,2},{7,3},{8,9},{9,8},{10,14... | collective-permute-start | bytes 4915208 | tf_op jit(solution)/shard_map/ppermute | solution.py:924
  372.4 47.8 %collective-permute-start.40 = (bf16[320,2560]{1,0:T(8,128)(2,1)}, bf16[320,2560]{1,0:T(8,128)(2,1)S(1)}, u32[]{:S(2)}, u32[]{:S(2)}) collective-permute-start(bf16[320,2560]{1,0:T(8,128)(2,1)} %shard_map.292), channel_id=1, source_target_pairs={{0,4},{1,5},{2,3},{3,2},{4,0},{5,1},{6,7},{7,6},{8,12},{9,13},{10,... | collective-permute-start | bytes 4915208 | tf_op jit(solution)/shard_map/ppermute | solution.py:924
  388.0 50.6 %collective-permute-start.42 = (bf16[320,2560]{1,0:T(8,128)(2,1)}, bf16[320,2560]{1,0:T(8,128)(2,1)}, u32[]{:S(2)}, u32[]{:S(2)}) collective-permute-start(bf16[320,2560]{1,0:T(8,128)(2,1)} %get-tuple-element.283), channel_id=1, source_target_pairs={{0,1},{1,0},{2,6},{3,7},{4,5},{5,4},{6,2},{7,3},{8,9},{9,8},{10,14... | collective-permute-start | bytes 4915208 | tf_op jit(solution)/shard_map/ppermute | solution.py:924
  388.3 31.9 %collective-permute-start.41 = (bf16[2,80,1280]{2,1,0:T(8,128)(2,1)}, bf16[2,80,1280]{2,1,0:T(8,128)(2,1)}, u32[]{:S(2)}, u32[]{:S(2)}) collective-permute-start(bf16[2,80,1280]{2,1,0:T(8,128)(2,1)} %get-tuple-element.349), channel_id=1, source_target_pairs={{0,4},{2,6},{4,0},{6,2},{8,12},{10,14},{12,8},{14,10},{16,20},{18,... | collective-permute-start | bytes 1228808 | tf_op jit(solution)/shard_map/ppermute | solution.py:911
  390.5 73.5 %collective-permute-start.46 = (bf16[320,2560]{1,0:T(8,128)(2,1)}, bf16[320,2560]{1,0:T(8,128)(2,1)}, u32[]{:S(2)}, u32[]{:S(2)}) collective-permute-start(bf16[320,2560]{1,0:T(8,128)(2,1)} %get-tuple-element.284), channel_id=1, source_target_pairs={{0,1},{1,0},{2,6},{3,7},{4,5},{5,4},{6,2},{7,3},{8,9},{9,8},{10,14... | collective-permute-start | bytes 4915208 | tf_op jit(solution)/shard_map/ppermute | solution.py:924
  425.7 97.8 %reduce-scatter.11.cloned.1.call-start = ((), (), s32[]{:S(2)}) async-start(), calls=%async_computation.8 | async-start | bytes 2048000 | tf_op jit(solution)/shard_map/reduce_scatter | solution.py:1028
  442.3 23.0 %collective-permute-start.47 = (bf16[320,2560]{1,0:T(8,128)(2,1)}, bf16[320,2560]{1,0:T(8,128)(2,1)}, u32[]{:S(2)}, u32[]{:S(2)}) collective-permute-start(bf16[320,2560]{1,0:T(8,128)(2,1)} %shard_map.299), channel_id=1, source_target_pairs={{0,4},{1,5},{2,3},{3,2},{4,0},{5,1},{6,7},{7,6},{8,12},{9,13},{10,... | collective-permute-start | bytes 4915208 | tf_op jit(solution)/shard_map/ppermute | solution.py:924
  445.2 17.4 %collective-permute-start.44 = (bf16[4,2,2,32,640]{4,3,2,1,0:T(8,128)(2,1)}, bf16[4,2,2,32,640]{4,3,2,1,0:T(8,128)(2,1)}, u32[]{:S(2)}, u32[]{:S(2)}) collective-permute-start(bf16[4,2,2,32,640]{4,3,2,1,0:T(8,128)(2,1)} %dynamic-slice_bitcast_fusion), channel_id=1, source_target_pairs={{0,2},{2,0},{4,6},{6,4},{8,10},{10,8},{12,14},{14,12},{16,18},{18,... | collective-permute-start | bytes 1966088 | tf_op jit(solution)/shard_map/ppermute | solution.py:911
  477.7 13.3 %collective-permute-start.49 = (bf16[4,2,32,640]{3,2,1,0:T(8,128)(2,1)S(1)}, bf16[4,2,32,640]{3,2,1,0:T(8,128)(2,1)S(1)}, u32[]{:S(2)}, u32[]{:S(2)}) collective-permute-start(bf16[4,2,32,640]{3,2,1,0:T(8,128)(2,1)S(1)} %dynamic-slice_bitcast_fusion.5), channel_id=1, source_target_pairs={{0,4},{2,6},{4,0},{6,2},{8,12},{10,14},{12,8},{14,10},{16,20},{18,... | collective-permute-start | bytes 983048 | tf_op jit(solution)/shard_map/ppermute | solution.py:911
  479.3 10.7 %collective-permute-start.50 = (bf16[40,2560]{1,0:T(8,128)(2,1)S(1)}, bf16[40,2560]{1,0:T(8,128)(2,1)S(1)}, u32[]{:S(2)}, u32[]{:S(2)}) collective-permute-start(bf16[40,2560]{1,0:T(8,128)(2,1)S(1)} %dynamic-slice_bitcast_fusion.9), channel_id=1, source_target_pairs={{0,8},{2,10},{4,12},{6,14},{8,0},{10,2},{12,4},{14,6},{16,24},{18,... | collective-permute-start | bytes 614408 | tf_op jit(solution)/shard_map/ppermute | solution.py:911
  481.0 10.0 %collective-permute-start.52 = (bf16[160,640]{1,0:T(8,128)(2,1)S(1)}, bf16[160,640]{1,0:T(8,128)(2,1)S(1)}, u32[]{:S(2)}, u32[]{:S(2)}) collective-permute-start(bf16[160,640]{1,0:T(8,128)(2,1)S(1)} %dynamic-slice_bitcast_fusion.7), channel_id=1, source_target_pairs={{0,2},{2,0},{4,6},{6,4},{8,10},{10,8},{12,14},{14,12},{16,18},{18,... | collective-permute-start | bytes 614408 | tf_op jit(solution)/shard_map/ppermute | solution.py:911
  491.3 13.3 %collective-permute-start.54 = (bf16[2,2,32,640]{3,2,1,0:T(8,128)(2,1)S(1)}, bf16[2,2,32,640]{3,2,1,0:T(8,128)(2,1)S(1)}, u32[]{:S(2)}, u32[]{:S(2)}) collective-permute-start(bf16[2,2,32,640]{3,2,1,0:T(8,128)(2,1)S(1)} %dynamic-slice_bitcast_fusion.11), channel_id=1, source_target_pairs={{0,8},{2,10},{4,12},{6,14},{8,0},{10,2},{12,4},{14,6},{16,24},{18,... | collective-permute-start | bytes 491528 | tf_op jit(solution)/shard_map/ppermute | solution.py:911
  509.1 10.1 %collective-permute-start.59 = (bf16[1,2,32,640]{3,2,1,0:T(8,128)(2,1)S(1)}, bf16[1,2,32,640]{3,2,1,0:T(8,128)(2,1)S(1)}, u32[]{:S(2)}, u32[]{:S(2)}) collective-permute-start(bf16[1,2,32,640]{3,2,1,0:T(8,128)(2,1)S(1)} %constant_dynamic-slice_fusion), channel_id=1, source_target_pairs={{0,16},{2,18},{4,20},{6,22},{8,24},{10,26},{12,28},{14,30},{16,0},... | collective-permute-start | bytes 245768 | tf_op jit(solution)/shard_map/ppermute | solution.py:911
  (77 other events, 547.8 us)
Sparse Core Ops, SparseCore 0:
  238.1 41.0 all-gather.1
  309.2 45.6 reduce-scatter.4
  365.1 36.5 reduce-scatter.6
  425.8 46.0 reduce-scatter.8
  476.3 43.9 reduce-scatter.10

commit v4 on v3

--- a/solution.py
+++ b/solution.py
@@ -183,10 +183,26 @@
 HALF_CHUNK = 640
 
 
+def unit_places(outer, inner, core):
+    mine = (outer ^ core, inner ^ (1 - core))
+    theirs = (outer ^ (1 - core), inner ^ core)
+    corner = (outer ^ 1, inner ^ 1)
+    return [
+        (outer, inner, core),
+        (outer, inner, 1 - core),
+        (*mine, core),
+        (*mine, 1 - core),
+        (*corner, core),
+        (*theirs, 1 - core),
+        (*theirs, core),
+        (*corner, 1 - core),
+    ]
+
+
 def part_copies(sources, columns, place, buffer, sems, half_rows, act):
-    shard, *parts = sources
+    shard, *units = sources
     query, outer, inner, core = (place[i] for i in range(4))
-    unit = parts[1].shape[0]
+    size = units[0].shape[0]
     act(
         pltpu.make_async_copy(
             shard.at[:, columns],
@@ -194,19 +210,15 @@
             sems.at[0],
         )
     )
-    for side in range(2):
-        c = core if side == 0 else 1 - core
-        for part in range(4):
-            zb, y = outer ^ (part // 2), inner ^ (part % 2)
-            row = (1 - query) * half_rows + ((zb * 2 + y) * 2 + c) * unit
-            source = parts[2 * side + part // 3]
-            act(
-                pltpu.make_async_copy(
-                    source.at[pl.ds(part % 3 * unit, unit), columns],
-                    buffer.at[pl.ds(pl.multiple_of(row, 16), unit), :],
-                    sems.at[1 + side * 4 + part],
-                )
+    for i, (unit, (zb, y, c)) in enumerate(zip(units, unit_places(outer, inner, core))):
+        row = (1 - query) * half_rows + ((zb * 2 + y) * 2 + c) * size
+        act(
+            pltpu.make_async_copy(
+                unit.at[:, columns],
+                buffer.at[pl.ds(pl.multiple_of(row, 16), size), :],
+                sems.at[1 + i],
             )
+        )
 
 
 def chunk_place(step, place, half):
@@ -223,14 +235,12 @@
 
 
 def down_copies(sources, place, step, buffer, sems, act):
-    shard, *parts = sources
+    shard, *units = sources
     query, outer, inner, core = (place[i] for i in range(4))
-    unit = parts[1].shape[0]
-    fold = shard.shape[0] // (8 * unit)
+    size = units[0].shape[0]
     steps = shard.shape[0] // CHUNK
     own = step < steps
     local = jnp.where(own, step, step - steps)
-    size = 2 * fold * unit
 
     @pl.when(own)
     def _():
@@ -240,25 +250,16 @@
             )
         )
 
-    for piece in range(CHUNK // size):
-        at = local * (CHUNK // size) + piece
-        part = ((at // 2) ^ outer) * 2 + ((at % 2) ^ inner)
-        for corner in range(2):
-
-            @pl.when(jnp.logical_and(jnp.logical_not(own), (part == 3) == (corner == 1)))
+    for piece in range(CHUNK // (2 * size)):
+        at = local * (CHUNK // (2 * size)) + piece
+        for i, (unit, (zb, y, c)) in enumerate(zip(units, unit_places(outer, inner, core))):
+
+            @pl.when(jnp.logical_and(jnp.logical_not(own), at == zb * 2 + y))
             def _():
-                row = 0 if corner else pl.multiple_of(part * unit, 16)
-                for side in range(2):
-                    c = core if side == 0 else 1 - core
-                    for k in range(fold):
-                        start = pl.multiple_of(piece * size + (c * fold + k) * unit, 16)
-                        act(
-                            pltpu.make_async_copy(
-                                parts[2 * side + corner].at[pl.ds(row, unit), pl.ds(k * D, D)],
-                                buffer.at[pl.ds(start, unit), :],
-                                sems.at[1 + (piece * 2 + side) * fold + k],
-                            )
-                        )
+                row = pl.multiple_of((piece * 2 + c) * size, 16)
+                act(
+                    pltpu.make_async_copy(unit, buffer.at[pl.ds(row, size), :], sems.at[1 + i])
+                )
 
 
 def stream(copies, buffer, sems):
@@ -284,7 +285,7 @@
 
 
 def up_kernel(place, second, bias, *refs):
-    sources, (active, slope, buffer, sems) = refs[:5], refs[5:]
+    sources, (active, slope, buffer, sems) = refs[:9], refs[9:]
     weights = stream(lambda *at: up_copies(sources, place, *at), buffer, sems)
     value, rise = gate(dot(second[...], weights[...]) + bias[...])
     active[...] = value.astype(BF16)
@@ -292,7 +293,7 @@
 
 
 def down_kernel(place, active, middle, bias, picker, *refs):
-    sources, (out, heads, buffer, sems) = refs[:5], refs[5:]
+    sources, (out, heads, buffer, sems) = refs[:9], refs[9:]
     weights = stream(lambda *at: down_copies(sources, place, *at), buffer, sems)
 
     @pl.when(pl.program_id(0) == 0)
@@ -307,8 +308,8 @@
 
 
 def back_kernel(place, branch, slope, *refs):
-    up, down = refs[:5], refs[5:10]
-    d_hidden, sums, out, buffer, sems, buffer_two, sems_two = refs[10:]
+    up, down = refs[:9], refs[9:18]
+    d_hidden, sums, out, buffer, sems, buffer_two, sems_two = refs[18:]
     up_part = stream(lambda *at: up_copies(up, place, *at), buffer, sems)
     down_part = stream(lambda *at: down_copies(down, place, *at), buffer_two, sems_two)
 
@@ -324,7 +325,7 @@
 
 
 def qkv_kernel(place, normed, bias, *refs):
-    sources, (out, buffer, sems) = refs[:5], refs[5:]
+    sources, (out, buffer, sems) = refs[:9], refs[9:]
 
     def copies(step, *at):
         columns = pl.ds(pl.multiple_of(step * CHUNK, 128), CHUNK)
@@ -335,7 +336,7 @@
 
 
 def qkv_back_kernel(place, back, *refs):
-    sources, (out, buffer, sems) = refs[:5], refs[5:]
+    sources, (out, buffer, sems) = refs[:9], refs[9:]
 
     def copies(step, *at):
         columns = pl.ds(pl.multiple_of(step * CHUNK, 128), CHUNK)
@@ -359,7 +360,7 @@
         grid_spec=pltpu.PrefetchScalarGridSpec(
             num_scalar_prefetch=1,
             grid=(columns // CHUNK,),
-            in_specs=specs + [pl.BlockSpec(memory_space=pl.ANY)] * 5,
+            in_specs=specs + [pl.BlockSpec(memory_space=pl.ANY)] * 9,
             out_specs=out_spec,
             scratch_shapes=[pltpu.VMEM((2, D, CHUNK), BF16), pltpu.SemaphoreType.DMA((2, 9))],
         ),
@@ -410,7 +411,7 @@
         shapes[name] = jax.ShapeDtypeStruct(block, BF16)
     scratch = []
     for slot in slots:
-        scratch += [pltpu.VMEM((2, *slot), BF16), pltpu.SemaphoreType.DMA((2, 17))]
+        scratch += [pltpu.VMEM((2, *slot), BF16), pltpu.SemaphoreType.DMA((2, 9))]
     return pl.pallas_call(
         kernel,
         grid_spec=pltpu.PrefetchScalarGridSpec(
@@ -430,14 +431,14 @@
 
 
 def feed_up(place, second, bias, up):
-    names = ["whole", "row"] + ["any"] * 5
+    names = ["whole", "row"] + ["any"] * 9
     return feed_call(
         up_kernel, second.shape[0], names, ["hidden", "hidden"], [UP_SLOT], place, second, bias, *up
     )
 
 
 def feed_down(place, active, middle, bias, picker, down):
-    names = ["hidden", "whole", "vector", "picker"] + ["any"] * 5
+    names = ["hidden", "whole", "vector", "picker"] + ["any"] * 9
     heads = jax.ShapeDtypeStruct((picker.shape[0], D), BF16)
     return feed_call(
         down_kernel, active.shape[0], names, ["whole", "heads"], [DOWN_SLOT],
@@ -446,7 +447,7 @@
 
 
 def feed_back(place, branch, slope, up, down):
-    names = ["whole", "hidden"] + ["any"] * 10
+    names = ["whole", "hidden"] + ["any"] * 18
     return feed_call(
         back_kernel, branch.shape[0], names, ["hidden", "row", "whole"], [UP_SLOT, DOWN_SLOT],
         place, branch, slope, *up, *down,
@@ -457,14 +458,14 @@
     cells = mine.shape[0]
     shape = (cells, gene.shape[0] // cells, gene.shape[1])
     parts = (gene[...].astype(F32) + got[...].astype(F32) + bias[...]).reshape(shape)
-    before = (mine[...] + other[...])[:, None, :] + parts
+    before = (mine[...].astype(F32) + other[...].astype(F32))[:, None, :] + parts
     value, rise = gate(before)
     row = weight[...].astype(F32)[None]
     logits = jnp.sum(value * row, axis=2, keepdims=True)
     slope = jax.nn.sigmoid(logits) - labels[...].astype(F32)
     grad = (rise * (slope * row)).astype(BF16)
     low[...] = grad.reshape(low.shape)
-    sums[...] = jnp.sum(grad.astype(F32), axis=1)
+    sums[...] = jnp.sum(grad.astype(F32), axis=1).astype(BF16)
     by_weight[...] = jnp.sum(jnp.sum(value * slope, axis=0), axis=0, keepdims=True)
 
 
@@ -474,7 +475,7 @@
         decode_kernel,
         out_shape=[
             jax.ShapeDtypeStruct((cells * queries, FF), BF16),
-            jax.ShapeDtypeStruct((cells, FF), F32),
+            jax.ShapeDtypeStruct((cells, FF), BF16),
             jax.ShapeDtypeStruct((1, FF), F32),
         ],
         compiler_params=pltpu.CompilerParams(vmem_limit_bytes=VMEM_ASKED),
@@ -657,6 +658,26 @@
     )(*arrays)
 
 
+def first_kernel(own, got, out):
+    out[...] = (own[...].astype(F32) + got[...].astype(F32)).astype(BF16)
+
+
+def add_first_call(own, got):
+    rows, columns = own.shape[-2:]
+    steps = 2
+    size = rows // steps
+    half = pl.BlockSpec((None, 2, size, columns), lambda r: (1, 0, r, 0))
+    return pl.pallas_call(
+        first_kernel,
+        grid=(steps,),
+        in_specs=[half, half],
+        out_specs=pl.BlockSpec((2, size, columns), lambda r: (0, r, 0)),
+        out_shape=jax.ShapeDtypeStruct((2, rows, columns), BF16),
+        compiler_params=pltpu.CompilerParams(vmem_limit_bytes=VMEM_ASKED),
+        cost_estimate=small_cost(),
+    )(own, got)
+
+
 def out_kernel(mixed, weight, tokens, bias, gain, shift, middle, second):
     values = tokens[...].astype(F32) + dot(mixed[...], weight[...]) + bias[...]
     middle[...] = values
@@ -982,7 +1003,7 @@
 
     def trade(self, value, axis, dim, column):
         mine, other = self.cut_step(value, axis, dim)
-        got = self.hop(other, axis) if axis != "zb" else self.hop(other, "z")
+        got = self.hop(other, axis) if axis != "zh" else self.hop(other, "z", 2)
         first = self.place(axis) == 0
         return jnp.concatenate(
             [jnp.where(first, mine, got), jnp.where(first, got, mine)], axis=column
@@ -1029,11 +1050,11 @@
             value, "dp", scatter_dimension=0, axis_index_groups=groups, tiled=True
         )
 
-    def scatter_high(self, value):
+    def scatter_low(self, value):
         stride, size = self.stride["z"], self.size["z"]
         groups = [
-            [(high * 2 + low) * stride + i for high in range(size // 2)]
-            for low in range(2)
+            [(high * 2 + low) * stride + i for low in range(2)]
+            for high in range(size // 2)
             for i in range(stride)
         ]
         return lax.psum_scatter(
@@ -1064,41 +1085,24 @@
                 )
         return jnp.concatenate(columns, axis=1) if len(columns) > 1 else columns[0]
 
-    def sides_of(self, first, after=()):
-        first = tie(first, *after)
-        return [self.hop(first, "y"), self.hop(first, "z")]
-
-    def corners_of(self, sides, after=()):
-        by_y, by_z = tie(sides, *after)
-        cut = by_y.shape[0] // 2 // 16 * 16
-        sent = (by_z[:cut], by_y[cut:])
-        return sent, [self.hop(sent[0], "y"), self.hop(sent[1], "z")]
-
-    def corner_cuts(self, sides):
-        by_y, by_z = sides
-        cut = by_y.shape[0] // 2 // 16 * 16
-        return [by_z[:cut], by_y[cut:]]
-
-    def most_of(self, first, sides, *after):
-        near = jnp.concatenate([tie(first, *after), *sides], axis=0)
-        return near, self.hop(near, "c")
-
-    def corner_of(self, corners, after=()):
-        near = jnp.concatenate(tie(corners, *after), axis=0)
-        return near, self.hop(near, "c")
-
-    def join(self, shard, parts, column):
+    def side_hop(self, value, turn):
+        pairs = []
+        for i in range(self.dp):
+            axis = "y" if i % 2 == turn else "z"
+            stride = self.stride[axis]
+            at = (i // stride) % self.size[axis]
+            pairs.append((i, i + ((at ^ 1) - at) * stride))
+        return lax.ppermute(value, "dp", pairs)
+
+    def join(self, shard, units, column):
         zb, y, c, x = self.place("z") % 2, self.place("y"), self.place("c"), self.place("x")
         rows, width = shard.shape
-        unit = rows // 8
+        size = rows // 8
         pieces, places = [(0, 0, rows, 0)], [x * rows]
-        for side in range(2):
-            c_ = c if side == 0 else 1 - c
-            for part in range(4):
-                place = ((zb ^ (part // 2)) * 2 + (y ^ (part % 2))) * 2 + c_
-                pieces.append((1 + 2 * side + part // 3, part % 3 * unit, unit, column))
-                places.append((1 - x) * rows + place * unit)
-        return assemble([shard, *parts], pieces, places, (2 * rows, width), 640)
+        for i, (zb_, y_, c_) in enumerate(unit_places(zb, y, c)):
+            pieces.append((1 + i, 0, size, column))
+            places.append((1 - x) * rows + ((zb_ * 2 + y_) * 2 + c_) * size)
+        return assemble([shard, *units], pieces, places, (2 * rows, width), 640)
 
     def places(self):
         return jnp.stack(
@@ -1129,21 +1133,26 @@
 
     def add_first(self, *after):
         own, got = tie((self.own, self.got), *after)
+        self.one_in = add_first_call(own, got)
+
+    def add_parts(self, *after):
+        own, got = tie((self.own, self.got), *after)
         self.parts = add_call(*[[(own, (1, k)), (got, (1, k))] for k in (1, 0)])
 
-    def go_first(self, part):
+    def go_part(self, part):
         return self.grid.turn_hop(self.parts[part], 0)
 
-    def add_second(self, one, *after):
-        own, got, one = tie((self.own, self.got, one), *after)
-        (self.two_in,) = add_call([(own, (0, 1)), (got, (0, 1)), (one, ())])
+    def go_first(self):
+        return self.grid.turn_hop(self.one_in, 0)
+
+    def add_second(self, one):
+        (self.two_in,) = add_call([(self.own, (0, 1)), (self.got, (0, 1)), one])
 
     def go_second(self):
         return self.grid.turn_hop(self.two_in, 1)
 
-    def add_last(self, one, two, *after):
-        own, got, one = tie((self.own, self.got, one), *after)
-        (whole,) = add_call([(own, (0, 0)), (got, (0, 0)), (one, ()), (two, ())])
+    def add_last(self, one, two):
+        (whole,) = add_call([(self.own, (0, 0)), (self.got, (0, 0)), one, (two, ())])
         size = self.grid.size["z"]
         self.last_in = whole.reshape(size, whole.shape[0] // size, whole.shape[1])
 
@@ -1207,54 +1216,63 @@
             qkv_first, normed_low, gene_found, up_part, down_part
         )
         up_first = grid.hop(up_part, "x")
-        qkv_sides = sync(*grid.sides_of(qkv_first))
-        qkv_sent = sync(*grid.corner_cuts(qkv_sides))
-        qkv_corners = [grid.hop(qkv_sent[0], "y"), grid.hop(qkv_sent[1], "z")]
-        qkv_near, qkv_far = grid.most_of(qkv_first, qkv_sides, qkv_sent)
-        *qkv_corners, qkv_near, up_first = sync(*qkv_corners, qkv_near, up_first)
-        up_sides = grid.sides_of(up_first)
-        qkv_end, qkv_end_far = grid.corner_of(qkv_corners)
-        qkv_end_far, qkv_far, up_first = sync(qkv_end_far, qkv_far, up_first)
+        qkv_near = grid.hop(qkv_first, "c")
+        qkv_side = grid.side_hop(qkv_first, 0)
+        qkv_near, qkv_side = sync(qkv_near, qkv_side)
+        qkv_side_two, qkv_corner = grid.side_hop(qkv_near, 0), grid.side_hop(qkv_side, 1)
+        qkv_far = grid.hop(qkv_side, "c")
+        qkv_side_two, qkv_corner, up_first = sync(qkv_side_two, qkv_corner, up_first)
+        up_near = grid.hop(up_first, "c")
+        up_side = grid.side_hop(up_first, 0)
+        qkv_far_two, qkv_far_corner = grid.hop(qkv_side_two, "c"), grid.hop(qkv_corner, "c")
+        qkv_far, qkv_far_two, qkv_far_corner = sync(qkv_far, qkv_far_two, qkv_far_corner)
         gene_hop = grid.hop(gene_found, "x")
         down_first = grid.hop(tie(down_part, up_first), "x")
-        qkv_weights = (w_qkv, qkv_near, qkv_end, qkv_far, qkv_end_far)
+        qkv_weights = (
+            w_qkv, qkv_first, qkv_near, qkv_side, qkv_side_two, qkv_corner,
+            qkv_far, qkv_far_two, qkv_far_corner,
+        )
         zeroes = jnp.zeros((D,), F32)
         qkv_bias = jnp.concatenate([proj_biases[0], zeroes, proj_biases[1]])
         qkv_low = project(where, normed_low, qkv_bias[None, :], qkv_weights)
+        qkv_low, up_near, up_side, gene_hop = sync(qkv_low, up_near, up_side, gene_hop)
+        up_side_two, up_corner = grid.side_hop(up_near, 0), grid.side_hop(up_side, 1)
+        up_far = grid.hop(up_side, "c")
         qkv_rows = qkv_low.reshape(row_count, ROW_LEN, 3 * D)
         mixed_rows, log_totals = attend(qkv_rows, segment)
-        mixed_rows, *up_sides, down_first, gene_hop = sync(mixed_rows, *up_sides, down_first, gene_hop)
-        up_sent = sync(*grid.corner_cuts(up_sides))
-        up_corners = [grid.hop(up_sent[0], "y"), grid.hop(up_sent[1], "z")]
-        up_near, up_far = grid.most_of(up_first, up_sides, up_sent)
-        down_sides = grid.sides_of(down_first, (up_near,))
         mixed_low = mixed_rows.reshape(token_count, D)
-        gene_rows = added(gene_found, gene_hop) if query_count == 2 else gene_found
+        gene_rows = added(gene_found, tie(gene_hop, mixed_low)) if query_count == 2 else gene_found
         gene_half = lax.dynamic_slice_in_dim(gene_rows, place * half_width, half_width, 1)
-        gene_partial = spread(tie(gene_half, up_near), dec_gene).reshape(query_count, pairs, FF)
+        gene_partial = spread(gene_half, dec_gene).reshape(query_count, pairs, FF)
+        mixed_low, gene_partial, up_side_two, up_corner, up_far, down_first = sync(
+            mixed_low, gene_partial, up_side_two, up_corner, up_far, down_first
+        )
         gene_mine, gene_sent = grid.cut_step(gene_partial, "x", 0)
-        *up_corners, up_far, gene_sent = sync(*up_corners, up_far, gene_sent)
-        up_end, up_end_far = grid.corner_of(up_corners)
-        up_parts = (up_near, up_end, up_far, up_end_far)
-        up_weights = (w_up, *up_parts)
-        full_out = grid.join(w_out, up_parts, FF)
+        down_near = grid.hop(down_first, "c")
+        down_side = grid.side_hop(down_first, 0)
+        up_far_two, up_far_corner = grid.hop(up_side_two, "c"), grid.hop(up_corner, "c")
+        up_units = (
+            up_first, up_near, up_side, up_side_two, up_corner, up_far, up_far_two, up_far_corner
+        )
+        up_weights = (w_up, *up_units)
+        full_out = grid.join(w_out, up_units, FF)
         middle, second_low = attend_out(
             mixed_low, full_out, row_tokens, proj_biases[2], ln_gains[1], ln_biases[1]
         )
-        second_low, down_first, *down_sides = sync(second_low, down_first, *down_sides)
-        down_sent = sync(*grid.corner_cuts(down_sides))
-        down_corners = [grid.hop(down_sent[0], "y"), grid.hop(down_sent[1], "z")]
-        down_near, down_far = grid.most_of(down_first, down_sides, down_sent)
+        second_low, down_near, down_side, gene_sent = sync(second_low, down_near, down_side, gene_sent)
+        down_side_two, down_corner = grid.side_hop(down_near, 0), grid.side_hop(down_side, 1)
+        down_far = grid.hop(down_side, "c")
         gene_got = grid.hop(gene_sent, "x")
-        gene_pair = grid.hop(gene_rows, "z")
-        active_low, slope = feed_up(
-            where, tie(second_low, down_near), ff_biases[0][None, :], up_weights
-        )
-        active_low, slope, *down_corners, down_far, gene_got, gene_pair = sync(
-            active_low, slope, *down_corners, down_far, gene_got, gene_pair
-        )
-        down_end, down_end_far = grid.corner_of(down_corners)
-        down_weights = (w_down, down_near, down_end, down_far, down_end_far)
+        gene_pair = grid.hop(gene_rows, "z", 2)
+        active_low, slope = feed_up(where, second_low, ff_biases[0][None, :], up_weights)
+        active_low, slope, down_side_two, down_corner, down_far, gene_got, gene_pair = sync(
+            active_low, slope, down_side_two, down_corner, down_far, gene_got, gene_pair
+        )
+        down_far_two, down_far_corner = grid.hop(down_side_two, "c"), grid.hop(down_corner, "c")
+        down_weights = (
+            w_down, down_first, down_near, down_side, down_side_two, down_corner,
+            down_far, down_far_two, down_far_corner,
+        )
         places = jnp.arange(ROW_LEN, dtype=jnp.int32)
         picker = (places[None, :, None] == starts[:, None, :]).astype(F32)
         rows_apart = jnp.arange(row_count)
@@ -1269,13 +1287,13 @@
         encoded_rows = encoded.reshape(row_count, ROW_LEN, D)
         cell_heads = grid.share(heads_low)
         heads_half = lax.dynamic_slice_in_dim(cell_heads, place * half_width, half_width, 1)
-        cell_half = dot(heads_half, dec_cell)
+        cell_half = dot(heads_half, dec_cell).astype(BF16)
         cell_hop = grid.hop(cell_half, "x") if query_count == 2 else cell_half
         before_low, before_sums, grad_logit = decode(
             cell_half, cell_hop, gene_mine, gene_got, ff_biases[1][None, :], dec_out[None, :], labels
         )
         before_low = before_low.reshape(pair_cells, local_queries, FF)
-        cell_total = grid.total(before_sums).astype(BF16)
+        cell_total = grid.total(before_sums)
         heads_part = dot_rt(cell_total, dec_cell).astype(BF16)
         heads_all = grid.share(heads_part, axis=1)
         heads_back = lax.dynamic_slice_in_dim(
@@ -1296,18 +1314,22 @@
         down_sums.own, down_sums.sent, before_hop = sync(down_sums.own, down_sums.sent, before_hop)
         down_sums.core()
         before_all = grid.joined(before_low, before_hop).reshape(query_count * pairs, FF)
-        before_mine, before_sent = grid.cut_half(before_all, "zb")
-        before_got = grid.hop(before_sent, "z")
+        before_mine, before_sent = grid.cut_half(before_all, "zh")
+        before_got = grid.hop(before_sent, "z", 2)
         hidden_low, up_bias_sums, grad_second = feed_back(
             where, tie(branch_low, down_sums.sent, before_sent), slope, up_weights, down_weights
         )
-        hidden_low, grad_second, before_got, down_sums.got = sync(
-            hidden_low, grad_second, before_got, down_sums.got
-        )
-        down_sums.add_first()
-        gene_wide = grid.joined_along(gene_rows, gene_pair, "zb")
-        before_wide = grid.joined_along(before_mine, before_got, "zb")
-        gene_left = grid.own_columns(gene_wide)
+        hidden_low, grad_second, down_sums.got = sync(hidden_low, grad_second, down_sums.got)
+        down_sums.add_parts()
+        down_sums.parts = sync(*down_sums.parts)
+        one, one_more = down_sums.go_part(0), down_sums.go_part(1)
+        grad_middle, attn_low, mixed_back, grad_gain_two, grad_shift_two = attend_out_back(
+            tie(grad_second, down_sums.parts), middle, ln_gains[1], grad_flat, full_out
+        )
+        gene_wide = grid.joined_along(gene_rows, gene_pair, "zh")
+        before_wide = grid.joined_along(before_mine, tie(before_got, mixed_back), "zh")
+        gene_left = grid.own_columns(gene_wide).reshape(gene_wide.shape[0], 2, 2, -1)
+        gene_left = gene_left.transpose(0, 2, 1, 3).reshape(gene_wide.shape[0], -1)
         gene_half = before_wide.shape[1] // 2
         core = grid.place("c")
         gene_mine, gene_sent = [
@@ -1317,30 +1339,33 @@
             ).astype(BF16)
             for at in (core, 1 - core)
         ]
-        *down_sums.parts, gene_sent, gene_mine = sync(*down_sums.parts, gene_sent, gene_mine)
-        one = down_sums.go_first(0)
         gene_got = grid.hop(gene_sent, "c")
-        grad_middle, attn_low, mixed_back, grad_gain_two, grad_shift_two = attend_out_back(
-            tie(grad_second, down_sums.parts), middle, ln_gains[1], grad_flat, full_out
-        )
         up_sums = Sums(grid)
-        up_sums.sent = weight_terms(where, False, (second_low, tie(hidden_low, mixed_back)))
-        up_sums.sent, one, gene_got, gathered = sync(up_sums.sent, one, gene_got, gathered)
-        one_more = down_sums.go_first(1)
-        down_sums.add_second(one)
+        up_sums.sent = weight_terms(where, False, (second_low, tie(hidden_low, mixed_back, gene_sent)))
+        up_sums.own = weight_terms(where, True, (second_low, tie(hidden_low, up_sums.sent)))
+        up_sums.sent, up_sums.own, one, one_more, gene_got, gathered = sync(
+            up_sums.sent, up_sums.own, one, one_more, gene_got, gathered
+        )
         up_sums.core()
+        down_sums.add_second((one, ()))
         two = down_sums.go_second()
-        up_sums.own = weight_terms(
-            where, True, (second_low, tie(hidden_low, up_sums.sent, down_sums.two_in))
-        )
-        (gene_sum,) = add_call([(gene_mine, ()), (tie(gene_got, up_sums.own), ())])
-        mixed_back, up_sums.own, up_sums.got, gene_sum = sync(
-            mixed_back, up_sums.own, up_sums.got, gene_sum
-        )
-        gene_sum = grid.scatter_high(gene_sum)
+        (gene_sum,) = add_call([(gene_mine, ()), (tie(gene_got, down_sums.two_in), ())])
+        genes_part = gather(tie(before_all, gene_sum), dec_gene)
+        choose = (
+            tie(ids, genes_part)[:, None] == jnp.arange(GENES, dtype=jnp.int32)[None, :]
+        ).astype(BF16)
+        table_terms = dot_lt(choose, genes_part).astype(BF16)
+        shape = [grid.size[axis] for axis in "zycx"]
+        table_terms = table_terms.reshape(*shape, -1, half_width)
+        table_mine, table_sent = grid.cut_step(table_terms, "c", 2)
+        mixed_back, up_sums.got, gene_sum, table_mine, table_sent = sync(
+            mixed_back, up_sums.got, gene_sum, table_mine, table_sent
+        )
+        gene_sum = grid.scatter_low(gene_sum)
+        table_got = grid.hop(table_sent, "c")
         up_sums.add_first()
-        *up_sums.parts, mixed_back = sync(*up_sums.parts, mixed_back)
-        up_one, up_more = up_sums.go_first(0), up_sums.go_first(1)
+        up_sums.one_in, mixed_back, two = sync(up_sums.one_in, mixed_back, two)
+        up_one = up_sums.go_first()
         qkv_back = attend_back(
             qkv_rows,
             segment,
@@ -1348,8 +1373,8 @@
             mixed_back.reshape(row_count, ROW_LEN, D),
             log_totals,
         )
-        qkv_back, one_more, two = sync(qkv_back, one_more, two)
-        down_sums.add_last(one_more, two)
+        qkv_back, table_got = sync(qkv_back, table_got)
+        down_sums.add_last((one_more, ()), two)
         down_sums.last()
         qkv_back_low = qkv_back.reshape(token_count, 3 * D)
         attn_sums = Sums(grid)
@@ -1362,52 +1387,39 @@
         attn_sums.sent, qkv_back_low, up_one, gene_sum = sync(
             attn_sums.sent, qkv_back_low, up_one, gene_sum
         )
-        gene_sum = gene_sum.reshape(2, grid.size["y"], -1, gene_sum.shape[-1])
-        gene_mine, gene_sent = grid.cut_step(gene_sum, "y", 1)
-        up_sums.add_second(up_one, gene_sent)
+        up_sums.add_second((up_one, (1,)))
         up_two = up_sums.go_second()
         attn_sums.core()
-        gene_got = grid.hop(gene_sent, "y")
         attn_sums.own = weight_terms(
             where, True, (normed_low, tie(qkv_back_low, up_sums.two_in)), (mixed_low, attn_low)
         )
         attn_sums.own, attn_sums.got = sync(attn_sums.own, attn_sums.got)
         attn_sums.add_first()
-        attn_sums.parts = sync(*attn_sums.parts)
-        one, one_more = attn_sums.go_first(0), attn_sums.go_first(1)
-        grad_normed = project_back(where, tie(qkv_back_low, attn_sums.parts), qkv_weights)
-        grad_normed, up_more, up_two, gene_got, down_sums.sum = sync(
-            grad_normed, up_more, up_two, gene_got, down_sums.sum
-        )
-        up_sums.add_last(up_more, up_two)
+        attn_sums.one_in, qkv_back_low, up_two = sync(attn_sums.one_in, qkv_back_low, up_two)
+        one = attn_sums.go_first()
+        table_mine, table_sent = grid.cut_fold(added(tie(table_mine, attn_sums.one_in), table_got), 1)
+        table_got = grid.hop(table_sent, "z", 1)
+        grad_normed = project_back(where, qkv_back_low, qkv_weights)
+        grad_normed, down_sums.sum = sync(grad_normed, down_sums.sum)
+        up_sums.add_last((up_one, (0,)), up_two)
         up_sums.last()
         grad_tokens, grad_gain_one, grad_shift_one = tokens_back(
             tie(grad_normed, up_sums.last_in), row_tokens, ln_gains[0], grad_middle
         )
-        gene_sum = added(tie(gene_mine, grad_tokens), gene_got).reshape(2, 2, -1, gene_mine.shape[-1])
-        genes_part = gather(tie(before_all, grad_tokens), dec_gene)
-        genes_part, gene_sum, one = sync(genes_part, gene_sum, one)
-        attn_sums.add_second(one)
+        one, grad_tokens, table_got = sync(one, grad_tokens, table_got)
+        attn_sums.add_second((one, (1,)))
         two = attn_sums.go_second()
 
-        gene_sum, genes_part = tie((gene_sum, genes_part), attn_sums.two_in)
-        gene_sum = grid.trade(gene_sum, "c", 1, 2)
+        table_mine, table_sent = grid.cut_fold(added(tie(table_mine, attn_sums.two_in), table_got), 2)
+        table_got = grid.hop(table_sent, "z", 2)
         grad_tokens = grad_tokens.reshape(row_count, ROW_LEN, D)
-        choose = (
-            tie(ids, genes_part)[:, None] == jnp.arange(GENES, dtype=jnp.int32)[None, :]
-        ).astype(BF16)
-        table_terms = dot_lt(choose, genes_part).astype(BF16)
-        shape = [grid.size[axis] for axis in "zycx"]
-        table_terms = table_terms.reshape(*shape, -1, half_width)
-        table_mine, table_sent = grid.cut_step(table_terms, "c", 2)
-        table_sum = added(table_mine, grid.hop(table_sent, "c"))
         late_ties = (qkv_back_low, attn_low, branch_low, up_bias_sums, before_sums)
-        qkv_late, attn_late, branch_late, up_bias_sums, sums_late = tie(late_ties, table_sent)
+        qkv_late, attn_late, branch_late, up_bias_sums, sums_late = tie(late_ties, attn_sums.two_in)
         grad_up_bias = up_bias_sums[0]
         bias_sums = jnp.sum(qkv_late, axis=0, dtype=F32)
         grad_attn_bias = jnp.sum(attn_late, axis=0, dtype=F32)
         grad_out_bias = jnp.sum(branch_late, axis=0, dtype=F32)
-        grad_dec_bias = jnp.sum(sums_late, axis=0)
+        grad_dec_bias = jnp.sum(sums_late, axis=0, dtype=F32)
         owners = dp_count * query_count
 
         def owned_cols(values):
@@ -1422,28 +1434,26 @@
         ]
         flat = [owned_cols(value) for value in small]
         sums = grid.scatter_step(grid.blocks(jnp.concatenate(flat, axis=1)), "c", 2, F32)
-        sums, table_sum, gene_sum, one_more, two, up_sums.sum = sync(
-            sums, table_sum, gene_sum, one_more, two, up_sums.sum
-        )
-        attn_sums.add_last(one_more, two)
+        sums, table_got, two, up_sums.sum = sync(sums, table_got, two, up_sums.sum)
+        attn_sums.add_last((one, (0,)), two)
         attn_sums.last()
 
-        sums, table_sum, gene_sum = tie((sums, table_sum, gene_sum), attn_sums.last_in)
+        sums, table_got, gene_sum = tie((sums, table_got, gene_sum), attn_sums.last_in)
         sums = grid.scatter_step(sums, "x", 2, F32)
-        table_sum = grid.scatter_step(table_sum, "y", 1, BF16)
-        grad_gene = grid.trade(gene_sum, "zb", 0, 1).astype(F32)
+        table_sum = grid.scatter_step(added(table_mine, table_got)[0], "y", 0, BF16)
+        gene_sum = grid.scatter_step(
+            gene_sum.reshape(2, grid.size["y"], -1, gene_sum.shape[-1]), "y", 1, BF16
+        )
         up_result, down_result = up_sums.result(attn_sums.last_in), down_sums.result(attn_sums.last_in)
-        sums, table_sum, grad_gene, up_result, down_result = sync(
-            sums, table_sum, grad_gene, up_result, down_result
+        sums, table_sum, gene_sum, up_result, down_result = sync(
+            sums, table_sum, gene_sum, up_result, down_result
         )
         sums = grid.scatter_step(sums, "y", 1, F32)
-        table_mine, table_sent = grid.cut_fold(table_sum, 1)
-        table_sum = added(table_mine, grid.hop(table_sent, "z", 1))
-        sums, table_sum = sync(sums, table_sum)
+        gene_sum = grid.trade(gene_sum.reshape(2, 2, -1, gene_sum.shape[-1]), "c", 1, 2)
+        grad_table = grid.trade(table_sum, "x", 0, 1).astype(F32)
+        sums, grad_table, gene_sum = sync(sums, grad_table, gene_sum)
         summed = grid.scatter_step(sums, "z", 0, F32).reshape(-1)
-        table_mine, table_sent = grid.cut_fold(table_sum, 2)
-        table_sum = added(table_mine, grid.hop(table_sent, "z", 2))[0]
-        grad_table = grid.trade(table_sum, "x", 0, 1).astype(F32)
+        grad_gene = grid.trade(gene_sum, "zh", 0, 1).astype(F32)
         all_heads, all_cells = jnp.split(tie(gathered, attn_sums.last_in), [D], axis=1)
         owned = D // (dp_count * query_count)
         mine = lax.axis_index("dp") * query_count + place

time: 540 us -> 501 us (0.928)
  local copies, waits for them, and re-layouts: 53.3 us -> 32.6 us
  waiting for transfers between devices: 124 us -> 106 us
    ppermute x39 -> x33, waiting for transfers between devices: 80 us -> 44.8 us  [hop(): return lax.ppermute(value, 'dp', pairs)]
    ppermute x39 -> x33, starting transfers between devices: 34.3 us -> 20.6 us  [hop(): return lax.ppermute(value, 'dp', pairs)]
    ppermute x0 -> x9, starting transfers between devices: none -> 12 us  [side_hop(): return lax.ppermute(value, 'dp', pairs)]
    pallas_call x10 -> x8, Pallas kernels: 40.2 us -> 30.9 us  [add_call(): pl.pallas_call(lambda *refs: add_kernel(len(groups), *refs), grid=(steps,...]
    pallas_call x0 -> x2, Pallas kernels: none -> 9.07 us  [add_first_call(): pl.pallas_call(first_kernel, grid=(steps,), in_specs=[half, half], out_sp...]
    ppermute x0 -> x9, waiting for transfers between devices: none -> 7.68 us  [side_hop(): return lax.ppermute(value, 'dp', pairs)]
    ppermute x13, waiting for transfers between devices: 19.6 us -> 27 us  [hop(): return lax.ppermute(value, 'query', pairs)]
    unnamed x125 -> x112, local copies, waits for them, and re-layouts: 16.9 us -> 9.61 us
  transfers between devices with their start and end apart: 66 -> 67, of which waited for: 32 -> 26; matrix products, arithmetic and copies ran while one was open for 10% -> 10% of each run, Pallas kernels for 41% -> 45%
where the time goes in v4:
time: 501 us; the launch traced here: 497 us
  Pallas kernels  246 us (49%)
  waiting for transfers between devices  106 us (21%)
  starting transfers between devices  55.8 us (11%)
  local copies, waits for them, and re-layouts  32.6 us (7%)
  other arithmetic  28.1 us (6%)
  between operations  15.5 us (3%)
  matrix products  12.4 us (2%)
    pallas_call x3, Pallas kernels, feed_call(): pl.pallas_call(kernel, grid_spec=pltpu.PrefetchScalarGridSpec(num_scalar_...  56.4 us
    ppermute x33, waiting for transfers between devices, hop(): return lax.ppermute(value, 'dp', pairs)  44.8 us
    pallas_call x4, Pallas kernels, weight_terms(): pl.pallas_call(lambda *refs: term_kernel(len(pairs), mine, units, *refs),...  38.9 us
    pallas_call x8, Pallas kernels, add_call(): pl.pallas_call(lambda *refs: add_kernel(len(groups), *refs), grid=(steps,...  30.9 us
    ppermute x13, waiting for transfers between devices, hop(): return lax.ppermute(value, 'query', pairs)  27 us
    ppermute x7, waiting for transfers between devices, turn_hop(): return lax.ppermute(value, ('dp', 'query'), pairs)  24.1 us
    pallas_call x2, Pallas kernels, qkv_call(): pl.pallas_call(kernel, grid_spec=pltpu.PrefetchScalarGridSpec(num_scalar_...  23.9 us
    ppermute x33, starting transfers between devices, hop(): return lax.ppermute(value, 'dp', pairs)  20.6 us
  transfers between devices with their start and end apart: 67, of which 26 were waited for; matrix products, arithmetic and copies ran while one was open for 10% of the time, Pallas kernels for 45%

profile of v4, /device:TPU:0, one launch (start us, length us, event | category | flops | bytes accessed | tf_op | source)
XLA Modules:
  0.0 496.6 jit_solution(17958612890183200565)
XLA Ops:
  9.5 2.9 collective-permute-start
  23.1 3.5 collective-permute-done.1
  30.5 7.1 %collective-permute-done.3.refs_3_ = bf16[80,3840]{1,0:T(8,128)(2,1)S(1)} collective-permute-done((bf16[80,3840]{1,0:T(8,128)(2,1)}, bf16[80,3840]{1,0:T(8,128)(2,1)S(1)}, u32[]{:S(2)}, u32[]{:S(2)}) %collective-permute-start.3) | collective-permute-done | bytes 614432 | tf_op jit(solution)/shard_map/ppermute | solution.py:1095
  40.9 12.8 %collective-permute-done.6.refs_2_.refs_1_ = bf16[80,6400]{1,0:T(8,128)(2,1)S(1)} collective-permute-done((bf16[80,6400]{1,0:T(8,128)(2,1)S(1)}, bf16[80,6400]{1,0:T(8,128)(2,1)S(1)}, u32[]{:S(2)}, u32[]{:S(2)}) %collective-permute-start.6) | collective-permute-done | bytes 1024032 | tf_op jit(solution)/shard_map/ppermute | solution.py:926
  61.7 11.4 %shard_map.272 = bf16[512,3840]{1,0:T(8,128)(2,1)} custom-call(s32[4]{0:T(128)} %pad_add_fusion.1.place.refs_0_, bf16[512,1280]{1,0:T(8,128)(2,1)} %fusion.5.normed.refs_1_, f32[1,3840]{1,0:T(1,128)} %broadcast_in_dim.23.bias, bf16[640,3840]{1,0:T(8,128)(2,1)} %refs_0_.9, bf16[80,3840]{1,0:T(8,128)(2,1)} %collective-permute-done.refs_1_, ...), custom_call_target="tpu_custom_call" | custom-call | flops 1 | bytes 1 | tf_op jit(solution)/shard_map/pallas_call | solution.py:358
  76.6 13.4 %shard_map.273 = (bf16[1,512,1280]{2,1,0:T(8,128)(2,1)}, f32[1,5,4,512]{3,2,1,0:T(4,128)}) custom-call(s32[1,1,512]{2,1,0:T(1,128)} %bitcast.219, s32[1,512,1]{2,1,0:T(8,128)} %copy.41.segment_column, bf16[1,512,3840]{2,1,0:T(8,128)(2,1)} %bitcast.170, bf16[1,512,3840]{2,1,0:T(8,128)(2,1)} %bitcast.171, bf16[1,512,3840]{2,1,0:T(8,128)(2,1)} %bitcast.172), custom_call_target="tpu_custom_call" | custom-call | flops 1 | bytes 1 | tf_op jit(solution)/shard_map/pallas_call | solution.py:95
  92.5 5.3 %shard_map.274 = bf16[128,5120]{1,0:T(8,128)(2,1)} custom-call(bf16[128,640]{1,0:T(8,128)(2,1)} %constant_dynamic-slice_fusion.6.left, bf16[640,5120]{1,0:T(8,128)(2,1)} %right.3), custom_call_target="tpu_custom_call" | custom-call | flops 1 | bytes 1 | tf_op jit(solution)/shard_map/pallas_call | solution.py:714
  99.9 2.6 collective-permute-start.25
  105.0 3.4 shard_map.275.weight
  110.2 6.2 %shard_map.276 = (f32[512,1280]{1,0:T(8,128)}, bf16[512,1280]{1,0:T(8,128)(2,1)}) custom-call(bf16[512,1280]{1,0:T(8,128)(2,1)} %bitcast.190, bf16[1280,1280]{1,0:T(8,128)(2,1)} %copy-done.2, bf16[512,1280]{1,0:T(8,128)(2,1)} %bitcast.186, f32[1,1280]{1,0:T(1,128)} %get-tuple-element.327.bias, f32[1,1280]{1,0:T(1,128)} %get-tuple-element.335.gain, ...), custom_call_target="tpu_custom_call" | custom-call | flops 1 | bytes 1 | tf_op jit(solution)/shard_map/pallas_call | solution.py:693
  121.3 16.8 %shard_map.277 = (bf16[512,5120]{1,0:T(8,128)(2,1)}, bf16[512,5120]{1,0:T(8,128)(2,1)}) custom-call(s32[4]{0:T(128)} %pad_add_fusion.1.place.refs_0_, bf16[512,1280]{1,0:T(8,128)(2,1)} %get-tuple-element.179.second.refs_1_, f32[1,5120]{1,0:T(1,128)} %get-tuple-element.321.bias, bf16[640,5120]{1,0:T(8,128)(2,1)} %refs_0_.8, bf16[80,6400]{1,0:T(8,128)(2,1)} %copy-done.3, ...), custom_call_target="tpu_custom_call" | custom-call | flops 1 | bytes 1 | tf_op jit(solution)/shard_map/pallas_call | solution.py:415
  142.7 15.4 %shard_map.278 = (f32[512,1280]{1,0:T(8,128)}, bf16[4,1280]{1,0:T(4,128)(2,1)}) custom-call(s32[4]{0:T(128)} %pad_add_fusion.1.place.refs_0_, bf16[512,5120]{1,0:T(8,128)(2,1)} %get-tuple-element.185.active.left, f32[512,1280]{1,0:T(8,128)} %get-tuple-element.186.middle, f32[1,1280]{1,0:T(1,128)} %get-tuple-element.326.bias, bf16[4,512]{1,0:T(4,128)(2,1)} %fusion.32.picker, ...), custom_call_target="tpu_custom_call" | custom-call | flops 1 | bytes 1 | tf_op jit(solution)/shard_map/pallas_call | solution.py:415
  159.2 2.8 collective-permute-done.28
  168.9 4.4 shard_map.279
  174.4 3.5 collective-permute-done.30
  178.8 4.6 convolution_convert_fusion.5
  191.3 15.8 %shard_map.280 = (bf16[2,2,4,320,640]{4,3,2,1,0:T(8,128)(2,1)}, bf16[2,2,4,320,640]{4,3,2,1,0:T(8,128)(2,1)}) custom-call(s32[4]{0:T(128)} %pad_add_fusion.1.place.refs_0_, bf16[512,5120]{1,0:T(8,128)(2,1)} %get-tuple-element.185.active.left, bf16[512,1280]{1,0:T(8,128)(2,1)} %get-tuple-element.261.right.branch), custom_call_target="tpu_custom_call" | custom-call | flops 1 | bytes 1 | tf_op jit(solution)/shard_map/pallas_call | solution.py:598
  211.8 24.2 %shard_map.281 = (bf16[512,5120]{1,0:T(8,128)(2,1)}, f32[1,5120]{1,0:T(1,128)}, f32[512,1280]{1,0:T(8,128)}) custom-call(s32[4]{0:T(128)} %pad_add_fusion.1.place.refs_0_, bf16[512,1280]{1,0:T(8,128)(2,1)} %get-tuple-element.261.right.branch, bf16[512,5120]{1,0:T(8,128)(2,1)} %get-tuple-element.202.slope, bf16[640,5120]{1,0:T(8,128)(2,1)} %refs_0_.8, ...), custom_call_target="tpu_custom_call" | custom-call | flops 1 | bytes 1 | tf_op jit(solution)/shard_map/pallas_call | solution.py:415
  236.1 4.4 shard_map.282
  242.5 8.8 %shard_map.283 = (f32[512,1280]{1,0:T(8,128)}, bf16[512,1280]{1,0:T(8,128)(2,1)}, bf16[512,1280]{1,0:T(8,128)(2,1)}, f32[1,1280]{1,0:T(1,128)}, f32[1,1280]{1,0:T(1,128)}) custom-call(f32[512,1280]{1,0:T(8,128)} %get-tuple-element.211.grad, f32[512,1280]{1,0:T(8,128)} %get-tuple-element.186.middle, f32[1,1280]{1,0:T(1,128)} %get-tuple-element.335.gain, ...), custom_call_target="tpu_custom_call" | custom-call | flops 1 | bytes 1 | tf_op jit(solution)/shard_map/pallas_call | solution.py:804
  254.2 9.2 %shard_map.284 = bf16[2,2,320,2560]{3,2,1,0:T(8,128)(2,1)} custom-call(s32[4]{0:T(128)} %pad_add_fusion.1.place.refs_0_, bf16[512,1280]{1,0:T(8,128)(2,1)} %get-tuple-element.179.second.refs_1_, bf16[512,5120]{1,0:T(8,128)(2,1)} %get-tuple-element.216.refs_2_.refs_3_, bf16[512,5120]{1,0:T(8,128)(2,1)} %get-tuple-element.216.refs_2_.refs_3_), custom_call_target="tpu_custom_call" | custom-call | flops 1 | bytes 1 | tf_op jit(solution)/shard_map/pallas_call | solution.py:549
  263.4 9.7 %shard_map.285.own.refs_0_ = bf16[2,2,320,2560]{3,2,1,0:T(8,128)(2,1)} custom-call(s32[4]{0:T(128)} %pad_add_fusion.1.place.refs_0_, bf16[512,1280]{1,0:T(8,128)(2,1)} %get-tuple-element.179.second.refs_1_, bf16[512,5120]{1,0:T(8,128)(2,1)} %get-tuple-element.216.refs_2_.refs_3_, bf16[512,5120]{1,0:T(8,128)(2,1)} %get-tuple-element.216.refs_2_.refs_3_), custom_call_target="tpu_custom_call" | custom-call | flops 1 | bytes 1 | tf_op jit(solution)/shard_map/pallas_call | solution.py:549
  273.1 6.3 %collective-permute-done.36.refs_2_ = bf16[1280,640]{1,0:T(8,128)(2,1)} collective-permute-done((bf16[1280,640]{1,0:T(8,128)(2,1)}, bf16[1280,640]{1,0:T(8,128)(2,1)}, u32[]{:S(2)}, u32[]{:S(2)}) %collective-permute-start.36) | collective-permute-done | bytes 1638432 | tf_op jit(solution)/shard_map/ppermute | solution.py:945
  279.5 3.4 collective-permute-start.38
  282.9 3.6 shard_map.286
  289.5 3.0 shard_map.287
  292.5 5.9 %shard_map.288 = bf16[128,640]{1,0:T(8,128)(2,1)} custom-call(bf16[128,5120]{1,0:T(8,128)(2,1)} %copy-done.9, bf16[640,5120]{1,0:T(8,128)(2,1)} %right.3), custom_call_target="tpu_custom_call" | custom-call | flops 1 | bytes 1 | tf_op jit(solution)/shard_map/pallas_call | solution.py:748
  300.1 4.5 shard_map.289
  304.6 3.3 collective-permute-done.39.refs_3_
  309.4 19.0 %shard_map.290 = bf16[1,512,3840]{2,1,0:T(8,128)(2,1)} custom-call(s32[1,1,512]{2,1,0:T(1,128)} %bitcast.220, s32[1,512,1]{2,1,0:T(8,128)} %copy.41.segment_column, bf16[1,512,3840]{2,1,0:T(8,128)(2,1)} %bitcast.173, bf16[1,512,3840]{2,1,0:T(8,128)(2,1)} %bitcast.174, bf16[1,512,3840]{2,1,0:T(8,128)(2,1)} %bitcast.175, ...), custom_call_target="tpu_custom_call" | custom-call | flops 1 | bytes 1 | tf_op jit(solution)/shard_map/pallas_call | solution.py:161
  328.4 4.3 shard_map.291
  332.7 9.9 %shard_map.292 = bf16[2,2,320,2560]{3,2,1,0:T(8,128)(2,1)} custom-call(s32[4]{0:T(128)} %pad_add_fusion.1.place.refs_0_, bf16[512,1280]{1,0:T(8,128)(2,1)} %fusion.5.normed.refs_1_, bf16[512,1280]{1,0:T(8,128)(2,1)} %bitcast.191, bf16[512,3840]{1,0:T(8,128)(2,1)} %bitcast.176, bf16[512,3840]{1,0:T(8,128)(2,1)} %bitcast.177, ...), custom_call_target="tpu_custom_call" | custom-call | flops 1 | bytes 1 | tf_op jit(solution)/shard_map/pallas_call | solution.py:549
  342.6 4.3 collective-permute-done.41.refs_2_
  346.9 3.6 shard_map.293
  351.8 10.1 %shard_map.294.own.refs_0_ = bf16[2,2,320,2560]{3,2,1,0:T(8,128)(2,1)} custom-call(s32[4]{0:T(128)} %pad_add_fusion.1.place.refs_0_, bf16[512,1280]{1,0:T(8,128)(2,1)} %fusion.5.normed.refs_1_, bf16[512,1280]{1,0:T(8,128)(2,1)} %bitcast.192, bf16[512,3840]{1,0:T(8,128)(2,1)} %bitcast.178, bf16[512,3840]{1,0:T(8,128)(2,1)} %bitcast.179, ...), custom_call_target="tpu_custom_call" | custom-call | flops 1 | bytes 1 | tf_op jit(solution)/shard_map/pallas_call | solution.py:549
  361.9 4.6 shard_map.295
  366.4 5.5 %collective-permute-done.43.refs_3_ = bf16[320,2560]{1,0:T(8,128)(2,1)} collective-permute-done((bf16[320,2560]{1,0:T(8,128)(2,1)}, bf16[320,2560]{1,0:T(8,128)(2,1)}, u32[]{:S(2)}, u32[]{:S(2)}) %collective-permute-start.43) | collective-permute-done | bytes 1638432 | tf_op jit(solution)/shard_map/ppermute | solution.py:945
  373.3 4.2 shard_map.297
  379.0 12.4 %shard_map.296.grad = f32[512,1280]{1,0:T(8,128)} custom-call(s32[4]{0:T(128)} %pad_add_fusion.1.place.refs_0_, bf16[512,3840]{1,0:T(8,128)(2,1)} %bitcast.180, bf16[640,3840]{1,0:T(8,128)(2,1)} %refs_0_.9, bf16[80,3840]{1,0:T(8,128)(2,1)} %collective-permute-done.refs_1_, bf16[80,3840]{1,0:T(8,128)(2,1)} %copy-done.16, bf16[80,3840]{1,0:T(8,128)(2,1)} %copy-done.17, ...), custom_call_target="tpu_custom_call" | custom-call | flops 1 | bytes 1 | tf_op jit(solution)/shard_map/pallas_call | solution.py:358
  393.5 5.2 %shard_map.298 = (f32[512,1280]{1,0:T(8,128)}, f32[1,1280]{1,0:T(1,128)}, f32[1,1280]{1,0:T(1,128)}) custom-call(f32[512,1280]{1,0:T(8,128)} %shard_map.296.grad, bf16[512,1280]{1,0:T(8,128)(2,1)} %bitcast.187, f32[1,1280]{1,0:T(1,128)} %get-tuple-element.333.gain, f32[512,1280]{1,0:T(8,128)} %get-tuple-element.247.flat), custom_call_target="tpu_custom_call" | custom-call | flops 1 | bytes 1 | tf_op jit(solution)/shard_map/pallas_call | solution.py:833
  400.5 13.4 %collective-permute-done.45 = bf16[2,2,2,32,640]{4,3,2,1,0:T(8,128)(2,1)S(1)} collective-permute-done((bf16[2,2,2,32,640]{4,3,2,1,0:T(8,128)(2,1)S(1)}, bf16[2,2,2,32,640]{4,3,2,1,0:T(8,128)(2,1)S(1)}, u32[]{:S(2)}, u32[]{:S(2)}) %collective-permute-start.45) | collective-permute-done | bytes 327712 | tf_op jit(solution)/shard_map/ppermute | solution.py:932
  414.7 3.7 shard_map.299
  420.2 3.0 convert_reduce_fusion
  428.4 6.6 %collective-permute-done.47 = bf16[1,2,2,32,640]{4,3,2,1,0:T(8,128)(2,1)S(1)} collective-permute-done((bf16[1,2,2,32,640]{4,3,2,1,0:T(8,128)(2,1)S(1)}, bf16[1,2,2,32,640]{4,3,2,1,0:T(8,128)(2,1)S(1)}, u32[]{:S(2)}, u32[]{:S(2)}) %collective-permute-start.47) | collective-permute-done | bytes 163872 | tf_op jit(solution)/shard_map/ppermute | solution.py:932
  435.0 4.8 collective-permute-done.48.refs_3_
  440.9 4.2 shard_map.300
  450.1 4.4 collective-permute-done.51
  471.3 14.2 %collective-permute-done.61 = bf16[40,2560]{1,0:T(8,128)(2,1)S(1)} collective-permute-done((bf16[40,2560]{1,0:T(8,128)(2,1)S(1)}, bf16[40,2560]{1,0:T(8,128)(2,1)S(1)}, u32[]{:S(2)}, u32[]{:S(2)}) %collective-permute-start.61) | collective-permute-done | bytes 204832 | tf_op jit(solution)/shard_map/ppermute | solution.py:932
  (368 shorter events, 125.8 us)
Async XLA Ops:
  7.2 265.9 %all-gather.2.cloned.1.call-start = ((), (), s32[]{:S(2)}) async-start(), calls=%async_computation.4 | async-start | bytes 1740800 | tf_op jit(solution)/shard_map/all_gather | solution.py:1309
  9.5 17.6 %collective-permute-start = (bf16[80,3840]{1,0:T(8,128)(2,1)}, bf16[80,3840]{1,0:T(8,128)(2,1)}, u32[]{:S(2)}, u32[]{:S(2)}) collective-permute-start(bf16[80,3840]{1,0:T(8,128)(2,1)} %constant_dynamic-slice_fusion.10), channel_id=1, source_target_pairs={{0,1},{1,0},{2,3},{3,2},{4,5},{5,4},{6,7},{7,6},{8,9},{9,8},{10,11... | collective-permute-start | bytes 1843208 | tf_op jit(solution)/shard_map/ppermute | solution.py:926
  13.2 13.4 %collective-permute-start.1 = (s32[1,64]{1,0:T(1,128)S(1)}, s32[1,64]{1,0:T(1,128)S(1)}, u32[]{:S(2)}, u32[]{:S(2)}) collective-permute-start(s32[1,64]{1,0:T(1,128)S(1)} %reshape.329), channel_id=1, source_target_pairs={{0,1},{1,0},{2,3},{3,2},{4,5},{5,4},{6,7},{7,6},{8,9},{9,8},{10,11... | collective-permute-start | bytes 776 | tf_op jit(solution)/shard_map/ppermute | solution.py:926
  27.2 10.4 %collective-permute-start.3 = (bf16[80,3840]{1,0:T(8,128)(2,1)}, bf16[80,3840]{1,0:T(8,128)(2,1)S(1)}, u32[]{:S(2)}, u32[]{:S(2)}) collective-permute-start(bf16[80,3840]{1,0:T(8,128)(2,1)} %collective-permute-done.refs_1_), channel_id=1, source_target_pairs={{0,4},{2,10},{4,0},{6,14},{8,12},{10,2},{12,8},{14,6},{16,20},{18,... | collective-permute-start | bytes 1843208 | tf_op jit(solution)/shard_map/ppermute | solution.py:1095
  29.0 24.7 %collective-permute-start.6 = (bf16[80,6400]{1,0:T(8,128)(2,1)S(1)}, bf16[80,6400]{1,0:T(8,128)(2,1)S(1)}, u32[]{:S(2)}, u32[]{:S(2)}) collective-permute-start(bf16[80,6400]{1,0:T(8,128)(2,1)S(1)} %copy-done.30), channel_id=1, source_target_pairs={{0,1},{1,0},{2,3},{3,2},{4,5},{5,4},{6,7},{7,6},{8,9},{9,8},{10,11... | collective-permute-start | bytes 3072008 | tf_op jit(solution)/shard_map/ppermute | solution.py:926
  37.6 16.6 %collective-permute-start.4 = (bf16[80,3840]{1,0:T(8,128)(2,1)S(1)}, bf16[80,3840]{1,0:T(8,128)(2,1)S(1)}, u32[]{:S(2)}, u32[]{:S(2)}) collective-permute-start(bf16[80,3840]{1,0:T(8,128)(2,1)S(1)} %collective-permute-done.2.refs_2_), channel_id=1, source_target_pairs={{0,4},{2,10},{4,0},{6,14},{8,12},{10,2},{12,8},{14,6},{16,20},{18,... | collective-permute-start | bytes 1843208 | tf_op jit(solution)/shard_map/ppermute | solution.py:1095
  39.4 14.8 %collective-permute-start.5 = (bf16[80,3840]{1,0:T(8,128)(2,1)S(1)}, bf16[80,3840]{1,0:T(8,128)(2,1)S(1)}, u32[]{:S(2)}, u32[]{:S(2)}) collective-permute-start(bf16[80,3840]{1,0:T(8,128)(2,1)S(1)} %collective-permute-done.3.refs_3_), channel_id=1, source_target_pairs={{0,8},{2,6},{4,12},{6,2},{8,0},{10,14},{12,4},{14,10},{16,24},{18,... | collective-permute-start | bytes 1843208 | tf_op jit(solution)/shard_map/ppermute | solution.py:1095
  40.9 15.7 %collective-permute-start.7 = (bf16[80,3840]{1,0:T(8,128)(2,1)S(1)}, bf16[80,3840]{1,0:T(8,128)(2,1)S(1)}, u32[]{:S(2)}, u32[]{:S(2)}) collective-permute-start(bf16[80,3840]{1,0:T(8,128)(2,1)S(1)} %collective-permute-done.3.refs_3_), channel_id=1, source_target_pairs={{0,2},{2,0},{4,6},{6,4},{8,10},{10,8},{12,14},{14,12},{16,18},{18,... | collective-permute-start | bytes 1843208 | tf_op jit(solution)/shard_map/ppermute | solution.py:932
  54.2 18.9 %collective-permute-start.10 = (bf16[80,6400]{1,0:T(8,128)(2,1)S(1)}, bf16[80,6400]{1,0:T(8,128)(2,1)S(1)}, u32[]{:S(2)}, u32[]{:S(2)}) collective-permute-start(bf16[80,6400]{1,0:T(8,128)(2,1)S(1)} %collective-permute-done.6.refs_2_.refs_1_), channel_id=1, source_target_pairs={{0,2},{2,0},{4,6},{6,4},{8,10},{10,8},{12,14},{14,12},{16,18},{18,... | collective-permute-start | bytes 3072008 | tf_op jit(solution)/shard_map/ppermute | solution.py:932
  54.3 18.9 %collective-permute-start.11 = (bf16[80,6400]{1,0:T(8,128)(2,1)S(1)}, bf16[80,6400]{1,0:T(8,128)(2,1)S(1)}, u32[]{:S(2)}, u32[]{:S(2)}) collective-permute-start(bf16[80,6400]{1,0:T(8,128)(2,1)S(1)} %collective-permute-done.6.refs_2_.refs_1_), channel_id=1, source_target_pairs={{0,4},{2,10},{4,0},{6,14},{8,12},{10,2},{12,8},{14,6},{16,20},{18,... | collective-permute-start | bytes 3072008 | tf_op jit(solution)/shard_map/ppermute | solution.py:1095
  56.7 16.4 %collective-permute-start.12 = (bf16[128,1280]{1,0:T(8,128)(2,1)S(1)}, bf16[128,1280]{1,0:T(8,128)(2,1)}, u32[]{:S(2)}, u32[]{:S(2)}) collective-permute-start(bf16[128,1280]{1,0:T(8,128)(2,1)S(1)} %convolution_convert_fusion.3), channel_id=1, source_target_pairs={{0,1},{1,0},{2,3},{3,2},{4,5},{5,4},{6,7},{7,6},{8,9},{9,8},{10,11... | collective-permute-start | bytes 983048 | tf_op jit(solution)/shard_map/ppermute | solution.py:926
  73.2 24.8 %collective-permute-start.13 = (bf16[80,6400]{1,0:T(8,128)(2,1)S(1)}, bf16[80,6400]{1,0:T(8,128)(2,1)}, u32[]{:S(2)}, u32[]{:S(2)}) collective-permute-start(bf16[80,6400]{1,0:T(8,128)(2,1)S(1)} %collective-permute-done.10.refs_3_.refs_2_), channel_id=1, source_target_pairs={{0,4},{2,10},{4,0},{6,14},{8,12},{10,2},{12,8},{14,6},{16,20},{18,... | collective-permute-start | bytes 3072008 | tf_op jit(solution)/shard_map/ppermute | solution.py:1095
  73.7 24.2 %collective-permute-start.14 = (bf16[80,6400]{1,0:T(8,128)(2,1)S(1)}, bf16[80,6400]{1,0:T(8,128)(2,1)}, u32[]{:S(2)}, u32[]{:S(2)}) collective-permute-start(bf16[80,6400]{1,0:T(8,128)(2,1)S(1)} %collective-permute-done.11.refs_4_.refs_3_), channel_id=1, source_target_pairs={{0,8},{2,6},{4,12},{6,2},{8,0},{10,14},{12,4},{14,10},{16,24},{18,... | collective-permute-start | bytes 3072008 | tf_op jit(solution)/shard_map/ppermute | solution.py:1095
  75.0 23.0 %collective-permute-start.15 = (bf16[80,6400]{1,0:T(8,128)(2,1)S(1)}, bf16[80,6400]{1,0:T(8,128)(2,1)}, u32[]{:S(2)}, u32[]{:S(2)}) collective-permute-start(bf16[80,6400]{1,0:T(8,128)(2,1)S(1)} %collective-permute-done.11.refs_4_.refs_3_), channel_id=1, source_target_pairs={{0,2},{2,0},{4,6},{6,4},{8,10},{10,8},{12,14},{14,12},{16,18},{18,... | collective-permute-start | bytes 3072008 | tf_op jit(solution)/shard_map/ppermute | solution.py:932
  75.0 22.8 %collective-permute-start.16 = (bf16[320,1280]{1,0:T(8,128)(2,1)}, bf16[320,1280]{1,0:T(8,128)(2,1)}, u32[]{:S(2)}, u32[]{:S(2)}) collective-permute-start(bf16[320,1280]{1,0:T(8,128)(2,1)} %constant_dynamic-slice_fusion.7), channel_id=1, source_target_pairs={{0,1},{1,0},{2,3},{3,2},{4,5},{5,4},{6,7},{7,6},{8,9},{9,8},{10,11... | collective-permute-start | bytes 2457608 | tf_op jit(solution)/shard_map/ppermute | solution.py:926
  98.0 7.0 %collective-permute-start.17 = (bf16[80,6400]{1,0:T(8,128)(2,1)}, bf16[80,6400]{1,0:T(8,128)(2,1)}, u32[]{:S(2)}, u32[]{:S(2)}) collective-permute-start(bf16[80,6400]{1,0:T(8,128)(2,1)} %collective-permute-done.13.refs_5_.refs_4_), channel_id=1, source_target_pairs={{0,2},{2,0},{4,6},{6,4},{8,10},{10,8},{12,14},{14,12},{16,18},{18,... | collective-permute-start | bytes 3072008 | tf_op jit(solution)/shard_map/ppermute | solution.py:932
  98.1 6.9 %collective-permute-start.18 = (bf16[80,6400]{1,0:T(8,128)(2,1)}, bf16[80,6400]{1,0:T(8,128)(2,1)}, u32[]{:S(2)}, u32[]{:S(2)}) collective-permute-start(bf16[80,6400]{1,0:T(8,128)(2,1)} %collective-permute-done.14.refs_6_.refs_5_), channel_id=1, source_target_pairs={{0,2},{2,0},{4,6},{6,4},{8,10},{10,8},{12,14},{14,12},{16,18},{18,... | collective-permute-start | bytes 3072008 | tf_op jit(solution)/shard_map/ppermute | solution.py:932
  98.5 17.8 %collective-permute-start.19 = (bf16[320,1280]{1,0:T(8,128)(2,1)}, bf16[320,1280]{1,0:T(8,128)(2,1)}, u32[]{:S(2)}, u32[]{:S(2)}) collective-permute-start(bf16[320,1280]{1,0:T(8,128)(2,1)} %collective-permute-done.16.refs_1_.refs_10_), channel_id=1, source_target_pairs={{0,2},{2,0},{4,6},{6,4},{8,10},{10,8},{12,14},{14,12},{16,18},{18,... | collective-permute-start | bytes 2457608 | tf_op jit(solution)/shard_map/ppermute | solution.py:932
  98.6 17.7 %collective-permute-start.20 = (bf16[320,1280]{1,0:T(8,128)(2,1)}, bf16[320,1280]{1,0:T(8,128)(2,1)}, u32[]{:S(2)}, u32[]{:S(2)}) collective-permute-start(bf16[320,1280]{1,0:T(8,128)(2,1)} %collective-permute-done.16.refs_1_.refs_10_), channel_id=1, source_target_pairs={{0,4},{2,10},{4,0},{6,14},{8,12},{10,2},{12,8},{14,6},{16,20},{18,... | collective-permute-start | bytes 2457608 | tf_op jit(solution)/shard_map/ppermute | solution.py:1095
  99.9 38.2 %collective-permute-start.25 = (bf16[128,1280]{1,0:T(8,128)(2,1)}, bf16[128,1280]{1,0:T(8,128)(2,1)}, u32[]{:S(2)}, u32[]{:S(2)}) collective-permute-start(bf16[128,1280]{1,0:T(8,128)(2,1)} %copy-done.23), channel_id=1, source_target_pairs={{0,16},{2,18},{4,20},{6,22},{8,24},{10,26},{12,28},{14,30},{16,0},... | collective-permute-start | bytes 983048 | tf_op jit(solution)/shard_map/ppermute | solution.py:932
  116.3 21.8 %collective-permute-start.22 = (bf16[320,1280]{1,0:T(8,128)(2,1)}, bf16[320,1280]{1,0:T(8,128)(2,1)S(1)}, u32[]{:S(2)}, u32[]{:S(2)}) collective-permute-start(bf16[320,1280]{1,0:T(8,128)(2,1)} %collective-permute-done.20.refs_3_.refs_12_), channel_id=1, source_target_pairs={{0,8},{2,6},{4,12},{6,2},{8,0},{10,14},{12,4},{14,10},{16,24},{18,... | collective-permute-start | bytes 2457608 | tf_op jit(solution)/shard_map/ppermute | solution.py:1095
  117.5 20.7 %collective-permute-start.23 = (bf16[320,1280]{1,0:T(8,128)(2,1)}, bf16[320,1280]{1,0:T(8,128)(2,1)S(1)}, u32[]{:S(2)}, u32[]{:S(2)}) collective-permute-start(bf16[320,1280]{1,0:T(8,128)(2,1)} %collective-permute-done.20.refs_3_.refs_12_), channel_id=1, source_target_pairs={{0,2},{2,0},{4,6},{6,4},{8,10},{10,8},{12,14},{14,12},{16,18},{18,... | collective-permute-start | bytes 2457608 | tf_op jit(solution)/shard_map/ppermute | solution.py:932
  118.5 19.6 %collective-permute-start.21 = (bf16[320,1280]{1,0:T(8,128)(2,1)}, bf16[320,1280]{1,0:T(8,128)(2,1)S(1)}, u32[]{:S(2)}, u32[]{:S(2)}) collective-permute-start(bf16[320,1280]{1,0:T(8,128)(2,1)} %collective-permute-done.19.refs_2_.refs_11_), channel_id=1, source_target_pairs={{0,4},{2,10},{4,0},{6,14},{8,12},{10,2},{12,8},{14,6},{16,20},{18,... | collective-permute-start | bytes 2457608 | tf_op jit(solution)/shard_map/ppermute | solution.py:1095
  119.3 18.8 %collective-permute-start.24 = (bf16[64,5120]{1,0:T(8,128)(2,1)}, bf16[64,5120]{1,0:T(8,128)(2,1)S(1)}, u32[]{:S(2)}, u32[]{:S(2)}) collective-permute-start(bf16[64,5120]{1,0:T(8,128)(2,1)} %get-tuple-element.184), channel_id=1, source_target_pairs={{0,1},{1,0},{2,3},{3,2},{4,5},{5,4},{6,7},{7,6},{8,9},{9,8},{10,11... | collective-permute-start | bytes 1966088 | tf_op jit(solution)/shard_map/ppermute | solution.py:926
  190.1 16.9 %collective-permute-start.32 = (bf16[8,8,5120]{2,1,0:T(8,128)(2,1)S(1)}, bf16[8,8,5120]{2,1,0:T(8,128)(2,1)S(1)}, u32[]{:S(2)}, u32[]{:S(2)}) collective-permute-start(bf16[8,8,5120]{2,1,0:T(8,128)(2,1)S(1)} %bitcast.208), channel_id=1, source_target_pairs={{0,1},{1,0},{2,3},{3,2},{4,5},{5,4},{6,7},{7,6},{8,9},{9,8},{10,11... | collective-permute-start | bytes 1966088 | tf_op jit(solution)/shard_map/ppermute | solution.py:926
  207.0 29.0 %collective-permute-start.33 = (bf16[2,2,1280,640]{3,2,1,0:T(8,128)(2,1)}, bf16[2,2,1280,640]{3,2,1,0:T(8,128)(2,1)}, u32[]{:S(2)}, u32[]{:S(2)}) collective-permute-start(bf16[2,2,1280,640]{3,2,1,0:T(8,128)(2,1)} %bitcast.224), channel_id=1, source_target_pairs={{0,2},{2,0},{4,6},{6,4},{8,10},{10,8},{12,14},{14,12},{16,18},{18,... | collective-permute-start | bytes 19660808 | tf_op jit(solution)/shard_map/ppermute | solution.py:932
  207.8 139.1 %reduce-scatter.5.cloned.1.call-start = ((), (), s32[]{:S(2)}) async-start(), calls=%async_computation.5 | async-start | bytes 2457600 | tf_op jit(solution)/shard_map/reduce_scatter | solution.py:1060
  209.0 42.3 %collective-permute-start.34 = (bf16[128,2560]{1,0:T(8,128)(2,1)}, bf16[128,2560]{1,0:T(8,128)(2,1)}, u32[]{:S(2)}, u32[]{:S(2)}) collective-permute-start(bf16[128,2560]{1,0:T(8,128)(2,1)} %broadcast_select_fusion.5), channel_id=1, source_target_pairs={{0,16},{2,18},{4,20},{6,22},{8,24},{10,26},{12,28},{14,30},{16,0},... | collective-permute-start | bytes 1966088 | tf_op jit(solution)/shard_map/ppermute | solution.py:932
  240.5 32.7 %collective-permute-start.35 = (bf16[1280,640]{1,0:T(8,128)(2,1)}, bf16[1280,640]{1,0:T(8,128)(2,1)}, u32[]{:S(2)}, u32[]{:S(2)}) collective-permute-start(bf16[1280,640]{1,0:T(8,128)(2,1)} %get-tuple-element.209), channel_id=1, source_target_pairs={{0,1},{1,0},{2,6},{3,7},{4,5},{5,4},{6,2},{7,3},{8,9},{9,8},{10,14... | collective-permute-start | bytes 4915208 | tf_op jit(solution)/shard_map/ppermute | solution.py:945
  241.9 37.6 %collective-permute-start.36 = (bf16[1280,640]{1,0:T(8,128)(2,1)}, bf16[1280,640]{1,0:T(8,128)(2,1)}, u32[]{:S(2)}, u32[]{:S(2)}) collective-permute-start(bf16[1280,640]{1,0:T(8,128)(2,1)} %get-tuple-element.210), channel_id=1, source_target_pairs={{0,1},{1,0},{2,6},{3,7},{4,5},{5,4},{6,2},{7,3},{8,9},{9,8},{10,14... | collective-permute-start | bytes 4915208 | tf_op jit(solution)/shard_map/ppermute | solution.py:945
  254.2 25.2 %collective-permute-start.37 = (bf16[640,1280]{1,0:T(8,128)(2,1)}, bf16[640,1280]{1,0:T(8,128)(2,1)}, u32[]{:S(2)}, u32[]{:S(2)}) collective-permute-start(bf16[640,1280]{1,0:T(8,128)(2,1)} %convolution_convert_fusion.2), channel_id=1, source_target_pairs={{0,2},{2,0},{4,6},{6,4},{8,10},{10,8},{12,14},{14,12},{16,18},{18,... | collective-permute-start | bytes 4915208 | tf_op jit(solution)/shard_map/ppermute | solution.py:932
  279.5 20.7 %collective-permute-start.38 = (bf16[2,2,320,2560]{3,2,1,0:T(8,128)(2,1)}, bf16[2,2,320,2560]{3,2,1,0:T(8,128)(2,1)}, u32[]{:S(2)}, u32[]{:S(2)}) collective-permute-start(bf16[2,2,320,2560]{3,2,1,0:T(8,128)(2,1)} %shard_map.284), channel_id=1, source_target_pairs={{0,2},{2,0},{4,6},{6,4},{8,10},{10,8},{12,14},{14,12},{16,18},{18,... | collective-permute-start | bytes 19660808 | tf_op jit(solution)/shard_map/ppermute | solution.py:932
  286.5 21.4 %collective-permute-start.39 = (bf16[1280,640]{1,0:T(8,128)(2,1)}, bf16[1280,640]{1,0:T(8,128)(2,1)}, u32[]{:S(2)}, u32[]{:S(2)}) collective-permute-start(bf16[1280,640]{1,0:T(8,128)(2,1)} %shard_map.286), channel_id=1, source_target_pairs={{0,4},{1,5},{2,3},{3,2},{4,0},{5,1},{6,7},{7,6},{8,12},{9,13},{10,... | collective-permute-start | bytes 4915208 | tf_op jit(solution)/shard_map/ppermute | solution.py:945
  307.9 39.0 %collective-permute-start.41 = (bf16[2,320,2560]{2,1,0:T(8,128)(2,1)}, bf16[2,320,2560]{2,1,0:T(8,128)(2,1)}, u32[]{:S(2)}, u32[]{:S(2)}) collective-permute-start(bf16[2,320,2560]{2,1,0:T(8,128)(2,1)} %shard_map.289), channel_id=1, source_target_pairs={{0,1},{1,0},{2,6},{3,7},{4,5},{5,4},{6,2},{7,3},{8,9},{9,8},{10,14... | collective-permute-start | bytes 9830408 | tf_op jit(solution)/shard_map/ppermute | solution.py:945
  309.3 82.2 %reduce-scatter.7.cloned.1.call-start = ((), (), s32[]{:S(2)}) async-start(), calls=%async_computation.6 | async-start | bytes 2048000 | tf_op jit(solution)/shard_map/reduce_scatter | solution.py:1049
  309.4 23.3 %collective-permute-start.40 = (bf16[4,2,2,32,640]{4,3,2,1,0:T(8,128)(2,1)S(1)}, bf16[4,2,2,32,640]{4,3,2,1,0:T(8,128)(2,1)S(1)}, u32[]{:S(2)}, u32[]{:S(2)}) collective-permute-start(bf16[4,2,2,32,640]{4,3,2,1,0:T(8,128)(2,1)S(1)} %get-tuple-element.228), channel_id=1, source_target_pairs={{0,2},{2,0},{4,6},{6,4},{8,10},{10,8},{12,14},{14,12},{16,18},{18,... | collective-permute-start | bytes 1966088 | tf_op jit(solution)/shard_map/ppermute | solution.py:932
  346.9 15.0 %collective-permute-start.42 = (bf16[2,2,320,2560]{3,2,1,0:T(8,128)(2,1)}, bf16[2,2,320,2560]{3,2,1,0:T(8,128)(2,1)}, u32[]{:S(2)}, u32[]{:S(2)}) collective-permute-start(bf16[2,2,320,2560]{3,2,1,0:T(8,128)(2,1)} %shard_map.292), channel_id=1, source_target_pairs={{0,2},{2,0},{4,6},{6,4},{8,10},{10,8},{12,14},{14,12},{16,18},{18,... | collective-permute-start | bytes 19660808 | tf_op jit(solution)/shard_map/ppermute | solution.py:932
  350.5 21.4 %collective-permute-start.43 = (bf16[320,2560]{1,0:T(8,128)(2,1)}, bf16[320,2560]{1,0:T(8,128)(2,1)}, u32[]{:S(2)}, u32[]{:S(2)}) collective-permute-start(bf16[320,2560]{1,0:T(8,128)(2,1)} %shard_map.293), channel_id=1, source_target_pairs={{0,4},{1,5},{2,3},{3,2},{4,0},{5,1},{6,7},{7,6},{8,12},{9,13},{10,... | collective-permute-start | bytes 4915208 | tf_op jit(solution)/shard_map/ppermute | solution.py:945
  351.8 76.7 %reduce-scatter.9.cloned.1.call-start = ((), (), s32[]{:S(2)}) async-start(), calls=%async_computation.7 | async-start | bytes 2048000 | tf_op jit(solution)/shard_map/reduce_scatter | solution.py:1049
  371.9 42.1 %collective-permute-start.44 = (bf16[2,320,2560]{2,1,0:T(8,128)(2,1)}, bf16[2,320,2560]{2,1,0:T(8,128)(2,1)}, u32[]{:S(2)}, u32[]{:S(2)}) collective-permute-start(bf16[2,320,2560]{2,1,0:T(8,128)(2,1)} %shard_map.295), channel_id=1, source_target_pairs={{0,1},{1,0},{2,6},{3,7},{4,5},{5,4},{6,2},{7,3},{8,9},{9,8},{10,14... | collective-permute-start | bytes 9830408 | tf_op jit(solution)/shard_map/ppermute | solution.py:945
  377.5 108.0 %reduce-scatter.11.cloned.1.call-start = ((), (), s32[]{:S(2)}) async-start(), calls=%async_computation.8 | async-start | bytes 2048000 | tf_op jit(solution)/shard_map/reduce_scatter | solution.py:1049
  391.7 22.2 %collective-permute-start.45 = (bf16[2,2,2,32,640]{4,3,2,1,0:T(8,128)(2,1)S(1)}, bf16[2,2,2,32,640]{4,3,2,1,0:T(8,128)(2,1)S(1)}, u32[]{:S(2)}, u32[]{:S(2)}) collective-permute-start(bf16[2,2,2,32,640]{4,3,2,1,0:T(8,128)(2,1)S(1)} %get-tuple-element.305), channel_id=1, source_target_pairs={{0,8},{2,10},{4,12},{6,14},{8,0},{10,2},{12,4},{14,6},{16,24},{18,... | collective-permute-start | bytes 983048 | tf_op jit(solution)/shard_map/ppermute | solution.py:932
  418.4 21.3 %collective-permute-start.48 = (bf16[320,2560]{1,0:T(8,128)(2,1)}, bf16[320,2560]{1,0:T(8,128)(2,1)S(1)}, u32[]{:S(2)}, u32[]{:S(2)}) collective-permute-start(bf16[320,2560]{1,0:T(8,128)(2,1)} %shard_map.299), channel_id=1, source_target_pairs={{0,4},{1,5},{2,3},{3,2},{4,0},{5,1},{6,7},{7,6},{8,12},{9,13},{10,... | collective-permute-start | bytes 4915208 | tf_op jit(solution)/shard_map/ppermute | solution.py:945
  425.3 9.7 %collective-permute-start.47 = (bf16[1,2,2,32,640]{4,3,2,1,0:T(8,128)(2,1)S(1)}, bf16[1,2,2,32,640]{4,3,2,1,0:T(8,128)(2,1)S(1)}, u32[]{:S(2)}, u32[]{:S(2)}) collective-permute-start(bf16[1,2,2,32,640]{4,3,2,1,0:T(8,128)(2,1)S(1)} %constant_dynamic-slice_fusion.4), channel_id=1, source_target_pairs={{0,16},{2,18},{4,20},{6,22},{8,24},{10,26},{12,28},{14,30},{16,0},... | collective-permute-start | bytes 491528 | tf_op jit(solution)/shard_map/ppermute | solution.py:932
  446.3 8.2 %collective-permute-start.51 = (bf16[2,80,1280]{2,1,0:T(8,128)(2,1)S(1)}, bf16[2,80,1280]{2,1,0:T(8,128)(2,1)S(1)}, u32[]{:S(2)}, u32[]{:S(2)}) collective-permute-start(bf16[2,80,1280]{2,1,0:T(8,128)(2,1)S(1)} %dynamic-slice_bitcast_fusion.4), channel_id=1, source_target_pairs={{0,4},{2,6},{4,0},{6,2},{8,12},{10,14},{12,8},{14,10},{16,20},{18,... | collective-permute-start | bytes 1228808 | tf_op jit(solution)/shard_map/ppermute | solution.py:932
  460.7 5.7 %collective-permute-start.59 = (f32[1,800]{1,0:T(1,128)S(1)}, f32[1,800]{1,0:T(1,128)S(1)}, u32[]{:S(2)}, u32[]{:S(2)}) collective-permute-start(f32[1,800]{1,0:T(1,128)S(1)} %get-tuple-element.331), channel_id=1, source_target_pairs={{0,24},{2,26},{4,28},{6,30},{8,16},{10,18},{12,20},{14,22},{16,8},... | collective-permute-start | bytes 9608 | tf_op jit(solution)/shard_map/ppermute | solution.py:932
  462.5 5.4 %collective-permute-start.58 = (f32[1,800]{1,0:T(1,128)S(1)}, f32[1,800]{1,0:T(1,128)S(1)}, u32[]{:S(2)}, u32[]{:S(2)}) collective-permute-start(f32[1,800]{1,0:T(1,128)S(1)} %get-tuple-element.332), channel_id=1, source_target_pairs={{0,16},{2,18},{4,20},{6,22},{8,24},{10,26},{12,28},{14,30},{16,0},... | collective-permute-start | bytes 9608 | tf_op jit(solution)/shard_map/ppermute | solution.py:932
  465.2 20.3 %collective-permute-start.61 = (bf16[40,2560]{1,0:T(8,128)(2,1)S(1)}, bf16[40,2560]{1,0:T(8,128)(2,1)S(1)}, u32[]{:S(2)}, u32[]{:S(2)}) collective-permute-start(bf16[40,2560]{1,0:T(8,128)(2,1)S(1)} %dynamic-slice_bitcast_fusion.7), channel_id=1, source_target_pairs={{0,16},{2,18},{4,20},{6,22},{8,24},{10,26},{12,28},{14,30},{16,0},... | collective-permute-start | bytes 614408 | tf_op jit(solution)/shard_map/ppermute | solution.py:932
  (76 other events, 607.6 us)
Sparse Core Ops, SparseCore 0:
  207.9 58.5 all-gather.1
  309.4 25.4 reduce-scatter.4
  351.9 34.9 reduce-scatter.6
  389.1 39.3 reduce-scatter.8
  445.3 36.7 reduce-scatter.10

commit v5 on v4

--- a/solution.py
+++ b/solution.py
@@ -1363,9 +1363,9 @@
         )
         gene_sum = grid.scatter_low(gene_sum)
         table_got = grid.hop(table_sent, "c")
-        up_sums.add_first()
-        up_sums.one_in, mixed_back, two = sync(up_sums.one_in, mixed_back, two)
-        up_one = up_sums.go_first()
+        up_sums.add_parts()
+        *up_sums.parts, mixed_back, two = sync(*up_sums.parts, mixed_back, two)
+        up_one, up_more = up_sums.go_part(0), up_sums.go_part(1)
         qkv_back = attend_back(
             qkv_rows,
             segment,
@@ -1376,7 +1376,9 @@
         qkv_back, table_got = sync(qkv_back, table_got)
         down_sums.add_last((one_more, ()), two)
         down_sums.last()
-        qkv_back_low = qkv_back.reshape(token_count, 3 * D)
+        qkv_back, up_one = sync(tie(qkv_back, down_sums.last_in), up_one)
+        up_sums.add_second((up_one, ()))
+        qkv_back_low = tie(qkv_back, up_sums.two_in).reshape(token_count, 3 * D)
         attn_sums = Sums(grid)
         attn_sums.sent = weight_terms(
             where,
@@ -1384,10 +1386,9 @@
             (normed_low, tie(qkv_back_low, down_sums.last_in)),
             (mixed_low, attn_low),
         )
-        attn_sums.sent, qkv_back_low, up_one, gene_sum = sync(
-            attn_sums.sent, qkv_back_low, up_one, gene_sum
-        )
-        up_sums.add_second((up_one, (1,)))
+        attn_sums.sent, qkv_back_low, up_more, gene_sum = sync(
+            attn_sums.sent, qkv_back_low, up_more, gene_sum
+        )
         up_two = up_sums.go_second()
         attn_sums.core()
         attn_sums.own = weight_terms(
@@ -1401,7 +1402,7 @@
         table_got = grid.hop(table_sent, "z", 1)
         grad_normed = project_back(where, qkv_back_low, qkv_weights)
         grad_normed, down_sums.sum = sync(grad_normed, down_sums.sum)
-        up_sums.add_last((up_one, (0,)), up_two)
+        up_sums.add_last((up_more, ()), up_two)
         up_sums.last()
         grad_tokens, grad_gain_one, grad_shift_one = tokens_back(
             tie(grad_normed, up_sums.last_in), row_tokens, ln_gains[0], grad_middle

time: 501 us -> 500 us (level)
    pallas_call x8 -> x9, Pallas kernels: 30.9 us -> 35.5 us  [add_call(): pl.pallas_call(lambda *refs: add_kernel(len(groups), *refs), grid=(steps,...]
    ppermute x7 -> x8, waiting for transfers between devices: 24.1 us -> 22.1 us  [turn_hop(): return lax.ppermute(value, ('dp', 'query'), pairs)]
  transfers between devices with their start and end apart: 67 -> 68, of which waited for: 26 -> 26; matrix products, arithmetic and copies ran while one was open for 10% -> 10% of each run, Pallas kernels for 45% -> 45%
where the time goes in v5:
time: 500 us; the launch traced here: 495 us
  Pallas kernels  246 us (49%)
  waiting for transfers between devices  105 us (21%)
  starting transfers between devices  55.8 us (11%)
  local copies, waits for them, and re-layouts  32.6 us (7%)
  other arithmetic  28.2 us (6%)
  between operations  15.5 us (3%)
  matrix products  12.4 us (2%)
    pallas_call x3, Pallas kernels, feed_call(): pl.pallas_call(kernel, grid_spec=pltpu.PrefetchScalarGridSpec(num_scalar_...  56.6 us
    ppermute x33, waiting for transfers between devices, hop(): return lax.ppermute(value, 'dp', pairs)  45.1 us
    pallas_call x4, Pallas kernels, weight_terms(): pl.pallas_call(lambda *refs: term_kernel(len(pairs), mine, units, *refs),...  38.7 us
    pallas_call x9, Pallas kernels, add_call(): pl.pallas_call(lambda *refs: add_kernel(len(groups), *refs), grid=(steps,...  35.5 us
    ppermute x13, waiting for transfers between devices, hop(): return lax.ppermute(value, 'query', pairs)  27.6 us
    pallas_call x2, Pallas kernels, qkv_call(): pl.pallas_call(kernel, grid_spec=pltpu.PrefetchScalarGridSpec(num_scalar_...  23.8 us
    ppermute x8, waiting for transfers between devices, turn_hop(): return lax.ppermute(value, ('dp', 'query'), pairs)  22.1 us
    ppermute x33, starting transfers between devices, hop(): return lax.ppermute(value, 'dp', pairs)  20.5 us
  transfers between devices with their start and end apart: 68, of which 26 were waited for; matrix products, arithmetic and copies ran while one was open for 10% of the time, Pallas kernels for 45%

profile of v5, /device:TPU:0, one launch (start us, length us, event | category | flops | bytes accessed | tf_op | source)
XLA Modules:
  0.0 495.3 jit_solution(11101817524658546705)
XLA Ops:
  9.5 2.9 collective-permute-start
  23.1 3.5 collective-permute-done.1
  30.5 7.1 %collective-permute-done.3.refs_3_ = bf16[80,3840]{1,0:T(8,128)(2,1)S(1)} collective-permute-done((bf16[80,3840]{1,0:T(8,128)(2,1)}, bf16[80,3840]{1,0:T(8,128)(2,1)S(1)}, u32[]{:S(2)}, u32[]{:S(2)}) %collective-permute-start.3) | collective-permute-done | bytes 614432 | tf_op jit(solution)/shard_map/ppermute | solution.py:1095
  40.9 12.8 %collective-permute-done.6.refs_2_.refs_1_ = bf16[80,6400]{1,0:T(8,128)(2,1)S(1)} collective-permute-done((bf16[80,6400]{1,0:T(8,128)(2,1)S(1)}, bf16[80,6400]{1,0:T(8,128)(2,1)S(1)}, u32[]{:S(2)}, u32[]{:S(2)}) %collective-permute-start.6) | collective-permute-done | bytes 1024032 | tf_op jit(solution)/shard_map/ppermute | solution.py:926
  61.6 11.4 %shard_map.272 = bf16[512,3840]{1,0:T(8,128)(2,1)} custom-call(s32[4]{0:T(128)} %pad_add_fusion.1.place.refs_0_, bf16[512,1280]{1,0:T(8,128)(2,1)} %fusion.5.normed.refs_1_, f32[1,3840]{1,0:T(1,128)} %broadcast_in_dim.23.bias, bf16[640,3840]{1,0:T(8,128)(2,1)} %refs_0_.9, bf16[80,3840]{1,0:T(8,128)(2,1)} %collective-permute-done.refs_1_, ...), custom_call_target="tpu_custom_call" | custom-call | flops 1 | bytes 1 | tf_op jit(solution)/shard_map/pallas_call | solution.py:358
  76.6 13.3 %shard_map.273 = (bf16[1,512,1280]{2,1,0:T(8,128)(2,1)}, f32[1,5,4,512]{3,2,1,0:T(4,128)}) custom-call(s32[1,1,512]{2,1,0:T(1,128)} %bitcast.219, s32[1,512,1]{2,1,0:T(8,128)} %copy.41.segment_column, bf16[1,512,3840]{2,1,0:T(8,128)(2,1)} %bitcast.170, bf16[1,512,3840]{2,1,0:T(8,128)(2,1)} %bitcast.171, bf16[1,512,3840]{2,1,0:T(8,128)(2,1)} %bitcast.172), custom_call_target="tpu_custom_call" | custom-call | flops 1 | bytes 1 | tf_op jit(solution)/shard_map/pallas_call | solution.py:95
  92.4 5.3 %shard_map.274 = bf16[128,5120]{1,0:T(8,128)(2,1)} custom-call(bf16[128,640]{1,0:T(8,128)(2,1)} %constant_dynamic-slice_fusion.6.left, bf16[640,5120]{1,0:T(8,128)(2,1)} %right.3), custom_call_target="tpu_custom_call" | custom-call | flops 1 | bytes 1 | tf_op jit(solution)/shard_map/pallas_call | solution.py:714
  99.9 2.6 collective-permute-start.25
  105.0 3.4 shard_map.275.weight
  110.2 6.1 %shard_map.276 = (f32[512,1280]{1,0:T(8,128)}, bf16[512,1280]{1,0:T(8,128)(2,1)}) custom-call(bf16[512,1280]{1,0:T(8,128)(2,1)} %bitcast.190, bf16[1280,1280]{1,0:T(8,128)(2,1)} %copy-done.2, bf16[512,1280]{1,0:T(8,128)(2,1)} %bitcast.186, f32[1,1280]{1,0:T(1,128)} %get-tuple-element.341.bias, f32[1,1280]{1,0:T(1,128)} %get-tuple-element.349.gain, ...), custom_call_target="tpu_custom_call" | custom-call | flops 1 | bytes 1 | tf_op jit(solution)/shard_map/pallas_call | solution.py:693
  121.3 16.9 %shard_map.277 = (bf16[512,5120]{1,0:T(8,128)(2,1)}, bf16[512,5120]{1,0:T(8,128)(2,1)}) custom-call(s32[4]{0:T(128)} %pad_add_fusion.1.place.refs_0_, bf16[512,1280]{1,0:T(8,128)(2,1)} %get-tuple-element.186.second.refs_1_, f32[1,5120]{1,0:T(1,128)} %get-tuple-element.335.bias, bf16[640,5120]{1,0:T(8,128)(2,1)} %refs_0_.8, bf16[80,6400]{1,0:T(8,128)(2,1)} %copy-done.3, ...), custom_call_target="tpu_custom_call" | custom-call | flops 1 | bytes 1 | tf_op jit(solution)/shard_map/pallas_call | solution.py:415
  142.8 15.4 %shard_map.278 = (f32[512,1280]{1,0:T(8,128)}, bf16[4,1280]{1,0:T(4,128)(2,1)}) custom-call(s32[4]{0:T(128)} %pad_add_fusion.1.place.refs_0_, bf16[512,5120]{1,0:T(8,128)(2,1)} %get-tuple-element.192.active.left, f32[512,1280]{1,0:T(8,128)} %get-tuple-element.193.middle, f32[1,1280]{1,0:T(1,128)} %get-tuple-element.340.bias, bf16[4,512]{1,0:T(4,128)(2,1)} %fusion.32.picker, ...), custom_call_target="tpu_custom_call" | custom-call | flops 1 | bytes 1 | tf_op jit(solution)/shard_map/pallas_call | solution.py:415
  159.2 2.9 collective-permute-done.28
  169.0 4.4 shard_map.279
  174.4 3.7 collective-permute-done.30
  179.0 4.6 convolution_convert_fusion.5
  184.7 2.6 collective-permute-done.31
  191.3 15.8 %shard_map.280 = (bf16[2,2,4,320,640]{4,3,2,1,0:T(8,128)(2,1)}, bf16[2,2,4,320,640]{4,3,2,1,0:T(8,128)(2,1)}) custom-call(s32[4]{0:T(128)} %pad_add_fusion.1.place.refs_0_, bf16[512,5120]{1,0:T(8,128)(2,1)} %get-tuple-element.192.active.left, bf16[512,1280]{1,0:T(8,128)(2,1)} %get-tuple-element.275.right.branch), custom_call_target="tpu_custom_call" | custom-call | flops 1 | bytes 1 | tf_op jit(solution)/shard_map/pallas_call | solution.py:598
  212.1 24.3 %shard_map.281 = (bf16[512,5120]{1,0:T(8,128)(2,1)}, f32[1,5120]{1,0:T(1,128)}, f32[512,1280]{1,0:T(8,128)}) custom-call(s32[4]{0:T(128)} %pad_add_fusion.1.place.refs_0_, bf16[512,1280]{1,0:T(8,128)(2,1)} %get-tuple-element.275.right.branch, bf16[512,5120]{1,0:T(8,128)(2,1)} %get-tuple-element.209.slope, bf16[640,5120]{1,0:T(8,128)(2,1)} %refs_0_.8, ...), custom_call_target="tpu_custom_call" | custom-call | flops 1 | bytes 1 | tf_op jit(solution)/shard_map/pallas_call | solution.py:415
  236.4 4.4 shard_map.282
  242.8 8.9 %shard_map.283 = (f32[512,1280]{1,0:T(8,128)}, bf16[512,1280]{1,0:T(8,128)(2,1)}, bf16[512,1280]{1,0:T(8,128)(2,1)}, f32[1,1280]{1,0:T(1,128)}, f32[1,1280]{1,0:T(1,128)}) custom-call(f32[512,1280]{1,0:T(8,128)} %get-tuple-element.218.grad, f32[512,1280]{1,0:T(8,128)} %get-tuple-element.193.middle, f32[1,1280]{1,0:T(1,128)} %get-tuple-element.349.gain, ...), custom_call_target="tpu_custom_call" | custom-call | flops 1 | bytes 1 | tf_op jit(solution)/shard_map/pallas_call | solution.py:804
  254.6 9.2 %shard_map.284 = bf16[2,2,320,2560]{3,2,1,0:T(8,128)(2,1)} custom-call(s32[4]{0:T(128)} %pad_add_fusion.1.place.refs_0_, bf16[512,1280]{1,0:T(8,128)(2,1)} %get-tuple-element.186.second.refs_1_, bf16[512,5120]{1,0:T(8,128)(2,1)} %get-tuple-element.223.refs_2_.refs_3_, bf16[512,5120]{1,0:T(8,128)(2,1)} %get-tuple-element.223.refs_2_.refs_3_), custom_call_target="tpu_custom_call" | custom-call | flops 1 | bytes 1 | tf_op jit(solution)/shard_map/pallas_call | solution.py:549
  263.8 9.7 %shard_map.285.refs_0_.refs_2_ = bf16[2,2,320,2560]{3,2,1,0:T(8,128)(2,1)} custom-call(s32[4]{0:T(128)} %pad_add_fusion.1.place.refs_0_, bf16[512,1280]{1,0:T(8,128)(2,1)} %get-tuple-element.186.second.refs_1_, bf16[512,5120]{1,0:T(8,128)(2,1)} %get-tuple-element.223.refs_2_.refs_3_, bf16[512,5120]{1,0:T(8,128)(2,1)} %get-tuple-element.223.refs_2_.refs_3_), custom_call_target="tpu_custom_call" | custom-call | flops 1 | bytes 1 | tf_op jit(solution)/shard_map/pallas_call | solution.py:549
  273.5 6.2 %collective-permute-done.36.refs_2_ = bf16[1280,640]{1,0:T(8,128)(2,1)} collective-permute-done((bf16[1280,640]{1,0:T(8,128)(2,1)}, bf16[1280,640]{1,0:T(8,128)(2,1)}, u32[]{:S(2)}, u32[]{:S(2)}) %collective-permute-start.36) | collective-permute-done | bytes 1638432 | tf_op jit(solution)/shard_map/ppermute | solution.py:945
  279.7 3.4 collective-permute-start.38
  284.9 3.6 shard_map.286
  289.7 3.0 shard_map.287
  292.7 5.9 %shard_map.288 = bf16[128,640]{1,0:T(8,128)(2,1)} custom-call(bf16[128,5120]{1,0:T(8,128)(2,1)} %copy-done.9, bf16[640,5120]{1,0:T(8,128)(2,1)} %right.3), custom_call_target="tpu_custom_call" | custom-call | flops 1 | bytes 1 | tf_op jit(solution)/shard_map/pallas_call | solution.py:748
  300.4 4.5 shard_map.289
  304.9 5.0 %collective-permute-done.39.refs_3_ = bf16[1280,640]{1,0:T(8,128)(2,1)} collective-permute-done((bf16[1280,640]{1,0:T(8,128)(2,1)}, bf16[1280,640]{1,0:T(8,128)(2,1)}, u32[]{:S(2)}, u32[]{:S(2)}) %collective-permute-start.39) | collective-permute-done | bytes 1638432 | tf_op jit(solution)/shard_map/ppermute | solution.py:945
  312.0 18.9 %shard_map.290 = bf16[1,512,3840]{2,1,0:T(8,128)(2,1)} custom-call(s32[1,1,512]{2,1,0:T(1,128)} %bitcast.220, s32[1,512,1]{2,1,0:T(8,128)} %copy.41.segment_column, bf16[1,512,3840]{2,1,0:T(8,128)(2,1)} %bitcast.173, bf16[1,512,3840]{2,1,0:T(8,128)(2,1)} %bitcast.174, bf16[1,512,3840]{2,1,0:T(8,128)(2,1)} %bitcast.175, ...), custom_call_target="tpu_custom_call" | custom-call | flops 1 | bytes 1 | tf_op jit(solution)/shard_map/pallas_call | solution.py:161
  330.8 4.3 shard_map.291
  335.2 3.6 shard_map.292
  338.7 9.8 %shard_map.293 = bf16[2,2,320,2560]{3,2,1,0:T(8,128)(2,1)} custom-call(s32[4]{0:T(128)} %pad_add_fusion.1.place.refs_0_, bf16[512,1280]{1,0:T(8,128)(2,1)} %fusion.5.normed.refs_1_, bf16[512,1280]{1,0:T(8,128)(2,1)} %bitcast.191, bf16[512,3840]{1,0:T(8,128)(2,1)} %bitcast.176, bf16[512,3840]{1,0:T(8,128)(2,1)} %bitcast.177, ...), custom_call_target="tpu_custom_call" | custom-call | flops 1 | bytes 1 | tf_op jit(solution)/shard_map/pallas_call | solution.py:549
  350.3 10.0 %shard_map.294.own.refs_0_ = bf16[2,2,320,2560]{3,2,1,0:T(8,128)(2,1)} custom-call(s32[4]{0:T(128)} %pad_add_fusion.1.place.refs_0_, bf16[512,1280]{1,0:T(8,128)(2,1)} %fusion.5.normed.refs_1_, bf16[512,1280]{1,0:T(8,128)(2,1)} %bitcast.192, bf16[512,3840]{1,0:T(8,128)(2,1)} %bitcast.178, bf16[512,3840]{1,0:T(8,128)(2,1)} %bitcast.179, ...), custom_call_target="tpu_custom_call" | custom-call | flops 1 | bytes 1 | tf_op jit(solution)/shard_map/pallas_call | solution.py:549
  360.3 4.6 shard_map.295
  364.9 5.6 %collective-permute-done.44.refs_3_ = bf16[320,2560]{1,0:T(8,128)(2,1)} collective-permute-done((bf16[320,2560]{1,0:T(8,128)(2,1)}, bf16[320,2560]{1,0:T(8,128)(2,1)}, u32[]{:S(2)}, u32[]{:S(2)}) %collective-permute-start.44) | collective-permute-done | bytes 1638432 | tf_op jit(solution)/shard_map/ppermute | solution.py:945
  372.1 4.2 shard_map.297
  377.9 12.4 %shard_map.296.grad = f32[512,1280]{1,0:T(8,128)} custom-call(s32[4]{0:T(128)} %pad_add_fusion.1.place.refs_0_, bf16[512,3840]{1,0:T(8,128)(2,1)} %bitcast.180, bf16[640,3840]{1,0:T(8,128)(2,1)} %refs_0_.9, bf16[80,3840]{1,0:T(8,128)(2,1)} %collective-permute-done.refs_1_, bf16[80,3840]{1,0:T(8,128)(2,1)} %copy-done.16, bf16[80,3840]{1,0:T(8,128)(2,1)} %copy-done.17, ...), custom_call_target="tpu_custom_call" | custom-call | flops 1 | bytes 1 | tf_op jit(solution)/shard_map/pallas_call | solution.py:358
  391.9 5.2 %shard_map.298 = (f32[512,1280]{1,0:T(8,128)}, f32[1,1280]{1,0:T(1,128)}, f32[1,1280]{1,0:T(1,128)}) custom-call(f32[512,1280]{1,0:T(8,128)} %shard_map.296.grad, bf16[512,1280]{1,0:T(8,128)(2,1)} %bitcast.187, f32[1,1280]{1,0:T(1,128)} %get-tuple-element.347.gain, f32[512,1280]{1,0:T(8,128)} %get-tuple-element.261.flat), custom_call_target="tpu_custom_call" | custom-call | flops 1 | bytes 1 | tf_op jit(solution)/shard_map/pallas_call | solution.py:833
  399.0 13.6 %collective-permute-done.46 = bf16[2,2,2,32,640]{4,3,2,1,0:T(8,128)(2,1)S(1)} collective-permute-done((bf16[2,2,2,32,640]{4,3,2,1,0:T(8,128)(2,1)S(1)}, bf16[2,2,2,32,640]{4,3,2,1,0:T(8,128)(2,1)S(1)}, u32[]{:S(2)}, u32[]{:S(2)}) %collective-permute-start.46) | collective-permute-done | bytes 327712 | tf_op jit(solution)/shard_map/ppermute | solution.py:932
  413.4 3.7 shard_map.299
  418.9 3.0 convert_reduce_fusion
  426.9 6.7 %collective-permute-done.48 = bf16[1,2,2,32,640]{4,3,2,1,0:T(8,128)(2,1)S(1)} collective-permute-done((bf16[1,2,2,32,640]{4,3,2,1,0:T(8,128)(2,1)S(1)}, bf16[1,2,2,32,640]{4,3,2,1,0:T(8,128)(2,1)S(1)}, u32[]{:S(2)}, u32[]{:S(2)}) %collective-permute-start.48) | collective-permute-done | bytes 163872 | tf_op jit(solution)/shard_map/ppermute | solution.py:932
  433.7 4.8 collective-permute-done.49.refs_3_
  439.6 4.2 shard_map.300
  448.8 4.4 collective-permute-done.52
  470.1 14.1 %collective-permute-done.62 = bf16[40,2560]{1,0:T(8,128)(2,1)S(1)} collective-permute-done((bf16[40,2560]{1,0:T(8,128)(2,1)S(1)}, bf16[40,2560]{1,0:T(8,128)(2,1)S(1)}, u32[]{:S(2)}, u32[]{:S(2)}) %collective-permute-start.62) | collective-permute-done | bytes 204832 | tf_op jit(solution)/shard_map/ppermute | solution.py:932
  (370 shorter events, 123.7 us)
Async XLA Ops:
  7.2 266.3 %all-gather.2.cloned.1.call-start = ((), (), s32[]{:S(2)}) async-start(), calls=%async_computation.4 | async-start | bytes 1740800 | tf_op jit(solution)/shard_map/all_gather | solution.py:1309
  9.5 17.6 %collective-permute-start = (bf16[80,3840]{1,0:T(8,128)(2,1)}, bf16[80,3840]{1,0:T(8,128)(2,1)}, u32[]{:S(2)}, u32[]{:S(2)}) collective-permute-start(bf16[80,3840]{1,0:T(8,128)(2,1)} %constant_dynamic-slice_fusion.10), channel_id=1, source_target_pairs={{0,1},{1,0},{2,3},{3,2},{4,5},{5,4},{6,7},{7,6},{8,9},{9,8},{10,11... | collective-permute-start | bytes 1843208 | tf_op jit(solution)/shard_map/ppermute | solution.py:926
  13.2 13.4 %collective-permute-start.1 = (s32[1,64]{1,0:T(1,128)S(1)}, s32[1,64]{1,0:T(1,128)S(1)}, u32[]{:S(2)}, u32[]{:S(2)}) collective-permute-start(s32[1,64]{1,0:T(1,128)S(1)} %reshape.329), channel_id=1, source_target_pairs={{0,1},{1,0},{2,3},{3,2},{4,5},{5,4},{6,7},{7,6},{8,9},{9,8},{10,11... | collective-permute-start | bytes 776 | tf_op jit(solution)/shard_map/ppermute | solution.py:926
  27.2 10.4 %collective-permute-start.3 = (bf16[80,3840]{1,0:T(8,128)(2,1)}, bf16[80,3840]{1,0:T(8,128)(2,1)S(1)}, u32[]{:S(2)}, u32[]{:S(2)}) collective-permute-start(bf16[80,3840]{1,0:T(8,128)(2,1)} %collective-permute-done.refs_1_), channel_id=1, source_target_pairs={{0,4},{2,10},{4,0},{6,14},{8,12},{10,2},{12,8},{14,6},{16,20},{18,... | collective-permute-start | bytes 1843208 | tf_op jit(solution)/shard_map/ppermute | solution.py:1095
  29.0 24.7 %collective-permute-start.6 = (bf16[80,6400]{1,0:T(8,128)(2,1)S(1)}, bf16[80,6400]{1,0:T(8,128)(2,1)S(1)}, u32[]{:S(2)}, u32[]{:S(2)}) collective-permute-start(bf16[80,6400]{1,0:T(8,128)(2,1)S(1)} %copy-done.30), channel_id=1, source_target_pairs={{0,1},{1,0},{2,3},{3,2},{4,5},{5,4},{6,7},{7,6},{8,9},{9,8},{10,11... | collective-permute-start | bytes 3072008 | tf_op jit(solution)/shard_map/ppermute | solution.py:926
  37.6 16.6 %collective-permute-start.4 = (bf16[80,3840]{1,0:T(8,128)(2,1)S(1)}, bf16[80,3840]{1,0:T(8,128)(2,1)S(1)}, u32[]{:S(2)}, u32[]{:S(2)}) collective-permute-start(bf16[80,3840]{1,0:T(8,128)(2,1)S(1)} %collective-permute-done.2.refs_2_), channel_id=1, source_target_pairs={{0,4},{2,10},{4,0},{6,14},{8,12},{10,2},{12,8},{14,6},{16,20},{18,... | collective-permute-start | bytes 1843208 | tf_op jit(solution)/shard_map/ppermute | solution.py:1095
  39.4 14.8 %collective-permute-start.5 = (bf16[80,3840]{1,0:T(8,128)(2,1)S(1)}, bf16[80,3840]{1,0:T(8,128)(2,1)S(1)}, u32[]{:S(2)}, u32[]{:S(2)}) collective-permute-start(bf16[80,3840]{1,0:T(8,128)(2,1)S(1)} %collective-permute-done.3.refs_3_), channel_id=1, source_target_pairs={{0,8},{2,6},{4,12},{6,2},{8,0},{10,14},{12,4},{14,10},{16,24},{18,... | collective-permute-start | bytes 1843208 | tf_op jit(solution)/shard_map/ppermute | solution.py:1095
  40.9 15.7 %collective-permute-start.7 = (bf16[80,3840]{1,0:T(8,128)(2,1)S(1)}, bf16[80,3840]{1,0:T(8,128)(2,1)S(1)}, u32[]{:S(2)}, u32[]{:S(2)}) collective-permute-start(bf16[80,3840]{1,0:T(8,128)(2,1)S(1)} %collective-permute-done.3.refs_3_), channel_id=1, source_target_pairs={{0,2},{2,0},{4,6},{6,4},{8,10},{10,8},{12,14},{14,12},{16,18},{18,... | collective-permute-start | bytes 1843208 | tf_op jit(solution)/shard_map/ppermute | solution.py:932
  54.2 18.9 %collective-permute-start.10 = (bf16[80,6400]{1,0:T(8,128)(2,1)S(1)}, bf16[80,6400]{1,0:T(8,128)(2,1)S(1)}, u32[]{:S(2)}, u32[]{:S(2)}) collective-permute-start(bf16[80,6400]{1,0:T(8,128)(2,1)S(1)} %collective-permute-done.6.refs_2_.refs_1_), channel_id=1, source_target_pairs={{0,2},{2,0},{4,6},{6,4},{8,10},{10,8},{12,14},{14,12},{16,18},{18,... | collective-permute-start | bytes 3072008 | tf_op jit(solution)/shard_map/ppermute | solution.py:932
  54.3 18.8 %collective-permute-start.11 = (bf16[80,6400]{1,0:T(8,128)(2,1)S(1)}, bf16[80,6400]{1,0:T(8,128)(2,1)S(1)}, u32[]{:S(2)}, u32[]{:S(2)}) collective-permute-start(bf16[80,6400]{1,0:T(8,128)(2,1)S(1)} %collective-permute-done.6.refs_2_.refs_1_), channel_id=1, source_target_pairs={{0,4},{2,10},{4,0},{6,14},{8,12},{10,2},{12,8},{14,6},{16,20},{18,... | collective-permute-start | bytes 3072008 | tf_op jit(solution)/shard_map/ppermute | solution.py:1095
  56.7 16.4 %collective-permute-start.12 = (bf16[128,1280]{1,0:T(8,128)(2,1)S(1)}, bf16[128,1280]{1,0:T(8,128)(2,1)}, u32[]{:S(2)}, u32[]{:S(2)}) collective-permute-start(bf16[128,1280]{1,0:T(8,128)(2,1)S(1)} %convolution_convert_fusion.3), channel_id=1, source_target_pairs={{0,1},{1,0},{2,3},{3,2},{4,5},{5,4},{6,7},{7,6},{8,9},{9,8},{10,11... | collective-permute-start | bytes 983048 | tf_op jit(solution)/shard_map/ppermute | solution.py:926
  73.1 24.8 %collective-permute-start.13 = (bf16[80,6400]{1,0:T(8,128)(2,1)S(1)}, bf16[80,6400]{1,0:T(8,128)(2,1)}, u32[]{:S(2)}, u32[]{:S(2)}) collective-permute-start(bf16[80,6400]{1,0:T(8,128)(2,1)S(1)} %collective-permute-done.10.refs_3_.refs_2_), channel_id=1, source_target_pairs={{0,4},{2,10},{4,0},{6,14},{8,12},{10,2},{12,8},{14,6},{16,20},{18,... | collective-permute-start | bytes 3072008 | tf_op jit(solution)/shard_map/ppermute | solution.py:1095
  73.7 24.2 %collective-permute-start.14 = (bf16[80,6400]{1,0:T(8,128)(2,1)S(1)}, bf16[80,6400]{1,0:T(8,128)(2,1)}, u32[]{:S(2)}, u32[]{:S(2)}) collective-permute-start(bf16[80,6400]{1,0:T(8,128)(2,1)S(1)} %collective-permute-done.11.refs_4_.refs_3_), channel_id=1, source_target_pairs={{0,8},{2,6},{4,12},{6,2},{8,0},{10,14},{12,4},{14,10},{16,24},{18,... | collective-permute-start | bytes 3072008 | tf_op jit(solution)/shard_map/ppermute | solution.py:1095
  74.9 23.0 %collective-permute-start.15 = (bf16[80,6400]{1,0:T(8,128)(2,1)S(1)}, bf16[80,6400]{1,0:T(8,128)(2,1)}, u32[]{:S(2)}, u32[]{:S(2)}) collective-permute-start(bf16[80,6400]{1,0:T(8,128)(2,1)S(1)} %collective-permute-done.11.refs_4_.refs_3_), channel_id=1, source_target_pairs={{0,2},{2,0},{4,6},{6,4},{8,10},{10,8},{12,14},{14,12},{16,18},{18,... | collective-permute-start | bytes 3072008 | tf_op jit(solution)/shard_map/ppermute | solution.py:932
  75.0 22.8 %collective-permute-start.16 = (bf16[320,1280]{1,0:T(8,128)(2,1)}, bf16[320,1280]{1,0:T(8,128)(2,1)}, u32[]{:S(2)}, u32[]{:S(2)}) collective-permute-start(bf16[320,1280]{1,0:T(8,128)(2,1)} %constant_dynamic-slice_fusion.7), channel_id=1, source_target_pairs={{0,1},{1,0},{2,3},{3,2},{4,5},{5,4},{6,7},{7,6},{8,9},{9,8},{10,11... | collective-permute-start | bytes 2457608 | tf_op jit(solution)/shard_map/ppermute | solution.py:926
  98.0 7.0 %collective-permute-start.17 = (bf16[80,6400]{1,0:T(8,128)(2,1)}, bf16[80,6400]{1,0:T(8,128)(2,1)}, u32[]{:S(2)}, u32[]{:S(2)}) collective-permute-start(bf16[80,6400]{1,0:T(8,128)(2,1)} %collective-permute-done.13.refs_5_.refs_4_), channel_id=1, source_target_pairs={{0,2},{2,0},{4,6},{6,4},{8,10},{10,8},{12,14},{14,12},{16,18},{18,... | collective-permute-start | bytes 3072008 | tf_op jit(solution)/shard_map/ppermute | solution.py:932
  98.0 6.9 %collective-permute-start.18 = (bf16[80,6400]{1,0:T(8,128)(2,1)}, bf16[80,6400]{1,0:T(8,128)(2,1)}, u32[]{:S(2)}, u32[]{:S(2)}) collective-permute-start(bf16[80,6400]{1,0:T(8,128)(2,1)} %collective-permute-done.14.refs_6_.refs_5_), channel_id=1, source_target_pairs={{0,2},{2,0},{4,6},{6,4},{8,10},{10,8},{12,14},{14,12},{16,18},{18,... | collective-permute-start | bytes 3072008 | tf_op jit(solution)/shard_map/ppermute | solution.py:932
  98.5 17.8 %collective-permute-start.19 = (bf16[320,1280]{1,0:T(8,128)(2,1)}, bf16[320,1280]{1,0:T(8,128)(2,1)}, u32[]{:S(2)}, u32[]{:S(2)}) collective-permute-start(bf16[320,1280]{1,0:T(8,128)(2,1)} %collective-permute-done.16.refs_1_.refs_10_), channel_id=1, source_target_pairs={{0,2},{2,0},{4,6},{6,4},{8,10},{10,8},{12,14},{14,12},{16,18},{18,... | collective-permute-start | bytes 2457608 | tf_op jit(solution)/shard_map/ppermute | solution.py:932
  98.5 17.7 %collective-permute-start.20 = (bf16[320,1280]{1,0:T(8,128)(2,1)}, bf16[320,1280]{1,0:T(8,128)(2,1)}, u32[]{:S(2)}, u32[]{:S(2)}) collective-permute-start(bf16[320,1280]{1,0:T(8,128)(2,1)} %collective-permute-done.16.refs_1_.refs_10_), channel_id=1, source_target_pairs={{0,4},{2,10},{4,0},{6,14},{8,12},{10,2},{12,8},{14,6},{16,20},{18,... | collective-permute-start | bytes 2457608 | tf_op jit(solution)/shard_map/ppermute | solution.py:1095
  99.9 38.3 %collective-permute-start.25 = (bf16[128,1280]{1,0:T(8,128)(2,1)}, bf16[128,1280]{1,0:T(8,128)(2,1)}, u32[]{:S(2)}, u32[]{:S(2)}) collective-permute-start(bf16[128,1280]{1,0:T(8,128)(2,1)} %copy-done.23), channel_id=1, source_target_pairs={{0,16},{2,18},{4,20},{6,22},{8,24},{10,26},{12,28},{14,30},{16,0},... | collective-permute-start | bytes 983048 | tf_op jit(solution)/shard_map/ppermute | solution.py:932
  116.3 22.0 %collective-permute-start.22 = (bf16[320,1280]{1,0:T(8,128)(2,1)}, bf16[320,1280]{1,0:T(8,128)(2,1)S(1)}, u32[]{:S(2)}, u32[]{:S(2)}) collective-permute-start(bf16[320,1280]{1,0:T(8,128)(2,1)} %collective-permute-done.20.refs_3_.refs_12_), channel_id=1, source_target_pairs={{0,8},{2,6},{4,12},{6,2},{8,0},{10,14},{12,4},{14,10},{16,24},{18,... | collective-permute-start | bytes 2457608 | tf_op jit(solution)/shard_map/ppermute | solution.py:1095
  117.4 20.9 %collective-permute-start.23 = (bf16[320,1280]{1,0:T(8,128)(2,1)}, bf16[320,1280]{1,0:T(8,128)(2,1)S(1)}, u32[]{:S(2)}, u32[]{:S(2)}) collective-permute-start(bf16[320,1280]{1,0:T(8,128)(2,1)} %collective-permute-done.20.refs_3_.refs_12_), channel_id=1, source_target_pairs={{0,2},{2,0},{4,6},{6,4},{8,10},{10,8},{12,14},{14,12},{16,18},{18,... | collective-permute-start | bytes 2457608 | tf_op jit(solution)/shard_map/ppermute | solution.py:932
  118.5 19.8 %collective-permute-start.21 = (bf16[320,1280]{1,0:T(8,128)(2,1)}, bf16[320,1280]{1,0:T(8,128)(2,1)S(1)}, u32[]{:S(2)}, u32[]{:S(2)}) collective-permute-start(bf16[320,1280]{1,0:T(8,128)(2,1)} %collective-permute-done.19.refs_2_.refs_11_), channel_id=1, source_target_pairs={{0,4},{2,10},{4,0},{6,14},{8,12},{10,2},{12,8},{14,6},{16,20},{18,... | collective-permute-start | bytes 2457608 | tf_op jit(solution)/shard_map/ppermute | solution.py:1095
  119.3 19.0 %collective-permute-start.24 = (bf16[64,5120]{1,0:T(8,128)(2,1)}, bf16[64,5120]{1,0:T(8,128)(2,1)S(1)}, u32[]{:S(2)}, u32[]{:S(2)}) collective-permute-start(bf16[64,5120]{1,0:T(8,128)(2,1)} %get-tuple-element.191), channel_id=1, source_target_pairs={{0,1},{1,0},{2,3},{3,2},{4,5},{5,4},{6,7},{7,6},{8,9},{9,8},{10,11... | collective-permute-start | bytes 1966088 | tf_op jit(solution)/shard_map/ppermute | solution.py:926
  190.4 16.8 %collective-permute-start.32 = (bf16[8,8,5120]{2,1,0:T(8,128)(2,1)S(1)}, bf16[8,8,5120]{2,1,0:T(8,128)(2,1)S(1)}, u32[]{:S(2)}, u32[]{:S(2)}) collective-permute-start(bf16[8,8,5120]{2,1,0:T(8,128)(2,1)S(1)} %bitcast.208), channel_id=1, source_target_pairs={{0,1},{1,0},{2,3},{3,2},{4,5},{5,4},{6,7},{7,6},{8,9},{9,8},{10,11... | collective-permute-start | bytes 1966088 | tf_op jit(solution)/shard_map/ppermute | solution.py:926
  207.2 29.2 %collective-permute-start.33 = (bf16[2,2,1280,640]{3,2,1,0:T(8,128)(2,1)}, bf16[2,2,1280,640]{3,2,1,0:T(8,128)(2,1)}, u32[]{:S(2)}, u32[]{:S(2)}) collective-permute-start(bf16[2,2,1280,640]{3,2,1,0:T(8,128)(2,1)} %bitcast.224), channel_id=1, source_target_pairs={{0,2},{2,0},{4,6},{6,4},{8,10},{10,8},{12,14},{14,12},{16,18},{18,... | collective-permute-start | bytes 19660808 | tf_op jit(solution)/shard_map/ppermute | solution.py:932
  207.9 141.0 %reduce-scatter.5.cloned.1.call-start = ((), (), s32[]{:S(2)}) async-start(), calls=%async_computation.5 | async-start | bytes 2457600 | tf_op jit(solution)/shard_map/reduce_scatter | solution.py:1060
  209.1 42.5 %collective-permute-start.34 = (bf16[128,2560]{1,0:T(8,128)(2,1)}, bf16[128,2560]{1,0:T(8,128)(2,1)}, u32[]{:S(2)}, u32[]{:S(2)}) collective-permute-start(bf16[128,2560]{1,0:T(8,128)(2,1)} %broadcast_select_fusion.5), channel_id=1, source_target_pairs={{0,16},{2,18},{4,20},{6,22},{8,24},{10,26},{12,28},{14,30},{16,0},... | collective-permute-start | bytes 1966088 | tf_op jit(solution)/shard_map/ppermute | solution.py:932
  240.8 32.8 %collective-permute-start.35 = (bf16[1280,640]{1,0:T(8,128)(2,1)}, bf16[1280,640]{1,0:T(8,128)(2,1)}, u32[]{:S(2)}, u32[]{:S(2)}) collective-permute-start(bf16[1280,640]{1,0:T(8,128)(2,1)} %get-tuple-element.216), channel_id=1, source_target_pairs={{0,1},{1,0},{2,6},{3,7},{4,5},{5,4},{6,2},{7,3},{8,9},{9,8},{10,14... | collective-permute-start | bytes 4915208 | tf_op jit(solution)/shard_map/ppermute | solution.py:945
  242.4 37.3 %collective-permute-start.36 = (bf16[1280,640]{1,0:T(8,128)(2,1)}, bf16[1280,640]{1,0:T(8,128)(2,1)}, u32[]{:S(2)}, u32[]{:S(2)}) collective-permute-start(bf16[1280,640]{1,0:T(8,128)(2,1)} %get-tuple-element.217), channel_id=1, source_target_pairs={{0,1},{1,0},{2,6},{3,7},{4,5},{5,4},{6,2},{7,3},{8,9},{9,8},{10,14... | collective-permute-start | bytes 4915208 | tf_op jit(solution)/shard_map/ppermute | solution.py:945
  254.6 25.1 %collective-permute-start.37 = (bf16[640,1280]{1,0:T(8,128)(2,1)}, bf16[640,1280]{1,0:T(8,128)(2,1)}, u32[]{:S(2)}, u32[]{:S(2)}) collective-permute-start(bf16[640,1280]{1,0:T(8,128)(2,1)} %convolution_convert_fusion.2), channel_id=1, source_target_pairs={{0,2},{2,0},{4,6},{6,4},{8,10},{10,8},{12,14},{14,12},{16,18},{18,... | collective-permute-start | bytes 4915208 | tf_op jit(solution)/shard_map/ppermute | solution.py:932
  279.7 20.6 %collective-permute-start.38 = (bf16[2,2,320,2560]{3,2,1,0:T(8,128)(2,1)}, bf16[2,2,320,2560]{3,2,1,0:T(8,128)(2,1)}, u32[]{:S(2)}, u32[]{:S(2)}) collective-permute-start(bf16[2,2,320,2560]{3,2,1,0:T(8,128)(2,1)} %shard_map.284), channel_id=1, source_target_pairs={{0,2},{2,0},{4,6},{6,4},{8,10},{10,8},{12,14},{14,12},{16,18},{18,... | collective-permute-start | bytes 19660808 | tf_op jit(solution)/shard_map/ppermute | solution.py:932
  288.5 21.4 %collective-permute-start.39 = (bf16[1280,640]{1,0:T(8,128)(2,1)}, bf16[1280,640]{1,0:T(8,128)(2,1)}, u32[]{:S(2)}, u32[]{:S(2)}) collective-permute-start(bf16[1280,640]{1,0:T(8,128)(2,1)} %shard_map.286), channel_id=1, source_target_pairs={{0,4},{1,5},{2,3},{3,2},{4,0},{5,1},{6,7},{7,6},{8,12},{9,13},{10,... | collective-permute-start | bytes 4915208 | tf_op jit(solution)/shard_map/ppermute | solution.py:945
  300.3 89.9 %reduce-scatter.7.cloned.1.call-start = ((), (), s32[]{:S(2)}) async-start(), calls=%async_computation.6 | async-start | bytes 2048000 | tf_op jit(solution)/shard_map/reduce_scatter | solution.py:1049
  310.0 25.2 %collective-permute-start.41 = (bf16[320,2560]{1,0:T(8,128)(2,1)}, bf16[320,2560]{1,0:T(8,128)(2,1)}, u32[]{:S(2)}, u32[]{:S(2)}) collective-permute-start(bf16[320,2560]{1,0:T(8,128)(2,1)} %get-tuple-element.242), channel_id=1, source_target_pairs={{0,1},{1,0},{2,6},{3,7},{4,5},{5,4},{6,2},{7,3},{8,9},{9,8},{10,14... | collective-permute-start | bytes 4915208 | tf_op jit(solution)/shard_map/ppermute | solution.py:945
  311.6 37.3 %collective-permute-start.42 = (bf16[320,2560]{1,0:T(8,128)(2,1)}, bf16[320,2560]{1,0:T(8,128)(2,1)}, u32[]{:S(2)}, u32[]{:S(2)}) collective-permute-start(bf16[320,2560]{1,0:T(8,128)(2,1)} %get-tuple-element.248), channel_id=1, source_target_pairs={{0,1},{1,0},{2,6},{3,7},{4,5},{5,4},{6,2},{7,3},{8,9},{9,8},{10,14... | collective-permute-start | bytes 4915208 | tf_op jit(solution)/shard_map/ppermute | solution.py:945
  312.0 23.2 %collective-permute-start.40 = (bf16[4,2,2,32,640]{4,3,2,1,0:T(8,128)(2,1)S(1)}, bf16[4,2,2,32,640]{4,3,2,1,0:T(8,128)(2,1)S(1)}, u32[]{:S(2)}, u32[]{:S(2)}) collective-permute-start(bf16[4,2,2,32,640]{4,3,2,1,0:T(8,128)(2,1)S(1)} %get-tuple-element.237), channel_id=1, source_target_pairs={{0,2},{2,0},{4,6},{6,4},{8,10},{10,8},{12,14},{14,12},{16,18},{18,... | collective-permute-start | bytes 1966088 | tf_op jit(solution)/shard_map/ppermute | solution.py:932
  348.9 11.4 %collective-permute-start.43 = (bf16[2,2,320,2560]{3,2,1,0:T(8,128)(2,1)}, bf16[2,2,320,2560]{3,2,1,0:T(8,128)(2,1)}, u32[]{:S(2)}, u32[]{:S(2)}) collective-permute-start(bf16[2,2,320,2560]{3,2,1,0:T(8,128)(2,1)} %shard_map.293), channel_id=1, source_target_pairs={{0,2},{2,0},{4,6},{6,4},{8,10},{10,8},{12,14},{14,12},{16,18},{18,... | collective-permute-start | bytes 19660808 | tf_op jit(solution)/shard_map/ppermute | solution.py:932
  349.1 21.4 %collective-permute-start.44 = (bf16[320,2560]{1,0:T(8,128)(2,1)}, bf16[320,2560]{1,0:T(8,128)(2,1)}, u32[]{:S(2)}, u32[]{:S(2)}) collective-permute-start(bf16[320,2560]{1,0:T(8,128)(2,1)} %shard_map.292), channel_id=1, source_target_pairs={{0,4},{1,5},{2,3},{3,2},{4,0},{5,1},{6,7},{7,6},{8,12},{9,13},{10,... | collective-permute-start | bytes 4915208 | tf_op jit(solution)/shard_map/ppermute | solution.py:945
  350.3 76.7 %reduce-scatter.9.cloned.1.call-start = ((), (), s32[]{:S(2)}) async-start(), calls=%async_computation.7 | async-start | bytes 2048000 | tf_op jit(solution)/shard_map/reduce_scatter | solution.py:1049
  370.5 42.2 %collective-permute-start.45 = (bf16[2,320,2560]{2,1,0:T(8,128)(2,1)}, bf16[2,320,2560]{2,1,0:T(8,128)(2,1)}, u32[]{:S(2)}, u32[]{:S(2)}) collective-permute-start(bf16[2,320,2560]{2,1,0:T(8,128)(2,1)} %shard_map.295), channel_id=1, source_target_pairs={{0,1},{1,0},{2,6},{3,7},{4,5},{5,4},{6,2},{7,3},{8,9},{9,8},{10,14... | collective-permute-start | bytes 9830408 | tf_op jit(solution)/shard_map/ppermute | solution.py:945
  376.4 107.9 %reduce-scatter.11.cloned.1.call-start = ((), (), s32[]{:S(2)}) async-start(), calls=%async_computation.8 | async-start | bytes 2048000 | tf_op jit(solution)/shard_map/reduce_scatter | solution.py:1049
  390.5 22.2 %collective-permute-start.46 = (bf16[2,2,2,32,640]{4,3,2,1,0:T(8,128)(2,1)S(1)}, bf16[2,2,2,32,640]{4,3,2,1,0:T(8,128)(2,1)S(1)}, u32[]{:S(2)}, u32[]{:S(2)}) collective-permute-start(bf16[2,2,2,32,640]{4,3,2,1,0:T(8,128)(2,1)S(1)} %get-tuple-element.319), channel_id=1, source_target_pairs={{0,8},{2,10},{4,12},{6,14},{8,0},{10,2},{12,4},{14,6},{16,24},{18,... | collective-permute-start | bytes 983048 | tf_op jit(solution)/shard_map/ppermute | solution.py:932
  417.1 21.3 %collective-permute-start.49 = (bf16[320,2560]{1,0:T(8,128)(2,1)}, bf16[320,2560]{1,0:T(8,128)(2,1)S(1)}, u32[]{:S(2)}, u32[]{:S(2)}) collective-permute-start(bf16[320,2560]{1,0:T(8,128)(2,1)} %shard_map.299), channel_id=1, source_target_pairs={{0,4},{1,5},{2,3},{3,2},{4,0},{5,1},{6,7},{7,6},{8,12},{9,13},{10,... | collective-permute-start | bytes 4915208 | tf_op jit(solution)/shard_map/ppermute | solution.py:945
  424.0 9.7 %collective-permute-start.48 = (bf16[1,2,2,32,640]{4,3,2,1,0:T(8,128)(2,1)S(1)}, bf16[1,2,2,32,640]{4,3,2,1,0:T(8,128)(2,1)S(1)}, u32[]{:S(2)}, u32[]{:S(2)}) collective-permute-start(bf16[1,2,2,32,640]{4,3,2,1,0:T(8,128)(2,1)S(1)} %constant_dynamic-slice_fusion.4), channel_id=1, source_target_pairs={{0,16},{2,18},{4,20},{6,22},{8,24},{10,26},{12,28},{14,30},{16,0},... | collective-permute-start | bytes 491528 | tf_op jit(solution)/shard_map/ppermute | solution.py:932
  445.0 8.2 %collective-permute-start.52 = (bf16[2,80,1280]{2,1,0:T(8,128)(2,1)S(1)}, bf16[2,80,1280]{2,1,0:T(8,128)(2,1)S(1)}, u32[]{:S(2)}, u32[]{:S(2)}) collective-permute-start(bf16[2,80,1280]{2,1,0:T(8,128)(2,1)S(1)} %dynamic-slice_bitcast_fusion.4), channel_id=1, source_target_pairs={{0,4},{2,6},{4,0},{6,2},{8,12},{10,14},{12,8},{14,10},{16,20},{18,... | collective-permute-start | bytes 1228808 | tf_op jit(solution)/shard_map/ppermute | solution.py:932
  459.4 5.7 %collective-permute-start.60 = (f32[1,800]{1,0:T(1,128)S(1)}, f32[1,800]{1,0:T(1,128)S(1)}, u32[]{:S(2)}, u32[]{:S(2)}) collective-permute-start(f32[1,800]{1,0:T(1,128)S(1)} %get-tuple-element.345), channel_id=1, source_target_pairs={{0,24},{2,26},{4,28},{6,30},{8,16},{10,18},{12,20},{14,22},{16,8},... | collective-permute-start | bytes 9608 | tf_op jit(solution)/shard_map/ppermute | solution.py:932
  463.9 20.3 %collective-permute-start.62 = (bf16[40,2560]{1,0:T(8,128)(2,1)S(1)}, bf16[40,2560]{1,0:T(8,128)(2,1)S(1)}, u32[]{:S(2)}, u32[]{:S(2)}) collective-permute-start(bf16[40,2560]{1,0:T(8,128)(2,1)S(1)} %dynamic-slice_bitcast_fusion.7), channel_id=1, source_target_pairs={{0,16},{2,18},{4,20},{6,22},{8,24},{10,26},{12,28},{14,30},{16,0},... | collective-permute-start | bytes 614408 | tf_op jit(solution)/shard_map/ppermute | solution.py:932
  (77 other events, 613.4 us)
Sparse Core Ops, SparseCore 0:
  208.0 58.8 all-gather.1
  300.5 25.4 reduce-scatter.4
  350.4 35.0 reduce-scatter.6
  387.7 39.2 reduce-scatter.8
  444.0 36.7 reduce-scatter.10
